TPU v7x, 32 devices: a whole 2x2x4 slice. The times are simulated.
32 devices in a mesh: rep: 8 (over z, y), grp: 4 (over x, core).
Axes of the slice: x: 2, y: 2, z: 4, core: 2. Of those that a mesh axis runs over, the one named last changes fastest.
Arguments:
- layer_input: bfloat16 [8, 1536, 1024], P('rep', 'grp'), may hold values from -4 to 4
- branch: int32 [8, 2], P('rep'), may hold values from 192 to 768, as said below
- attention_gain: bfloat16 [1024], P('grp'), may hold values from 0.5 to 1.5
- factor_weight: bfloat16 [1024, 800], P('grp'), may hold values from -0.3125 to 0.3125
- output_weight: bfloat16 [1024, 1024], P('grp'), may hold values from -0.375 to 0.375
- feed_gain: bfloat16 [1024], P('grp'), may hold values from 0.5 to 1.5
- gate_weight: bfloat16 [1024, 2816], P('grp'), may hold values from -0.1875 to 0.1875
- up_weight: bfloat16 [1024, 2816], P('grp'), may hold values from -0.1875 to 0.1875
- down_weight: bfloat16 [2816, 1024], P('grp'), may hold values from -0.109375 to 0.109375
- cotangent: bfloat16 [8, 1536, 1024], P('rep', 'grp'), may hold values from -4 to 4
Outputs:
- layer_output: bfloat16 [8, 1536, 1024], P('rep', 'grp')
- input_grad: float32 [8, 1536, 1024], P('rep', 'grp')
- attention_gain_grad: float32 [1024], P('grp')
- factor_weight_grad: float32 [1024, 800], P('grp')
- output_weight_grad: float32 [1024, 1024], P('grp')
- feed_gain_grad: float32 [1024], P('grp')
- gate_weight_grad: float32 [1024, 2816], P('grp')
- up_weight_grad: float32 [1024, 2816], P('grp')
- down_weight_grad: float32 [2816, 1024], P('grp')
Inputs may be any that keep to these rules, and one draw needn't show every extreme that they name: Continuation c of group g follows the first branch[g, c] prompt tokens; in every group one continuation follows all 768.
All inputs are finite; a program needn't handle non-finite values.
Results may differ from a plain program's by a relative error of at most 0.024.
The roundings to bfloat16 on the way count: a program that leaves them out, or rounds other values in their place, can miss the bound.
Values may be sent and summed in bfloat16 or wider, within the bound.
No kernel may reach another device: no remote copies, remote signals or barrier semaphores. Data moves between devices by JAX's collectives and lax.ppermute only.
A program may use at most 128 MiB of HBM per device.

v0:
```python
import jax
import jax.numpy as jnp
from jax import lax
from jax.sharding import PartitionSpec as P

HEADS = 16
HDIM = 64
QRANK = 6
KRANK = 2


highest = lax.Precision.HIGHEST


def rms_scale(values):
    return lax.rsqrt(jnp.mean(values * values, axis=-1, keepdims=True) + 1e-05)


def angles(positions, half_width):
    freqs = 10000.0 ** (-jnp.arange(half_width).astype(jnp.float32) / half_width)
    phase = positions.astype(jnp.float32)[:, None] * freqs[None, :]
    return (jnp.cos(phase), jnp.sin(phase))


def rotate(matrix, cosine, sine, ranks):
    half_cols = matrix.shape[1] // (2 * ranks)
    pieces = matrix.reshape(matrix.shape[0], ranks, 2, half_cols)
    first_half = pieces[:, :, 0]
    second_half = pieces[:, :, 1]
    cos_wide = cosine[:, None, :]
    sin_wide = sine[:, None, :]
    turned = jnp.stack(
        [
            first_half * cos_wide - second_half * sin_wide,
            second_half * cos_wide + first_half * sin_wide,
        ],
        axis=2,
    )
    return turned.reshape(matrix.shape)


def cut_points():
    first_cut = QRANK * HEADS
    second_cut = first_cut + QRANK * HDIM
    third_cut = second_cut + KRANK * HEADS
    fourth_cut = third_cut + KRANK * HDIM
    fifth_cut = fourth_cut + KRANK * HEADS
    return (first_cut, second_cut, third_cut, fourth_cut, fifth_cut)


def turn_factors(values, cosine, sine):
    cuts = cut_points()
    return jnp.concatenate(
        [
            values[:, : cuts[0]],
            rotate(values[:, cuts[0] : cuts[1]], cosine, sine, QRANK),
            values[:, cuts[1] : cuts[2]],
            rotate(values[:, cuts[2] : cuts[3]], cosine, sine, KRANK),
            values[:, cuts[3] :],
        ],
        axis=1,
    )


def expand(head_part, dim_part, ranks, head_low, head_high):
    tokens_here = head_part.shape[0]
    left_factor = head_part.reshape(tokens_here, ranks, HEADS)[:, :, head_low:head_high]
    right_factor = dim_part.reshape(tokens_here, ranks, HDIM)
    return (
        jnp.einsum("nrh,nrd->nhd", left_factor, right_factor, preferred_element_type=jnp.float32)
        / ranks
    )


def pair_grads(head_part, dim_part, grad_heads, ranks, head_low, head_high):
    tokens_here = head_part.shape[0]
    left_factor = head_part.reshape(tokens_here, ranks, HEADS)[:, :, head_low:head_high].astype(
        jnp.float32
    )
    right_factor = dim_part.reshape(tokens_here, ranks, HDIM).astype(jnp.float32)
    left_grad = jnp.einsum("nhd,nrd->nrh", grad_heads, right_factor, precision=highest) / ranks
    left_grad = jnp.pad(left_grad, ((0, 0), (0, 0), (head_low, HEADS - head_high)))
    right_grad = jnp.einsum("nhd,nrh->nrd", grad_heads, left_factor, precision=highest) / ranks
    return (
        left_grad.reshape(tokens_here, ranks * HEADS),
        right_grad.reshape(tokens_here, ranks * HDIM),
    )


def geometry(index, table, local_rows, prompt_len):
    cont_count = table.shape[0]
    inside = index < prompt_len
    segment = jnp.where(inside, -1, (index - prompt_len) // local_rows)
    chosen = jnp.sum(
        jnp.where(jnp.arange(cont_count)[None, :] == segment[:, None], table[None, :], 0), axis=1
    )
    position = jnp.where(inside, index, chosen + (index - prompt_len) % local_rows)
    limit = jnp.where(inside, 0, chosen)
    return (segment, position, limit)


def keep_state(state):
    return state


def norm_back(grad_hidden, normed, scale, gain_vector):
    grad_normed = grad_hidden * gain_vector
    gain_grad = jnp.sum(grad_hidden * normed, axis=0)
    grad_values = scale * (
        grad_normed - normed * jnp.mean(grad_normed * normed, axis=-1, keepdims=True)
    )
    return (gain_grad, grad_values)


def local(
    layer_input,
    branch,
    attention_gain,
    factor_weight,
    output_weight,
    feed_gain,
    gate_weight,
    up_weight,
    down_weight,
    cotangent,
):
    gathered = (
        lax.all_gather(attention_gain, "grp", axis=0, tiled=True),
        lax.all_gather(factor_weight, "grp", axis=0, tiled=True),
        lax.all_gather(output_weight, "grp", axis=0, tiled=True),
        lax.all_gather(feed_gain, "grp", axis=0, tiled=True),
        lax.all_gather(gate_weight, "grp", axis=0, tiled=True),
        lax.all_gather(up_weight, "grp", axis=0, tiled=True),
        lax.all_gather(down_weight, "grp", axis=0, tiled=True),
    )
    local_rows = layer_input.shape[1]
    shard_count = lax.axis_size("grp")
    shard_place = lax.axis_index("grp")
    prompt_len = local_rows * (shard_count // 2)
    token_total = local_rows * shard_count
    query_index = shard_place * local_rows + jnp.arange(local_rows, dtype=jnp.int32)
    query_seg, query_pos, query_lim = geometry(query_index, branch[0], local_rows, prompt_len)
    cuts = cut_points()
    offsets = (cuts[2] - cuts[1], cuts[3] - cuts[1], cuts[4] - cuts[1])
    residual_in = layer_input[0].astype(jnp.float32)
    scale_one = rms_scale(residual_in)
    normed_one = residual_in * scale_one
    gain_one = gathered[0].astype(jnp.float32)
    hidden_one = (normed_one * gain_one).astype(jnp.bfloat16)
    raw_factors = jnp.dot(hidden_one, gathered[1], preferred_element_type=jnp.float32)
    cosine, sine = angles(query_pos, HDIM // 2)
    factors = turn_factors(raw_factors, cosine, sine).astype(jnp.bfloat16)
    key_table = lax.all_gather(factors[:, cuts[1] :], "grp", axis=0, tiled=True)
    table_cols = key_table.shape[1]
    queries = expand(factors[:, : cuts[0]], factors[:, cuts[0] : cuts[1]], QRANK, 0, HEADS).astype(
        jnp.bfloat16
    )
    block_rows = 512
    block_count = token_total // block_rows
    head_span = HEADS // 2
    block_numbers = jnp.arange(block_count)

    def visible(number):
        key_index = number * block_rows + jnp.arange(block_rows, dtype=jnp.int32)
        key_seg = jnp.where(key_index < prompt_len, -1, (key_index - prompt_len) // local_rows)
        same_line = (key_seg[None, :] == query_seg[:, None]) & (
            key_index[None, :] <= query_index[:, None]
        )
        from_prompt = (key_seg[None, :] == -1) & (key_index[None, :] < query_lim[:, None])
        return same_line | from_prompt

    def key_values(number, head_low, head_high):
        key_piece = lax.dynamic_slice_in_dim(key_table, number * block_rows, block_rows, 0)
        keys_now = expand(
            key_piece[:, : offsets[0]],
            key_piece[:, offsets[0] : offsets[1]],
            KRANK,
            head_low,
            head_high,
        ).astype(jnp.bfloat16)
        values_now = expand(
            key_piece[:, offsets[1] : offsets[2]],
            key_piece[:, offsets[2] :],
            KRANK,
            head_low,
            head_high,
        ).astype(jnp.bfloat16)
        return (key_piece, keys_now, values_now)

    def scores(query_half, keys_now, visible_now):
        logits = jnp.einsum(
            "qhd,khd->hqk", query_half, keys_now, preferred_element_type=jnp.float32
        ) * HDIM ** (-0.5)
        return jnp.where(visible_now[None], logits, -1e30)

    def half_forward(head_low, head_high):
        query_half = queries[:, head_low:head_high]

        def totals_step(carry, number):
            visible_now = visible(number)

            def totals_update(state):
                running_top, running_mass = state
                _, keys_now, _ = key_values(number, head_low, head_high)
                logits = scores(query_half, keys_now, visible_now)
                new_top = jnp.maximum(running_top, jnp.max(logits, axis=-1))
                new_mass = running_mass * jnp.exp(running_top - new_top) + jnp.sum(
                    jnp.exp(logits - new_top[..., None]), axis=-1
                )
                return (new_top, new_mass)

            return (lax.cond(jnp.any(visible_now), totals_update, keep_state, carry), None)

        start_state = (
            jnp.full((head_span, local_rows), -1e30, jnp.float32),
            jnp.zeros((head_span, local_rows), jnp.float32),
        )
        (final_top, final_mass), _ = lax.scan(totals_step, start_state, block_numbers)
        log_total = final_top + jnp.log(final_mass)

        def output_step(carry, number):
            visible_now = visible(number)

            def output_update(state):
                main_sum, rest_sum = state
                _, keys_now, values_now = key_values(number, head_low, head_high)
                probs = jnp.exp(scores(query_half, keys_now, visible_now) - log_total[..., None])
                probs_low = probs.astype(jnp.bfloat16)
                probs_rest = (probs - probs_low.astype(jnp.float32)).astype(jnp.bfloat16)
                main_sum = main_sum + jnp.einsum(
                    "hqk,khd->qhd", probs_low, values_now, preferred_element_type=jnp.float32
                )
                rest_sum = rest_sum + jnp.einsum(
                    "hqk,khd->qhd", probs_rest, values_now, preferred_element_type=jnp.float32
                )
                return (main_sum, rest_sum)

            return (lax.cond(jnp.any(visible_now), output_update, keep_state, carry), None)

        zero_out = jnp.zeros((local_rows, head_span, HDIM), jnp.float32)
        (main_sum, rest_sum), _ = lax.scan(output_step, (zero_out, zero_out), block_numbers)
        return (log_total, main_sum, main_sum + rest_sum)

    first_pass = half_forward(0, head_span)
    second_pass = half_forward(head_span, HEADS)
    attended = (
        jnp.concatenate([first_pass[1], second_pass[1]], axis=1)
        .reshape(local_rows, HEADS * HDIM)
        .astype(jnp.bfloat16)
    )
    middle = residual_in + jnp.dot(attended, gathered[2], preferred_element_type=jnp.float32)
    scale_two = rms_scale(middle)
    normed_two = middle * scale_two
    gain_two = gathered[3].astype(jnp.float32)
    hidden_two = (normed_two * gain_two).astype(jnp.bfloat16)
    gate_values = jnp.dot(hidden_two, gathered[4], preferred_element_type=jnp.float32)
    up_values = jnp.dot(hidden_two, gathered[5], preferred_element_type=jnp.float32)
    sigmoid_gate = jax.nn.sigmoid(gate_values)
    active = (gate_values * sigmoid_gate * up_values).astype(jnp.bfloat16)
    result = middle + jnp.dot(active, gathered[6], preferred_element_type=jnp.float32)
    upstream = cotangent[0]
    down_grad = jnp.einsum("tf,td->fd", active, upstream, preferred_element_type=jnp.float32)
    active_grad = jnp.einsum("td,fd->tf", upstream, gathered[6], preferred_element_type=jnp.float32)
    gate_grad = (
        active_grad * up_values * sigmoid_gate * (1.0 + gate_values * (1.0 - sigmoid_gate))
    ).astype(jnp.bfloat16)
    up_grad = (active_grad * gate_values * sigmoid_gate).astype(jnp.bfloat16)
    gate_weight_grad = jnp.einsum(
        "td,tf->df", hidden_two, gate_grad, preferred_element_type=jnp.float32
    )
    up_weight_grad = jnp.einsum(
        "td,tf->df", hidden_two, up_grad, preferred_element_type=jnp.float32
    )
    hidden_two_grad = jnp.einsum(
        "tf,df->td", gate_grad, gathered[4], preferred_element_type=jnp.float32
    ) + jnp.einsum("tf,df->td", up_grad, gathered[5], preferred_element_type=jnp.float32)
    feed_gain_grad, middle_grad = norm_back(
        hidden_two_grad, normed_two, scale_two, gathered[3].astype(jnp.float32)
    )
    middle_grad = middle_grad + upstream.astype(jnp.float32)
    branch_grad = middle_grad.astype(jnp.bfloat16)
    output_weight_grad = jnp.einsum(
        "tf,td->fd", attended, branch_grad, preferred_element_type=jnp.float32
    )
    grad_heads = (
        jnp.einsum("td,fd->tf", branch_grad, gathered[2], preferred_element_type=jnp.float32)
        .astype(jnp.bfloat16)
        .reshape(local_rows, HEADS, HDIM)
    )

    def half_backward(head_low, head_high, log_total, exact_half):
        query_half = queries[:, head_low:head_high]
        grad_half = grad_heads[:, head_low:head_high]
        delta = jnp.sum(grad_half.astype(jnp.float32) * exact_half, axis=-1).T

        def grad_step(carry, number):
            visible_now = visible(number)

            def grad_update(query_grad):
                key_piece, keys_now, values_now = key_values(number, head_low, head_high)
                probs = jnp.exp(scores(query_half, keys_now, visible_now) - log_total[..., None])
                prob_grad = jnp.einsum(
                    "qhd,khd->hqk", grad_half, values_now, preferred_element_type=jnp.float32
                )
                score_grad = (probs * (prob_grad - delta[..., None])).astype(jnp.bfloat16)
                query_grad = query_grad + jnp.einsum(
                    "hqk,khd->qhd", score_grad, keys_now, preferred_element_type=jnp.float32
                ) * HDIM ** (-0.5)
                key_grad = jnp.einsum(
                    "hqk,qhd->khd", score_grad, query_half, preferred_element_type=jnp.float32
                ) * HDIM ** (-0.5)
                value_grad = jnp.einsum(
                    "hqk,qhd->khd",
                    probs.astype(jnp.bfloat16),
                    grad_half,
                    preferred_element_type=jnp.float32,
                )
                key_heads, key_dims = pair_grads(
                    key_piece[:, : offsets[0]],
                    key_piece[:, offsets[0] : offsets[1]],
                    key_grad,
                    KRANK,
                    head_low,
                    head_high,
                )
                value_heads, value_dims = pair_grads(
                    key_piece[:, offsets[1] : offsets[2]],
                    key_piece[:, offsets[2] :],
                    value_grad,
                    KRANK,
                    head_low,
                    head_high,
                )
                return (
                    query_grad,
                    jnp.concatenate([key_heads, key_dims, value_heads, value_dims], axis=1),
                )

            def skip_block(query_grad):
                return (query_grad, jnp.zeros((block_rows, table_cols), jnp.float32))

            return lax.cond(jnp.any(visible_now), grad_update, skip_block, carry)

        query_grad, table_grads = lax.scan(
            grad_step, jnp.zeros((local_rows, head_span, HDIM), jnp.float32), block_numbers
        )
        return (query_grad, table_grads.reshape(token_total, table_cols))

    first_back = half_backward(0, head_span, first_pass[0], first_pass[2])
    second_back = half_backward(head_span, HEADS, second_pass[0], second_pass[2])
    query_grad = jnp.concatenate([first_back[0], second_back[0]], axis=1)
    own_table_grad = lax.psum_scatter(
        (first_back[1] + second_back[1]).astype(jnp.bfloat16),
        "grp",
        scatter_dimension=0,
        tiled=True,
    ).astype(jnp.float32)
    query_heads, query_dims = pair_grads(
        factors[:, : cuts[0]], factors[:, cuts[0] : cuts[1]], query_grad, QRANK, 0, HEADS
    )
    factor_grad = jnp.concatenate([query_heads, query_dims, own_table_grad], axis=1)
    raw_grad = turn_factors(factor_grad, cosine, -sine).astype(jnp.bfloat16)
    factor_weight_grad = jnp.einsum(
        "td,tf->df", hidden_one, raw_grad, preferred_element_type=jnp.float32
    )
    hidden_one_grad = jnp.einsum(
        "tf,df->td", raw_grad, gathered[1], preferred_element_type=jnp.float32
    )
    attention_gain_grad, input_part = norm_back(
        hidden_one_grad, normed_one, scale_one, gathered[0].astype(jnp.float32)
    )
    input_grad = middle_grad + input_part
    shard_grads = (
        lax.psum_scatter(
            attention_gain_grad.astype(jnp.bfloat16), "grp", scatter_dimension=0, tiled=True
        ).astype(jnp.float32),
        lax.psum_scatter(
            factor_weight_grad.astype(jnp.bfloat16), "grp", scatter_dimension=0, tiled=True
        ).astype(jnp.float32),
        lax.psum_scatter(
            output_weight_grad.astype(jnp.bfloat16), "grp", scatter_dimension=0, tiled=True
        ).astype(jnp.float32),
        lax.psum_scatter(
            feed_gain_grad.astype(jnp.bfloat16), "grp", scatter_dimension=0, tiled=True
        ).astype(jnp.float32),
        lax.psum_scatter(
            gate_weight_grad.astype(jnp.bfloat16), "grp", scatter_dimension=0, tiled=True
        ).astype(jnp.float32),
        lax.psum_scatter(
            up_weight_grad.astype(jnp.bfloat16), "grp", scatter_dimension=0, tiled=True
        ).astype(jnp.float32),
        lax.psum_scatter(
            down_grad.astype(jnp.bfloat16), "grp", scatter_dimension=0, tiled=True
        ).astype(jnp.float32),
    )
    final_grads = (
        lax.psum(shard_grads[0].astype(jnp.bfloat16), "rep").astype(jnp.float32),
        lax.psum(shard_grads[1].astype(jnp.bfloat16), "rep").astype(jnp.float32),
        lax.psum(shard_grads[2].astype(jnp.bfloat16), "rep").astype(jnp.float32),
        lax.psum(shard_grads[3].astype(jnp.bfloat16), "rep").astype(jnp.float32),
        lax.psum(shard_grads[4].astype(jnp.bfloat16), "rep").astype(jnp.float32),
        lax.psum(shard_grads[5].astype(jnp.bfloat16), "rep").astype(jnp.float32),
        lax.psum(shard_grads[6].astype(jnp.bfloat16), "rep").astype(jnp.float32),
    )
    return (
        result.astype(jnp.bfloat16)[None],
        input_grad[None],
        final_grads[0],
        final_grads[1],
        final_grads[2],
        final_grads[3],
        final_grads[4],
        final_grads[5],
        final_grads[6],
    )


def solution(mesh):
    in_specs = (
        P("rep", "grp", None),
        P("rep", None),
        P("grp"),
        P("grp", None),
        P("grp", None),
        P("grp"),
        P("grp", None),
        P("grp", None),
        P("grp", None),
        P("rep", "grp", None),
    )
    out_specs = (
        P("rep", "grp", None),
        P("rep", "grp", None),
        P("grp"),
        P("grp", None),
        P("grp", None),
        P("grp"),
        P("grp", None),
        P("grp", None),
        P("grp", None),
    )
    return jax.shard_map(local, mesh=mesh, in_specs=in_specs, out_specs=out_specs, check_vma=False)
```

profile of v0, /device:TPU:0, one launch (start us, length us, event | category | flops | bytes accessed | tf_op | source)
XLA Modules:
  0.0 1229.1 jit_solution(16655373652148109157)
XLA Ops:
  10.8 6.0 all-gather
  23.9 8.6 all-gather.8.cloned.1.call-done
  35.3 10.2 all_gather.26
  49.0 14.9 %while.102 = (s32[]{:T(128)}, f32[8,384]{1,0:T(8,128)S(1)}, f32[8,384]{1,0:T(8,128)S(1)}, s32[3]{0:T(128)S(1)}, s32[384]{0:T(512)S(1)}, /*index=5*/bf16[1536,320...) while((s32[]{:T(128)}, f32[8,384]{1,0:T(8,128)S(1)}, ...), condition=%wide.region_8.9_spmd.clone.clone, body=%wide.region_2.8_spmd.clone.clone.sunk | while | flops 215309312 | bytes 15594281 | solution.py:218
  51.9 6.0 conditional.24
  66.4 35.9 %while.103 = (s32[]{:T(128)}, f32[384,8,64]{0,2,1:T(8,128)}, f32[384,8,64]{0,2,1:T(8,128)}, s32[3]{0:T(128)}, s32[384]{0:T(512)S(1)}, /*index=5*/bf16[1536,320]{...) while((s32[]{:T(128)}, f32[384,8,64]{0,2,1:T(8,128)}, ...), condition=%wide.region_13.14_spmd.clone.clone, body=%wide.region_9.13_spmd.clone.clone.sunk | while | flops 626738176 | bytes 35529648 | solution.py:241
  71.1 22.6 %conditional.25 = ((f32[384,8,64]{0,2,1:T(8,128)}, f32[384,8,64]{0,2,1:T(8,128)})) conditional(s32[]{:T(128)} %convert_element_type.413, (f32[384,8,64]{0,2,1:T(8,128)}, f32[384,8,64]{0,2,1:T(8,128)}) %tuple.365, (s32[]{:T(128)}, bf16[1536,320]{0,1:T(8,128)(2,1)}, pred[384,512]{0,1:T(8,128)(4,1)}, bf16[384,8,64]{0,2,1:T(8,128)(2,1)S(1)}, ...), branch_computations={%region_11.11_spmd, %region_12.12_spmd} | conditional | flops 625344512 | bytes 35315920 | solution.py:238
  106.5 16.2 %while.104 = (s32[]{:T(128)}, f32[8,384]{1,0:T(8,128)S(1)}, f32[8,384]{1,0:T(8,128)S(1)}, s32[3]{0:T(128)S(1)}, s32[384]{0:T(512)S(1)}, /*index=5*/bf16[1536,320...) while((s32[]{:T(128)}, f32[8,384]{1,0:T(8,128)S(1)}, ...), condition=%wide.region_20.21_spmd.clone.clone, body=%wide.region_14.20_spmd.clone.clone.sunk | while | flops 215309312 | bytes 15594281 | solution.py:218
  109.7 7.1 conditional.26
  125.2 36.8 %while.105 = (s32[]{:T(128)}, f32[384,8,64]{0,2,1:T(8,128)}, f32[384,8,64]{0,2,1:T(8,128)}, s32[3]{0:T(128)}, s32[384]{0:T(512)S(1)}, /*index=5*/bf16[1536,320]{...) while((s32[]{:T(128)}, f32[384,8,64]{0,2,1:T(8,128)}, ...), condition=%wide.region_25.26_spmd.clone.clone, body=%wide.region_21.25_spmd.clone.clone.sunk | while | flops 626738176 | bytes 35529648 | solution.py:241
  129.4 23.6 %conditional.27 = ((f32[384,8,64]{0,2,1:T(8,128)}, f32[384,8,64]{0,2,1:T(8,128)})) conditional(s32[]{:T(128)} %convert_element_type.415, (f32[384,8,64]{0,2,1:T(8,128)}, f32[384,8,64]{0,2,1:T(8,128)}) %tuple.377, (s32[]{:T(128)}, bf16[1536,320]{0,1:T(8,128)(2,1)}, pred[384,512]{0,1:T(8,128)(4,1)}, bf16[384,8,64]{0,2,1:T(8,128)(2,1)}, ...), branch_computations={%region_23.23_spmd, %region_24.24_spmd} | conditional | flops 625344512 | bytes 35315920 | solution.py:238
  167.7 7.7 fusion.214
  175.3 7.2 fusion.215
  182.5 9.1 all-gather.16.cloned.1.call-done
  191.6 10.2 multiply_convert_fusion.22
  201.8 6.7 fusion.216
  221.8 96.9 %while.106 = (s32[]{:T(128)}, f32[384,8,64]{0,2,1:T(8,128)}, f32[3,512,320]{1,2,0:T(8,128)}, s32[3]{0:T(128)}, s32[384]{0:T(512)S(1)}, /*index=5*/bf16[1536,320]...) while((s32[]{:T(128)}, f32[384,8,64]{0,2,1:T(8,128)}, ...), condition=%wide.region_33.34_spmd.clone.clone, body=%wide.region_29.33_spmd.clone.clone.sunk | while | flops 1053885440 | bytes 72340984 | solution.py:344
  226.3 63.3 %conditional.28 = (f32[384,8,64]{0,2,1:T(8,128)}, f32[1,512,320]{1,2,0:T(8,128)}) conditional(s32[]{:T(128)} %convert_element_type.416, f32[384,8,64]{0,2,1:T(8,128)} %get-tuple-element.2557, (s32[]{:T(128)}, bf16[1536,320]{0,1:T(8,128)(2,1)}, pred[384,512]{0,1:T(8,128)(4,1)}, bf16[384,8,64]{0,2,1:T(8,128)(2,1)S(1)}, f32[8,384]{1,0:T(8,128)S(1)}, ...), branch_computations={%region_31.31_spmd, %region_32.32_spmd} | conditional | flops 1052491776 | bytes 70816016 | solution.py:342
  321.8 81.0 %while.107 = (s32[]{:T(128)}, f32[384,8,64]{0,2,1:T(8,128)}, f32[3,512,320]{1,2,0:T(8,128)}, s32[3]{0:T(128)}, s32[384]{0:T(512)S(1)}, /*index=5*/bf16[1536,320]...) while((s32[]{:T(128)}, f32[384,8,64]{0,2,1:T(8,128)}, ...), condition=%wide.region_39.40_spmd.clone.clone, body=%wide.region_35.39_spmd.clone.clone.sunk | while | flops 1053885440 | bytes 72193544 | solution.py:344
  326.1 60.0 %conditional.29 = (f32[384,8,64]{0,2,1:T(8,128)}, f32[1,512,320]{1,2,0:T(8,128)}) conditional(s32[]{:T(128)} %convert_element_type.417, f32[384,8,64]{0,2,1:T(8,128)} %get-tuple-element.2518, (s32[]{:T(128)}, bf16[1536,320]{0,1:T(8,128)(2,1)}, pred[384,512]{0,1:T(8,128)(4,1)}, bf16[384,8,64]{0,2,1:T(8,128)(2,1)}, f32[8,384]{1,0:T(8,128)S(1)}, ...), branch_computations={%region_37.37_spmd, %region_38.38_spmd} | conditional | flops 1052491776 | bytes 70668576 | solution.py:342
  430.5 354.4 %reduce-scatter.7.cloned.1.call-done = bf16[384,320]{1,0:T(8,128)(2,1)} async-done(((bf16[1536,320]{1,0:T(8,128)(2,1)}), bf16[384,320]{1,0:T(8,128)(2,1)}) %reduce-scatter.7.cloned.1.call-update) | async-done | bytes 245776 | tf_op jit(solution)/shard_map/reduce_scatter | solution.py:352
  793.7 6.9 convolution_convert_fusion.2
  800.7 6.9 convolution_convert_fusion.1
  808.7 6.8 convolution_convert_fusion
  819.0 31.2 %reduce-scatter.9.cloned.1.call-done = bf16[256,800]{0,1:T(8,128)(2,1)} async-done(((bf16[1024,800]{0,1:T(8,128)(2,1)}), bf16[256,800]{0,1:T(8,128)(2,1)}) %reduce-scatter.9.cloned.1.call-update) | async-done | bytes 409616 | tf_op jit(solution)/shard_map/reduce_scatter | solution.py:377
  850.2 57.6 %reduce-scatter.13.cloned.1.call-done = bf16[256,2816]{1,0:T(8,128)(2,1)} async-done(((bf16[1024,2816]{1,0:T(8,128)(2,1)}), bf16[256,2816]{1,0:T(8,128)(2,1)}) %reduce-scatter.13.cloned.1.call-update) | async-done | bytes 1441808 | tf_op jit(solution)/shard_map/reduce_scatter | solution.py:386
  907.8 57.3 %reduce-scatter.15.cloned.1.call-done = bf16[256,2816]{1,0:T(8,128)(2,1)} async-done(((bf16[1024,2816]{1,0:T(8,128)(2,1)}), bf16[256,2816]{1,0:T(8,128)(2,1)}) %reduce-scatter.15.cloned.1.call-update) | async-done | bytes 1441808 | tf_op jit(solution)/shard_map/reduce_scatter | solution.py:389
  965.1 57.6 %reduce-scatter.17.cloned.1.call-done = bf16[704,1024]{1,0:T(8,128)(2,1)} async-done(((bf16[2816,1024]{1,0:T(8,128)(2,1)}), bf16[704,1024]{1,0:T(8,128)(2,1)}) %reduce-scatter.17.cloned.1.call-update) | async-done | bytes 1441808 | tf_op jit(solution)/shard_map/reduce_scatter | solution.py:392
  1024.6 6.7 fusion.165
  1034.9 6.0 all-reduce.8
  1041.1 22.2 %all-reduce.6 = (bf16[256]{0:T(256)(128)(2,1)S(1)}, bf16[256]{0:T(256)(128)(2,1)S(1)}) all-reduce(bf16[256]{0:T(256)(128)(2,1)S(1)} %dynamic-slice.1, bf16[256]{0:T(256)(128)(2,1)S(1)} %dynamic-slice.3), channel_id=1, replica_groups=mesh['rep'=8,'grp'=4] {'rep'}, use_global_device_ids=true, to_apply=%region_44.45 | all-reduce | flops 512 | bytes 2048 | tf_op jit(solution)/shard_map/psum | solution.py:397
  1067.5 145.4 %all-reduce.11.cloned.1.call-done = (bf16[256,800]{0,1:T(8,128)(2,1)}, bf16[256,1024]{1,0:T(8,128)(2,1)}, bf16[256,2816]{1,0:T(8,128)(2,1)}, bf16[256,2816]{1,0:T(8,128)(2,1)}, bf16[704,1024]{1,0:T(8,128)(2,1)}) async-done(((bf16[256,800]{0,1:T(8,128)(2,1)}, bf16[256,1024]{1,0:T(8,128)(2,1)}, bf16[256,2816]{1,0:T(8,128)(2,1)}, bf16[256,2816]{1,0:T(8,128)(2,1)}, bf16[704,1024]{1,0:T(8,128)(2,1)}), ...) | async-done | bytes 5259280 | tf_op jit(solution)/shard_map/psum | solution.py:398
  (477 shorter events, 349.5 us)
Async XLA Ops:
  7.2 25.3 %all-gather.8.cloned.1.call-start = ((), (), s32[]{:S(2)}) async-start(), calls=%async_computation.6 | async-start | bytes 2048000 | tf_op jit(solution)/shard_map/all_gather | solution.py:129
  7.9 156.5 %all-gather.10.cloned.1.call-start = ((), (), s32[]{:S(2)}) async-start(), calls=%async_computation.7 | async-start | bytes 2621440 | tf_op jit(solution)/shard_map/all_gather | solution.py:130
  8.7 8.1 copy-start.13
  8.7 159.0 %all-gather.12.cloned.1.call-start = ((), (), s32[]{:S(2)}) async-start(), calls=%async_computation.8 | async-start | bytes 7208960 | tf_op jit(solution)/shard_map/all_gather | solution.py:132
  9.4 7.6 copy-start.58
  9.4 165.9 %all-gather.14.cloned.1.call-start = ((), (), s32[]{:S(2)}) async-start(), calls=%async_computation.9 | async-start | bytes 7208960 | tf_op jit(solution)/shard_map/all_gather | solution.py:133
  10.0 181.6 %all-gather.16.cloned.1.call-start = ((), (), s32[]{:S(2)}) async-start(), calls=%async_computation.10 | async-start | bytes 7208960 | tf_op jit(solution)/shard_map/all_gather | solution.py:134
  10.6 774.2 %reduce-scatter.7.cloned.1.call-start = ((), (), s32[]{:S(2)}) async-start(), calls=%async_computation.11 | async-start | bytes 1474560 | tf_op jit(solution)/shard_map/reduce_scatter | solution.py:352
  16.8 18.2 %copy-start.44 = (f32[4,1,256]{2,1,0:T(1,128)}, f32[4,1,256]{2,1,0:T(1,128)S(1)}, u32[]{:S(2)}) copy-start(f32[4,1,256]{2,1,0:T(1,128)S(1)} %convert_element_type.281) | copy-start | bytes 12292
  17.1 18.0 %copy-start.51 = (f32[384]{0:T(512)}, f32[384]{0:T(512)S(1)}, u32[]{:S(2)}) copy-start(f32[384]{0:T(512)S(1)} %add_rsqrt_fusion.1) | copy-start | bytes 4612
  23.9 21.6 %copy-start.33 = (f32[384,32]{0,1:T(8,128)}, f32[384,32]{0,1:T(8,128)S(1)}, u32[]{:S(2)}) copy-start(f32[384,32]{0,1:T(8,128)S(1)} %get-tuple-element.1907) | copy-start | bytes 147460
  167.4 44.3 %copy-start.8 = (f32[384,1024]{1,0:T(8,128)}, f32[384,1024]{1,0:T(8,128)S(1)}, u32[]{:S(2)}) copy-start(f32[384,1024]{1,0:T(8,128)S(1)} %get-tuple-element.1913) | copy-start | bytes 4718596
  167.6 7.7 copy-start.35
  175.3 16.3 %copy-start.37 = (bf16[1,384,1024]{2,1,0:T(8,128)(2,1)S(1)}, bf16[1,384,1024]{2,1,0:T(8,128)(2,1)}, u32[]{:S(2)}) copy-start(bf16[1,384,1024]{2,1,0:T(8,128)(2,1)} %param.43) | copy-start | bytes 2359300
  201.8 6.7 copy-start.61
  201.8 6.7 copy-start.60
  201.8 6.7 copy-start.55
  356.4 6.7 copy-start.22
  406.8 412.3 %reduce-scatter.11.cloned.1.call-start = ((), (), s32[]{:S(2)}) async-start(), calls=%async_computation.13 | async-start | bytes 2621440 | tf_op jit(solution)/shard_map/reduce_scatter | solution.py:380
  409.9 440.3 %reduce-scatter.9.cloned.1.call-start = ((), (), s32[]{:S(2)}) async-start(), calls=%async_computation.12 | async-start | bytes 2048000 | tf_op jit(solution)/shard_map/reduce_scatter | solution.py:377
  421.6 8.0 copy-start.34
  421.6 8.0 copy-start.41
  429.6 360.5 %copy-start.15 = (bf16[1,384,1024]{2,1,0:T(8,128)(2,1)S(1)}, bf16[1,384,1024]{2,1,0:T(8,128)(2,1)}, u32[]{:S(2)}) copy-start(bf16[1,384,1024]{2,1,0:T(8,128)(2,1)} %param.34) | copy-start | bytes 2359300
  429.6 360.5 %copy-start.45 = (f32[4,1,256]{2,1,0:T(1,128)S(1)}, f32[4,1,256]{2,1,0:T(1,128)}, u32[]{:S(2)}) copy-start(f32[4,1,256]{2,1,0:T(1,128)} %copy-done.44) | copy-start | bytes 12292
  429.7 360.5 %copy-start.52 = (f32[384]{0:T(512)S(1)}, f32[384]{0:T(512)}, u32[]{:S(2)}) copy-start(f32[384]{0:T(512)} %copy-done.51) | copy-start | bytes 4612
  793.7 114.2 %reduce-scatter.13.cloned.1.call-start = ((), (), s32[]{:S(2)}) async-start(), calls=%async_computation.14 | async-start | bytes 7208960 | tf_op jit(solution)/shard_map/reduce_scatter | solution.py:386
  800.6 164.5 %reduce-scatter.15.cloned.1.call-start = ((), (), s32[]{:S(2)}) async-start(), calls=%async_computation.15 | async-start | bytes 7208960 | tf_op jit(solution)/shard_map/reduce_scatter | solution.py:389
  807.6 215.1 %reduce-scatter.17.cloned.1.call-start = ((), (), s32[]{:S(2)}) async-start(), calls=%async_computation.16 | async-start | bytes 7208960 | tf_op jit(solution)/shard_map/reduce_scatter | solution.py:392
  815.5 397.4 %all-reduce.11.cloned.1.call-start = ((), (), s32[]{:S(2)}) async-start(), calls=%async_computation.17 | async-start | bytes 10518528 | tf_op jit(solution)/shard_map/psum | solution.py:398
  1024.6 6.7 copy-start.16
  1024.6 6.7 copy-start.56
  1031.4 33.1 %copy-start.17 = (bf16[1,384,1024]{2,1,0:T(8,128)(2,1)S(1)}, bf16[1,384,1024]{2,1,0:T(8,128)(2,1)}, u32[]{:S(2)}) copy-start(bf16[1,384,1024]{2,1,0:T(8,128)(2,1)} %param.34) | copy-start | bytes 2359300
  (42 other events, 119.9 us)
Sparse Core Ops, SparseCore 0:
  9.6 22.9 all-gather.7
  34.1 22.7 all-gather.9
  58.4 43.4 all-gather.11
  103.3 43.3 all-gather.13
  148.2 43.3 all-gather.15
  406.9 377.9 reduce-scatter.6
  787.5 31.4 reduce-scatter.10
  821.6 28.5 reduce-scatter.8
  852.9 54.8 reduce-scatter.12
  910.2 54.8 reduce-scatter.14
  967.8 54.8 reduce-scatter.16
  1026.9 185.9 all-reduce.10
where the time goes:
time: 1240 us; the launch traced here: 1230 us
  waiting for transfers between devices  728 us (59%)
  matrix products  203 us (16%)
  local copies, waits for them, and re-layouts  130 us (10%)
  other arithmetic  59.7 us (5%)
  blocking collectives  49.8 us (4%)
  loops' own time  43 us (3%)
  between operations  15.8 us (1%)
    reduce_scatter x1, waiting for transfers between devices, local(): lax.psum_scatter((first_back[1] + second_back[1]).astype(jnp.bfloat16), '...  354 us
    psum x1, waiting for transfers between devices, local(): lax.psum(shard_grads[1].astype(jnp.bfloat16), 'rep').astype(jnp.float32)  145 us
    reduce_scatter x1, waiting for transfers between devices, local(): lax.psum_scatter(gate_weight_grad.astype(jnp.bfloat16), 'grp', scatter_di...  57.6 us
    reduce_scatter x1, waiting for transfers between devices, local(): lax.psum_scatter(down_grad.astype(jnp.bfloat16), 'grp', scatter_dimension...  57.6 us
    reduce_scatter x1, waiting for transfers between devices, local(): lax.psum_scatter(up_weight_grad.astype(jnp.bfloat16), 'grp', scatter_dime...  57.3 us
    reduce_scatter x1, waiting for transfers between devices, local(): lax.psum_scatter(factor_weight_grad.astype(jnp.bfloat16), 'grp', scatter_...  31.2 us
  transfers between devices with their start and end apart: 12, of which 9 were waited for; matrix products, arithmetic and copies ran while one was open for 15% of the time, Pallas kernels for 0%

commit v1 on v0

v1 whole, which is shorter than its diff:
```python
import functools

import jax
import jax.numpy as jnp
import numpy as np
from jax import lax
from jax.experimental import pallas as pl
from jax.experimental.pallas import tpu as pltpu
from jax.sharding import PartitionSpec as P

HEADS = 16
HDIM = 64
QRANK = 6
KRANK = 2
HALF = HDIM // 2
QCOLS = QRANK * HEADS + QRANK * HDIM
KVCOLS = 2 * (KRANK * HEADS + KRANK * HDIM)
AQ, BQ = 0, QRANK * HEADS
AK, BK = 0, KRANK * HEADS
AV = BK + KRANK * HDIM
BV = AV + KRANK * HEADS
SCALE = HDIM**-0.5
EXP_SCALE = SCALE * float(np.log2(np.e))
NEG = -1e30
DEPTH = 128
EPS = 1e-05
VMEM_LIMIT = 60 * 2**20

f32 = jnp.float32
bf16 = jnp.bfloat16
NN = (((1,), (0,)), ((), ()))
NT = (((1,), (1,)), ((), ()))
TN = (((0,), (0,)), ((), ()))


def mm(left, right, dims=NN):
    return lax.dot_general(left, right, dims, preferred_element_type=f32)


def vmem():
    return pl.BlockSpec(memory_space=pltpu.VMEM)


def smem():
    return pl.BlockSpec(memory_space=pltpu.SMEM)


def params():
    return pltpu.CompilerParams(vmem_limit_bytes=VMEM_LIMIT)


def cost(flops, nbytes):
    return pl.CostEstimate(flops=int(flops), bytes_accessed=int(nbytes), transcendentals=0)


def turn(part, cosine, sine):
    first, second = part[:HALF], part[HALF:]
    return first * cosine - second * sine, second * cosine + first * sine


def front_kernel(x_ref, gain_ref, w_ref, cos_ref, sin_ref, fac_ref, hid_ref):
    xf = x_ref[...].astype(f32)
    scale = lax.rsqrt(jnp.mean(xf * xf, axis=-1, keepdims=True) + EPS)
    hidden = (xf * scale * gain_ref[...]).astype(bf16)
    hid_ref[...] = jnp.transpose(hidden)
    raw = jnp.transpose(mm(hidden, w_ref[...]))
    cosine, sine = cos_ref[...], sin_ref[...]
    fac_ref[...] = raw.astype(bf16)
    starts = [BQ + r * HDIM for r in range(QRANK)] + [QCOLS + BK + r * HDIM for r in range(KRANK)]
    for at in starts:
        one, two = turn(raw[at : at + HDIM], cosine, sine)
        fac_ref[at : at + HALF, :] = one.astype(bf16)
        fac_ref[at + HALF : at + HDIM, :] = two.astype(bf16)


def front(x, gain, weight, cosine, sine):
    rows, width = x.shape
    cols = weight.shape[1]
    return pl.pallas_call(
        front_kernel,
        out_shape=[
            jax.ShapeDtypeStruct((cols, rows), bf16),
            jax.ShapeDtypeStruct((width, rows), bf16),
        ],
        in_specs=[vmem()] * 5,
        out_specs=[vmem()] * 2,
        compiler_params=params(),
        cost_estimate=cost(2 * rows * width * cols, 4 * width * (cols + rows)),
        name="front",
    )(x, gain, weight, cosine, sine)


def load_factors(fac_ref, kv_ref, facf, kvf, qT, me, npc):
    facf[...] = fac_ref[...].astype(f32)

    def load(j, _):
        kvf[j] = kv_ref[j].astype(f32)
        return 0

    lax.fori_loop(0, npc, load, 0)
    load(me, 0)
    row = lax.broadcasted_iota(jnp.int32, (DEPTH - HDIM, qT.shape[1]), 0)
    qT[HDIM:DEPTH, :] = jnp.where(row == 0, 1.0, 0.0).astype(bf16)


def build_query(facf, qT, h):
    total = facf[pl.ds(AQ + h, 1), :] * facf[BQ : BQ + HDIM, :]
    for r in range(1, QRANK):
        total += facf[pl.ds(AQ + r * HEADS + h, 1), :] * facf[BQ + r * HDIM : BQ + (r + 1) * HDIM, :]
    qT[0:HDIM, :] = (total * (1.0 / QRANK)).astype(bf16)


def build_pair(kvf, j, h, a_at, b_at):
    total = kvf[j, pl.ds(a_at + h, 1), :] * kvf[j, b_at : b_at + HDIM, :]
    for r in range(1, KRANK):
        total += (
            kvf[j, pl.ds(a_at + r * HEADS + h, 1), :]
            * kvf[j, b_at + r * HDIM : b_at + (r + 1) * HDIM, :]
        )
    return (total * (1.0 / KRANK)).astype(bf16)


def build_key(kvf, kT, j, h, limit):
    span = kT.shape[1]
    kT[0:HDIM, :] = build_pair(kvf, j, h, AK, BK)
    if limit is None:
        kT[HDIM:DEPTH, :] = jnp.zeros((DEPTH - HDIM, span), bf16)
    else:
        row = lax.broadcasted_iota(jnp.int32, (DEPTH - HDIM, span), 0)
        key = j * span + lax.broadcasted_iota(jnp.int32, (DEPTH - HDIM, span), 1)
        kT[HDIM:DEPTH, :] = jnp.where((row == 0) & (key >= limit), NEG, 0.0).astype(bf16)


def causal(scores):
    key = lax.broadcasted_iota(jnp.int32, scores.shape, 0)
    query = lax.broadcasted_iota(jnp.int32, scores.shape, 1)
    return jnp.where(key <= query, scores, NEG)


def attend_kernel(info_ref, fac_ref, kv_ref, out_ref, lse_ref, facf, kvf, qT, kT, s_ref):
    me, npc, limit = info_ref[0], info_ref[1], info_ref[2]
    rows = fac_ref.shape[1]
    load_factors(fac_ref, kv_ref, facf, kvf, qT, me, npc)

    def head(h, _):
        build_query(facf, qT, h)

        def chunk(j, top):
            build_key(kvf, kT, j, h, limit)
            scores = mm(kT[...], qT[...], TN)
            s_ref[j] = scores
            return jnp.maximum(top, jnp.max(scores, axis=0, keepdims=True))

        top = lax.fori_loop(0, npc, chunk, jnp.full((1, rows), NEG, f32))
        build_key(kvf, kT, me, h, None)
        scores = causal(mm(kT[...], qT[...], TN))
        s_ref[npc] = scores
        top = jnp.maximum(top, jnp.max(scores, axis=0, keepdims=True)) * EXP_SCALE

        def weigh(j, mass):
            probs = jnp.exp2(s_ref[j] * EXP_SCALE - top)
            s_ref[j] = probs
            return mass + jnp.sum(probs, axis=0, keepdims=True)

        mass = lax.fori_loop(0, npc + 1, weigh, jnp.zeros((1, rows), f32))
        lse_ref[pl.ds(h, 1), :] = top + jnp.log2(mass)
        share = 1.0 / mass

        def gather(j, total):
            at = jnp.where(j == npc, me, j)
            return total + mm(build_pair(kvf, at, h, AV, BV), (s_ref[j] * share).astype(bf16))

        total = lax.fori_loop(0, npc + 1, gather, jnp.zeros((HDIM, rows), f32))
        out_ref[pl.ds(pl.multiple_of(h * HDIM, HDIM), HDIM), :] = total.astype(bf16)
        return 0

    lax.fori_loop(0, HEADS, head, 0)


def attend(info, fac, kv):
    parts, cols, rows = kv.shape
    seen = min(parts, parts // 2 + 1)
    return pl.pallas_call(
        attend_kernel,
        out_shape=[
            jax.ShapeDtypeStruct((HEADS * HDIM, rows), bf16),
            jax.ShapeDtypeStruct((HEADS, rows), f32),
        ],
        in_specs=[smem(), vmem(), vmem()],
        out_specs=[vmem()] * 2,
        scratch_shapes=[
            pltpu.VMEM((QCOLS, rows), f32),
            pltpu.VMEM((parts, cols, rows), f32),
            pltpu.VMEM((DEPTH, rows), bf16),
            pltpu.VMEM((DEPTH, rows), bf16),
            pltpu.VMEM((seen, rows, rows), f32),
        ],
        compiler_params=params(),
        cost_estimate=cost(16 * 2 * HEADS * 256 * rows * rows * seen, 4 * cols * rows * parts),
        name="attend",
    )(info, fac, kv)


def attend_back_kernel(
    info_ref, fac_ref, kv_ref, grad_ref, lse_ref, dq_ref, dkv_ref, facf, kvf, dkvf, qT, kTs, p_ref, dp_ref
):
    me, npc, limit = info_ref[0], info_ref[1], info_ref[2]
    parts, _, rows = kv_ref.shape
    load_factors(fac_ref, kv_ref, facf, kvf, qT, me, npc)

    def clear(j, _):
        dkvf[j] = jnp.zeros(dkvf.shape[1:], f32)
        return 0

    lax.fori_loop(0, parts, clear, 0)
    dq_ref[...] = jnp.zeros(dq_ref.shape, f32)

    def head(h, _):
        build_query(facf, qT, h)
        at_head = pl.ds(pl.multiple_of(h * HDIM, HDIM), HDIM)
        grad = grad_ref[at_head, :]
        lse = lse_ref[pl.ds(h, 1), :]

        def probe(slot, at, scores, delta):
            probs = jnp.exp2(scores * EXP_SCALE - lse)
            p_ref[slot] = probs
            prob_grad = mm(build_pair(kvf, at, h, AV, BV), grad, TN)
            dp_ref[slot] = prob_grad
            return delta + jnp.sum(probs * prob_grad, axis=0, keepdims=True)

        def chunk(j, delta):
            build_key(kvf, kTs.at[j], j, h, limit)
            return probe(j, j, mm(kTs[j], qT[...], TN), delta)

        delta = lax.fori_loop(0, npc, chunk, jnp.zeros((1, rows), f32))
        build_key(kvf, kTs.at[npc], me, h, None)
        delta = probe(npc, me, causal(mm(kTs[npc], qT[...], TN)), delta)

        def pull(j, total):
            at = jnp.where(j == npc, me, j)
            probs = p_ref[j]
            score_grad = (probs * (dp_ref[j] - delta)).astype(bf16)
            key_grad = mm(qT[0:HDIM, :], score_grad, NT) * (SCALE / KRANK)
            value_grad = mm(grad, probs.astype(bf16), NT) * (1.0 / KRANK)
            for a_at, b_at, got in ((AK, BK, key_grad), (AV, BV, value_grad)):
                for r in range(KRANK):
                    a_row = pl.ds(a_at + r * HEADS + h, 1)
                    b_rows = slice(b_at + r * HDIM, b_at + (r + 1) * HDIM)
                    dkvf[at, a_row, :] = jnp.sum(got * kvf[at, b_rows, :], axis=0, keepdims=True)
                    dkvf[at, b_rows, :] += got * kvf[at, a_row, :]
            return total + mm(kTs[j, 0:HDIM, :], score_grad)

        query_grad = lax.fori_loop(0, npc + 1, pull, jnp.zeros((HDIM, rows), f32)) * (SCALE / QRANK)
        for r in range(QRANK):
            a_row = pl.ds(AQ + r * HEADS + h, 1)
            b_rows = slice(BQ + r * HDIM, BQ + (r + 1) * HDIM)
            dq_ref[a_row, :] = jnp.sum(query_grad * facf[b_rows, :], axis=0, keepdims=True)
            dq_ref[b_rows, :] += query_grad * facf[a_row, :]
        return 0

    lax.fori_loop(0, HEADS, head, 0)

    def store(j, _):
        dkv_ref[j] = dkvf[j].astype(bf16)
        return 0

    lax.fori_loop(0, parts, store, 0)


def attend_back(info, fac, kv, grad, lse):
    parts, cols, rows = kv.shape
    seen = min(parts, parts // 2 + 1)
    return pl.pallas_call(
        attend_back_kernel,
        out_shape=[
            jax.ShapeDtypeStruct((QCOLS, rows), f32),
            jax.ShapeDtypeStruct((parts, cols, rows), bf16),
        ],
        in_specs=[smem()] + [vmem()] * 4,
        out_specs=[vmem()] * 2,
        scratch_shapes=[
            pltpu.VMEM((QCOLS, rows), f32),
            pltpu.VMEM((parts, cols, rows), f32),
            pltpu.VMEM((parts, cols, rows), f32),
            pltpu.VMEM((DEPTH, rows), bf16),
            pltpu.VMEM((seen, DEPTH, rows), bf16),
            pltpu.VMEM((seen, rows, rows), f32),
            pltpu.VMEM((seen, rows, rows), f32),
        ],
        compiler_params=params(),
        cost_estimate=cost(40 * 2 * HEADS * 256 * rows * rows * seen, 8 * cols * rows * parts),
        name="attend_back",
    )(info, fac, kv, grad, lse)


def rms_scale(values):
    return lax.rsqrt(jnp.mean(values * values, axis=-1, keepdims=True) + EPS)


def norm_back(grad_hidden, normed, scale, gain_vector):
    grad_normed = grad_hidden * gain_vector
    gain_grad = jnp.sum(grad_hidden * normed, axis=0)
    grad_values = scale * (
        grad_normed - normed * jnp.mean(grad_normed * normed, axis=-1, keepdims=True)
    )
    return gain_grad, grad_values


def turn_back(grads, cosine, sine):
    starts = [BQ + r * HDIM for r in range(QRANK)] + [QCOLS + BK + r * HDIM for r in range(KRANK)]
    pieces, at = [], 0
    for start in starts:
        pieces.append(grads[at:start])
        pieces.extend(turn(grads[start : start + HDIM], cosine, -sine))
        at = start + HDIM
    pieces.append(grads[at:])
    return jnp.concatenate(pieces, axis=0)


def local(
    layer_input,
    branch,
    attention_gain,
    factor_weight,
    output_weight,
    feed_gain,
    gate_weight,
    up_weight,
    down_weight,
    cotangent,
):
    def everywhere(values):
        return lax.all_gather(values, "grp", axis=0, tiled=True)

    rows = layer_input.shape[1]
    parts = lax.axis_size("grp")
    me = lax.axis_index("grp")
    prompt_parts = parts // 2
    follows = me >= prompt_parts
    chosen = branch[0, jnp.maximum(me - prompt_parts, 0)]
    limit = jnp.where(follows, chosen, me * rows)
    npc = (limit + rows - 1) // rows
    position = jnp.where(follows, chosen, me * rows) + jnp.arange(rows, dtype=jnp.int32)
    info = jnp.stack([me, npc, limit]).astype(jnp.int32)
    freqs = 10000.0 ** (-jnp.arange(HALF).astype(f32) / HALF)
    phase = freqs[:, None] * position.astype(f32)[None, :]
    cosine, sine = jnp.cos(phase), jnp.sin(phase)

    gain_one = everywhere(attention_gain).astype(f32)
    gain_two = everywhere(feed_gain).astype(f32)
    w_fac = everywhere(factor_weight)
    w_out = everywhere(output_weight)
    w_gate = everywhere(gate_weight)
    w_up = everywhere(up_weight)
    w_down = everywhere(down_weight)

    x = layer_input[0]
    upstream = cotangent[0]
    fac, hid_one = front(x, gain_one[None], w_fac, cosine, sine)
    kv = lax.all_gather(fac[QCOLS:], "grp", axis=0, tiled=False)
    fac_q = fac[:QCOLS]
    mixed, lse = attend(info, fac_q, kv)

    residual_in = x.astype(f32)
    middle = residual_in + mm(mixed, w_out, TN)
    scale_two = rms_scale(middle)
    normed_two = middle * scale_two
    hidden_two = (normed_two * gain_two).astype(bf16)
    gate_values = mm(hidden_two, w_gate)
    up_values = mm(hidden_two, w_up)
    sigmoid_gate = jax.nn.sigmoid(gate_values)
    active = (gate_values * sigmoid_gate * up_values).astype(bf16)
    result = middle + mm(active, w_down)
    down_grad = mm(active, upstream, TN)
    active_grad = mm(upstream, w_down, NT)
    gate_grad = (
        active_grad * up_values * sigmoid_gate * (1.0 + gate_values * (1.0 - sigmoid_gate))
    ).astype(bf16)
    up_grad = (active_grad * gate_values * sigmoid_gate).astype(bf16)
    gate_weight_grad = mm(hidden_two, gate_grad, TN)
    up_weight_grad = mm(hidden_two, up_grad, TN)
    hidden_two_grad = mm(gate_grad, w_gate, NT) + mm(up_grad, w_up, NT)
    feed_gain_grad, middle_grad = norm_back(hidden_two_grad, normed_two, scale_two, gain_two)
    middle_grad = middle_grad + upstream.astype(f32)
    branch_grad = middle_grad.astype(bf16)
    output_weight_grad = mm(mixed, branch_grad)
    mixed_grad = mm(w_out, branch_grad, NT).astype(bf16)

    dq, dkv = attend_back(info, fac_q, kv, mixed_grad, lse)
    own = lax.psum_scatter(dkv, "grp", scatter_dimension=0, tiled=False)
    draw = turn_back(jnp.concatenate([dq, own.astype(f32)], axis=0), cosine, sine).astype(bf16)
    factor_weight_grad = mm(hid_one, draw, NT)
    hidden_one_grad = mm(draw, w_fac, (((0,), (1,)), ((), ())))
    scale_one = rms_scale(residual_in)
    attention_gain_grad, input_part = norm_back(
        hidden_one_grad, residual_in * scale_one, scale_one, gain_one
    )
    input_grad = middle_grad + input_part

    def reduced(values):
        shard = lax.psum_scatter(values.astype(bf16), "grp", scatter_dimension=0, tiled=True)
        return lax.psum(shard, "rep").astype(f32)

    return (
        result.astype(bf16)[None],
        input_grad[None],
        reduced(attention_gain_grad),
        reduced(factor_weight_grad),
        reduced(output_weight_grad),
        reduced(feed_gain_grad),
        reduced(gate_weight_grad),
        reduced(up_weight_grad),
        reduced(down_grad),
    )


def solution(mesh):
    in_specs = (
        P("rep", "grp", None),
        P("rep", None),
        P("grp"),
        P("grp", None),
        P("grp", None),
        P("grp"),
        P("grp", None),
        P("grp", None),
        P("grp", None),
        P("rep", "grp", None),
    )
    out_specs = (
        P("rep", "grp", None),
        P("rep", "grp", None),
        P("grp"),
        P("grp", None),
        P("grp", None),
        P("grp"),
        P("grp", None),
        P("grp", None),
        P("grp", None),
    )
    return jax.shard_map(local, mesh=mesh, in_specs=in_specs, out_specs=out_specs, check_vma=False)
```

time: 1240 us -> 734 us (0.59)
  waiting for transfers between devices: 728 us -> 517 us
  matrix products: 203 us -> 75.1 us
  local copies, waits for them, and re-layouts: 130 us -> 12.8 us
  loops' own time: 43 us -> 0 us
  other arithmetic: 59.7 us -> 22.7 us
  Pallas kernels: 0 us -> 35.3 us
    reduce_scatter x6, waiting for transfers between devices: 562 us -> 250 us  [the longest x5 209 us: reduced(): lax.psum_scatter(values.astype(bf16), 'grp', scatter_dimension=0, tiled=T...]
    dot_general x54 -> x14, matrix products: 203 us -> 75.1 us  [mm(): return lax.dot_general(left, right, dims, preferred_element_type=f32)]
    all_gather x5, waiting for transfers between devices: 17.7 us -> 119 us  [everywhere(): return lax.all_gather(values, 'grp', axis=0, tiled=True)]
    another operation x24 -> x0, loops' own time: 43 us -> none  [the longest x2 21.3 us: half_backward(): lax.scan(grad_step, jnp.zeros((local_rows, head_span, HDIM), jnp.float32)...]
    pallas_call x0 -> x3, Pallas kernels: none -> 35.3 us  [the longest x1 18.8 us: attend_back(): pl.pallas_call(attend_back_kernel, out_shape=[jax.ShapeDtypeStruct((QCOLS...]
    reduce_or x18 -> x0, other arithmetic: 25.9 us -> none  [the longest x6 10 us: grad_step(): return lax.cond(jnp.any(visible_now), grad_update, skip_block, carry)]
    dynamic_slice x18 -> x1, local copies, waits for them, and re-layouts: 18.5 us -> 0.59 us  [local(): chosen = branch[0, jnp.maximum(me - prompt_parts, 0)]]
    slice x33 -> x2, local copies, waits for them, and re-layouts: 19.3 us -> 2.73 us  [the longest x1 1.76 us: local(): fac_q = fac[:QCOLS]]
  transfers between devices with their start and end apart: 12 -> 12, of which waited for: 9 -> 11; matrix products, arithmetic and copies ran while one was open for 15% -> 10% of each run, Pallas kernels for 0% -> 2%
where the time goes in v1:
time: 734 us; the launch traced here: 733 us
  waiting for transfers between devices  517 us (70%)
  matrix products  75.1 us (10%)
  blocking collectives  54.3 us (7%)
  Pallas kernels  35.3 us (5%)
  other arithmetic  22.7 us (3%)
  between operations  15.9 us (2%)
  local copies, waits for them, and re-layouts  12.8 us (2%)
    reduce_scatter x5, waiting for transfers between devices, reduced(): lax.psum_scatter(values.astype(bf16), 'grp', scatter_dimension=0, tiled=T...  209 us
    psum x1, waiting for transfers between devices, reduced(): return lax.psum(shard, 'rep').astype(f32)  145 us
    all_gather x5, waiting for transfers between devices, everywhere(): return lax.all_gather(values, 'grp', axis=0, tiled=True)  119 us
    dot_general x14, matrix products, mm(): return lax.dot_general(left, right, dims, preferred_element_type=f32)  75.1 us
    reduce_scatter x1, waiting for transfers between devices, local(): own = lax.psum_scatter(dkv, 'grp', scatter_dimension=0, tiled=False)  41.1 us
    psum x1, blocking collectives, reduced(): return lax.psum(shard, 'rep').astype(f32)  22.3 us
    pallas_call x1, Pallas kernels, attend_back(): pl.pallas_call(attend_back_kernel, out_shape=[jax.ShapeDtypeStruct((QCOLS...  18.8 us
    all_gather x1, blocking collectives, local(): kv = lax.all_gather(fac[QCOLS:], 'grp', axis=0, tiled=False)  14.7 us
  transfers between devices with their start and end apart: 12, of which 11 were waited for; matrix products, arithmetic and copies ran while one was open for 10% of the time, Pallas kernels for 2%

profile of v1, /device:TPU:0, one launch (start us, length us, event | category | flops | bytes accessed | tf_op | source)
XLA Modules:
  0.0 733.1 jit_solution(665618339479565749)
XLA Ops:
  13.3 6.0 all-gather.1
  19.8 5.4 all-gather.2
  26.7 7.3 all-gather.9.cloned.1.call-done.w_ref
  34.0 3.8 front.1
  40.6 14.7 %all-gather = bf16[1280,384]{1,0:T(8,128)(2,1)} all-gather(bf16[320,384]{1,0:T(8,128)(2,1)S(1)} %slice.109), channel_id=2, replica_groups=mesh['rep'=8,'grp'=4] {'grp'}, dimensions={0}, use_global_device_ids=true | all-gather | bytes 1228800 | tf_op jit(solution)/shard_map/all_gather | solution.py:360
  55.3 12.7 %attend.1 = (bf16[1024,384]{1,0:T(8,128)(2,1)}, f32[16,384]{1,0:T(8,128)}) custom-call(s32[3]{0:T(128)} %pad_add_fusion.info_ref, bf16[480,384]{1,0:T(8,128)(2,1)} %slice.108.fac_ref, bf16[4,320,384]{2,1,0:T(8,128)(2,1)} %bitcast.102), custom_call_target="tpu_custom_call" | custom-call | flops 57982058496 | bytes 1966080 | tf_op jit(solution)/shard_map/attend/pallas_call | solution.py:183
  68.0 3.0 multiply_reduce_fusion.2
  71.3 35.9 %all-gather.13.cloned.1.call-done = bf16[1024,2816]{1,0:T(8,128)(2,1)} async-done(((bf16[256,2816]{1,0:T(8,128)(2,1)}), bf16[1024,2816]{1,0:T(8,128)(2,1)}) %all-gather.13.cloned.1.call-update) | async-done | bytes 5767184 | tf_op jit(solution)/shard_map/all_gather | solution.py:333
  107.2 7.1 fusion.68
  114.3 37.8 %all-gather.15.cloned.1.call-done = bf16[1024,2816]{1,0:T(8,128)(2,1)} async-done(((bf16[256,2816]{1,0:T(8,128)(2,1)}), bf16[1024,2816]{1,0:T(8,128)(2,1)}) %all-gather.15.cloned.1.call-update) | async-done | bytes 5767184 | tf_op jit(solution)/shard_map/all_gather | solution.py:333
  152.1 7.1 fusion.69
  159.2 37.7 %all-gather.17.cloned.1.call-done = bf16[2816,1024]{1,0:T(8,128)(2,1)} async-done(((bf16[704,1024]{1,0:T(8,128)(2,1)}), bf16[2816,1024]{1,0:T(8,128)(2,1)}) %all-gather.17.cloned.1.call-update) | async-done | bytes 5767184 | tf_op jit(solution)/shard_map/all_gather | solution.py:333
  196.9 10.2 %multiply_convert_fusion = (bf16[384,2816]{1,0:T(8,128)(2,1)S(1)}, bf16[384,2816]{1,0:T(8,128)(2,1)S(1)}, bf16[384,2816]{1,0:T(8,128)(2,1)}) fusion(f32[384,2816]{1,0:T(8,128)} %fusion.68, f32[384,2816]{1,0:T(8,128)} %fusion.69, bf16[2816,1024]{1,0:T(8,128)(2,1)} %all-gather.17.cloned.1.call-done, bf16[1,384,1024]{2,1,0:T(8,128)(2,1)S(1)} %copy-done.17), kind=kOutput, calls=%fused_computation.3 | convolution fusion | flops 2231894016 | bytes 21692416 | tf_op jit(solution)/shard_map/dot_general | solution.py:37
  207.2 6.7 fusion.70
  213.9 3.2 multiply_reduce_fusion
  220.9 18.8 %attend_back.1 = (f32[480,384]{1,0:T(8,128)}, bf16[4,320,384]{2,1,0:T(8,128)(2,1)}) custom-call(s32[3]{0:T(128)} %pad_add_fusion.info_ref, bf16[480,384]{1,0:T(8,128)(2,1)} %slice.108.fac_ref, bf16[4,320,384]{2,1,0:T(8,128)(2,1)} %bitcast.103, bf16[1024,384]{1,0:T(8,128)(2,1)} %fusion.11.grad_ref, f32[16,384]{1,0:T(8,128)} %get-tuple-element.17.lse_ref), custom_call_target="tpu_custom_call" | custom-call | flops 144955146240 | bytes 3932160 | tf_op jit(solution)/shard_map/attend_back/pallas_call | solution.py:273
  247.9 41.1 %reduce-scatter.7.cloned.1.call-done = bf16[1,320,384]{2,1,0:T(8,128)(2,1)} async-done(((bf16[4,320,384]{2,1,0:T(8,128)(2,1)}), bf16[1,320,384]{2,1,0:T(8,128)(2,1)}) %reduce-scatter.7.cloned.1.call-update) | async-done | bytes 245776 | tf_op jit(solution)/shard_map/reduce_scatter | solution.py:390
  292.8 3.6 convolution_convert_fusion.4
  296.5 6.9 convolution_convert_fusion.2
  303.5 6.6 convolution_convert_fusion.1
  311.2 6.7 convolution_convert_fusion
  318.0 5.2 reduce-scatter.11.cloned.1.call-done
  323.2 31.2 %reduce-scatter.9.cloned.1.call-done = bf16[256,800]{0,1:T(8,128)(2,1)} async-done(((bf16[1024,800]{0,1:T(8,128)(2,1)}), bf16[256,800]{0,1:T(8,128)(2,1)}) %reduce-scatter.9.cloned.1.call-update) | async-done | bytes 409616 | tf_op jit(solution)/shard_map/reduce_scatter | solution.py:401
  354.4 57.6 %reduce-scatter.13.cloned.1.call-done = bf16[256,2816]{1,0:T(8,128)(2,1)} async-done(((bf16[1024,2816]{1,0:T(8,128)(2,1)}), bf16[256,2816]{1,0:T(8,128)(2,1)}) %reduce-scatter.13.cloned.1.call-update) | async-done | bytes 1441808 | tf_op jit(solution)/shard_map/reduce_scatter | solution.py:401
  412.0 57.3 %reduce-scatter.15.cloned.1.call-done = bf16[256,2816]{1,0:T(8,128)(2,1)} async-done(((bf16[1024,2816]{1,0:T(8,128)(2,1)}), bf16[256,2816]{1,0:T(8,128)(2,1)}) %reduce-scatter.15.cloned.1.call-update) | async-done | bytes 1441808 | tf_op jit(solution)/shard_map/reduce_scatter | solution.py:401
  469.3 57.6 %reduce-scatter.17.cloned.1.call-done = bf16[704,1024]{1,0:T(8,128)(2,1)} async-done(((bf16[2816,1024]{1,0:T(8,128)(2,1)}), bf16[704,1024]{1,0:T(8,128)(2,1)}) %reduce-scatter.17.cloned.1.call-update) | async-done | bytes 1441808 | tf_op jit(solution)/shard_map/reduce_scatter | solution.py:401
  530.2 6.7 fusion.10
  539.4 6.0 all-reduce.4
  545.6 22.3 %all-reduce.2 = (bf16[256]{0:T(256)(128)(2,1)S(1)}, bf16[256]{0:T(256)(128)(2,1)S(1)}) all-reduce(bf16[256]{0:T(256)(128)(2,1)S(1)} %dynamic-slice.1, bf16[256]{0:T(256)(128)(2,1)S(1)} %dynamic-slice.3), channel_id=1, replica_groups=mesh['rep'=8,'grp'=4] {'rep'}, use_global_device_ids=true, to_apply=%region_7.8 | all-reduce | flops 512 | bytes 2048 | tf_op jit(solution)/shard_map/psum | solution.py:402
  569.0 3.0 fusion.7
  572.0 145.1 %all-reduce.7.cloned.1.call-done = (bf16[256,800]{0,1:T(8,128)(2,1)}, bf16[256,1024]{1,0:T(8,128)(2,1)}, bf16[256,2816]{1,0:T(8,128)(2,1)}, bf16[256,2816]{1,0:T(8,128)(2,1)}, bf16[704,1024]{1,0:T(8,128)(2,1)}) async-done(((bf16[256,800]{0,1:T(8,128)(2,1)}, bf16[256,1024]{1,0:T(8,128)(2,1)}, bf16[256,2816]{1,0:T(8,128)(2,1)}, bf16[256,2816]{1,0:T(8,128)(2,1)}, bf16[704,1024]{1,0:T(8,128)(2,1)}), ...) | async-done | bytes 5259280 | tf_op jit(solution)/shard_map/psum | solution.py:402
  717.1 3.2 convert_element_type.120
  (146 shorter events, 39.5 us)
Async XLA Ops:
  7.2 4.8 copy-start
  7.2 26.8 %all-gather.9.cloned.1.call-start = ((), (), s32[]{:S(2)}) async-start(), calls=%async_computation.6 | async-start | bytes 2293760 | tf_op jit(solution)/shard_map/all_gather | solution.py:333
  9.2 58.7 %all-gather.11.cloned.1.call-start = ((), (), s32[]{:S(2)}) async-start(), calls=%async_computation.7 | async-start | bytes 2621440 | tf_op jit(solution)/shard_map/all_gather | solution.py:333
  10.0 9.8 %copy-start.31 = (bf16[256]{0:T(256)(128)(2,1)S(1)}, bf16[256]{0:T(256)(128)(2,1)}, u32[]{:S(2)}) copy-start(bf16[256]{0:T(256)(128)(2,1)} %param.15) | copy-start | bytes 1540
  10.0 97.2 %all-gather.13.cloned.1.call-start = ((), (), s32[]{:S(2)}) async-start(), calls=%async_computation.8 | async-start | bytes 7208960 | tf_op jit(solution)/shard_map/all_gather | solution.py:333
  10.8 141.3 %all-gather.15.cloned.1.call-start = ((), (), s32[]{:S(2)}) async-start(), calls=%async_computation.9 | async-start | bytes 7208960 | tf_op jit(solution)/shard_map/all_gather | solution.py:333
  11.3 185.6 %all-gather.17.cloned.1.call-start = ((), (), s32[]{:S(2)}) async-start(), calls=%async_computation.10 | async-start | bytes 7208960 | tf_op jit(solution)/shard_map/all_gather | solution.py:333
  11.9 277.1 %reduce-scatter.7.cloned.1.call-start = ((), (), s32[]{:S(2)}) async-start(), calls=%async_computation.11 | async-start | bytes 1228800 | tf_op jit(solution)/shard_map/reduce_scatter | solution.py:390
  25.8 29.5 %copy-start.19 = (f32[384]{0:T(512)}, f32[384]{0:T(512)S(1)}, u32[]{:S(2)}) copy-start(f32[384]{0:T(512)S(1)} %add_convert_fusion.1) | copy-start | bytes 4612
  55.3 12.7 %copy-start.6 = (bf16[1,384,1024]{2,1,0:T(8,128)(2,1)S(1)}, bf16[1,384,1024]{2,1,0:T(8,128)(2,1)}, u32[]{:S(2)}) copy-start(bf16[1,384,1024]{2,1,0:T(8,128)(2,1)} %param.10) | copy-start | bytes 2359300
  71.0 146.1 %copy-start.4 = (f32[384,1024]{1,0:T(8,128)}, f32[384,1024]{1,0:T(8,128)S(1)}, u32[]{:S(2)}) copy-start(f32[384,1024]{1,0:T(8,128)S(1)} %get-tuple-element.40) | copy-start | bytes 4718596
  71.2 80.8 %copy-start.15 = (bf16[384,1024]{1,0:T(8,128)(2,1)}, bf16[384,1024]{1,0:T(8,128)(2,1)S(1)}, u32[]{:S(2)}) copy-start(bf16[384,1024]{1,0:T(8,128)(2,1)S(1)} %multiply_convert_fusion.3) | copy-start | bytes 2359300
  114.3 82.7 %copy-start.17 = (bf16[1,384,1024]{2,1,0:T(8,128)(2,1)S(1)}, bf16[1,384,1024]{2,1,0:T(8,128)(2,1)}, u32[]{:S(2)}) copy-start(bf16[1,384,1024]{2,1,0:T(8,128)(2,1)} %param.19) | copy-start | bytes 2359300
  207.1 6.7 copy-start.34
  207.2 6.7 copy-start.33
  207.2 6.7 copy-start.29
  220.9 19.8 %copy-start.3 = (f32[384,1024]{1,0:T(8,128)S(1)}, f32[384,1024]{1,0:T(8,128)}, u32[]{:S(2)}) copy-start(f32[384,1024]{1,0:T(8,128)} %copy-done.2) | copy-start | bytes 4718596
  220.9 19.8 %copy-start.9 = (bf16[1024,384]{1,0:T(8,128)(2,1)S(1)}, bf16[1024,384]{1,0:T(8,128)(2,1)}, u32[]{:S(2)}) copy-start(bf16[1024,384]{1,0:T(8,128)(2,1)} %get-tuple-element.16) | copy-start | bytes 2359300
  239.8 83.4 %reduce-scatter.11.cloned.1.call-start = ((), (), s32[]{:S(2)}) async-start(), calls=%async_computation.13 | async-start | bytes 2621440 | tf_op jit(solution)/shard_map/reduce_scatter | solution.py:401
  243.5 110.9 %reduce-scatter.9.cloned.1.call-start = ((), (), s32[]{:S(2)}) async-start(), calls=%async_computation.12 | async-start | bytes 2048000 | tf_op jit(solution)/shard_map/reduce_scatter | solution.py:401
  292.8 3.7 copy-start.26
  292.8 3.7 copy-start.16
  296.5 115.5 %reduce-scatter.13.cloned.1.call-start = ((), (), s32[]{:S(2)}) async-start(), calls=%async_computation.14 | async-start | bytes 7208960 | tf_op jit(solution)/shard_map/reduce_scatter | solution.py:401
  303.4 165.9 %reduce-scatter.15.cloned.1.call-start = ((), (), s32[]{:S(2)}) async-start(), calls=%async_computation.15 | async-start | bytes 7208960 | tf_op jit(solution)/shard_map/reduce_scatter | solution.py:401
  310.1 216.8 %reduce-scatter.17.cloned.1.call-start = ((), (), s32[]{:S(2)}) async-start(), calls=%async_computation.16 | async-start | bytes 7208960 | tf_op jit(solution)/shard_map/reduce_scatter | solution.py:401
  318.0 399.1 %all-reduce.7.cloned.1.call-start = ((), (), s32[]{:S(2)}) async-start(), calls=%async_computation.17 | async-start | bytes 10518528 | tf_op jit(solution)/shard_map/psum | solution.py:402
  530.2 6.8 copy-start.7
  530.2 6.8 copy-start.12
  530.2 6.8 copy-start.25
  530.2 6.8 copy-start.27
  537.0 32.0 %copy-start.8 = (bf16[1,384,1024]{2,1,0:T(8,128)(2,1)S(1)}, bf16[1,384,1024]{2,1,0:T(8,128)(2,1)}, u32[]{:S(2)}) copy-start(bf16[1,384,1024]{2,1,0:T(8,128)(2,1)} %param.10) | copy-start | bytes 2359300
  722.3 4.0 copy-start.1
  (15 other events, 28.6 us)
Sparse Core Ops, SparseCore 0:
  10.2 23.8 all-gather.8
  35.6 26.4 all-gather.10
  63.7 43.4 all-gather.12
  108.6 43.4 all-gather.14
  153.5 43.3 all-gather.16
  239.9 49.0 reduce-scatter.6
  291.7 31.4 reduce-scatter.10
  325.8 28.5 reduce-scatter.8
  357.1 54.8 reduce-scatter.12
  414.4 54.8 reduce-scatter.14
  472.0 54.8 reduce-scatter.16
  531.1 185.9 all-reduce.6

commit v2 on v1

v2 whole, which is shorter than its diff:
```python
import functools

import jax
import jax.numpy as jnp
import numpy as np
from jax import lax
from jax.experimental import pallas as pl
from jax.experimental.pallas import tpu as pltpu
from jax.sharding import PartitionSpec as P

HEADS = 16
HDIM = 64
QRANK = 6
KRANK = 2
HALF = HDIM // 2
QCOLS = QRANK * HEADS + QRANK * HDIM
KVCOLS = 2 * (KRANK * HEADS + KRANK * HDIM)
AQ, BQ = 0, QRANK * HEADS
AK, BK = 0, KRANK * HEADS
AV = BK + KRANK * HDIM
BV = AV + KRANK * HEADS
SCALE = HDIM**-0.5
EXP_SCALE = SCALE * float(np.log2(np.e))
NEG = -1e30
DEPTH = 128
EPS = 1e-05
VMEM_LIMIT = 60 * 2**20

f32 = jnp.float32
bf16 = jnp.bfloat16
NN = (((1,), (0,)), ((), ()))
NT = (((1,), (1,)), ((), ()))
TN = (((0,), (0,)), ((), ()))


def mm(left, right, dims=NN):
    return lax.dot_general(left, right, dims, preferred_element_type=f32)


def vmem():
    return pl.BlockSpec(memory_space=pltpu.VMEM)


def smem():
    return pl.BlockSpec(memory_space=pltpu.SMEM)


def params():
    return pltpu.CompilerParams(vmem_limit_bytes=VMEM_LIMIT)


def cost(flops, nbytes):
    return pl.CostEstimate(flops=int(flops), bytes_accessed=int(nbytes), transcendentals=0)


def turn(part, cosine, sine):
    first, second = part[:HALF], part[HALF:]
    return first * cosine - second * sine, second * cosine + first * sine


def front_kernel(count, cols, offs, x_ref, cos_ref, sin_ref, *refs):
    pieces = refs[:count]
    fac_ref, kv_ref, hid_ref, gains_ref, w, sems = refs[count:]
    w_in = Mover(sems).pieces(offs, pieces, w)
    xf = x_ref[...].astype(f32)
    normed = xf * lax.rsqrt(jnp.mean(xf * xf, axis=-1, keepdims=True) + EPS)
    wait(w_in)
    last = w.shape[1] - 128
    gains = jnp.transpose(w[:, last:])[cols - last : cols - last + 16].astype(f32)
    gains_ref[...] = gains[0:8]
    hidden = (normed * gains[0:1]).astype(bf16)
    hid_ref[...] = jnp.transpose(hidden)
    raw = jnp.transpose(mm(hidden, w[...]))
    cosine, sine = cos_ref[...], sin_ref[...]
    fac_ref[...] = raw[:QCOLS].astype(bf16)
    kv_ref[...] = raw[QCOLS:cols].astype(bf16)
    for ref, first, at in [(fac_ref, 0, BQ + r * HDIM) for r in range(QRANK)] + [
        (kv_ref, QCOLS, BK + r * HDIM) for r in range(KRANK)
    ]:
        one, two = turn(raw[first + at : first + at + HDIM], cosine, sine)
        ref[at : at + HALF, :] = one.astype(bf16)
        ref[at + HALF : at + HDIM, :] = two.astype(bf16)


def front(offs, x, cosine, sine, w_fac, cols):
    rows, width = x.shape
    wide = w_fac[0].shape[1]
    count = len(w_fac)
    return pl.pallas_call(
        functools.partial(front_kernel, count, cols),
        out_shape=[
            like(QCOLS, rows),
            like(cols - QCOLS, rows),
            like(width, rows),
            like(8, width, dtype=f32),
        ],
        in_specs=[smem()] + [vmem()] * 3 + [anywhere()] * count,
        out_specs=[vmem()] * 4,
        scratch_shapes=[scratch(width, wide), pltpu.SemaphoreType.DMA((count,))],
        compiler_params=params(),
        cost_estimate=cost(2 * rows * width * cols, 4 * width * (cols + rows)),
        name="front",
    )(offs, x, cosine, sine, *w_fac)


def load_factors(fac_ref, kv_refs, facf, kvf, qT, me):
    facf[...] = fac_ref[...].astype(f32)
    if len(kv_refs) == 1:

        def load(j, _):
            kvf[j] = kv_refs[0][j].astype(f32)
            return 0

        lax.fori_loop(0, kvf.shape[0], load, 0)
    else:
        for flip, ref in enumerate(kv_refs):
            kvf[me ^ flip] = ref[...].astype(f32)
    row = lax.broadcasted_iota(jnp.int32, (DEPTH - HDIM, qT.shape[1]), 0)
    qT[HDIM:DEPTH, :] = jnp.where(row == 0, 1.0, 0.0).astype(bf16)


def build_query(facf, qT, h):
    total = facf[pl.ds(AQ + h, 1), :] * facf[BQ : BQ + HDIM, :]
    for r in range(1, QRANK):
        total += facf[pl.ds(AQ + r * HEADS + h, 1), :] * facf[BQ + r * HDIM : BQ + (r + 1) * HDIM, :]
    qT[0:HDIM, :] = (total * (1.0 / QRANK)).astype(bf16)


def build_pair(kvf, j, h, a_at, b_at):
    total = kvf[j, pl.ds(a_at + h, 1), :] * kvf[j, b_at : b_at + HDIM, :]
    for r in range(1, KRANK):
        total += (
            kvf[j, pl.ds(a_at + r * HEADS + h, 1), :]
            * kvf[j, b_at + r * HDIM : b_at + (r + 1) * HDIM, :]
        )
    return (total * (1.0 / KRANK)).astype(bf16)


def build_key(kvf, kT, j, h, limit):
    span = kT.shape[1]
    kT[0:HDIM, :] = build_pair(kvf, j, h, AK, BK)
    if limit is None:
        kT[HDIM:DEPTH, :] = jnp.zeros((DEPTH - HDIM, span), bf16)
    else:
        row = lax.broadcasted_iota(jnp.int32, (DEPTH - HDIM, span), 0)
        key = j * span + lax.broadcasted_iota(jnp.int32, (DEPTH - HDIM, span), 1)
        kT[HDIM:DEPTH, :] = jnp.where((row == 0) & (key >= limit), NEG, 0.0).astype(bf16)


def causal(scores):
    key = lax.broadcasted_iota(jnp.int32, scores.shape, 0)
    query = lax.broadcasted_iota(jnp.int32, scores.shape, 1)
    return jnp.where(key <= query, scores, NEG)


def attend_kernel(first, heads, count, info_ref, fac_ref, *refs):
    kv_refs, (out_ref, lse_ref, facf, kvf, qT, kT, s_ref) = refs[:count], refs[count:]
    me, npc, limit = info_ref[0], info_ref[1], info_ref[2]
    rows = fac_ref.shape[1]
    load_factors(fac_ref, kv_refs, facf, kvf, qT, me)

    def head(step, _):
        h = first + step
        build_query(facf, qT, h)

        def chunk(j, top):
            build_key(kvf, kT, j, h, limit)
            scores = mm(kT[...], qT[...], TN)
            s_ref[j] = scores
            return jnp.maximum(top, jnp.max(scores, axis=0, keepdims=True))

        top = lax.fori_loop(0, npc, chunk, jnp.full((1, rows), NEG, f32))
        build_key(kvf, kT, me, h, None)
        scores = causal(mm(kT[...], qT[...], TN))
        s_ref[npc] = scores
        top = jnp.maximum(top, jnp.max(scores, axis=0, keepdims=True)) * EXP_SCALE

        def weigh(j, mass):
            probs = jnp.exp2(s_ref[j] * EXP_SCALE - top)
            s_ref[j] = probs
            return mass + jnp.sum(probs, axis=0, keepdims=True)

        mass = lax.fori_loop(0, npc + 1, weigh, jnp.zeros((1, rows), f32))
        lse_ref[pl.ds(step, 1), :] = top + jnp.log2(mass)
        share = 1.0 / mass

        def gather(j, total):
            at = jnp.where(j == npc, me, j)
            return total + mm(build_pair(kvf, at, h, AV, BV), (s_ref[j] * share).astype(bf16))

        total = lax.fori_loop(0, npc + 1, gather, jnp.zeros((HDIM, rows), f32))
        out_ref[pl.ds(pl.multiple_of(step * HDIM, HDIM), HDIM), :] = total.astype(bf16)
        return 0

    lax.fori_loop(0, heads, head, 0)


def kv_sizes(kv):
    return kv[0].shape if len(kv) == 1 else (len(kv),) + kv[0].shape


def attend(info, fac, kv, first, heads):
    parts, cols, rows = kv_sizes(kv)
    seen = min(parts, parts // 2 + 1)
    return pl.pallas_call(
        functools.partial(attend_kernel, first, heads, len(kv)),
        out_shape=[
            jax.ShapeDtypeStruct((heads * HDIM, rows), bf16),
            jax.ShapeDtypeStruct((heads, rows), f32),
        ],
        in_specs=[smem(), vmem()] + [vmem()] * len(kv),
        out_specs=[vmem()] * 2,
        scratch_shapes=[
            pltpu.VMEM((QCOLS, rows), f32),
            pltpu.VMEM((parts, cols, rows), f32),
            pltpu.VMEM((DEPTH, rows), bf16),
            pltpu.VMEM((DEPTH, rows), bf16),
            pltpu.VMEM((seen, rows, rows), f32),
        ],
        compiler_params=params(),
        cost_estimate=cost(16 * 2 * heads * 256 * rows * rows * seen, 4 * cols * rows * parts),
        name="attend",
    )(info, fac, *kv)


def attend_back_kernel(first, heads, final, count, info_ref, fac_ref, grad_ref, lse_ref, *refs):
    kv_refs, refs = refs[:count], refs[count:]
    if first:
        dq_in, dkv_in, *refs = refs
    dq_ref, *refs = refs
    if final:
        keep_ref, send_ref, *refs = refs
        *refs, dkvf = refs
    else:
        dkvf, *refs = refs
    facf, kvf, qT, kTs, p_ref, dp_ref = refs
    me, npc, limit = info_ref[0], info_ref[1], info_ref[2]
    parts, _, rows = kvf.shape
    load_factors(fac_ref, kv_refs, facf, kvf, qT, me)

    def begin(j, _):
        dkvf[j] = dkv_in[j] if first else jnp.zeros(dkvf.shape[1:], f32)
        return 0

    lax.fori_loop(0, parts, begin, 0)
    dq_ref[...] = dq_in[...] if first else jnp.zeros(dq_ref.shape, f32)

    def head(step, _):
        h = first + step
        build_query(facf, qT, h)
        grad = grad_ref[pl.ds(pl.multiple_of(h * HDIM, HDIM), HDIM), :]
        lse = lse_ref[pl.ds(h, 1), :]

        def probe(slot, at, scores, delta):
            probs = jnp.exp2(scores * EXP_SCALE - lse)
            p_ref[slot] = probs
            prob_grad = mm(build_pair(kvf, at, h, AV, BV), grad, TN)
            dp_ref[slot] = prob_grad
            return delta + jnp.sum(probs * prob_grad, axis=0, keepdims=True)

        def chunk(j, delta):
            build_key(kvf, kTs.at[j], j, h, limit)
            return probe(j, j, mm(kTs[j], qT[...], TN), delta)

        delta = lax.fori_loop(0, npc, chunk, jnp.zeros((1, rows), f32))
        build_key(kvf, kTs.at[npc], me, h, None)
        delta = probe(npc, me, causal(mm(kTs[npc], qT[...], TN)), delta)

        def pull(j, total):
            at = jnp.where(j == npc, me, j)
            probs = p_ref[j]
            score_grad = (probs * (dp_ref[j] - delta)).astype(bf16)
            key_grad = mm(qT[0:HDIM, :], score_grad, NT) * (SCALE / KRANK)
            value_grad = mm(grad, probs.astype(bf16), NT) * (1.0 / KRANK)
            for a_at, b_at, got in ((AK, BK, key_grad), (AV, BV, value_grad)):
                for r in range(KRANK):
                    a_row = pl.ds(a_at + r * HEADS + h, 1)
                    b_rows = slice(b_at + r * HDIM, b_at + (r + 1) * HDIM)
                    dkvf[at, a_row, :] = jnp.sum(got * kvf[at, b_rows, :], axis=0, keepdims=True)
                    dkvf[at, b_rows, :] += got * kvf[at, a_row, :]
            return total + mm(kTs[j, 0:HDIM, :], score_grad)

        query_grad = lax.fori_loop(0, npc + 1, pull, jnp.zeros((HDIM, rows), f32)) * (SCALE / QRANK)
        for r in range(QRANK):
            a_row = pl.ds(AQ + r * HEADS + h, 1)
            b_rows = slice(BQ + r * HDIM, BQ + (r + 1) * HDIM)
            dq_ref[a_row, :] = jnp.sum(query_grad * facf[b_rows, :], axis=0, keepdims=True)
            dq_ref[b_rows, :] += query_grad * facf[a_row, :]
        return 0

    lax.fori_loop(0, heads, head, 0)
    if final:
        for j in range(parts // 2):
            keep_ref[j] = dkvf[me ^ (2 * j)].astype(bf16)
            send_ref[j] = dkvf[me ^ (2 * j + 1)].astype(bf16)


def attend_back(info, fac, kv, grad, lse, first, heads, so_far):
    parts, cols, rows = kv_sizes(kv)
    seen = min(parts, parts // 2 + 1)
    final = first + heads == HEADS
    gathered = [like(parts // 2, cols, rows)] * 2 if final else [like(parts, cols, rows, dtype=f32)]
    return pl.pallas_call(
        functools.partial(attend_back_kernel, first, heads, final, len(kv)),
        out_shape=[like(QCOLS, rows, dtype=f32)] + gathered,
        in_specs=[smem()] + [vmem()] * (3 + len(kv) + len(so_far)),
        out_specs=[vmem()] * (1 + len(gathered)),
        scratch_shapes=[
            pltpu.VMEM((QCOLS, rows), f32),
            pltpu.VMEM((parts, cols, rows), f32),
            pltpu.VMEM((DEPTH, rows), bf16),
            pltpu.VMEM((seen, DEPTH, rows), bf16),
            pltpu.VMEM((seen, rows, rows), f32),
            pltpu.VMEM((seen, rows, rows), f32),
        ]
        + ([pltpu.VMEM((parts, cols, rows), f32)] if final else []),
        compiler_params=params(),
        cost_estimate=cost(40 * 2 * heads * 256 * rows * rows * seen, 8 * cols * rows * parts),
        name="attend_back",
    )(info, fac, grad, lse, *kv, *so_far)


class Mover:
    def __init__(self, sems):
        self.sems = sems
        self.used = 0

    def start(self, src, dst):
        copy = pltpu.make_async_copy(src, dst, self.sems.at[self.used])
        self.used += 1
        copy.start()
        return copy

    def pieces(self, offsets, refs, dst):
        copies = []
        for i, piece in enumerate(refs):
            rows, cols = piece.shape
            at = pl.ds(pl.multiple_of(offsets[2 * i], 16), rows)
            if cols == dst.shape[1]:
                where = dst.at[at]
            else:
                where = dst.at[at, pl.ds(pl.multiple_of(offsets[2 * i + 1], 128), cols)]
            copies.append(self.start(piece, where))
        return copies


def wait(copies):
    for copy in copies:
        copy.wait()


def anywhere():
    return pl.BlockSpec(memory_space=pl.ANY)


def like(*shape, dtype=bf16):
    return jax.ShapeDtypeStruct(shape, dtype)


def scratch(*shape, dtype=bf16):
    return pltpu.VMEM(shape, dtype)


TILE = 256


def norm_back(grad_hidden, normed, scale, gain):
    grad_normed = grad_hidden * gain
    gain_grad = jnp.sum(grad_hidden * normed, axis=0, keepdims=True)
    mean = jnp.mean(grad_normed * normed, axis=-1, keepdims=True)
    return gain_grad, scale * (grad_normed - normed * mean)


def shard_products(me, left, right, keep, send, mover, keep_out, send_out, cut=2816):
    copies = []
    count, rows, cols = keep.shape
    step = rows if rows <= 352 else rows // 2
    for odd, dst, out in ((1, send, send_out), (0, keep, keep_out)):
        for j in range(count):
            row = (me ^ (2 * j + odd)) * rows
            for low in range(0, rows, step):
                lhs = left[pl.ds(pl.multiple_of(row + low, 16), step), :]
                for at in range(0, cols, 1408 if cols % 1408 == 0 else cols):
                    width = 1408 if cols % 1408 == 0 else cols
                    dst[j, low : low + step, at : at + width] = mm(
                        lhs, right[:, at : at + width]
                    ).astype(bf16)
            copies.append(mover.start(dst.at[j], out.at[j]))
    return copies


def feed_kernel(count, offs, who, mix_ref, x_ref, gain_ref, up_ref, *refs):
    out_pieces, gate_pieces, lift_pieces = (refs[i * count : (i + 1) * count] for i in range(3))
    refs = refs[3 * count :]
    (mid_o, hid_o, act_o, slope_o, lin_o, keep_o, send_o) = refs[:7]
    (wo, wg, wu, mid, hid, hidT, act, slope, lin, actT, keep, send, sems) = refs[7:]
    mover = Mover(sems)
    wo_in = mover.pieces(offs, out_pieces, wo)
    wg_in = mover.pieces(offs, gate_pieces, wg)
    wu_in = mover.pieces(offs, lift_pieces, wu)
    mix = jnp.transpose(mix_ref[...])
    wait(wo_in)
    middle = x_ref[...].astype(f32) + mm(mix, wo[...])
    mid[...] = middle
    scale = lax.rsqrt(jnp.mean(middle * middle, axis=-1, keepdims=True) + EPS)
    hidden = (middle * scale * gain_ref[...]).astype(bf16)
    hid[...] = hidden
    hidT[...] = jnp.transpose(hidden)
    done = [mover.start(mid, mid_o), mover.start(hidT, hid_o)]
    wait(wg_in)
    wait(wu_in)

    def tile(j, _):
        cols = pl.ds(pl.multiple_of(j * TILE, TILE), TILE)
        gate = mm(hid[...], wg[:, cols])
        up = mm(hid[...], wu[:, cols])
        sig = jax.nn.sigmoid(gate)
        line = gate * sig
        active = (line * up).astype(bf16)
        act[:, cols] = active
        lin[:, cols] = line.astype(bf16)
        slope[:, cols] = (up * sig * (1.0 + gate * (1.0 - sig))).astype(bf16)
        actT[cols, :] = jnp.transpose(active)
        return 0

    lax.fori_loop(0, wg.shape[1] // TILE, tile, 0)
    done += [mover.start(act, act_o), mover.start(lin, lin_o), mover.start(slope, slope_o)]
    done += shard_products(who[0], actT, up_ref, keep, send, mover, keep_o, send_o)
    wait(done)


def feed(offs, who, mix, x, gain, upstream, w_out, w_gate, w_up, parts):
    rows, width = x.shape
    inner = w_gate[0].shape[1]
    count = len(w_gate)
    down = (parts // 2, inner // parts, width)
    return pl.pallas_call(
        functools.partial(feed_kernel, count),
        out_shape=[
            like(rows, width, dtype=f32),
            like(width, rows),
            like(rows, inner),
            like(rows, inner),
            like(rows, inner),
            like(*down),
            like(*down),
        ],
        in_specs=[smem(), smem()] + [vmem()] * 4 + [anywhere()] * (3 * count),
        out_specs=[anywhere()] * 7,
        scratch_shapes=[
            scratch(width, width),
            scratch(width, inner),
            scratch(width, inner),
            scratch(rows, width, dtype=f32),
            scratch(rows, width),
            scratch(width, rows),
            scratch(rows, inner),
            scratch(rows, inner),
            scratch(rows, inner),
            scratch(inner, rows),
            scratch(*down),
            scratch(*down),
            pltpu.SemaphoreType.DMA((3 * count + 5 + parts,)),
        ],
        compiler_params=params(),
        cost_estimate=cost(2 * rows * width * (width + 3 * inner), 2 * inner * (3 * width + 3 * rows)),
        name="feed",
    )(offs, who, mix, x, gain, upstream, *w_out, *w_gate, *w_up)


def slopes_kernel(c_ref, slope_ref, lin_ref, wd, dg, du):

    def tile(j, _):
        cols = pl.ds(pl.multiple_of(j * TILE, TILE), TILE)
        grad = mm(c_ref[...], wd[cols, :], NT)
        dg[:, cols] = (grad * slope_ref[:, cols].astype(f32)).astype(bf16)
        du[:, cols] = (grad * lin_ref[:, cols].astype(f32)).astype(bf16)
        return 0

    lax.fori_loop(0, wd.shape[0] // TILE, tile, 0)


def slopes(upstream, w_down, slope, lin):
    rows, width = upstream.shape
    inner = slope.shape[1]
    return pl.pallas_call(
        slopes_kernel,
        out_shape=[like(rows, inner)] * 2,
        in_specs=[vmem()] * 4,
        out_specs=[vmem()] * 2,
        compiler_params=params(),
        cost_estimate=cost(2 * rows * width * inner, 2 * inner * (width + 4 * rows)),
        name="slopes",
    )(upstream, slope, lin, w_down)


def widths_kernel(who, hid_ref, dg_ref, du_ref, gkeep_o, gsend_o, ukeep_o, usend_o, gkeep, gsend, ukeep, usend, sems):
    mover = Mover(sems)
    done = shard_products(who[0], hid_ref, dg_ref, gkeep, gsend, mover, gkeep_o, gsend_o)
    done += shard_products(who[0], hid_ref, du_ref, ukeep, usend, mover, ukeep_o, usend_o)
    wait(done)


def widths(who, hidT, dg, du, parts):
    width, rows = hidT.shape
    inner = dg.shape[1]
    shard = (parts // 2, width // parts, inner)
    return pl.pallas_call(
        widths_kernel,
        out_shape=[like(*shard)] * 4,
        in_specs=[smem()] + [vmem()] * 3,
        out_specs=[anywhere()] * 4,
        scratch_shapes=[scratch(*shard)] * 4 + [pltpu.SemaphoreType.DMA((2 * parts,))],
        compiler_params=params(),
        cost_estimate=cost(4 * rows * width * inner, 4 * inner * (width + rows)),
        name="widths",
    )(who, hidT, dg, du)


def settle_kernel(count, offs, who, c_ref, gain_ref, down_full, *refs):
    out_pieces, gate_pieces, lift_pieces = (refs[i * count : (i + 1) * count] for i in range(3))
    refs = refs[3 * count :]
    (act_i, mid_i, dg_i, du_i, mix_i) = refs[:5]
    (res_o, dmid_o, fgain_o, dmix_o, keep_o, send_o) = refs[5:11]
    (wd, wg, wu, wo, act, mid, dg, du, mix, dhid, res, fgain, dmix, keep, send, sems) = refs[11:]
    mover = Mover(sems)
    in_dg, in_du = mover.start(dg_i, dg), mover.start(du_i, du)
    in_wg = mover.pieces(offs, gate_pieces, wg)
    in_wu = mover.pieces(offs, lift_pieces, wu)
    in_mid, in_mix = mover.start(mid_i, mid), mover.start(mix_i, mix)
    in_wo = mover.pieces(offs, out_pieces, wo)
    in_act = mover.start(act_i, act)
    in_wd = [mover.start(down_full, wd)]
    width = wd.shape[1]

    wait([in_dg] + in_wg)

    def back(which, j):
        at = pl.ds(pl.multiple_of(j * TILE, TILE), TILE)
        if which == 0:
            dhid[:, at] = mm(dg[...], wg[at, :], NT)
        else:
            dhid[:, at] += mm(du[...], wu[at, :], NT)
        return 0

    lax.fori_loop(0, width // TILE, lambda j, _: back(0, j), 0)
    wait([in_du] + in_wu)
    lax.fori_loop(0, width // TILE, lambda j, _: back(1, j), 0)
    wait([in_mid, in_mix] + in_wo)
    middle = mid[...]
    scale = lax.rsqrt(jnp.mean(middle * middle, axis=-1, keepdims=True) + EPS)
    gain_grad, part = norm_back(dhid[...], middle * scale, scale, gain_ref[...])
    fgain[...] = jnp.broadcast_to(gain_grad, fgain.shape)
    total = c_ref[...].astype(f32) + part
    dhid[...] = total
    branch = total.astype(bf16)
    done = [mover.start(dhid, dmid_o), mover.start(fgain, fgain_o)]
    dmix[...] = mm(wo[...], branch, NT).astype(bf16)
    done += [mover.start(dmix, dmix_o)]
    done += shard_products(who[0], mix, branch, keep, send, mover, keep_o, send_o)
    wait([in_act] + in_wd)

    def forth(j, _):
        at = pl.ds(pl.multiple_of(j * TILE, TILE), TILE)
        res[:, at] = (mid[:, at] + mm(act[...], wd[:, at])).astype(bf16)
        return 0

    lax.fori_loop(0, width // TILE, forth, 0)
    done += [mover.start(res, res_o)]
    wait(done)


def settle(offs, who, upstream, gain, w_out, w_down, w_gate, w_up, act, mid, dg, du, mix, parts):
    rows, width = upstream.shape
    inner = act.shape[1]
    count = len(w_gate)
    shard = (parts // 2, width // parts, width)
    return pl.pallas_call(
        functools.partial(settle_kernel, count),
        out_shape=[
            like(rows, width),
            like(rows, width, dtype=f32),
            like(8, width, dtype=f32),
            like(width, rows),
            like(*shard),
            like(*shard),
        ],
        in_specs=[smem()] * 2 + [vmem()] * 2 + [anywhere()] * (3 * count + 6),
        out_specs=[anywhere()] * 6,
        scratch_shapes=[
            scratch(inner, width),
            scratch(width, inner),
            scratch(width, inner),
            scratch(width, width),
            scratch(rows, inner),
            scratch(rows, width, dtype=f32),
            scratch(rows, inner),
            scratch(rows, inner),
            scratch(width, rows),
            scratch(rows, width, dtype=f32),
            scratch(rows, width),
            scratch(8, width, dtype=f32),
            scratch(width, rows),
            scratch(*shard),
            scratch(*shard),
            pltpu.SemaphoreType.DMA((3 * count + 10 + parts,)),
        ],
        compiler_params=params(),
        cost_estimate=cost(2 * rows * width * (3 * inner + 2 * width), 2 * inner * (3 * width + 3 * rows)),
        name="settle",
    )(offs, who, upstream, gain, w_down, *w_out, *w_gate, *w_up, act, mid, dg, du, mix)


def tail_kernel(count, cols, offs, who, dq_ref, own_ref, cos_ref, sin_ref, hid_ref, x_ref, gain_ref, dmid_ref, fgain_ref, *refs):
    pieces = refs[:count]
    grad_ref, keep_o, send_o = refs[count : count + 3]
    w, raw, keep, send, sems = refs[count + 3 :]
    mover = Mover(sems)
    w_in = mover.pieces(offs, pieces, w)
    cosine, sine = cos_ref[...], -sin_ref[...]
    raw[0:QCOLS, :] = dq_ref[...].astype(bf16)
    raw[QCOLS:cols, :] = own_ref[...]
    raw[cols:, :] = jnp.zeros((raw.shape[0] - cols, raw.shape[1]), bf16)
    for r in range(QRANK):
        at = BQ + r * HDIM
        one, two = turn(dq_ref[at : at + HDIM, :], cosine, sine)
        raw[at : at + HALF, :] = one.astype(bf16)
        raw[at + HALF : at + HDIM, :] = two.astype(bf16)
    for r in range(KRANK):
        at = BK + r * HDIM
        one, two = turn(own_ref[at : at + HDIM, :].astype(f32), cosine, sine)
        raw[QCOLS + at : QCOLS + at + HALF, :] = one.astype(bf16)
        raw[QCOLS + at + HALF : QCOLS + at + HDIM, :] = two.astype(bf16)
    draw = jnp.transpose(raw[...])
    wait(w_in)
    xf = x_ref[...].astype(f32)
    scale = lax.rsqrt(jnp.mean(xf * xf, axis=-1, keepdims=True) + EPS)
    dhid = mm(draw, w[...], NT)
    gain_grad, part = norm_back(dhid, xf * scale, scale, gain_ref[...])
    grad_ref[...] = dmid_ref[...] + part
    width = raw.shape[0]
    line = lax.broadcasted_iota(jnp.int32, (128, gain_grad.shape[1]), 0) + (width - 128)
    both = jnp.where(line == cols, gain_grad, jnp.where(line == cols + 1, fgain_ref[0:1, :], 0.0))
    both = jnp.transpose(both)
    raw_gain = both.astype(bf16)
    w[:, 0:128] = raw_gain
    count_j, rows, _ = keep.shape
    done = []
    for odd, dst, out in ((1, send, send_o), (0, keep, keep_o)):
        for j in range(count_j):
            at = pl.ds(pl.multiple_of((who[0] ^ (2 * j + odd)) * rows, 16), rows)
            got = mm(hid_ref[at, :], draw)
            dst[j, :, 0 : width - 128] = got[:, 0 : width - 128].astype(bf16)
            dst[j, :, width - 128 :] = (got[:, width - 128 :] + w[at, 0:128].astype(f32)).astype(bf16)
            done.append(mover.start(dst.at[j], out.at[j]))
    wait(done)


def tail(offs, who, dq, own, cosine, sine, hidT, x, gain, dmid, fgain, w_fac, cols, parts):
    rows, width = x.shape
    wide = w_fac[0].shape[1]
    count = len(w_fac)
    shard = (parts // 2, width // parts, wide)
    return pl.pallas_call(
        functools.partial(tail_kernel, count, cols),
        out_shape=[like(rows, width, dtype=f32), like(*shard), like(*shard)],
        in_specs=[smem()] * 2 + [vmem()] * 9 + [anywhere()] * count,
        out_specs=[vmem()] + [anywhere()] * 2,
        scratch_shapes=[
            scratch(width, wide),
            scratch(wide, rows),
            scratch(*shard),
            scratch(*shard),
            pltpu.SemaphoreType.DMA((count + parts,)),
        ],
        compiler_params=params(),
        cost_estimate=cost(4 * rows * width * cols, 4 * width * (cols + 3 * rows)),
        name="tail",
    )(offs, who, dq, own, cosine, sine, hidT, x, gain, dmid, fgain, *w_fac)


def partner(values, axis, flip):
    size = lax.axis_size(axis)
    return lax.ppermute(values, axis, [(i, i ^ flip) for i in range(size)])


def finish_kernel(count, place_ref, *refs):
    near, far, out = refs[:count], refs[count], refs[count + 1]
    low, high = place_ref[0], place_ref[1]
    rows = near[0].shape[0]
    for j, piece in enumerate(near):
        at = (high ^ j) * 2 * rows
        out[pl.ds(pl.multiple_of(at + low * rows, 8), rows), :] = piece[...].astype(f32)
        out[pl.ds(pl.multiple_of(at + (1 - low) * rows, 8), rows), :] = far[j].astype(f32)


def finish(place, near, far):
    rows, cols = near[0].shape
    count = len(near)
    return pl.pallas_call(
        functools.partial(finish_kernel, count),
        out_shape=like(2 * count * rows, cols, dtype=f32),
        in_specs=[smem()] + [vmem()] * (count + 1),
        out_specs=vmem(),
        compiler_params=params(),
        cost_estimate=cost(0, 12 * count * rows * cols),
        name="finish",
    )(place, *near, far)


def after(value, *earlier):
    return lax.optimization_barrier((value, *earlier))[0]


def places(pieces, rows, half):
    me = lax.axis_index("grp")
    at = []
    for flip, which in pieces:
        row = (me ^ flip) * rows
        at += [row if which is None else row + which * half, 0]
    return jnp.stack([jnp.asarray(v, jnp.int32) for v in at])


def add(*terms):
    total = terms[0].astype(f32)
    for term in terms[1:]:
        total = total + term.astype(f32)
    return total.astype(bf16)


def scatter_all(keep, send):
    parts = lax.axis_size("grp")
    me = lax.axis_index("grp")
    both = jnp.stack([keep, send], axis=1).reshape((parts,) + keep.shape[1:])
    both = jnp.take(both, jnp.arange(parts) ^ me, axis=0)
    return lax.psum_scatter(both, "grp", scatter_dimension=0, tiled=False)


class Order:
    def __init__(self):
        self.last = None

    def __call__(self, value, *earlier):
        earlier = earlier if self.last is None else earlier + (self.last,)
        return after(value, *earlier) if earlier else value

    def ran(self, value):
        self.last = value
        return value


class Chunk:
    def __init__(self, order, keep, send):
        self.order, self.keep, self.send = order, keep, send

    def core(self, *earlier):
        self.got = partner(after(self.send, *earlier) if earlier else self.send, "grp", 1)

    def add_core(self):
        kept = self.order(self.keep)
        self.other = self.order.ran(add(kept[1], self.got[1]))
        self.mine = add(kept[0], self.got[0])

    def cross(self, *earlier):
        self.got = partner(after(self.other, *earlier) if earlier else self.other, "grp", 2)

    def add_cross(self):
        low = lax.axis_index("rep") % 2
        rows, cols = self.mine.shape
        cut = lambda v, i: lax.dynamic_index_in_dim(v.reshape(4, 2, rows // 8, cols), i, 1, False)
        mine = self.order(self.mine)
        self.other = self.order.ran(add(cut(mine, 1 - low), cut(self.got, 1 - low)))
        self.mine = add(cut(mine, low), cut(self.got, low))

    def side(self):
        self.got = partner(self.other, "rep", 1)

    def add_side(self):
        high = lax.axis_index("rep") // 2
        cut = lambda v, i: lax.dynamic_index_in_dim(v, i, 0, False)
        mine = self.order(self.mine)
        self.other = [add(cut(mine, high ^ j), cut(self.got, high ^ j)) for j in range(1, 4)]
        self.mine = self.order.ran(add(cut(mine, high), cut(self.got, high)))

    def line(self):
        self.got = [partner(value, "rep", 2 * (j + 1)) for j, value in enumerate(self.other)]

    def add_line(self):
        self.mine = self.order.ran(add(self.order(self.mine), *self.got))

    def gather(self):
        self.whole = lax.all_gather(self.mine, "rep", axis=0, tiled=True)
        return self.whole.astype(f32)

    def spread_line(self):
        self.near = [self.mine] + [partner(self.mine, "rep", 2 * j) for j in range(1, 4)]

    def spread_side(self):
        self.far = partner(self.order.ran(jnp.stack([self.order(self.mine)] + self.near[1:])), "rep", 1)

    def finish(self):
        place = jnp.stack([lax.axis_index("rep") % 2, lax.axis_index("rep") // 2])
        near = [self.order(self.mine)] + self.near[1:]
        return self.order.ran(finish(place.astype(jnp.int32), near, self.far))


def local(
    layer_input,
    branch,
    attention_gain,
    factor_weight,
    output_weight,
    feed_gain,
    gate_weight,
    up_weight,
    down_weight,
    cotangent,
):
    rows = layer_input.shape[1]
    parts = lax.axis_size("grp")
    me = lax.axis_index("grp")
    prompt_parts = parts // 2
    follows = me >= prompt_parts
    chosen = branch[0, jnp.maximum(me - prompt_parts, 0)]
    limit = jnp.where(follows, chosen, me * rows)
    npc = (limit + rows - 1) // rows
    position = jnp.where(follows, chosen, me * rows) + jnp.arange(rows, dtype=jnp.int32)
    info = jnp.stack([me, npc, limit]).astype(jnp.int32)
    freqs = 10000.0 ** (-jnp.arange(HALF).astype(f32) / HALF)
    phase = freqs[:, None] * position.astype(f32)[None, :]
    cosine, sine = jnp.cos(phase), jnp.sin(phase)

    x = layer_input[0]
    upstream = cotangent[0]
    shard_rows, cols = factor_weight.shape
    wide = (cols // 128 + 1) * 128
    factor_wide = jnp.concatenate(
        [
            factor_weight,
            attention_gain[:, None],
            feed_gain[:, None],
            jnp.zeros((shard_rows, wide - cols - 2), bf16),
        ],
        axis=1,
    )
    gather = lambda value: lax.all_gather(value, "grp", axis=0, tiled=True)

    if parts != 4 or lax.axis_size("rep") != 8:
        whole = jnp.zeros((2,), jnp.int32)
        w_fac, w_out, w_down = [gather(factor_wide)], [gather(output_weight)], gather(down_weight)
        w_gate, w_up = [gather(gate_weight)], [gather(up_weight)]
        fac, kv_own, hid_one, gains = front(whole, x, cosine, sine, w_fac, cols)
        kv = [lax.all_gather(kv_own, "grp", axis=0, tiled=False)]
        mixed, lse = attend(info, fac, kv, 0, HEADS)
        mid, hid_two, act, slope, lin, *down_terms = feed(
            whole, info, mixed, x, gains[1:2], upstream, w_out, w_gate, w_up, parts
        )
        dgate, dup = slopes(upstream, w_down, slope, lin)
        gk, gs, uk, us = widths(info, hid_two, dgate, dup, parts)
        result, dmid, fgain, dmix, *out_terms = settle(
            whole, info, upstream, gains[1:2], w_out, w_down, w_gate, w_up,
            act, mid, dgate, dup, mixed, parts,
        )
        dq, *dkv = attend_back(info, fac, kv, dmix, lse, 0, HEADS, ())
        input_grad, *fac_terms = tail(
            whole, info, dq, scatter_all(*dkv), cosine, sine, hid_one, x, gains[0:1], dmid, fgain,
            w_fac, cols, parts,
        )
        terms = (fac_terms, out_terms, (gk, gs), (uk, us), down_terms)
        sums = [lax.psum(scatter_all(*pair), "rep").astype(f32) for pair in terms]
        fac_grad, out_grad, gate_grad, up_grad, down_grad = sums
    else:
        order = Order()
        low = lax.axis_index("rep") % 2
        even = (lax.axis_index("rep") // 2) % 2
        half = shard_rows // 2
        take = lambda v, which: lax.dynamic_slice_in_dim(v, which * half, half, 0)
        quarter = places([(k, None) for k in range(4)], shard_rows, half)
        by_side = places(
            [(0, None), (1, None), (2, low), (2, 1 - low), (3, low), (3, 1 - low)], shard_rows, half
        )
        fac_x = partner(factor_wide, "grp", 2)
        fac_c = partner(factor_wide, "grp", 1)
        fac_xc = partner(fac_x, "grp", 1)
        gate_x = partner(after(take(gate_weight, low), fac_x), "grp", 2)
        gate_c = partner(after(gate_weight, fac_x), "grp", 1)
        w_fac = [factor_wide, fac_c, fac_x, fac_xc]
        fac, kv_own, hid_one, gains = front(quarter, x, cosine, sine, w_fac, cols)
        kv_x = partner(kv_own, "grp", 2)
        kv_c = partner(kv_own, "grp", 1)
        out_x = partner(after(take(output_weight, low), gate_x), "grp", 2)
        out_c = partner(after(output_weight, gate_x), "grp", 1)
        up_c = partner(after(up_weight, gate_x), "grp", 1)
        gate_y = partner(gate_x, "rep", 1)
        gate_xc = partner(gate_x, "grp", 1)
        up_x = partner(after(take(up_weight, low), gate_x, kv_x), "grp", 2)
        kv_xc = partner(kv_x, "grp", 1)
        kv = [kv_own, kv_c, kv_x, kv_xc]
        part = HEADS // 4
        heads = []
        heads.append(attend(info, after(fac, gate_x), kv, 0, part))
        order.ran(heads[-1][0])
        out_y = partner(order(out_x), "rep", 1)
        out_xc = partner(order(out_x), "grp", 1)
        heads.append(attend(info, order(fac, out_x), kv, part, part))
        order.ran(heads[-1][0])
        up_y = partner(order(up_x), "rep", 1)
        up_xc = partner(order(up_x), "grp", 1)
        gate_yc = partner(order(gate_y), "grp", 1)
        out_yc = partner(order(out_y), "grp", 1)
        heads.append(attend(info, order(fac, up_x, gate_y, out_y), kv, 2 * part, part))
        order.ran(heads[-1][0])
        w_down = gather(after(down_weight, up_x))
        heads.append(attend(info, order(fac), kv, 3 * part, part))
        order.ran(heads[-1][0])
        up_yc = partner(order(up_y), "grp", 1)
        mixed = jnp.concatenate([got for got, _ in heads], axis=0)
        lse = jnp.concatenate([got for _, got in heads], axis=0)
        w_out = [output_weight, out_c, out_x, out_y, out_xc, out_yc]
        w_gate = [gate_weight, gate_c, gate_x, gate_y, gate_xc, gate_yc]
        w_up = [up_weight, up_c, up_x, up_y, up_xc, up_yc]

        mid, hid_two, act, slope, lin, *terms = feed(
            by_side, info, mixed, x, gains[1:2], upstream, w_out, w_gate, w_up, parts
        )
        down = Chunk(order, *terms)
        down.core()
        dgate, dup = slopes(upstream, w_down, slope, lin)
        order.ran(dgate)
        down.add_core()
        down.cross()
        gk, gs, uk, us = widths(info, order(hid_two), dgate, dup, parts)
        order.ran(gk)
        gate, up = Chunk(order, gk, gs), Chunk(order, uk, us)
        gate.core()
        up.core(gate.got)
        result, dmid, fgain, dmix, *terms = settle(
            by_side, info, upstream, gains[1:2], w_out, w_down, w_gate, w_up,
            act, mid, dgate, order(dup), mixed, parts,
        )
        order.ran(dmix)
        out = Chunk(order, *terms)
        out.core()
        gate.add_core()
        gate.cross(down.got)
        down.add_cross()
        down.side()
        state = attend_back(info, fac, kv, order(dmix), lse, 0, part, ())
        order.ran(state[0])
        up.add_core()
        out.add_core()
        down.add_side()
        down.line()
        state = attend_back(info, fac, kv, order(dmix), lse, part, part, state)
        order.ran(state[0])
        gate.add_cross()
        gate.side()
        up.cross(gate.other)
        down.add_line()
        down_grad = down.gather()
        state = attend_back(info, fac, kv, order(dmix), lse, 2 * part, part, state)
        order.ran(state[0])
        gate.add_side()
        gate.line()
        dq, *terms = attend_back(info, fac, kv, order(dmix), lse, 3 * part, part, state)
        order.ran(dq)
        dkv = Chunk(order, *terms)
        dkv.core()
        gate.add_line()
        gate_grad = gate.gather()
        dkv.add_core()
        dkv.cross(up.got)
        up.add_cross()
        up.side()
        out.cross(dkv.got)
        own = order.ran(add(order(dkv.mine), dkv.got))
        input_grad, *terms = tail(
            quarter, info, dq, own, cosine, sine, hid_one, x, gains[0:1], dmid, fgain, w_fac, cols, parts
        )
        order.ran(input_grad)
        factor = Chunk(order, *terms)
        factor.core()
        up.add_side()
        up.line()
        factor.add_core()
        factor.cross()
        out.add_cross()
        out.side()
        up.add_line()
        up.spread_line()
        factor.add_cross()
        factor.side()
        out.add_side()
        out.line()
        up.spread_side()
        factor.add_side()
        factor.line()
        out.add_line()
        out.spread_line()
        factor.add_line()
        factor.spread_line()
        out.spread_side()
        up_grad = up.finish()
        factor.spread_side()
        out_grad = out.finish()
        fac_grad = factor.finish()
    return (
        result[None],
        input_grad[None],
        fac_grad[:, cols],
        fac_grad[:, :cols],
        out_grad,
        fac_grad[:, cols + 1],
        gate_grad,
        up_grad,
        down_grad,
    )


def solution(mesh):
    in_specs = (
        P("rep", "grp", None),
        P("rep", None),
        P("grp"),
        P("grp", None),
        P("grp", None),
        P("grp"),
        P("grp", None),
        P("grp", None),
        P("grp", None),
        P("rep", "grp", None),
    )
    out_specs = (
        P("rep", "grp", None),
        P("rep", "grp", None),
        P("grp"),
        P("grp", None),
        P("grp", None),
        P("grp"),
        P("grp", None),
        P("grp", None),
        P("grp", None),
    )
    return jax.shard_map(local, mesh=mesh, in_specs=in_specs, out_specs=out_specs, check_vma=False)
```

time: 734 us -> 454 us (0.62)
  waiting for transfers between devices: 517 us -> 141 us
  starting transfers between devices: 0.48 us -> 98.8 us
  Pallas kernels: 35.3 us -> 131 us
  matrix products: 75.1 us -> 0 us
  blocking collectives: 54.3 us -> 0 us
  other arithmetic: 22.7 us -> 43.8 us
    reduce_scatter x6 -> x0, waiting for transfers between devices: 250 us -> none  [the longest x5 209 us: reduced(): lax.psum_scatter(values.astype(bf16), 'grp', scatter_dimension=0, tiled=T...]
    psum x1 -> x0, waiting for transfers between devices: 145 us -> none  [reduced(): return lax.psum(shard, 'rep').astype(f32)]
    ppermute x0 -> x65, waiting for transfers between devices: none -> 141 us  [partner(): return lax.ppermute(values, axis, [(i, i ^ flip) for i in range(size)])]
    all_gather x5 -> x3, waiting for transfers between devices: 119 us -> 0.02 us  [the longest x2 0.02 us: gather(): self.whole = lax.all_gather(self.mine, 'rep', axis=0, tiled=True)]
    ppermute x0 -> x65, starting transfers between devices: none -> 98.2 us  [partner(): return lax.ppermute(values, axis, [(i, i ^ flip) for i in range(size)])]
    pallas_call x3 -> x17, Pallas kernels: 35.3 us -> 131 us  [the longest x4 32.1 us: attend_back(): pl.pallas_call(functools.partial(attend_back_kernel, first, heads, final,...]
    dot_general x14 -> x0, matrix products: 75.1 us -> none  [mm(): return lax.dot_general(left, right, dims, preferred_element_type=f32)]
    convert_element_type x11 -> x24, other arithmetic: 11.9 us -> 40.8 us  [the longest x22 34.4 us: add(): return total.astype(bf16)]
  transfers between devices with their start and end apart: 12 -> 68, of which waited for: 11 -> 20; matrix products, arithmetic and copies ran while one was open for 10% -> 10% of each run, Pallas kernels for 2% -> 26%
where the time goes in v2:
time: 454 us; the launch traced here: 449 us
  waiting for transfers between devices  141 us (31%)
  Pallas kernels  131 us (29%)
  starting transfers between devices  98.8 us (22%)
  other arithmetic  43.8 us (10%)
  local copies, waits for them, and re-layouts  18.9 us (4%)
  between operations  15.3 us (3%)
    ppermute x65, waiting for transfers between devices, partner(): return lax.ppermute(values, axis, [(i, i ^ flip) for i in range(size)])  141 us
    ppermute x65, starting transfers between devices, partner(): return lax.ppermute(values, axis, [(i, i ^ flip) for i in range(size)])  98.2 us
    convert_element_type x22, other arithmetic, add(): return total.astype(bf16)  34.4 us
    pallas_call x4, Pallas kernels, attend_back(): pl.pallas_call(functools.partial(attend_back_kernel, first, heads, final,...  32.1 us
    pallas_call x1, Pallas kernels, feed(): pl.pallas_call(functools.partial(feed_kernel, count), out_shape=[like(row...  19.7 us
    pallas_call x4, Pallas kernels, attend(): pl.pallas_call(functools.partial(attend_kernel, first, heads, len(kv)), o...  19.5 us
    pallas_call x1, Pallas kernels, settle(): pl.pallas_call(functools.partial(settle_kernel, count), out_shape=[like(r...  18.4 us
    pallas_call x1, Pallas kernels, slopes(): pl.pallas_call(slopes_kernel, out_shape=[like(rows, inner)] * 2, in_specs...  10.9 us
  transfers between devices with their start and end apart: 68, of which 20 were waited for; matrix products, arithmetic and copies ran while one was open for 10% of the time, Pallas kernels for 26%

profile of v2, /device:TPU:0, one launch (start us, length us, event | category | flops | bytes accessed | tf_op | source)
XLA Modules:
  0.0 449.4 jit_solution(645583053511113397)
XLA Ops:
  13.2 10.5 %collective-permute-done.1.refs_2_ = bf16[256,896]{1,0:T(8,128)(2,1)S(1)} collective-permute-done((bf16[256,896]{1,0:T(8,128)(2,1)S(1)}, bf16[256,896]{1,0:T(8,128)(2,1)S(1)}, u32[]{:S(2)}, u32[]{:S(2)}) %collective-permute-start.1) | collective-permute-done | bytes 458784 | tf_op jit(solution)/shard_map/ppermute | solution.py:684
  30.6 4.8 %front.1 = (bf16[480,384]{1,0:T(8,128)(2,1)}, bf16[320,384]{1,0:T(8,128)(2,1)}, bf16[1024,384]{1,0:T(8,128)(2,1)}, f32[8,1024]{1,0:T(8,128)}) custom-call(s32[8]{0:T(128)} %stack.117.offs, bf16[384,1024]{1,0:T(8,128)(2,1)} %bitcast.169, f32[32,384]{1,0:T(8,128)} %get-tuple-element.270.cos_ref, f32[32,384]{1,0:T(8,128)} %get-tuple-element.269.sin_ref, ...), custom_call_target="tpu_custom_call" | custom-call | flops 629145600 | bytes 4849664 | tf_op jit(solution)/shard_map/front/pallas_call | solution.py:89
  36.9 13.7 %collective-permute-done.4.refs_2_ = bf16[320,384]{1,0:T(8,128)(2,1)S(1)} collective-permute-done((bf16[320,384]{1,0:T(8,128)(2,1)}, bf16[320,384]{1,0:T(8,128)(2,1)S(1)}, u32[]{:S(2)}, u32[]{:S(2)}) %collective-permute-start.4) | collective-permute-done | bytes 245792 | tf_op jit(solution)/shard_map/ppermute | solution.py:684
  54.0 15.8 %collective-permute-done.5.refs_14_ = bf16[128,2816]{1,0:T(8,128)(2,1)} collective-permute-done((bf16[128,2816]{1,0:T(8,128)(2,1)S(1)}, bf16[128,2816]{1,0:T(8,128)(2,1)}, u32[]{:S(2)}, u32[]{:S(2)}) %collective-permute-start.5) | collective-permute-done | bytes 720928 | tf_op jit(solution)/shard_map/ppermute | solution.py:684
  72.8 4.8 %attend.4 = (bf16[256,384]{1,0:T(8,128)(2,1)}, f32[4,384]{1,0:T(4,128)}) custom-call(s32[3]{0:T(128)} %pad_add_fusion.info_ref.who, bf16[480,384]{1,0:T(8,128)(2,1)} %get-tuple-element.127.fac_ref, bf16[320,384]{1,0:T(8,128)(2,1)} %get-tuple-element.109.refs_0_, bf16[320,384]{1,0:T(8,128)(2,1)} %copy-done.43, bf16[320,384]{1,0:T(8,128)(2,1)} %copy-done.42, ...), custom_call_target="tpu_custom_call" | custom-call | flops 14495514624 | bytes 1966080 | tf_op jit(solution)/shard_map/attend/pallas_call | solution.py:205
  78.4 5.0 %attend.5 = (bf16[256,384]{1,0:T(8,128)(2,1)}, f32[4,384]{1,0:T(4,128)}) custom-call(s32[3]{0:T(128)} %pad_add_fusion.info_ref.who, bf16[480,384]{1,0:T(8,128)(2,1)} %get-tuple-element.127.fac_ref, bf16[320,384]{1,0:T(8,128)(2,1)} %get-tuple-element.109.refs_0_, bf16[320,384]{1,0:T(8,128)(2,1)} %copy-done.43, bf16[320,384]{1,0:T(8,128)(2,1)} %copy-done.42, ...), custom_call_target="tpu_custom_call" | custom-call | flops 14495514624 | bytes 1966080 | tf_op jit(solution)/shard_map/attend/pallas_call | solution.py:205
  83.5 11.6 %collective-permute-done.10.refs_3_ = bf16[128,1024]{1,0:T(8,128)(2,1)S(1)} collective-permute-done((bf16[128,1024]{1,0:T(8,128)(2,1)S(1)}, bf16[128,1024]{1,0:T(8,128)(2,1)S(1)}, u32[]{:S(2)}, u32[]{:S(2)}) %collective-permute-start.10) | collective-permute-done | bytes 262176 | tf_op jit(solution)/shard_map/ppermute | solution.py:684
  96.9 4.8 %attend.6 = (bf16[256,384]{1,0:T(8,128)(2,1)}, f32[4,384]{1,0:T(4,128)}) custom-call(s32[3]{0:T(128)} %pad_add_fusion.info_ref.who, bf16[480,384]{1,0:T(8,128)(2,1)} %get-tuple-element.127.fac_ref, bf16[320,384]{1,0:T(8,128)(2,1)} %get-tuple-element.109.refs_0_, bf16[320,384]{1,0:T(8,128)(2,1)} %copy-done.43, bf16[320,384]{1,0:T(8,128)(2,1)} %copy-done.42, ...), custom_call_target="tpu_custom_call" | custom-call | flops 14495514624 | bytes 1966080 | tf_op jit(solution)/shard_map/attend/pallas_call | solution.py:205
  101.7 12.2 %collective-permute-done.18.refs_15_ = bf16[128,2816]{1,0:T(8,128)(2,1)} collective-permute-done((bf16[128,2816]{1,0:T(8,128)(2,1)}, bf16[128,2816]{1,0:T(8,128)(2,1)}, u32[]{:S(2)}, u32[]{:S(2)}) %collective-permute-start.18) | collective-permute-done | bytes 720928 | tf_op jit(solution)/shard_map/ppermute | solution.py:684
  113.9 4.8 %attend.7 = (bf16[256,384]{1,0:T(8,128)(2,1)}, f32[4,384]{1,0:T(4,128)}) custom-call(s32[3]{0:T(128)} %pad_add_fusion.info_ref.who, bf16[480,384]{1,0:T(8,128)(2,1)} %get-tuple-element.127.fac_ref, bf16[320,384]{1,0:T(8,128)(2,1)} %get-tuple-element.109.refs_0_, bf16[320,384]{1,0:T(8,128)(2,1)} %copy-done.43, bf16[320,384]{1,0:T(8,128)(2,1)} %copy-done.42, ...), custom_call_target="tpu_custom_call" | custom-call | flops 14495514624 | bytes 1966080 | tf_op jit(solution)/shard_map/attend/pallas_call | solution.py:205
  127.5 19.7 %feed.1 = (f32[384,1024]{1,0:T(8,128)}, bf16[1024,384]{1,0:T(8,128)(2,1)}, bf16[384,2816]{1,0:T(8,128)(2,1)}, bf16[384,2816]{1,0:T(8,128)(2,1)}, bf16[384,2816]{...) custom-call(s32[12]{0:T(128)} %stack.110.offs, s32[3]{0:T(128)} %pad_add_fusion.info_ref.who, ...), custom_call_target="tpu_custom_call" | custom-call | flops 7449083904 | bytes 23789568 | tf_op jit(solution)/shard_map/feed/pallas_call | solution.py:437
  147.7 10.9 %slopes.1 = (bf16[384,2816]{1,0:T(8,128)(2,1)}, bf16[384,2816]{1,0:T(8,128)(2,1)}) custom-call(bf16[384,1024]{1,0:T(8,128)(2,1)} %bitcast.176, bf16[384,2816]{1,0:T(8,128)(2,1)} %get-tuple-element.132.slope_ref, bf16[384,2816]{1,0:T(8,128)(2,1)} %get-tuple-element.133.lin_ref, bf16[2816,1024]{1,0:T(8,128)(2,1)} %all-gather.4.cloned.1.call-done.wd.down_full), custom_call_target="tpu_custom_call" | custom-call | flops 2214592512 | bytes 14417920 | tf_op jit(solution)/shard_map/slopes/pallas_call | solution.py:486
  158.6 5.3 %fusion.2 = (bf16[704,1024]{1,0:T(8,128)(2,1)S(1)}, bf16[704,1024]{1,0:T(8,128)(2,1)}) fusion(bf16[2,704,1024]{2,1,0:T(8,128)(2,1)} %collective-permute-done.21, bf16[2,704,1024]{2,1,0:T(8,128)(2,1)} %get-tuple-element.138), kind=kLoop, calls=%fused_computation.8 | loop fusion | flops 5767168 | bytes 8650752 | tf_op jit(solution)/shard_map/convert_element_type | solution.py:728
  163.8 10.3 %widths.1 = (bf16[2,256,2816]{2,1,0:T(8,128)(2,1)}, bf16[2,256,2816]{2,1,0:T(8,128)(2,1)}, bf16[2,256,2816]{2,1,0:T(8,128)(2,1)}, bf16[2,256,2816]{2,1,0:T(8,128)(2,1)}) custom-call(s32[3]{0:T(128)} %pad_add_fusion.info_ref.who, bf16[1024,384]{1,0:T(8,128)(2,1)} %get-tuple-element.140.hid_ref, bf16[384,2816]{1,0:T(8,128)(2,1)} %get-tuple-element.134.dg_ref.refs_20_, ...), custom_call_target="tpu_custom_call" | custom-call | flops 4429185024 | bytes 15859712 | tf_op jit(solution)/shard_map/widths/pallas_call | solution.py:508
  179.0 18.4 %settle.1 = (bf16[384,1024]{1,0:T(8,128)(2,1)}, f32[384,1024]{1,0:T(8,128)}, f32[8,1024]{1,0:T(8,128)}, bf16[1024,384]{1,0:T(8,128)(2,1)}, bf16[2,256,1024]{2,1,0:T(8,128)(2,1)}, /*index=5*/bf16[2,256,1024]{2,1,0:T(8,128)(2,1)}) custom-call(s32[12]{0:T(128)} %stack.110.offs, s32[3]{0:T(128)} %pad_add_fusion.info_ref.who, bf16[384,1024]{1,0:T(8,128)(2,1)} %bitcast.177, ...), custom_call_target="tpu_custom_call" | custom-call | flops 8254390272 | bytes 23789568 | tf_op jit(solution)/shard_map/settle/pallas_call | solution.py:578
  201.9 9.5 %collective-permute-done.23 = bf16[704,1024]{1,0:T(8,128)(2,1)} collective-permute-done((bf16[704,1024]{1,0:T(8,128)(2,1)}, bf16[704,1024]{1,0:T(8,128)(2,1)}, u32[]{:S(2)}, u32[]{:S(2)}) %collective-permute-start.23) | collective-permute-done | bytes 1441824 | tf_op jit(solution)/shard_map/ppermute | solution.py:684
  216.0 7.3 %attend_back.4 = (f32[480,384]{1,0:T(8,128)}, f32[4,320,384]{2,1,0:T(8,128)}) custom-call(s32[3]{0:T(128)} %pad_add_fusion.info_ref.who, bf16[480,384]{1,0:T(8,128)(2,1)} %get-tuple-element.127.fac_ref, bf16[1024,384]{1,0:T(8,128)(2,1)} %get-tuple-element.172.grad_ref, f32[16,384]{1,0:T(8,128)} %pad_maximum_fusion.3.lse_ref, ...), custom_call_target="tpu_custom_call" | custom-call | flops 36238786560 | bytes 3932160 | tf_op jit(solution)/shard_map/attend_back/pallas_call | solution.py:303
  223.3 7.9 %collective-permute-start.27 = (bf16[256,2816]{1,0:T(8,128)(2,1)}, bf16[256,2816]{1,0:T(8,128)(2,1)}, u32[]{:S(2)}, u32[]{:S(2)}) collective-permute-start(bf16[256,2816]{1,0:T(8,128)(2,1)} %get-tuple-element.166), channel_id=1, source_target_pairs={{0,2},{1,3},{2,0},{3,1},{4,6},{5,7},{6,4},{7,5},{8,10},{9,11},{10,... | collective-permute-start | bytes 4325384 | tf_op jit(solution)/shard_map/ppermute | solution.py:684
  231.2 4.5 fusion.5
  240.2 8.2 %attend_back.5 = (f32[480,384]{1,0:T(8,128)}, f32[4,320,384]{2,1,0:T(8,128)}) custom-call(s32[3]{0:T(128)} %pad_add_fusion.info_ref.who, bf16[480,384]{1,0:T(8,128)(2,1)} %get-tuple-element.127.fac_ref, bf16[1024,384]{1,0:T(8,128)(2,1)} %get-tuple-element.172.grad_ref, f32[16,384]{1,0:T(8,128)} %pad_maximum_fusion.3.lse_ref, ...), custom_call_target="tpu_custom_call" | custom-call | flops 36238786560 | bytes 3932160 | tf_op jit(solution)/shard_map/attend_back/pallas_call | solution.py:303
  252.8 10.9 %collective-permute-done.27 = bf16[256,2816]{1,0:T(8,128)(2,1)} collective-permute-done((bf16[256,2816]{1,0:T(8,128)(2,1)}, bf16[256,2816]{1,0:T(8,128)(2,1)}, u32[]{:S(2)}, u32[]{:S(2)}) %collective-permute-start.27) | collective-permute-done | bytes 1441824 | tf_op jit(solution)/shard_map/ppermute | solution.py:684
  269.8 8.5 %attend_back.6 = (f32[480,384]{1,0:T(8,128)}, f32[4,320,384]{2,1,0:T(8,128)}) custom-call(s32[3]{0:T(128)} %pad_add_fusion.info_ref.who, bf16[480,384]{1,0:T(8,128)(2,1)} %get-tuple-element.127.fac_ref, bf16[1024,384]{1,0:T(8,128)(2,1)} %get-tuple-element.172.grad_ref, f32[16,384]{1,0:T(8,128)} %pad_maximum_fusion.3.lse_ref, ...), custom_call_target="tpu_custom_call" | custom-call | flops 36238786560 | bytes 3932160 | tf_op jit(solution)/shard_map/attend_back/pallas_call | solution.py:303
  278.3 8.1 %collective-permute-done.31 = bf16[4,32,2816]{2,1,0:T(8,128)(2,1)S(1)} collective-permute-done((bf16[4,32,2816]{2,1,0:T(8,128)(2,1)}, bf16[4,32,2816]{2,1,0:T(8,128)(2,1)S(1)}, u32[]{:S(2)}, u32[]{:S(2)}) %collective-permute-start.31) | collective-permute-done | bytes 720928 | tf_op jit(solution)/shard_map/ppermute | solution.py:684
  291.7 8.0 %attend_back.7 = (f32[480,384]{1,0:T(8,128)}, bf16[2,320,384]{2,1,0:T(8,128)(2,1)}, bf16[2,320,384]{2,1,0:T(8,128)(2,1)}) custom-call(s32[3]{0:T(128)} %pad_add_fusion.info_ref.who, bf16[480,384]{1,0:T(8,128)(2,1)} %get-tuple-element.127.fac_ref, bf16[1024,384]{1,0:T(8,128)(2,1)} %get-tuple-element.172.grad_ref, f32[16,384]{1,0:T(8,128)} %pad_maximum_fusion.3.lse_ref, ...), custom_call_target="tpu_custom_call" | custom-call | flops 36238786560 | bytes 3932160 | tf_op jit(solution)/shard_map/attend_back/pallas_call | solution.py:303
  299.7 10.2 %collective-permute-done.33 = bf16[32,2816]{1,0:T(8,128)(2,1)S(1)} collective-permute-done((bf16[32,2816]{1,0:T(8,128)(2,1)}, bf16[32,2816]{1,0:T(8,128)(2,1)S(1)}, u32[]{:S(2)}, u32[]{:S(2)}) %collective-permute-start.33) | collective-permute-done | bytes 180256 | tf_op jit(solution)/shard_map/ppermute | solution.py:684
  319.6 8.1 %tail.1 = (f32[384,1024]{1,0:T(8,128)}, bf16[2,256,896]{2,1,0:T(8,128)(2,1)}, bf16[2,256,896]{2,1,0:T(8,128)(2,1)}) custom-call(s32[8]{0:T(128)} %stack.117.offs, s32[3]{0:T(128)} %pad_add_fusion.info_ref.who, f32[480,384]{1,0:T(8,128)} %get-tuple-element.174.dq_ref, bf16[320,384]{1,0:T(8,128)(2,1)} %add_convert_fusion.18.own_ref, ...), custom_call_target="tpu_custom_call" | custom-call | flops 1258291200 | bytes 7995392 | tf_op jit(solution)/shard_map/tail/pallas_call | solution.py:664
  333.8 7.5 %collective-permute-start.41 = (bf16[32,2816]{1,0:T(8,128)(2,1)S(1)}, bf16[32,2816]{1,0:T(8,128)(2,1)S(1)}, u32[]{:S(2)}, u32[]{:S(2)}) collective-permute-start(bf16[32,2816]{1,0:T(8,128)(2,1)S(1)} %get-tuple-element.241), channel_id=1, source_target_pairs={{0,8},{4,12},{8,0},{12,4},{16,24},{20,28},{24,16},{28,20},{1,9},{5... | collective-permute-start | bytes 540680 | tf_op jit(solution)/shard_map/ppermute | solution.py:684
  351.1 8.2 %collective-permute-done.42 = bf16[32,2816]{1,0:T(8,128)(2,1)S(1)} collective-permute-done((bf16[32,2816]{1,0:T(8,128)(2,1)S(1)}, bf16[32,2816]{1,0:T(8,128)(2,1)S(1)}, u32[]{:S(2)}, u32[]{:S(2)}) %collective-permute-start.42) | collective-permute-done | bytes 180256 | tf_op jit(solution)/shard_map/ppermute | solution.py:684
  360.6 6.2 %collective-permute-start.46 = (bf16[32,2816]{1,0:T(8,128)(2,1)S(1)}, bf16[32,2816]{1,0:T(8,128)(2,1)S(1)}, u32[]{:S(2)}, u32[]{:S(2)}) collective-permute-start(bf16[32,2816]{1,0:T(8,128)(2,1)S(1)} %add_convert_fusion.23.refs_0_), channel_id=1, source_target_pairs={{0,8},{4,12},{8,0},{12,4},{16,24},{20,28},{24,16},{28,20},{1,9},{5... | collective-permute-start | bytes 540680 | tf_op jit(solution)/shard_map/ppermute | solution.py:684
  373.6 15.4 %collective-permute-done.47.refs_2_ = bf16[32,2816]{1,0:T(8,128)(2,1)S(1)} collective-permute-done((bf16[32,2816]{1,0:T(8,128)(2,1)S(1)}, bf16[32,2816]{1,0:T(8,128)(2,1)S(1)}, u32[]{:S(2)}, u32[]{:S(2)}) %collective-permute-start.47) | collective-permute-done | bytes 180256 | tf_op jit(solution)/shard_map/ppermute | solution.py:684
  389.8 8.0 %collective-permute-start.50 = (bf16[32,1024]{1,0:T(8,128)(2,1)S(1)}, bf16[32,1024]{1,0:T(8,128)(2,1)S(1)}, u32[]{:S(2)}, u32[]{:S(2)}) collective-permute-start(bf16[32,1024]{1,0:T(8,128)(2,1)S(1)} %get-tuple-element.259), channel_id=1, source_target_pairs={{0,8},{4,12},{8,0},{12,4},{16,24},{20,28},{24,16},{28,20},{1,9},{5... | collective-permute-start | bytes 196616 | tf_op jit(solution)/shard_map/ppermute | solution.py:684
  404.2 4.8 %collective-permute-start.55 = (bf16[32,896]{1,0:T(8,128)(2,1)S(1)}, bf16[32,896]{1,0:T(8,128)(2,1)S(1)}, u32[]{:S(2)}, u32[]{:S(2)}) collective-permute-start(bf16[32,896]{1,0:T(8,128)(2,1)S(1)} %get-tuple-element.264), channel_id=1, source_target_pairs={{0,24},{4,28},{8,16},{12,20},{16,8},{20,12},{24,0},{28,4},{1,25},{... | collective-permute-start | bytes 172040 | tf_op jit(solution)/shard_map/ppermute | solution.py:684
  (266 shorter events, 140.2 us)
Async XLA Ops:
  7.2 140.5 %all-gather.4.cloned.1.call-start = ((), (), s32[]{:S(2)}) async-start(), calls=%async_computation | async-start | bytes 7208960 | tf_op jit(solution)/shard_map/all_gather | solution.py:846
  27.0 23.7 %collective-permute-start.3 = (bf16[128,2816]{1,0:T(8,128)(2,1)S(1)}, bf16[128,2816]{1,0:T(8,128)(2,1)}, u32[]{:S(2)}, u32[]{:S(2)}) collective-permute-start(bf16[128,2816]{1,0:T(8,128)(2,1)S(1)} %constant_dynamic-slice_fusion.1), channel_id=1, source_target_pairs={{0,2},{1,3},{2,0},{3,1},{4,6},{5,7},{6,4},{7,5},{8,10},{9,11},{10,... | collective-permute-start | bytes 2162696 | tf_op jit(solution)/shard_map/ppermute | solution.py:684
  50.7 19.2 %collective-permute-start.5 = (bf16[128,2816]{1,0:T(8,128)(2,1)S(1)}, bf16[128,2816]{1,0:T(8,128)(2,1)}, u32[]{:S(2)}, u32[]{:S(2)}) collective-permute-start(bf16[128,2816]{1,0:T(8,128)(2,1)S(1)} %constant_dynamic-slice_fusion.2), channel_id=1, source_target_pairs={{0,2},{1,3},{2,0},{3,1},{4,6},{5,7},{6,4},{7,5},{8,10},{9,11},{10,... | collective-permute-start | bytes 2162696 | tf_op jit(solution)/shard_map/ppermute | solution.py:684
  52.4 18.0 %collective-permute-start.8 = (bf16[320,384]{1,0:T(8,128)(2,1)S(1)}, bf16[320,384]{1,0:T(8,128)(2,1)S(1)}, u32[]{:S(2)}, u32[]{:S(2)}) collective-permute-start(bf16[320,384]{1,0:T(8,128)(2,1)S(1)} %copy-done.41), channel_id=1, source_target_pairs={{0,1},{1,0},{2,3},{3,2},{4,5},{5,4},{6,7},{7,6},{8,9},{9,8},{10,11... | collective-permute-start | bytes 737288 | tf_op jit(solution)/shard_map/ppermute | solution.py:684
  52.4 18.6 %collective-permute-start.9 = (bf16[320,384]{1,0:T(8,128)(2,1)S(1)}, bf16[320,384]{1,0:T(8,128)(2,1)S(1)}, u32[]{:S(2)}, u32[]{:S(2)}) collective-permute-start(bf16[320,384]{1,0:T(8,128)(2,1)S(1)} %collective-permute-done.4.refs_2_), channel_id=1, source_target_pairs={{0,1},{1,0},{2,3},{3,2},{4,5},{5,4},{6,7},{7,6},{8,9},{9,8},{10,11... | collective-permute-start | bytes 737288 | tf_op jit(solution)/shard_map/ppermute | solution.py:684
  53.6 71.1 %collective-permute-start.13 = (bf16[256,2816]{1,0:T(8,128)(2,1)}, bf16[256,2816]{1,0:T(8,128)(2,1)}, u32[]{:S(2)}, u32[]{:S(2)}) collective-permute-start(bf16[256,2816]{1,0:T(8,128)(2,1)} %refs_6_.3), channel_id=1, source_target_pairs={{0,1},{1,0},{2,3},{3,2},{4,5},{5,4},{6,7},{7,6},{8,9},{9,8},{10,11... | collective-permute-start | bytes 4325384 | tf_op jit(solution)/shard_map/ppermute | solution.py:684
  53.7 24.0 %collective-permute-start.7 = (bf16[128,1024]{1,0:T(8,128)(2,1)S(1)}, bf16[128,1024]{1,0:T(8,128)(2,1)S(1)}, u32[]{:S(2)}, u32[]{:S(2)}) collective-permute-start(bf16[128,1024]{1,0:T(8,128)(2,1)S(1)} %constant_dynamic-slice_fusion), channel_id=1, source_target_pairs={{0,2},{1,3},{2,0},{3,1},{4,6},{5,7},{6,4},{7,5},{8,10},{9,11},{10,... | collective-permute-start | bytes 786440 | tf_op jit(solution)/shard_map/ppermute | solution.py:684
  69.9 56.7 %collective-permute-start.17 = (bf16[256,2816]{1,0:T(8,128)(2,1)}, bf16[256,2816]{1,0:T(8,128)(2,1)}, u32[]{:S(2)}, u32[]{:S(2)}) collective-permute-start(bf16[256,2816]{1,0:T(8,128)(2,1)} %refs_12_.3), channel_id=1, source_target_pairs={{0,1},{1,0},{2,3},{3,2},{4,5},{5,4},{6,7},{7,6},{8,9},{9,8},{10,11... | collective-permute-start | bytes 4325384 | tf_op jit(solution)/shard_map/ppermute | solution.py:684
  69.9 356.5 %all-gather.8.cloned.1.call-start = ((), (), s32[]{:S(2)}) async-start(), calls=%async_computation.2 | async-start | bytes 1622016 | tf_op jit(solution)/shard_map/all_gather | solution.py:792
  70.5 51.2 %collective-permute-start.6 = (bf16[256,1024]{1,0:T(8,128)(2,1)S(1)}, bf16[256,1024]{1,0:T(8,128)(2,1)S(1)}, u32[]{:S(2)}, u32[]{:S(2)}) collective-permute-start(bf16[256,1024]{1,0:T(8,128)(2,1)S(1)} %copy-done.28), channel_id=1, source_target_pairs={{0,1},{1,0},{2,3},{3,2},{4,5},{5,4},{6,7},{7,6},{8,9},{9,8},{10,11... | collective-permute-start | bytes 1572872 | tf_op jit(solution)/shard_map/ppermute | solution.py:684
  71.1 24.0 %collective-permute-start.14 = (bf16[128,2816]{1,0:T(8,128)(2,1)}, bf16[128,2816]{1,0:T(8,128)(2,1)}, u32[]{:S(2)}, u32[]{:S(2)}) collective-permute-start(bf16[128,2816]{1,0:T(8,128)(2,1)} %collective-permute-done.3.refs_8_), channel_id=1, source_target_pairs={{0,4},{4,0},{8,12},{12,8},{16,20},{20,16},{24,28},{28,24},{1,5},{5... | collective-permute-start | bytes 2162696 | tf_op jit(solution)/shard_map/ppermute | solution.py:684
  95.1 26.7 %collective-permute-start.15 = (bf16[128,2816]{1,0:T(8,128)(2,1)}, bf16[128,2816]{1,0:T(8,128)(2,1)S(1)}, u32[]{:S(2)}, u32[]{:S(2)}) collective-permute-start(bf16[128,2816]{1,0:T(8,128)(2,1)} %collective-permute-done.3.refs_8_), channel_id=1, source_target_pairs={{0,1},{1,0},{2,3},{3,2},{4,5},{5,4},{6,7},{7,6},{8,9},{9,8},{10,11... | collective-permute-start | bytes 2162696 | tf_op jit(solution)/shard_map/ppermute | solution.py:684
  95.1 18.9 %collective-permute-start.18 = (bf16[128,2816]{1,0:T(8,128)(2,1)}, bf16[128,2816]{1,0:T(8,128)(2,1)}, u32[]{:S(2)}, u32[]{:S(2)}) collective-permute-start(bf16[128,2816]{1,0:T(8,128)(2,1)} %collective-permute-done.5.refs_14_), channel_id=1, source_target_pairs={{0,4},{4,0},{8,12},{12,8},{16,20},{20,16},{24,28},{28,24},{1,5},{5... | collective-permute-start | bytes 2162696 | tf_op jit(solution)/shard_map/ppermute | solution.py:684
  174.1 23.4 %collective-permute-start.22 = (bf16[2,256,2816]{2,1,0:T(8,128)(2,1)}, bf16[2,256,2816]{2,1,0:T(8,128)(2,1)}, u32[]{:S(2)}, u32[]{:S(2)}) collective-permute-start(bf16[2,256,2816]{2,1,0:T(8,128)(2,1)} %get-tuple-element.146), channel_id=1, source_target_pairs={{0,1},{1,0},{2,3},{3,2},{4,5},{5,4},{6,7},{7,6},{8,9},{9,8},{10,11... | collective-permute-start | bytes 8650760 | tf_op jit(solution)/shard_map/ppermute | solution.py:684
  175.0 36.4 %collective-permute-start.23 = (bf16[704,1024]{1,0:T(8,128)(2,1)}, bf16[704,1024]{1,0:T(8,128)(2,1)}, u32[]{:S(2)}, u32[]{:S(2)}) collective-permute-start(bf16[704,1024]{1,0:T(8,128)(2,1)} %get-tuple-element.228), channel_id=1, source_target_pairs={{0,2},{1,3},{2,0},{3,1},{4,6},{5,7},{6,4},{7,5},{8,10},{9,11},{10,... | collective-permute-start | bytes 4325384 | tf_op jit(solution)/shard_map/ppermute | solution.py:684
  197.3 38.3 %collective-permute-start.25 = (bf16[2,256,1024]{2,1,0:T(8,128)(2,1)}, bf16[2,256,1024]{2,1,0:T(8,128)(2,1)}, u32[]{:S(2)}, u32[]{:S(2)}) collective-permute-start(bf16[2,256,1024]{2,1,0:T(8,128)(2,1)} %get-tuple-element.160), channel_id=1, source_target_pairs={{0,1},{1,0},{2,3},{3,2},{4,5},{5,4},{6,7},{7,6},{8,9},{9,8},{10,11... | collective-permute-start | bytes 3145736 | tf_op jit(solution)/shard_map/ppermute | solution.py:684
  214.5 23.6 %collective-permute-start.26 = (bf16[4,88,1024]{2,1,0:T(8,128)(2,1)}, bf16[4,88,1024]{2,1,0:T(8,128)(2,1)}, u32[]{:S(2)}, u32[]{:S(2)}) collective-permute-start(bf16[4,88,1024]{2,1,0:T(8,128)(2,1)} %get-tuple-element.236), channel_id=1, source_target_pairs={{0,4},{4,0},{8,12},{12,8},{16,20},{20,16},{24,28},{28,24},{1,5},{5... | collective-permute-start | bytes 2162696 | tf_op jit(solution)/shard_map/ppermute | solution.py:684
  223.3 40.5 %collective-permute-start.27 = (bf16[256,2816]{1,0:T(8,128)(2,1)}, bf16[256,2816]{1,0:T(8,128)(2,1)}, u32[]{:S(2)}, u32[]{:S(2)}) collective-permute-start(bf16[256,2816]{1,0:T(8,128)(2,1)} %get-tuple-element.166), channel_id=1, source_target_pairs={{0,2},{1,3},{2,0},{3,1},{4,6},{5,7},{6,4},{7,5},{8,10},{9,11},{10,... | collective-permute-start | bytes 4325384 | tf_op jit(solution)/shard_map/ppermute | solution.py:684
  248.4 20.5 %collective-permute-start.28 = (bf16[88,1024]{1,0:T(8,128)(2,1)}, bf16[88,1024]{1,0:T(8,128)(2,1)S(1)}, u32[]{:S(2)}, u32[]{:S(2)}) collective-permute-start(bf16[88,1024]{1,0:T(8,128)(2,1)} %get-tuple-element.249), channel_id=1, source_target_pairs={{0,8},{4,12},{8,0},{12,4},{16,24},{20,28},{24,16},{28,20},{1,9},{5... | collective-permute-start | bytes 540680 | tf_op jit(solution)/shard_map/ppermute | solution.py:684
  250.0 18.9 %collective-permute-start.29 = (bf16[88,1024]{1,0:T(8,128)(2,1)}, bf16[88,1024]{1,0:T(8,128)(2,1)S(1)}, u32[]{:S(2)}, u32[]{:S(2)}) collective-permute-start(bf16[88,1024]{1,0:T(8,128)(2,1)} %get-tuple-element.251), channel_id=1, source_target_pairs={{0,16},{4,20},{8,24},{12,28},{16,0},{20,4},{24,8},{28,12},{1,17},{... | collective-permute-start | bytes 540680 | tf_op jit(solution)/shard_map/ppermute | solution.py:684
  266.6 19.7 %collective-permute-start.31 = (bf16[4,32,2816]{2,1,0:T(8,128)(2,1)}, bf16[4,32,2816]{2,1,0:T(8,128)(2,1)S(1)}, u32[]{:S(2)}, u32[]{:S(2)}) collective-permute-start(bf16[4,32,2816]{2,1,0:T(8,128)(2,1)} %get-tuple-element.234), channel_id=1, source_target_pairs={{0,4},{4,0},{8,12},{12,8},{16,20},{20,16},{24,28},{28,24},{1,5},{5... | collective-permute-start | bytes 2162696 | tf_op jit(solution)/shard_map/ppermute | solution.py:684
  267.2 44.8 %collective-permute-start.36 = (bf16[256,2816]{1,0:T(8,128)(2,1)}, bf16[256,2816]{1,0:T(8,128)(2,1)}, u32[]{:S(2)}, u32[]{:S(2)}) collective-permute-start(bf16[256,2816]{1,0:T(8,128)(2,1)} %get-tuple-element.180), channel_id=1, source_target_pairs={{0,2},{1,3},{2,0},{3,1},{4,6},{5,7},{6,4},{7,5},{8,10},{9,11},{10,... | collective-permute-start | bytes 4325384 | tf_op jit(solution)/shard_map/ppermute | solution.py:684
  269.7 160.0 %all-gather.6.cloned.1.call-start = ((), (), s32[]{:S(2)}) async-start(), calls=%async_computation.1 | async-start | bytes 1622016 | tf_op jit(solution)/shard_map/all_gather | solution.py:792
  289.0 20.9 %collective-permute-start.33 = (bf16[32,2816]{1,0:T(8,128)(2,1)}, bf16[32,2816]{1,0:T(8,128)(2,1)S(1)}, u32[]{:S(2)}, u32[]{:S(2)}) collective-permute-start(bf16[32,2816]{1,0:T(8,128)(2,1)} %get-tuple-element.247), channel_id=1, source_target_pairs={{0,16},{4,20},{8,24},{12,28},{16,0},{20,4},{24,8},{28,12},{1,17},{... | collective-permute-start | bytes 540680 | tf_op jit(solution)/shard_map/ppermute | solution.py:684
  290.2 19.7 %collective-permute-start.34 = (bf16[32,2816]{1,0:T(8,128)(2,1)}, bf16[32,2816]{1,0:T(8,128)(2,1)S(1)}, u32[]{:S(2)}, u32[]{:S(2)}) collective-permute-start(bf16[32,2816]{1,0:T(8,128)(2,1)} %get-tuple-element.246), channel_id=1, source_target_pairs={{0,24},{4,28},{8,16},{12,20},{16,8},{20,12},{24,0},{28,4},{1,25},{... | collective-permute-start | bytes 540680 | tf_op jit(solution)/shard_map/ppermute | solution.py:684
  327.8 18.3 %collective-permute-start.40 = (bf16[256,1024]{1,0:T(8,128)(2,1)}, bf16[256,1024]{1,0:T(8,128)(2,1)S(1)}, u32[]{:S(2)}, u32[]{:S(2)}) collective-permute-start(bf16[256,1024]{1,0:T(8,128)(2,1)} %get-tuple-element.192), channel_id=1, source_target_pairs={{0,2},{1,3},{2,0},{3,1},{4,6},{5,7},{6,4},{7,5},{8,10},{9,11},{10,... | collective-permute-start | bytes 1572872 | tf_op jit(solution)/shard_map/ppermute | solution.py:684
  345.9 24.0 %collective-permute-start.44 = (bf16[256,896]{1,0:T(8,128)(2,1)S(1)}, bf16[256,896]{1,0:T(8,128)(2,1)S(1)}, u32[]{:S(2)}, u32[]{:S(2)}) collective-permute-start(bf16[256,896]{1,0:T(8,128)(2,1)S(1)} %get-tuple-element.240), channel_id=1, source_target_pairs={{0,2},{1,3},{2,0},{3,1},{4,6},{5,7},{6,4},{7,5},{8,10},{9,11},{10,... | collective-permute-start | bytes 1376264 | tf_op jit(solution)/shard_map/ppermute | solution.py:684
  346.2 24.5 %collective-permute-start.45 = (bf16[4,32,1024]{2,1,0:T(8,128)(2,1)S(1)}, bf16[4,32,1024]{2,1,0:T(8,128)(2,1)S(1)}, u32[]{:S(2)}, u32[]{:S(2)}) collective-permute-start(bf16[4,32,1024]{2,1,0:T(8,128)(2,1)S(1)} %get-tuple-element.254), channel_id=1, source_target_pairs={{0,4},{4,0},{8,12},{12,8},{16,20},{20,16},{24,28},{28,24},{1,5},{5... | collective-permute-start | bytes 786440 | tf_op jit(solution)/shard_map/ppermute | solution.py:684
  366.8 22.2 %collective-permute-start.47 = (bf16[32,2816]{1,0:T(8,128)(2,1)S(1)}, bf16[32,2816]{1,0:T(8,128)(2,1)S(1)}, u32[]{:S(2)}, u32[]{:S(2)}) collective-permute-start(bf16[32,2816]{1,0:T(8,128)(2,1)S(1)} %add_convert_fusion.23.refs_0_), channel_id=1, source_target_pairs={{0,16},{4,20},{8,24},{12,28},{16,0},{20,4},{24,8},{28,12},{1,17},{... | collective-permute-start | bytes 540680 | tf_op jit(solution)/shard_map/ppermute | solution.py:684
  368.5 20.5 %collective-permute-start.48 = (bf16[32,2816]{1,0:T(8,128)(2,1)S(1)}, bf16[32,2816]{1,0:T(8,128)(2,1)S(1)}, u32[]{:S(2)}, u32[]{:S(2)}) collective-permute-start(bf16[32,2816]{1,0:T(8,128)(2,1)S(1)} %add_convert_fusion.23.refs_0_), channel_id=1, source_target_pairs={{0,24},{4,28},{8,16},{12,20},{16,8},{20,12},{24,0},{28,4},{1,25},{... | collective-permute-start | bytes 540680 | tf_op jit(solution)/shard_map/ppermute | solution.py:684
  370.1 30.7 %collective-permute-start.49 = (bf16[4,32,896]{2,1,0:T(8,128)(2,1)S(1)}, bf16[4,32,896]{2,1,0:T(8,128)(2,1)S(1)}, u32[]{:S(2)}, u32[]{:S(2)}) collective-permute-start(bf16[4,32,896]{2,1,0:T(8,128)(2,1)S(1)} %get-tuple-element.258), channel_id=1, source_target_pairs={{0,4},{4,0},{8,12},{12,8},{16,20},{20,16},{24,28},{28,24},{1,5},{5... | collective-permute-start | bytes 688136 | tf_op jit(solution)/shard_map/ppermute | solution.py:684
  389.1 32.9 %collective-permute-start.59 = (bf16[4,32,2816]{2,1,0:T(8,128)(2,1)S(1)}, bf16[4,32,2816]{2,1,0:T(8,128)(2,1)S(1)}, u32[]{:S(2)}, u32[]{:S(2)}) collective-permute-start(bf16[4,32,2816]{2,1,0:T(8,128)(2,1)S(1)} %pad_maximum_fusion), channel_id=1, source_target_pairs={{0,4},{4,0},{8,12},{12,8},{16,20},{20,16},{24,28},{28,24},{1,5},{5... | collective-permute-start | bytes 2162696 | tf_op jit(solution)/shard_map/ppermute | solution.py:684
  (81 other events, 940.5 us)
Sparse Core Ops, SparseCore 0:
  70.0 45.1 all-gather.3
  269.8 50.7 all-gather.7
  327.9 68.5 all-gather.5

commit v3 on v2

v3 whole, which is shorter than its diff:
```python
import functools

import jax
import jax.numpy as jnp
import numpy as np
from jax import lax
from jax.experimental import pallas as pl
from jax.experimental.pallas import tpu as pltpu
from jax.sharding import PartitionSpec as P

HEADS = 16
HDIM = 64
QRANK = 6
KRANK = 2
HALF = HDIM // 2
QCOLS = QRANK * HEADS + QRANK * HDIM
KVCOLS = 2 * (KRANK * HEADS + KRANK * HDIM)
AQ, BQ = 0, QRANK * HEADS
AK, BK = 0, KRANK * HEADS
AV = BK + KRANK * HDIM
BV = AV + KRANK * HEADS
SCALE = HDIM**-0.5
EXP_SCALE = SCALE * float(np.log2(np.e))
NEG = -1e30
DEPTH = 128
EPS = 1e-05
VMEM_LIMIT = 60 * 2**20

f32 = jnp.float32
bf16 = jnp.bfloat16
NN = (((1,), (0,)), ((), ()))
NT = (((1,), (1,)), ((), ()))
TN = (((0,), (0,)), ((), ()))


def mm(left, right, dims=NN):
    return lax.dot_general(left, right, dims, preferred_element_type=f32)


def vmem():
    return pl.BlockSpec(memory_space=pltpu.VMEM)


def smem():
    return pl.BlockSpec(memory_space=pltpu.SMEM)


def params():
    return pltpu.CompilerParams(vmem_limit_bytes=VMEM_LIMIT)


def cost(flops, nbytes):
    return pl.CostEstimate(flops=int(flops) // 10**5, bytes_accessed=int(nbytes) // 10**5, transcendentals=0)


def weighty(micros):
    return pl.CostEstimate(flops=int(micros * 1.1e9), bytes_accessed=0, transcendentals=0)


def turn(part, cosine, sine):
    first, second = part[:HALF], part[HALF:]
    return first * cosine - second * sine, second * cosine + first * sine


def front_kernel(count, cols, offs, x_ref, cos_ref, sin_ref, *refs):
    pieces = refs[:count]
    fac_ref, kv_ref, hid_ref, gains_ref, w, sems = refs[count:]
    w_in = Mover(sems).pieces(offs, pieces, w)
    xf = x_ref[...].astype(f32)
    normed = xf * lax.rsqrt(jnp.mean(xf * xf, axis=-1, keepdims=True) + EPS)
    wait(w_in)
    last = w.shape[1] - 128
    gains = jnp.transpose(w[:, last:])[cols - last : cols - last + 16].astype(f32)
    gains_ref[...] = gains[0:8]
    hidden = (normed * gains[0:1]).astype(bf16)
    hid_ref[...] = jnp.transpose(hidden)
    raw = jnp.transpose(mm(hidden, w[...]))
    cosine, sine = cos_ref[...], sin_ref[...]
    fac_ref[...] = raw[:QCOLS].astype(bf16)
    kv_ref[...] = raw[QCOLS:cols].astype(bf16)
    for ref, first, at in [(fac_ref, 0, BQ + r * HDIM) for r in range(QRANK)] + [
        (kv_ref, QCOLS, BK + r * HDIM) for r in range(KRANK)
    ]:
        one, two = turn(raw[first + at : first + at + HDIM], cosine, sine)
        ref[at : at + HALF, :] = one.astype(bf16)
        ref[at + HALF : at + HDIM, :] = two.astype(bf16)


def front(offs, x, cosine, sine, w_fac, cols):
    rows, width = x.shape
    wide = w_fac[0].shape[1]
    count = len(w_fac)
    return pl.pallas_call(
        functools.partial(front_kernel, count, cols),
        out_shape=[
            like(QCOLS, rows),
            like(cols - QCOLS, rows),
            like(width, rows),
            like(8, width, dtype=f32),
        ],
        in_specs=[smem()] + [vmem()] * 3 + [anywhere()] * count,
        out_specs=[vmem()] * 4,
        scratch_shapes=[scratch(width, wide), pltpu.SemaphoreType.DMA((count,))],
        compiler_params=params(),
        cost_estimate=cost(2 * rows * width * cols, 4 * width * (cols + rows)),
        name="front",
    )(offs, x, cosine, sine, *w_fac)


def load_factors(fac_ref, kv_refs, facf, kvf, qT, me):
    facf[...] = fac_ref[...].astype(f32)
    if len(kv_refs) == 1:

        def load(j, _):
            kvf[j] = kv_refs[0][j].astype(f32)
            return 0

        lax.fori_loop(0, kvf.shape[0], load, 0)
    else:
        for flip, ref in enumerate(kv_refs):
            kvf[me ^ flip] = ref[...].astype(f32)
    row = lax.broadcasted_iota(jnp.int32, (DEPTH - HDIM, qT.shape[1]), 0)
    qT[HDIM:DEPTH, :] = jnp.where(row == 0, 1.0, 0.0).astype(bf16)


def build_query(facf, qT, h):
    total = facf[pl.ds(AQ + h, 1), :] * facf[BQ : BQ + HDIM, :]
    for r in range(1, QRANK):
        total += facf[pl.ds(AQ + r * HEADS + h, 1), :] * facf[BQ + r * HDIM : BQ + (r + 1) * HDIM, :]
    qT[0:HDIM, :] = (total * (1.0 / QRANK)).astype(bf16)


def build_pair(kvf, j, h, a_at, b_at):
    total = kvf[j, pl.ds(a_at + h, 1), :] * kvf[j, b_at : b_at + HDIM, :]
    for r in range(1, KRANK):
        total += (
            kvf[j, pl.ds(a_at + r * HEADS + h, 1), :]
            * kvf[j, b_at + r * HDIM : b_at + (r + 1) * HDIM, :]
        )
    return (total * (1.0 / KRANK)).astype(bf16)


def build_key(kvf, kT, j, h, limit):
    span = kT.shape[1]
    kT[0:HDIM, :] = build_pair(kvf, j, h, AK, BK)
    if limit is None:
        kT[HDIM:DEPTH, :] = jnp.zeros((DEPTH - HDIM, span), bf16)
    else:
        row = lax.broadcasted_iota(jnp.int32, (DEPTH - HDIM, span), 0)
        key = j * span + lax.broadcasted_iota(jnp.int32, (DEPTH - HDIM, span), 1)
        kT[HDIM:DEPTH, :] = jnp.where((row == 0) & (key >= limit), NEG, 0.0).astype(bf16)


def causal(scores):
    key = lax.broadcasted_iota(jnp.int32, scores.shape, 0)
    query = lax.broadcasted_iota(jnp.int32, scores.shape, 1)
    return jnp.where(key <= query, scores, NEG)


def attend_kernel(first, heads, count, info_ref, fac_ref, *refs):
    kv_refs, (out_ref, lse_ref, facf, kvf, qT, kT, s_ref) = refs[:count], refs[count:]
    me, npc, limit = info_ref[0], info_ref[1], info_ref[2]
    rows = fac_ref.shape[1]
    load_factors(fac_ref, kv_refs, facf, kvf, qT, me)

    def head(step, _):
        h = first + step
        build_query(facf, qT, h)

        def chunk(j, top):
            build_key(kvf, kT, j, h, limit)
            scores = mm(kT[...], qT[...], TN)
            s_ref[j] = scores
            return jnp.maximum(top, jnp.max(scores, axis=0, keepdims=True))

        top = lax.fori_loop(0, npc, chunk, jnp.full((1, rows), NEG, f32))
        build_key(kvf, kT, me, h, None)
        scores = causal(mm(kT[...], qT[...], TN))
        s_ref[npc] = scores
        top = jnp.maximum(top, jnp.max(scores, axis=0, keepdims=True)) * EXP_SCALE

        def weigh(j, mass):
            probs = jnp.exp2(s_ref[j] * EXP_SCALE - top)
            s_ref[j] = probs
            return mass + jnp.sum(probs, axis=0, keepdims=True)

        mass = lax.fori_loop(0, npc + 1, weigh, jnp.zeros((1, rows), f32))
        lse_ref[pl.ds(step, 1), :] = top + jnp.log2(mass)
        share = 1.0 / mass

        def gather(j, total):
            at = jnp.where(j == npc, me, j)
            return total + mm(build_pair(kvf, at, h, AV, BV), (s_ref[j] * share).astype(bf16))

        total = lax.fori_loop(0, npc + 1, gather, jnp.zeros((HDIM, rows), f32))
        out_ref[pl.ds(pl.multiple_of(step * HDIM, HDIM), HDIM), :] = total.astype(bf16)
        return 0

    lax.fori_loop(0, heads, head, 0)


def kv_sizes(kv):
    return kv[0].shape if len(kv) == 1 else (len(kv),) + kv[0].shape


def attend(info, fac, kv, first, heads):
    parts, cols, rows = kv_sizes(kv)
    seen = min(parts, parts // 2 + 1)
    return pl.pallas_call(
        functools.partial(attend_kernel, first, heads, len(kv)),
        out_shape=[
            jax.ShapeDtypeStruct((heads * HDIM, rows), bf16),
            jax.ShapeDtypeStruct((heads, rows), f32),
        ],
        in_specs=[smem(), vmem()] + [vmem()] * len(kv),
        out_specs=[vmem()] * 2,
        scratch_shapes=[
            pltpu.VMEM((QCOLS, rows), f32),
            pltpu.VMEM((parts, cols, rows), f32),
            pltpu.VMEM((DEPTH, rows), bf16),
            pltpu.VMEM((DEPTH, rows), bf16),
            pltpu.VMEM((seen, rows, rows), f32),
        ],
        compiler_params=params(),
        cost_estimate=cost(16 * 2 * heads * 256 * rows * rows * seen, 4 * cols * rows * parts),
        name="attend",
    )(info, fac, *kv)


def attend_back_kernel(
    first, heads, final, count, count_out, blocks, info_ref, fac_ref, grad_ref, *refs
):
    kv_refs, lse_refs, refs = refs[:count], refs[count : count + blocks], refs[count + blocks :]
    if first:
        dq_in, dkv_in, *refs = refs
    dq_ref, *refs = refs
    if final:
        outs, refs = refs[:count_out], refs[count_out:]
        dkvf, *refs = refs
    else:
        dkvf, *refs = refs
    facf, kvf, qT, kTs, p_ref, dp_ref, lse_ref = refs
    for i, ref in enumerate(lse_refs):
        lse_ref[i * ref.shape[0] : (i + 1) * ref.shape[0], :] = ref[...]
    me, npc, limit = info_ref[0], info_ref[1], info_ref[2]
    parts, _, rows = kvf.shape
    load_factors(fac_ref, kv_refs, facf, kvf, qT, me)

    def begin(j, _):
        dkvf[j] = dkv_in[j] if first else jnp.zeros(dkvf.shape[1:], f32)
        return 0

    lax.fori_loop(0, parts, begin, 0)
    dq_ref[...] = dq_in[...] if first else jnp.zeros(dq_ref.shape, f32)

    def head(step, _):
        h = first + step
        build_query(facf, qT, h)
        grad = grad_ref[pl.ds(pl.multiple_of(h * HDIM, HDIM), HDIM), :]
        lse = lse_ref[pl.ds(h, 1), :]

        def probe(slot, at, scores, delta):
            probs = jnp.exp2(scores * EXP_SCALE - lse)
            p_ref[slot] = probs
            prob_grad = mm(build_pair(kvf, at, h, AV, BV), grad, TN)
            dp_ref[slot] = prob_grad
            return delta + jnp.sum(probs * prob_grad, axis=0, keepdims=True)

        def chunk(j, delta):
            build_key(kvf, kTs.at[j], j, h, limit)
            return probe(j, j, mm(kTs[j], qT[...], TN), delta)

        delta = lax.fori_loop(0, npc, chunk, jnp.zeros((1, rows), f32))
        build_key(kvf, kTs.at[npc], me, h, None)
        delta = probe(npc, me, causal(mm(kTs[npc], qT[...], TN)), delta)

        def pull(j, total):
            at = jnp.where(j == npc, me, j)
            probs = p_ref[j]
            score_grad = (probs * (dp_ref[j] - delta)).astype(bf16)
            key_grad = mm(qT[0:HDIM, :], score_grad, NT) * (SCALE / KRANK)
            value_grad = mm(grad, probs.astype(bf16), NT) * (1.0 / KRANK)
            for a_at, b_at, got in ((AK, BK, key_grad), (AV, BV, value_grad)):
                for r in range(KRANK):
                    a_row = pl.ds(a_at + r * HEADS + h, 1)
                    b_rows = slice(b_at + r * HDIM, b_at + (r + 1) * HDIM)
                    dkvf[at, a_row, :] = jnp.sum(got * kvf[at, b_rows, :], axis=0, keepdims=True)
                    dkvf[at, b_rows, :] += got * kvf[at, a_row, :]
            return total + mm(kTs[j, 0:HDIM, :], score_grad)

        query_grad = lax.fori_loop(0, npc + 1, pull, jnp.zeros((HDIM, rows), f32)) * (SCALE / QRANK)
        for r in range(QRANK):
            a_row = pl.ds(AQ + r * HEADS + h, 1)
            b_rows = slice(BQ + r * HDIM, BQ + (r + 1) * HDIM)
            dq_ref[a_row, :] = jnp.sum(query_grad * facf[b_rows, :], axis=0, keepdims=True)
            dq_ref[b_rows, :] += query_grad * facf[a_row, :]
        return 0

    lax.fori_loop(0, heads, head, 0)
    if final:
        for flip in range(parts):
            outs[flip % 2][flip // 2] = dkvf[me ^ flip].astype(bf16)


def attend_back(info, fac, kv, grad, lse, first, heads, so_far, declared=None):
    parts, cols, rows = kv_sizes(kv)
    seen = min(parts, parts // 2 + 1)
    final = first + heads == HEADS
    gathered = [like(parts // 2, cols, rows)] * 2 if final else [like(parts, cols, rows, dtype=f32)]
    return pl.pallas_call(
        functools.partial(
            attend_back_kernel, first, heads, final, len(kv), len(gathered), len(lse)
        ),
        out_shape=[like(QCOLS, rows, dtype=f32)] + gathered,
        in_specs=[smem()] + [vmem()] * (2 + len(kv) + len(lse) + len(so_far)),
        out_specs=[vmem()] * (1 + len(gathered)),
        scratch_shapes=([pltpu.VMEM((parts, cols, rows), f32)] if final else [])
        + [
            pltpu.VMEM((QCOLS, rows), f32),
            pltpu.VMEM((parts, cols, rows), f32),
            pltpu.VMEM((DEPTH, rows), bf16),
            pltpu.VMEM((seen, DEPTH, rows), bf16),
            pltpu.VMEM((seen, rows, rows), f32),
            pltpu.VMEM((seen, rows, rows), f32),
            pltpu.VMEM((HEADS, rows), f32),
        ],
        compiler_params=params(),
        cost_estimate=declared or cost(heads * rows * rows, 8 * cols * rows * parts),
        name="attend_back",
    )(info, fac, grad, *kv, *lse, *so_far)


class Mover:
    def __init__(self, sems):
        self.sems = sems
        self.used = 0

    def start(self, src, dst):
        copy = pltpu.make_async_copy(src, dst, self.sems.at[self.used])
        self.used += 1
        copy.start()
        return copy

    def pieces(self, offsets, refs, dst, first=0):
        copies = []
        for i, piece in enumerate(refs):
            rows, cols = piece.shape
            at = pl.ds(pl.multiple_of(offsets[first + 2 * i], 16), rows)
            if cols == dst.shape[1]:
                where = dst.at[at]
            else:
                where = dst.at[at, pl.ds(pl.multiple_of(offsets[first + 2 * i + 1], 128), cols)]
            copies.append(self.start(piece, where))
        return copies


def wait(copies):
    for copy in copies:
        copy.wait()


def anywhere():
    return pl.BlockSpec(memory_space=pl.ANY)


def like(*shape, dtype=bf16):
    return jax.ShapeDtypeStruct(shape, dtype)


def scratch(*shape, dtype=bf16):
    return pltpu.VMEM(shape, dtype)


TILE = 256


def norm_back(grad_hidden, normed, scale, gain):
    grad_normed = grad_hidden * gain
    gain_grad = jnp.sum(grad_hidden * normed, axis=0, keepdims=True)
    mean = jnp.mean(grad_normed * normed, axis=-1, keepdims=True)
    return gain_grad, scale * (grad_normed - normed * mean)


def shard_products(me, left, right, pair, mover, pair_out):
    copies = []
    count, rows, cols = pair[0].shape
    step = rows if rows <= 352 else rows // 2
    width = cols // 2 if cols % 256 == 0 and cols > 2048 else cols
    for odd in (1, 0):
        for j in range(count):
            row = (me ^ (2 * j + odd)) * rows
            for low in range(0, rows, step):
                lhs = left[pl.ds(pl.multiple_of(row + low, 16), step), :]
                for at in range(0, cols, width):
                    pair[odd][j, low : low + step, at : at + width] = mm(
                        lhs, right[:, at : at + width]
                    ).astype(bf16)
            copies.append(mover.start(pair[odd].at[j], pair_out[odd].at[j]))
    return copies


def feed_kernel(count, blocks, offs, x_ref, gain_ref, *refs):
    mix_refs, refs = refs[:blocks], refs[blocks:]
    out_pieces, gate_pieces, lift_pieces = (refs[i * count : (i + 1) * count] for i in range(3))
    refs = refs[3 * count :]
    (mid_o, hid_o, act_o, slope_o, lin_o, actT_o) = refs[:6]
    (wo, wg, wu, mid, hid, hidT, act, slope, lin, actT, sems) = refs[6:]
    mover = Mover(sems)
    wo_in = mover.pieces(offs, out_pieces, wo)
    wg_in = mover.pieces(offs, gate_pieces, wg)
    wu_in = mover.pieces(offs, lift_pieces, wu, 2 * count)
    mix = jnp.concatenate([jnp.transpose(ref[...]) for ref in mix_refs], axis=1)
    wait(wo_in)
    middle = x_ref[...].astype(f32) + mm(mix, wo[...])
    mid[...] = middle
    scale = lax.rsqrt(jnp.mean(middle * middle, axis=-1, keepdims=True) + EPS)
    hidden = (middle * scale * gain_ref[...]).astype(bf16)
    hid[...] = hidden
    hidT[...] = jnp.transpose(hidden)
    done = [mover.start(mid, mid_o), mover.start(hidT, hid_o)]
    wait(wg_in)
    wait(wu_in)

    def tile(j, _):
        cols = pl.ds(pl.multiple_of(j * TILE, TILE), TILE)
        gate = mm(hid[...], wg[:, cols])
        up = mm(hid[...], wu[:, cols])
        sig = jax.nn.sigmoid(gate)
        line = gate * sig
        active = (line * up).astype(bf16)
        act[:, cols] = active
        lin[:, cols] = line.astype(bf16)
        slope[:, cols] = (up * sig * (1.0 + gate * (1.0 - sig))).astype(bf16)
        actT[cols, :] = jnp.transpose(active)
        return 0

    lax.fori_loop(0, wg.shape[1] // TILE, tile, 0, unroll=True)
    done += [mover.start(act, act_o), mover.start(lin, lin_o), mover.start(slope, slope_o)]
    done.append(mover.start(actT, actT_o))
    wait(done)


def feed(offs, mix, x, gain, w_out, w_gate, w_up):
    rows, width = x.shape
    inner = w_gate[0].shape[1]
    count = len(w_gate)
    return pl.pallas_call(
        functools.partial(feed_kernel, count, len(mix)),
        out_shape=[
            like(rows, width, dtype=f32),
            like(width, rows),
            like(rows, inner),
            like(rows, inner),
            like(rows, inner),
        ]
        + [like(inner, rows)],
        in_specs=[smem()] + [vmem()] * (2 + len(mix)) + [anywhere()] * (3 * count),
        out_specs=[anywhere()] * 6,
        scratch_shapes=[
            scratch(width, width),
            scratch(width, inner),
            scratch(width, inner),
            scratch(rows, width, dtype=f32),
            scratch(rows, width),
            scratch(width, rows),
            scratch(rows, inner),
            scratch(rows, inner),
            scratch(rows, inner),
            scratch(inner, rows),
            pltpu.SemaphoreType.DMA((3 * count + 6,)),
        ],
        compiler_params=params(),
        cost_estimate=cost(2 * rows * width * (width + 3 * inner), 2 * inner * (3 * width + 3 * rows)),
        name="feed",
    )(offs, x, gain, *mix, *w_out, *w_gate, *w_up)


def slopes_kernel(count, offs, slope_ref, lin_ref, c_ref, *refs):
    pieces, (dg_o, du_o, wd, dg, du, sems) = refs[:count], refs[count:]
    mover = Mover(sems)
    wait(mover.pieces(offs, pieces, wd))

    def tile(j, _):
        cols = pl.ds(pl.multiple_of(j * TILE, 128), TILE)
        grad = mm(c_ref[...], wd[cols, :], NT)
        dg[:, cols] = (grad * slope_ref[:, cols].astype(f32)).astype(bf16)
        du[:, cols] = (grad * lin_ref[:, cols].astype(f32)).astype(bf16)
        return 0

    lax.fori_loop(0, wd.shape[0] // TILE, tile, 0, unroll=True)
    wait([mover.start(dg, dg_o), mover.start(du, du_o)])


def slopes(offs, upstream, w_down, slope, lin):
    rows, width = upstream.shape
    inner = slope.shape[1]
    count = len(w_down)
    return pl.pallas_call(
        functools.partial(slopes_kernel, count),
        out_shape=[like(rows, inner)] * 2,
        in_specs=[smem()] + [vmem()] * 3 + [anywhere()] * count,
        out_specs=[anywhere()] * 2,
        scratch_shapes=[
            scratch(inner, width),
            scratch(rows, inner),
            scratch(rows, inner),
            pltpu.SemaphoreType.DMA((count + 2,)),
        ],
        compiler_params=params(),
        cost_estimate=cost(2 * rows * width * inner, 2 * inner * (width + 4 * rows)),
        name="slopes",
    )(offs, slope, lin, upstream, *w_down)


def products_kernel(who, left, right, *refs):
    outs, pair, sems = refs[0:2], refs[2:4], refs[4]
    wait(shard_products(who[0], left, right, pair, Mover(sems), outs))


def products(who, left, right, parts):
    width, rows = left.shape
    inner = right.shape[1]
    pair = (parts // 2, width // parts, inner)
    return pl.pallas_call(
        products_kernel,
        out_shape=[like(*pair)] * 2,
        in_specs=[smem()] + [vmem()] * 2,
        out_specs=[anywhere()] * 2,
        scratch_shapes=[scratch(*pair)] * 2 + [pltpu.SemaphoreType.DMA((parts,))],
        compiler_params=params(),
        cost_estimate=cost(2 * rows * width * inner, 2 * inner * (width + rows)),
        name="products",
    )(who, left, right)


def middle_kernel(count, blocks, offs, who, c_ref, gain_ref, *refs):
    out_pieces, gate_pieces, lift_pieces = (refs[i * count : (i + 1) * count] for i in range(3))
    mix_refs, refs = refs[3 * count : 3 * count + blocks], refs[3 * count + blocks :]
    dg_i, du_i, mid_i, dmid_o, fgain, dmix, *refs = refs
    outs, (wg, wu, wo, dg, du, mid, dhid, branch, mix), pair, sems = refs[:2], refs[2:11], refs[11:13], refs[13]
    mover = Mover(sems)
    in_dg = [mover.start(dg_i, dg)]
    in_wg = mover.pieces(offs, gate_pieces, wg)
    in_du = [mover.start(du_i, du)]
    in_wu = mover.pieces(offs, lift_pieces, wu, 2 * count)
    in_mid = [mover.start(mid_i, mid)]
    in_wo = mover.pieces(offs, out_pieces, wo)
    width = wg.shape[0]

    def back(which, j):
        at = pl.ds(pl.multiple_of(j * TILE, TILE), TILE)
        if which == 0:
            dhid[:, at] = mm(dg[...], wg[at, :], NT)
        else:
            dhid[:, at] += mm(du[...], wu[at, :], NT)
        return 0

    wait(in_dg + in_wg)
    lax.fori_loop(0, width // TILE, lambda j, _: back(0, j), 0, unroll=True)
    wait(in_du + in_wu)
    lax.fori_loop(0, width // TILE, lambda j, _: back(1, j), 0, unroll=True)
    wait(in_mid + in_wo)
    middle = mid[...]
    scale = lax.rsqrt(jnp.mean(middle * middle, axis=-1, keepdims=True) + EPS)
    gain_grad, part = norm_back(dhid[...], middle * scale, scale, gain_ref[...])
    fgain[...] = jnp.broadcast_to(gain_grad, fgain.shape)
    total = c_ref[...].astype(f32) + part
    dhid[...] = total
    branch[...] = total.astype(bf16)
    done = [mover.start(dhid, dmid_o)]
    for i, ref in enumerate(mix_refs):
        size = ref.shape[0]
        mix[i * size : (i + 1) * size, :] = ref[...]
    done += shard_products(who[0], mix, branch, pair, mover, outs)
    dmix[...] = mm(wo[...], branch[...], NT).astype(bf16)
    wait(done)


def middle_grads(offs, who, upstream, gain, mix, w_out, w_gate, w_up, dg, du, mid, parts):
    rows, width = upstream.shape
    pair = (parts // 2, width // parts, width)
    inner = dg.shape[1]
    count = len(w_gate)
    return pl.pallas_call(
        functools.partial(middle_kernel, count, len(mix)),
        out_shape=[
            like(rows, width, dtype=f32),
            like(8, width, dtype=f32),
            like(width, rows),
            like(*pair),
            like(*pair),
        ],
        in_specs=[smem()] * 2
        + [vmem()] * 2
        + [anywhere()] * (3 * count)
        + [vmem()] * len(mix)
        + [anywhere()] * 3,
        out_specs=[anywhere()] + [vmem()] * 2 + [anywhere()] * 2,
        scratch_shapes=[
            scratch(width, inner),
            scratch(width, inner),
            scratch(width, width),
            scratch(rows, inner),
            scratch(rows, inner),
            scratch(rows, width, dtype=f32),
            scratch(rows, width, dtype=f32),
            scratch(rows, width),
            scratch(width, rows),
            scratch(*pair),
            scratch(*pair),
            pltpu.SemaphoreType.DMA((3 * count + 4 + parts,)),
        ],
        compiler_params=params(),
        cost_estimate=cost(2 * rows * width * (2 * inner + width), 4 * inner * (width + rows)),
        name="middle_grads",
    )(offs, who, upstream, gain, *w_out, *w_gate, *w_up, *mix, dg, du, mid)


def settle_kernel(count, offs, who, hid_ref, dg_ref, act_i, mid_i, *refs):
    pieces, (res, *outs, wd, act, mid, keep, send, sems) = refs[:count], refs[count:]
    mover = Mover(sems)
    later = [mover.start(act_i, act), mover.start(mid_i, mid)] + mover.pieces(offs, pieces, wd)
    done = shard_products(who[0], hid_ref, dg_ref, (keep, send), mover, outs)
    wait(later)

    def forth(j, _):
        at = pl.ds(pl.multiple_of(j * TILE, TILE), TILE)
        res[:, at] = (mid[:, at] + mm(act[...], wd[:, at])).astype(bf16)
        return 0

    lax.fori_loop(0, wd.shape[1] // TILE, forth, 0, unroll=True)
    wait(done)


def settle(offs, who, hidT, dg, act, mid, w_down, parts):
    rows, width = mid.shape
    count = len(w_down)
    inner = act.shape[1]
    pair = (parts // 2, width // parts, inner)
    return pl.pallas_call(
        functools.partial(settle_kernel, count),
        out_shape=[like(rows, width), like(*pair), like(*pair)],
        in_specs=[smem()] * 2 + [vmem()] * 2 + [anywhere()] * (2 + count),
        out_specs=[vmem()] + [anywhere()] * 2,
        scratch_shapes=[
            scratch(inner, width),
            scratch(rows, inner),
            scratch(rows, width, dtype=f32),
            scratch(*pair),
            scratch(*pair),
            pltpu.SemaphoreType.DMA((2 + count + parts,)),
        ],
        compiler_params=params(),
        cost_estimate=cost(2 * rows * width * (2 * inner + width), 2 * inner * (3 * width + rows)),
        name="settle",
    )(offs, who, hidT, dg, act, mid, *w_down)


def tail_kernel(count, cols, offs, who, dq_ref, own_ref, cos_ref, sin_ref, hid_ref, x_ref, gain_ref, dmid_ref, fgain_ref, *refs):
    pieces = refs[:count]
    grad_ref, *outs = refs[count:]
    *outs, w, raw, sems = outs
    mover = Mover(sems)
    w_in = mover.pieces(offs, pieces, w)
    cosine, sine = cos_ref[...], -sin_ref[...]
    raw[0:QCOLS, :] = dq_ref[...].astype(bf16)
    raw[QCOLS:cols, :] = own_ref[...]
    raw[cols:, :] = jnp.zeros((raw.shape[0] - cols, raw.shape[1]), bf16)
    for r in range(QRANK):
        at = BQ + r * HDIM
        one, two = turn(dq_ref[at : at + HDIM, :], cosine, sine)
        raw[at : at + HALF, :] = one.astype(bf16)
        raw[at + HALF : at + HDIM, :] = two.astype(bf16)
    for r in range(KRANK):
        at = BK + r * HDIM
        one, two = turn(own_ref[at : at + HDIM, :].astype(f32), cosine, sine)
        raw[QCOLS + at : QCOLS + at + HALF, :] = one.astype(bf16)
        raw[QCOLS + at + HALF : QCOLS + at + HDIM, :] = two.astype(bf16)
    draw = jnp.transpose(raw[...])
    wait(w_in)
    xf = x_ref[...].astype(f32)
    scale = lax.rsqrt(jnp.mean(xf * xf, axis=-1, keepdims=True) + EPS)
    dhid = mm(draw, w[...], NT)
    gain_grad, part = norm_back(dhid, xf * scale, scale, gain_ref[...])
    grad_ref[...] = dmid_ref[...] + part
    width = raw.shape[0]
    line = lax.broadcasted_iota(jnp.int32, (128, gain_grad.shape[1]), 0) + (width - 128)
    both = jnp.where(line == cols, gain_grad, jnp.where(line == cols + 1, fgain_ref[0:1, :], 0.0))
    both = jnp.transpose(both)
    raw_gain = both.astype(bf16)
    w[:, 0:128] = raw_gain
    count_out, rows, _ = outs[0].shape
    for flip in range(2 * count_out):
        at = pl.ds(pl.multiple_of((who[0] ^ flip) * rows, 16), rows)
        got = mm(hid_ref[at, :], draw)
        out = outs[flip % 2]
        out[flip // 2, :, 0 : width - 128] = got[:, 0 : width - 128].astype(bf16)
        out[flip // 2, :, width - 128 :] = (got[:, width - 128 :] + w[at, 0:128].astype(f32)).astype(bf16)


def tail(offs, who, dq, own, cosine, sine, hidT, x, gain, dmid, fgain, w_fac, cols, parts):
    rows, width = x.shape
    wide = w_fac[0].shape[1]
    count = len(w_fac)
    shard = (parts // 2, width // parts, wide)
    return pl.pallas_call(
        functools.partial(tail_kernel, count, cols),
        out_shape=[like(rows, width, dtype=f32)] + [like(*shard)] * 2,
        in_specs=[smem()] * 2 + [vmem()] * 9 + [anywhere()] * count,
        out_specs=[vmem()] * 3,
        scratch_shapes=[
            scratch(width, wide),
            scratch(wide, rows),
            pltpu.SemaphoreType.DMA((count,)),
        ],
        compiler_params=params(),
        cost_estimate=cost(4 * rows * width * cols, 4 * width * (cols + 3 * rows)),
        name="tail",
    )(offs, who, dq, own, cosine, sine, hidT, x, gain, dmid, fgain, *w_fac)


def partner(values, axis, flip):
    size = lax.axis_size(axis)
    return lax.ppermute(values, axis, [(i, i ^ flip) for i in range(size)])


def after(value, *earlier):
    if not earlier:
        return value
    return lax.optimization_barrier((value, *earlier))[0]


def places(pieces, rows, half):
    me = lax.axis_index("grp")
    at = []
    for flip, which in pieces:
        row = (me ^ flip) * rows
        at += [row if which is None else row + which * half, 0]
    return jnp.stack([jnp.asarray(v, jnp.int32) for v in at])


def total(*terms):
    got = terms[0].astype(f32)
    for term in terms[1:]:
        got = got + term.astype(f32)
    return got.astype(bf16)


def add_pairs_kernel(*refs):
    mine, other = refs[-2:]
    at = 0
    for keep, got in zip(refs[:-2:2], refs[1:-2:2]):
        cols = slice(at, at + keep.shape[2])
        mine[:, cols] = total(keep[0], got[0])
        other[:, cols] = total(keep[1], got[1])
        at += keep.shape[2]


def add_pairs(groups):
    rows = groups[0][0].shape[1]
    wide = sum(keep.shape[2] for keep, _ in groups)
    steps = next(n for n in (4, 2, 1) if n == 1 or (rows % (16 * n) == 0 and rows * wide > 2**19))
    out = pl.BlockSpec((rows // steps, wide), lambda i: (i, 0))
    terms = [term for group in groups for term in group]
    return pl.pallas_call(
        add_pairs_kernel,
        grid=(steps,),
        out_shape=[like(rows, wide)] * 2,
        in_specs=[pl.BlockSpec((2, rows // steps, v.shape[2]), lambda i: (0, i, 0)) for v in terms],
        out_specs=[out] * 2,
        compiler_params=params(),
        cost_estimate=cost(1, 1),
        name="add_pairs",
    )(*terms)


def halve_kernel(place, keep_one, keep_two, send_one, send_two, keep, send):
    keep[...] = total(keep_one[...], keep_two[...])
    send[...] = total(send_one[...], send_two[...])


def halve(place, one, two):
    rows, cols = one.shape[0] // 8, one.shape[1]
    one, two = (v.reshape(8, rows, cols) for v in (one, two))

    def piece(flip):
        def index(i, place):
            at = place[0] ^ ((i >> 1) * place[2]) ^ ((i & 1) * place[3])
            return (at ^ place[1] if flip else at, 0, 0)

        return pl.BlockSpec((1, rows, cols), index)

    out = pl.BlockSpec((1, rows, cols), lambda i, place: (i, 0, 0))
    return pl.pallas_call(
        halve_kernel,
        grid_spec=pltpu.PrefetchScalarGridSpec(
            num_scalar_prefetch=1,
            grid=(4,),
            in_specs=[piece(False)] * 2 + [piece(True)] * 2,
            out_specs=[out] * 2,
        ),
        out_shape=[like(4, rows, cols)] * 2,
        compiler_params=params(),
        cost_estimate=cost(1, 1),
        name="halve",
    )(place, one, two, one, two)


def batch_kernel(tasks, *refs):
    ins, outs = refs[: 2 * len(tasks)], list(refs[2 * len(tasks) :])
    for i, (kind, flip) in enumerate(tasks):
        one, two = ins[2 * i : 2 * i + 2]
        out = outs.pop(0)
        if kind == "split":
            half = out.shape[0]
            out[...] = total(one[:half], two[:half])
            outs.pop(0)[...] = total(one[half:], two[half:])
        elif kind == "pair":
            out[...] = total(one[0], two[0])
            outs.pop(0)[...] = total(one[1], two[1])
        elif kind == "join":
            half = one.shape[0]
            out[:half] = one[...]
            out[half:] = two[...]
        elif flip:
            for k in range(out.shape[0]):
                out[k] = total(one[k], two[k ^ flip])
        else:
            out[...] = total(one[...], two[...])


def batch(tasks):
    shapes, counts = [], []
    for kind, _, one, _ in tasks:
        first, rest = one.shape[0], one.shape[1:]
        got = {
            "split": [(first // 2,) + rest] * 2,
            "pair": [rest] * 2,
            "join": [(2 * first,) + rest],
            "sum": [one.shape],
        }[kind]
        shapes += got
        counts.append(len(got))
    outs = pl.pallas_call(
        functools.partial(batch_kernel, [task[:2] for task in tasks]),
        out_shape=[like(*shape) for shape in shapes],
        in_specs=[vmem()] * (2 * len(tasks)),
        out_specs=[vmem()] * len(shapes),
        compiler_params=params(),
        cost_estimate=cost(1, 1),
        name="batch",
    )(*[value for task in tasks for value in task[2:]])
    groups = []
    for count in counts:
        groups.append(outs[:count])
        outs = outs[count:]
    return groups


def finish_kernel(widths, place, near, far, *outs):
    _, rows, wide = near.shape
    last = wide - 128
    for side, value in ((0, near), (1, far)):
        for k in range(4):
            at = place[0] ^ (side * place[1]) ^ ((k >> 1) * place[2]) ^ ((k & 1) * place[3])
            row = pl.ds(pl.multiple_of(at * rows, 8), rows)
            col = 0
            for out, cols in zip(outs, widths):
                out[row, :] = value[k, :, col : col + cols].astype(f32)
                col += cols
            if col < wide:
                outs[-1][row, :] = value[k, :, last:].astype(f32)
    if sum(widths) < wide:
        outs[-2][...] = jnp.transpose(outs[-1][...])[sum(widths) - last : sum(widths) - last + 8]


def finish(place, near, far, widths):
    _, rows, wide = near.shape
    shapes = [like(8 * rows, cols, dtype=f32) for cols in widths]
    more = sum(widths) < wide
    return pl.pallas_call(
        functools.partial(finish_kernel, widths),
        out_shape=shapes + ([like(8, 8 * rows, dtype=f32)] if more else []),
        in_specs=[smem()] + [vmem()] * 2,
        out_specs=[vmem()] * (len(shapes) + more),
        scratch_shapes=[scratch(8 * rows, 128, dtype=f32)] if more else [],
        compiler_params=params(),
        cost_estimate=cost(1, 1),
        name="finish",
    )(place, near, far)


def scatter_all(keep, send):
    me = lax.axis_index("grp")
    both = jnp.stack([keep, send], axis=1)
    both = both.reshape((-1,) + both.shape[2:])
    both = jnp.take(both, jnp.arange(both.shape[0]) ^ me, axis=0)
    return lax.psum_scatter(both, "grp", scatter_dimension=0, tiled=False)


class Order:
    def __init__(self):
        self.last = None
        self.before = ()
        self.tasks = []

    def add(self, kind, flip, one, two, then):
        self.tasks.append(((kind, flip, self.free(one), two), then))

    def flush(self):
        groups = batch([task for task, _ in self.tasks])
        for (_, then), group in zip(self.tasks, groups):
            then(*group)
        self.tasks = []

    def __call__(self, value, *earlier):
        earlier = earlier if self.last is None else earlier + (self.last,)
        return after(value, *earlier) if earlier else value

    def phase(self, *results):
        self.before = results
        self.last = None

    def now(self, value, *earlier):
        last = () if self.last is None else (self.last,)
        return after(value, *self.before, *earlier, *last)

    def free(self, value):
        return after(value, *self.before)

    def ran(self, value):
        self.last = value
        return value


BITS = ((1, 2, 4), (2, 1, 4))


def along(values, step):
    reps, parts = lax.axis_size("rep"), lax.axis_size("grp")
    pairs = [
        (r * parts + g, (r ^ BITS[g % 2][step]) * parts + g)
        for r in range(reps)
        for g in range(parts)
    ]
    return lax.ppermute(values, ("rep", "grp"), pairs)


class Chunk:
    def __init__(self, order, place, *pairs):
        self.order, self.place, self.pairs = order, place, pairs

    def core(self):
        send = [after(pair[1], *self.order.before) for pair in self.pairs]
        self.got = [partner(value, "grp", 1) for value in send]

    def add_core(self):
        keep = [self.order.now(self.pairs[0][0])] + [pair[0] for pair in self.pairs[1:]]
        self.mine, self.other = add_pairs(list(zip(keep, self.got)))
        self.order.ran(self.other)

    def cross(self):
        self.got = partner(self.other, "grp", 2)

    def fold(self, step):
        def then(mine, other):
            self.mine, self.other = mine, other
            self.got = along(other, step)

        if step == 0:
            then(*halve(self.place, self.order.now(self.mine), self.got))
            self.order.ran(self.other)
        else:
            self.order.add("split", 0, self.mine, self.got, then)

    def pair(self):
        def then(mine, other):
            self.mine = mine
            self.got = partner(other, "grp", 2)

        self.order.add("pair", 0, self.pairs[0][0], self.got[0], then)

    def swap(self, step):
        def then(mine):
            self.mine = mine
            self.got = along(mine, step % 3)

        self.order.add("sum", (0, 0, 2, 1)[step] if self.mine.shape[0] > 1 else 0, self.mine, self.got, then)

    def open(self, step):
        def then(mine):
            self.mine = mine
            self.got = along(mine, step)

        self.order.add("join", 0, self.mine, self.got, then)

    def finish(self, *widths):
        got = finish(self.place, self.order.now(self.mine), self.got, widths)
        self.order.ran(got[0])
        return got


def local(
    layer_input,
    branch,
    attention_gain,
    factor_weight,
    output_weight,
    feed_gain,
    gate_weight,
    up_weight,
    down_weight,
    cotangent,
):
    rows = layer_input.shape[1]
    parts = lax.axis_size("grp")
    me = lax.axis_index("grp")
    prompt_parts = parts // 2
    follows = me >= prompt_parts
    chosen = branch[0, jnp.maximum(me - prompt_parts, 0)]
    limit = jnp.where(follows, chosen, me * rows)
    npc = (limit + rows - 1) // rows
    position = jnp.where(follows, chosen, me * rows) + jnp.arange(rows, dtype=jnp.int32)
    info = jnp.stack([me, npc, limit]).astype(jnp.int32)
    freqs = 10000.0 ** (-jnp.arange(HALF).astype(f32) / HALF)
    phase = freqs[:, None] * position.astype(f32)[None, :]
    cosine, sine = jnp.cos(phase), jnp.sin(phase)

    x = layer_input[0]
    upstream = cotangent[0]
    shard_rows, cols = factor_weight.shape
    wide = (cols // 128 + 1) * 128
    factor_wide = jnp.concatenate(
        [
            factor_weight,
            attention_gain[:, None],
            feed_gain[:, None],
            jnp.zeros((shard_rows, wide - cols - 2), bf16),
        ],
        axis=1,
    )
    gather = lambda value: lax.all_gather(value, "grp", axis=0, tiled=True)

    if parts != 4 or lax.axis_size("rep") != 8:
        whole = jnp.zeros((4,), jnp.int32)
        w_fac, w_out, w_down = ([gather(v)] for v in (factor_wide, output_weight, down_weight))
        w_gate, w_up = [gather(gate_weight)], [gather(up_weight)]
        fac, kv_own, hid_one, gains = front(whole, x, cosine, sine, w_fac, cols)
        kv = [lax.all_gather(kv_own, "grp", axis=0, tiled=False)]
        mixed, lse = ([got] for got in attend(info, fac, kv, 0, HEADS))
        mid, hid_two, act, slope, lin, act_rows = feed(
            whole, mixed, x, gains[1:2], w_out, w_gate, w_up
        )
        down_pair = products(info, act_rows, upstream, parts)
        dgate, dup = slopes(whole, upstream, w_down, slope, lin)
        up_pair = products(info, hid_two, dup, parts)
        dmid, fgain, dmix, *out_pair = middle_grads(
            whole, info, upstream, gains[1:2], mixed, w_out, w_gate, w_up, dgate, dup, mid, parts
        )
        result, *gate_pair = settle(whole, info, hid_two, dgate, act, mid, w_down, parts)
        dq, *dkv = attend_back(info, fac, kv, dmix, lse, 0, HEADS, ())
        input_grad, *fac_pair = tail(
            whole, info, dq, scatter_all(*dkv), cosine, sine, hid_one, x, gains[0:1], dmid, fgain,
            w_fac, cols, parts,
        )
        pairs = (fac_pair, out_pair, gate_pair, up_pair, down_pair)
        shards = [scatter_all(*pair) for pair in pairs]
        sums = [lax.psum(shard, "rep").astype(f32) for shard in shards]
        fac_grad, out_grad, gate_grad, up_grad, down_grad = sums
        fac_grad, gain_grads = fac_grad[:, :cols], fac_grad[:, cols : cols + 2].T
    else:
        order = Order()
        low = lax.axis_index("rep") % 2
        even = (lax.axis_index("rep") // 2) % 2
        take = lambda v, which: lax.dynamic_slice_in_dim(v, which * (v.shape[0] // 2), v.shape[0] // 2, 0)
        quarter = places([(k, None) for k in range(4)], shard_rows, 0)
        halves = lambda v, rows: places(
            [(0, None), (1, None), (2, v), (2, 1 - v), (3, v), (3, 1 - v)], rows, rows // 2
        )
        by_side, by_line = halves(low, shard_rows), halves(even, shard_rows)
        by_down = halves(low, down_weight.shape[0])
        grp = lambda value, flip: partner(order.free(value), "grp", flip)
        rep = lambda value, flip: partner(order.free(value), "rep", flip)
        fac_x = partner(factor_wide, "grp", 2)
        fac_c = partner(factor_wide, "grp", 1)
        gate_c = partner(gate_weight, "grp", 1)
        up_c = partner(up_weight, "grp", 1)
        out_c = partner(output_weight, "grp", 1)
        gate_half, up_half = take(gate_weight, low), take(up_weight, even)
        out_half, down_half = take(output_weight, low), take(down_weight, low)
        order.phase(fac_x, fac_c, gate_c, up_c, out_c, gate_half, up_half, out_half, down_half)
        fac_xc = grp(fac_x, 1)
        gate_x = grp(gate_half, 2)
        w_fac = [factor_wide, fac_c, fac_x, fac_xc]
        fac, kv_own, hid_one, gains = front(quarter, order.now(x), cosine, sine, w_fac, cols)
        kv_x = partner(kv_own, "grp", 2)
        kv_c = partner(kv_own, "grp", 1)
        kv_xc = partner(kv_x, "grp", 1)
        kv = [kv_own, kv_c, kv_x, kv_xc]

        order.phase(gate_x, kv_x, kv_c, kv_xc)
        up_x = grp(up_half, 2)
        out_x = grp(out_half, 2)
        gate_y = rep(gate_x, 1)
        gate_xc = grp(gate_x, 1)
        down_c = grp(down_weight, 1)
        part = HEADS // 2
        heads = [attend(info, order.now(fac), kv, 0, part)]

        order.phase(up_x, out_x, gate_y, gate_xc, down_c, heads[0][0])
        down_x = grp(down_half, 2)
        up_z = rep(up_x, 2)
        up_xc = grp(up_x, 1)
        out_y = rep(out_x, 1)
        gate_yc = grp(gate_y, 1)
        heads.append(attend(info, order.now(fac), kv, part, part))
        mixed, lse = ([got[i] for got in heads] for i in range(2))

        order.phase(down_x, up_z, up_xc, out_y, gate_yc, heads[1][0])
        up_zc = grp(up_z, 1)
        out_xc = grp(out_x, 1)
        out_yc = grp(out_y, 1)
        w_out = [output_weight, out_c, out_x, out_y, out_xc, out_yc]
        w_gate = [gate_weight, gate_c, gate_x, gate_y, gate_xc, gate_yc]
        w_up = [up_weight, up_c, up_x, up_z, up_xc, up_zc]
        offs_feed = jnp.concatenate([by_side, by_line])

        order.phase(up_zc, out_xc, out_yc)
        odd = me % 2
        place = jnp.stack([lax.axis_index("rep"), 1 + odd, 2 - odd, jnp.full_like(odd, 4)])
        place = place.astype(jnp.int32)
        chunk = functools.partial(Chunk, order, place)
        down_y = rep(down_x, 1)
        down_xc = grp(down_x, 1)
        mid, hid_two, act, slope, lin, act_rows = feed(
            offs_feed, mixed, order.now(x), gains[1:2], w_out, w_gate, w_up
        )

        order.phase(down_y, down_xc, mid)
        down_yc = grp(down_y, 1)
        w_down = [down_weight, down_c, down_x, down_y, down_xc, down_yc]
        down = chunk(products(info, order.now(act_rows), upstream, parts))

        order.phase(down_yc, down.pairs[0][0])
        down.core()
        dgate, dup = slopes(by_down, order.now(upstream), w_down, slope, lin)
        up = chunk(products(info, hid_two, dup, parts))

        order.phase(*down.got, up.pairs[0][0])
        down.add_core()
        down.cross()
        up.core()
        dmid, fgain, dmix, *out_pair = middle_grads(
            offs_feed, info, order.free(upstream), gains[1:2], mixed, w_out, w_gate, w_up,
            dgate, dup, mid, parts,
        )
        out = chunk(out_pair)
        out.core()
        result, *terms = settle(
            by_down, info, after(hid_two, dmix), dgate, act, mid, w_down, parts
        )
        gate = chunk(terms)

        order.phase(down.got, *up.got, *out.got, result)
        both = chunk(*up.pairs, *out.pairs)
        both.got = up.got + out.got
        both.add_core()
        both.cross()
        down.fold(0)
        gate.core()
        part = 3 * HEADS // 4
        state = attend_back(info, fac, kv, order.free(dmix), lse, 0, part, ())

        order.phase(both.got, down.got, *gate.got, state[0])
        gate.add_core()
        gate.cross()
        both.fold(0)
        down.fold(1)
        order.flush()
        dq, *terms = attend_back(info, fac, kv, order.free(dmix), lse, part, HEADS - part, state)

        order.phase(both.got, down.got, dq)
        dkv = chunk(terms)
        dkv.core()
        both.fold(1)
        down.fold(2)
        order.flush()

        order.phase(*dkv.got, both.got, down.got, gate.got)
        dkv.pair()
        both.fold(2)
        order.flush()
        gate.fold(0)

        order.phase(dkv.got, both.got, gate.got)
        sums = []
        order.add("sum", 0, dkv.mine, dkv.got, sums.append)
        both.swap(2)
        gate.fold(1)
        order.flush()
        input_grad, *terms = tail(
            quarter, info, dq, sums[0], cosine, sine, hid_one, x, gains[0:1], dmid, fgain,
            w_fac, cols, parts,
        )

        order.phase(both.got, gate.got, input_grad)
        factor = chunk(terms)
        factor.core()
        both.open(1)
        gate.fold(2)
        down.swap(2)
        order.flush()

        order.phase(*factor.got, both.got, gate.got, down.got)
        factor.pair()
        both.open(0)
        gate.swap(2)
        down.open(1)
        order.flush()

        order.phase(factor.got, both.got, gate.got, down.got)
        factor.fold(0)
        gate.open(1)
        down.open(0)
        order.flush()
        up_grad, out_grad = both.finish(up_weight.shape[1], output_weight.shape[1])

        order.phase(factor.got, gate.got, down.got, up_grad)
        factor.swap(1)
        gate.open(0)
        order.flush()
        (down_grad,) = down.finish(down_weight.shape[1])

        order.phase(factor.got, gate.got, down_grad)
        factor.swap(2)
        order.flush()
        (gate_grad,) = gate.finish(gate_weight.shape[1])

        order.phase(factor.got, gate_grad)
        factor.swap(3)
        order.flush()

        order.phase(factor.got)
        fac_grad, gain_grads = factor.finish(cols)
    return (
        result[None],
        input_grad[None],
        gain_grads[0],
        fac_grad,
        out_grad,
        gain_grads[1],
        gate_grad,
        up_grad,
        down_grad,
    )


def solution(mesh):
    in_specs = (
        P("rep", "grp", None),
        P("rep", None),
        P("grp"),
        P("grp", None),
        P("grp", None),
        P("grp"),
        P("grp", None),
        P("grp", None),
        P("grp", None),
        P("rep", "grp", None),
    )
    out_specs = (
        P("rep", "grp", None),
        P("rep", "grp", None),
        P("grp"),
        P("grp", None),
        P("grp", None),
        P("grp"),
        P("grp", None),
        P("grp", None),
        P("grp", None),
    )
    return jax.shard_map(local, mesh=mesh, in_specs=in_specs, out_specs=out_specs, check_vma=False)
```

time: 454 us -> 435 us (0.958)
  Pallas kernels: 131 us -> 184 us
  starting transfers between devices: 98.8 us -> 56.7 us
  other arithmetic: 43.8 us -> 3.27 us
  waiting for transfers between devices: 141 us -> 155 us
  between operations: 15.3 us -> 1.95 us
  local copies, waits for them, and re-layouts: 18.9 us -> 27.7 us
    ppermute x0 -> x22, waiting for transfers between devices: none -> 78.3 us  [along(): return lax.ppermute(values, ('rep', 'grp'), pairs)]
    pallas_call x6 -> x26, Pallas kernels: 48.3 us -> 123 us  [the longest x10 25.1 us: batch(): pl.pallas_call(functools.partial(batch_kernel, [task[:2] for task in task...]
    ppermute x65 -> x37, starting transfers between devices: 98.2 us -> 26.4 us  [partner(): return lax.ppermute(values, axis, [(i, i ^ flip) for i in range(size)])]
    ppermute x65 -> x37, waiting for transfers between devices: 141 us -> 76.6 us  [partner(): return lax.ppermute(values, axis, [(i, i ^ flip) for i in range(size)])]
    convert_element_type x24 -> x0, other arithmetic: 40.8 us -> none  [the longest x22 34.4 us: add(): return total.astype(bf16)]
    ppermute x0 -> x22, starting transfers between devices: none -> 30.4 us  [along(): return lax.ppermute(values, ('rep', 'grp'), pairs)]
    pallas_call x4 -> x2, Pallas kernels: 32.1 us -> 23.3 us  [attend_back(): pl.pallas_call(functools.partial(attend_back_kernel, first, heads, final,...]
    unnamed x95 -> x98, local copies, waits for them, and re-layouts: 8.61 us -> 15.9 us
  transfers between devices with their start and end apart: 68 -> 59, of which waited for: 20 -> 28; matrix products, arithmetic and copies ran while one was open for 10% -> 4% of each run, Pallas kernels for 26% -> 36%
where the time goes in v3:
time: 435 us; the launch traced here: 429 us
  Pallas kernels  184 us (42%)
  waiting for transfers between devices  155 us (36%)
  starting transfers between devices  56.7 us (13%)
  local copies, waits for them, and re-layouts  27.7 us (6%)
    ppermute x22, waiting for transfers between devices, along(): return lax.ppermute(values, ('rep', 'grp'), pairs)  78.3 us
    ppermute x37, waiting for transfers between devices, partner(): return lax.ppermute(values, axis, [(i, i ^ flip) for i in range(size)])  76.6 us
    ppermute x22, starting transfers between devices, along(): return lax.ppermute(values, ('rep', 'grp'), pairs)  30.4 us
    ppermute x37, starting transfers between devices, partner(): return lax.ppermute(values, axis, [(i, i ^ flip) for i in range(size)])  26.4 us
    pallas_call x10, Pallas kernels, batch(): pl.pallas_call(functools.partial(batch_kernel, [task[:2] for task in task...  25.1 us
    pallas_call x2, Pallas kernels, attend_back(): pl.pallas_call(functools.partial(attend_back_kernel, first, heads, final,...  23.3 us
    pallas_call x4, Pallas kernels, halve(): pl.pallas_call(halve_kernel, grid_spec=pltpu.PrefetchScalarGridSpec(num_s...  17.9 us
    pallas_call x3, Pallas kernels, add_pairs(): pl.pallas_call(add_pairs_kernel, grid=(steps,), out_shape=[like(rows, wid...  16.3 us
  transfers between devices with their start and end apart: 59, of which 28 were waited for; matrix products, arithmetic and copies ran while one was open for 4% of the time, Pallas kernels for 36%

profile of v3, /device:TPU:0, one launch (start us, length us, event | category | flops | bytes accessed | tf_op | source)
XLA Modules:
  0.0 428.9 jit_solution(17004150834626293617)
XLA Ops:
  14.2 6.2 %collective-permute-done.refs_2_ = bf16[256,896]{1,0:T(8,128)(2,1)} collective-permute-done((bf16[256,896]{1,0:T(8,128)(2,1)S(1)}, bf16[256,896]{1,0:T(8,128)(2,1)}, u32[]{:S(2)}, u32[]{:S(2)}) %collective-permute-start) | collective-permute-done | bytes 458784 | tf_op jit(solution)/shard_map/ppermute | solution.py:724
  25.9 4.7 %front.1 = (bf16[480,384]{1,0:T(8,128)(2,1)}, bf16[320,384]{1,0:T(8,128)(2,1)}, bf16[1024,384]{1,0:T(8,128)(2,1)}, f32[8,1024]{1,0:T(8,128)}) custom-call(s32[8]{0:T(128)} %stack.111.offs, bf16[384,1024]{1,0:T(8,128)(2,1)} %bitcast.43, f32[32,384]{1,0:T(8,128)} %get-tuple-element.320.cos_ref, f32[32,384]{1,0:T(8,128)} %get-tuple-element.319.sin_ref, ...), custom_call_target="tpu_custom_call" | custom-call | flops 6291 | bytes 48 | tf_op jit(solution)/shard_map/front/pallas_call | solution.py:93
  31.0 14.8 %collective-permute-done.7.refs_2_ = bf16[320,384]{1,0:T(8,128)(2,1)S(1)} collective-permute-done((bf16[320,384]{1,0:T(8,128)(2,1)}, bf16[320,384]{1,0:T(8,128)(2,1)S(1)}, u32[]{:S(2)}, u32[]{:S(2)}) %collective-permute-start.7) | collective-permute-done | bytes 245792 | tf_op jit(solution)/shard_map/ppermute | solution.py:724
  52.1 7.5 %attend.2 = (bf16[512,384]{1,0:T(8,128)(2,1)}, f32[8,384]{1,0:T(8,128)}) custom-call(s32[3]{0:T(128)} %pad_add_fusion.info_ref.who, bf16[480,384]{1,0:T(8,128)(2,1)} %get-tuple-element.168.fac_ref, bf16[320,384]{1,0:T(8,128)(2,1)} %get-tuple-element.156.refs_0_, bf16[320,384]{1,0:T(8,128)(2,1)} %copy-done.10, bf16[320,384]{1,0:T(8,128)(2,1)} %copy-done.9, ...), custom_call_target="tpu_custom_call" | custom-call | flops 289910 | bytes 19 | tf_op jit(solution)/shard_map/attend/pallas_call | solution.py:209
  59.6 12.4 %collective-permute-done.11.refs_4_.refs_2_ = bf16[128,1024]{1,0:T(8,128)(2,1)} collective-permute-done((bf16[128,1024]{1,0:T(8,128)(2,1)}, bf16[128,1024]{1,0:T(8,128)(2,1)}, u32[]{:S(2)}, u32[]{:S(2)}) %collective-permute-start.11) | collective-permute-done | bytes 262176 | tf_op jit(solution)/shard_map/ppermute | solution.py:724
  77.0 7.6 %attend.3 = (bf16[512,384]{1,0:T(8,128)(2,1)}, f32[8,384]{1,0:T(8,128)}) custom-call(s32[3]{0:T(128)} %pad_add_fusion.info_ref.who, bf16[480,384]{1,0:T(8,128)(2,1)} %get-tuple-element.168.fac_ref, bf16[320,384]{1,0:T(8,128)(2,1)} %get-tuple-element.156.refs_0_, bf16[320,384]{1,0:T(8,128)(2,1)} %copy-done.10, bf16[320,384]{1,0:T(8,128)(2,1)} %copy-done.9, ...), custom_call_target="tpu_custom_call" | custom-call | flops 289910 | bytes 19 | tf_op jit(solution)/shard_map/attend/pallas_call | solution.py:209
  84.7 6.3 %collective-permute-done.15.refs_17_.refs_15_ = bf16[128,2816]{1,0:T(8,128)(2,1)S(1)} collective-permute-done((bf16[128,2816]{1,0:T(8,128)(2,1)}, bf16[128,2816]{1,0:T(8,128)(2,1)S(1)}, u32[]{:S(2)}, u32[]{:S(2)}) %collective-permute-start.15) | collective-permute-done | bytes 720928 | tf_op jit(solution)/shard_map/ppermute | solution.py:724
  100.3 15.5 %feed.1 = (f32[384,1024]{1,0:T(8,128)}, bf16[1024,384]{1,0:T(8,128)(2,1)}, bf16[384,2816]{1,0:T(8,128)(2,1)}, bf16[384,2816]{1,0:T(8,128)(2,1)}, bf16[384,2816]{1,0:T(8,128)(2,1)}, /*index=5*/bf16[2816,384]{1,0:T(8,128)(2,1)}) custom-call(s32[24]{0:T(128)} %concatenate.6.offs, bf16[384,1024]{1,0:T(8,128)(2,1)} %bitcast.44, ...), custom_call_target="tpu_custom_call" | custom-call | flops 74490 | bytes 237 | tf_op jit(solution)/shard_map/feed/pallas_call | solution.py:447
  116.0 6.2 %products.2 = (bf16[2,704,1024]{2,1,0:T(8,128)(2,1)}, bf16[2,704,1024]{2,1,0:T(8,128)(2,1)}) custom-call(s32[3]{0:T(128)} %pad_add_fusion.info_ref.who, bf16[2816,384]{1,0:T(8,128)(2,1)} %get-tuple-element.179.left, bf16[384,1024]{1,0:T(8,128)(2,1)} %bitcast.46), custom_call_target="tpu_custom_call" | custom-call | flops 22145 | bytes 65 | tf_op jit(solution)/shard_map/products/pallas_call | solution.py:524
  124.1 9.9 %slopes.1 = (bf16[384,2816]{1,0:T(8,128)(2,1)}, bf16[384,2816]{1,0:T(8,128)(2,1)}) custom-call(s32[12]{0:T(128)} %stack.94.offs, bf16[384,2816]{1,0:T(8,128)(2,1)} %get-tuple-element.184.slope_ref, bf16[384,2816]{1,0:T(8,128)(2,1)} %get-tuple-element.185.lin_ref, bf16[384,1024]{1,0:T(8,128)(2,1)} %bitcast.47, bf16[704,1024]{1,0:T(8,128)(2,1)} %refs_0_.5, ...), custom_call_target="tpu_custom_call" | custom-call | flops 22145 | bytes 144 | tf_op jit(solution)/shard_map/slopes/pallas_call | solution.py:498
  134.1 6.6 %products.3 = (bf16[2,256,2816]{2,1,0:T(8,128)(2,1)}, bf16[2,256,2816]{2,1,0:T(8,128)(2,1)}) custom-call(s32[3]{0:T(128)} %pad_add_fusion.info_ref.who, bf16[1024,384]{1,0:T(8,128)(2,1)} %get-tuple-element.192.left.hid_ref, bf16[384,2816]{1,0:T(8,128)(2,1)} %get-tuple-element.187.right.refs_21_), custom_call_target="tpu_custom_call" | custom-call | flops 22145 | bytes 79 | tf_op jit(solution)/shard_map/products/pallas_call | solution.py:524
  142.2 4.7 %add_pairs.3 = (bf16[704,1024]{1,0:T(8,128)(2,1)}, bf16[704,1024]{1,0:T(8,128)(2,1)}) custom-call(bf16[2,704,1024]{2,1,0:T(8,128)(2,1)} %get-tuple-element.195.refs_0_, bf16[2,704,1024]{2,1,0:T(8,128)(2,1)} %copy-done.15), custom_call_target="tpu_custom_call" | custom-call | tf_op jit(solution)/shard_map/add_pairs/pallas_call | solution.py:765
  148.5 13.5 %middle_grads.1 = (f32[384,1024]{1,0:T(8,128)}, f32[8,1024]{1,0:T(8,128)}, bf16[1024,384]{1,0:T(8,128)(2,1)}, bf16[2,256,1024]{2,1,0:T(8,128)(2,1)}, bf16[2,256,1024]{2,1,0:T(8,128)(2,1)}) custom-call(s32[24]{0:T(128)} %concatenate.6.offs, s32[3]{0:T(128)} %pad_add_fusion.info_ref.who, bf16[384,1024]{1,0:T(8,128)(2,1)} %bitcast.48, ...), custom_call_target="tpu_custom_call" | custom-call | flops 52344 | bytes 158 | tf_op jit(solution)/shard_map/middle_grads/pallas_call | solution.py:584
  162.1 11.2 %settle.1 = (bf16[384,1024]{1,0:T(8,128)(2,1)}, bf16[2,256,2816]{2,1,0:T(8,128)(2,1)}, bf16[2,256,2816]{2,1,0:T(8,128)(2,1)}) custom-call(s32[12]{0:T(128)} %stack.94.offs, s32[3]{0:T(128)} %pad_add_fusion.info_ref.who, bf16[1024,384]{1,0:T(8,128)(2,1)} %get-tuple-element.192.left.hid_ref, bf16[384,2816]{1,0:T(8,128)(2,1)} %get-tuple-element.190.refs_20_.dg_ref, ...), custom_call_target="tpu_custom_call" | custom-call | flops 52344 | bytes 194 | tf_op jit(solution)/shard_map/settle/pallas_call | solution.py:640
  173.3 7.4 %collective-permute-done.27 = bf16[704,1024]{1,0:T(8,128)(2,1)S(1)} collective-permute-done((bf16[704,1024]{1,0:T(8,128)(2,1)}, bf16[704,1024]{1,0:T(8,128)(2,1)S(1)}, u32[]{:S(2)}, u32[]{:S(2)}) %collective-permute-start.27) | collective-permute-done | bytes 1441824 | tf_op jit(solution)/shard_map/ppermute | solution.py:724
  180.7 6.1 %add_pairs.4 = (bf16[256,3840]{1,0:T(8,128)(2,1)}, bf16[256,3840]{1,0:T(8,128)(2,1)}) custom-call(bf16[2,256,2816]{2,1,0:T(8,128)(2,1)} %get-tuple-element.201.refs_0_, bf16[2,256,2816]{2,1,0:T(8,128)(2,1)} %collective-permute-done.28.refs_1_, bf16[2,256,1024]{2,1,0:T(8,128)(2,1)} %get-tuple-element.202.refs_2_, bf16[2,256,1024]{2,1,0:T(8,128)(2,1)} %copy-done.22), custom_call_target="tpu_custom_call" | custom-call | tf_op jit(solution)/shard_map/add_pairs/pallas_call | solution.py:765
  189.0 4.6 %halve.4 = (bf16[4,88,1024]{2,1,0:T(8,128)(2,1)}, bf16[4,88,1024]{2,1,0:T(8,128)(2,1)}) custom-call(s32[4]{0:T(128)} %pad_add_fusion.1.place, bf16[8,88,1024]{2,1,0:T(8,128)(2,1)} %bitcast.49, bf16[8,88,1024]{2,1,0:T(8,128)(2,1)} %bitcast.51, bf16[8,88,1024]{2,1,0:T(8,128)(2,1)} %bitcast.50, bf16[8,88,1024]{2,1,0:T(8,128)(2,1)} %bitcast.52), custom_call_target="tpu_custom_call" | custom-call | tf_op jit(solution)/shard_map/halve/pallas_call | solution.py:794
  194.6 15.2 %attend_back.2 = (f32[480,384]{1,0:T(8,128)}, f32[4,320,384]{2,1,0:T(8,128)}) custom-call(s32[3]{0:T(128)} %pad_add_fusion.info_ref.who, bf16[480,384]{1,0:T(8,128)(2,1)} %get-tuple-element.168.fac_ref, bf16[1024,384]{1,0:T(8,128)(2,1)} %get-tuple-element.213.grad_ref, bf16[320,384]{1,0:T(8,128)(2,1)} %get-tuple-element.156.refs_0_, ...), custom_call_target="tpu_custom_call" | custom-call | flops 17 | bytes 39 | tf_op jit(solution)/shard_map/attend_back/pallas_call | solution.py:310
  209.7 22.5 %collective-permute-done.30 = bf16[256,3840]{1,0:T(8,128)(2,1)S(1)} collective-permute-done((bf16[256,3840]{1,0:T(8,128)(2,1)}, bf16[256,3840]{1,0:T(8,128)(2,1)S(1)}, u32[]{:S(2)}, u32[]{:S(2)}) %collective-permute-start.30) | collective-permute-done | bytes 1966112 | tf_op jit(solution)/shard_map/ppermute | solution.py:724
  232.2 5.5 %add_pairs.5 = (bf16[256,2816]{1,0:T(8,128)(2,1)}, bf16[256,2816]{1,0:T(8,128)(2,1)}) custom-call(bf16[2,256,2816]{2,1,0:T(8,128)(2,1)} %get-tuple-element.220.refs_0_, bf16[2,256,2816]{2,1,0:T(8,128)(2,1)} %collective-permute-done.32.refs_1_), custom_call_target="tpu_custom_call" | custom-call | tf_op jit(solution)/shard_map/add_pairs/pallas_call | solution.py:765
  237.7 4.9 %halve.5 = (bf16[4,32,3840]{2,1,0:T(8,128)(2,1)}, bf16[4,32,3840]{2,1,0:T(8,128)(2,1)}) custom-call(s32[4]{0:T(128)} %pad_add_fusion.1.place, bf16[8,32,3840]{2,1,0:T(8,128)(2,1)} %bitcast.39, bf16[8,32,3840]{2,1,0:T(8,128)(2,1)} %bitcast.41, bf16[8,32,3840]{2,1,0:T(8,128)(2,1)} %bitcast.40, bf16[8,32,3840]{2,1,0:T(8,128)(2,1)} %bitcast.42), custom_call_target="tpu_custom_call" | custom-call | tf_op jit(solution)/shard_map/halve/pallas_call | solution.py:794
  247.8 8.1 %attend_back.3 = (f32[480,384]{1,0:T(8,128)}, bf16[2,320,384]{2,1,0:T(8,128)(2,1)}, bf16[2,320,384]{2,1,0:T(8,128)(2,1)}) custom-call(s32[3]{0:T(128)} %pad_add_fusion.info_ref.who, bf16[480,384]{1,0:T(8,128)(2,1)} %get-tuple-element.168.fac_ref, bf16[1024,384]{1,0:T(8,128)(2,1)} %get-tuple-element.213.grad_ref, ...), custom_call_target="tpu_custom_call" | custom-call | flops 5 | bytes 39 | tf_op jit(solution)/shard_map/attend_back/pallas_call | solution.py:310
  267.6 7.9 %collective-permute-done.37.refs_5_ = bf16[1,88,1024]{2,1,0:T(8,128)(2,1)S(1)} collective-permute-done((bf16[1,88,1024]{2,1,0:T(8,128)(2,1)}, bf16[1,88,1024]{2,1,0:T(8,128)(2,1)S(1)}, u32[]{:S(2)}, u32[]{:S(2)}) %collective-permute-start.37) | collective-permute-done | bytes 180256 | tf_op jit(solution)/shard_map/ppermute | solution.py:946
  277.5 4.6 %halve.6 = (bf16[4,32,2816]{2,1,0:T(8,128)(2,1)}, bf16[4,32,2816]{2,1,0:T(8,128)(2,1)}) custom-call(s32[4]{0:T(128)} %pad_add_fusion.1.place, bf16[8,32,2816]{2,1,0:T(8,128)(2,1)} %bitcast.53, bf16[8,32,2816]{2,1,0:T(8,128)(2,1)} %bitcast.55, bf16[8,32,2816]{2,1,0:T(8,128)(2,1)} %bitcast.54, bf16[8,32,2816]{2,1,0:T(8,128)(2,1)} %bitcast.56), custom_call_target="tpu_custom_call" | custom-call | tf_op jit(solution)/shard_map/halve/pallas_call | solution.py:794
  293.0 7.8 %collective-permute-done.40.refs_3_ = bf16[1,32,3840]{2,1,0:T(8,128)(2,1)S(1)} collective-permute-done((bf16[1,32,3840]{2,1,0:T(8,128)(2,1)}, bf16[1,32,3840]{2,1,0:T(8,128)(2,1)S(1)}, u32[]{:S(2)}, u32[]{:S(2)}) %collective-permute-start.40) | collective-permute-done | bytes 245792 | tf_op jit(solution)/shard_map/ppermute | solution.py:946
  307.3 7.1 %tail.1 = (f32[384,1024]{1,0:T(8,128)}, bf16[2,256,896]{2,1,0:T(8,128)(2,1)}, bf16[2,256,896]{2,1,0:T(8,128)(2,1)}) custom-call(s32[8]{0:T(128)} %stack.111.offs, s32[3]{0:T(128)} %pad_add_fusion.info_ref.who, f32[480,384]{1,0:T(8,128)} %get-tuple-element.215.dq_ref, bf16[320,384]{1,0:T(8,128)(2,1)} %get-tuple-element.248.own_ref, ...), custom_call_target="tpu_custom_call" | custom-call | flops 12582 | bytes 79 | tf_op jit(solution)/shard_map/tail/pallas_call | solution.py:706
  322.3 9.6 %collective-permute-done.46.refs_5_ = bf16[1,32,2816]{2,1,0:T(8,128)(2,1)S(1)} collective-permute-done((bf16[1,32,2816]{2,1,0:T(8,128)(2,1)}, bf16[1,32,2816]{2,1,0:T(8,128)(2,1)S(1)}, u32[]{:S(2)}, u32[]{:S(2)}) %collective-permute-start.46) | collective-permute-done | bytes 180256 | tf_op jit(solution)/shard_map/ppermute | solution.py:946
  331.9 5.8 %collective-permute-done.47.refs_7_ = bf16[1,88,1024]{2,1,0:T(8,128)(2,1)S(1)} collective-permute-done((bf16[1,88,1024]{2,1,0:T(8,128)(2,1)}, bf16[1,88,1024]{2,1,0:T(8,128)(2,1)S(1)}, u32[]{:S(2)}, u32[]{:S(2)}) %collective-permute-start.47) | collective-permute-done | bytes 180256 | tf_op jit(solution)/shard_map/ppermute | solution.py:946
  348.2 9.8 %collective-permute-done.50.refs_1_ = bf16[1,32,2816]{2,1,0:T(8,128)(2,1)S(1)} collective-permute-done((bf16[1,32,2816]{2,1,0:T(8,128)(2,1)}, bf16[1,32,2816]{2,1,0:T(8,128)(2,1)S(1)}, u32[]{:S(2)}, u32[]{:S(2)}) %collective-permute-start.50) | collective-permute-done | bytes 180256 | tf_op jit(solution)/shard_map/ppermute | solution.py:946
  374.6 6.4 %collective-permute-done.52.refs_1_ = bf16[4,32,896]{2,1,0:T(8,128)(2,1)S(1)} collective-permute-done((bf16[4,32,896]{2,1,0:T(8,128)(2,1)}, bf16[4,32,896]{2,1,0:T(8,128)(2,1)S(1)}, u32[]{:S(2)}, u32[]{:S(2)}) %collective-permute-start.52) | collective-permute-done | bytes 229408 | tf_op jit(solution)/shard_map/ppermute | solution.py:946
  404.8 8.8 %collective-permute-done.57.refs_1_ = bf16[4,32,896]{2,1,0:T(8,128)(2,1)S(1)} collective-permute-done((bf16[4,32,896]{2,1,0:T(8,128)(2,1)}, bf16[4,32,896]{2,1,0:T(8,128)(2,1)S(1)}, u32[]{:S(2)}, u32[]{:S(2)}) %collective-permute-start.57) | collective-permute-done | bytes 229408 | tf_op jit(solution)/shard_map/ppermute | solution.py:946
  417.2 5.1 %collective-permute-done.58.far = bf16[4,32,896]{2,1,0:T(8,128)(2,1)S(1)} collective-permute-done((bf16[4,32,896]{2,1,0:T(8,128)(2,1)}, bf16[4,32,896]{2,1,0:T(8,128)(2,1)S(1)}, u32[]{:S(2)}, u32[]{:S(2)}) %collective-permute-start.58) | collective-permute-done | bytes 229408 | tf_op jit(solution)/shard_map/ppermute | solution.py:946
  (236 shorter events, 152.9 us)
Async XLA Ops:
  0.7 19.7 %collective-permute-start.2 = (bf16[256,2816]{1,0:T(8,128)(2,1)}, bf16[256,2816]{1,0:T(8,128)(2,1)}, u32[]{:S(2)}, u32[]{:S(2)}) collective-permute-start(bf16[256,2816]{1,0:T(8,128)(2,1)} %refs_6_.1), channel_id=1, source_target_pairs={{0,1},{1,0},{2,3},{3,2},{4,5},{5,4},{6,7},{7,6},{8,9},{9,8},{10,11... | collective-permute-start | bytes 4325384 | tf_op jit(solution)/shard_map/ppermute | solution.py:724
  1.2 19.2 %collective-permute-start.3 = (bf16[256,2816]{1,0:T(8,128)(2,1)}, bf16[256,2816]{1,0:T(8,128)(2,1)}, u32[]{:S(2)}, u32[]{:S(2)}) collective-permute-start(bf16[256,2816]{1,0:T(8,128)(2,1)} %refs_12_.1), channel_id=1, source_target_pairs={{0,1},{1,0},{2,3},{3,2},{4,5},{5,4},{6,7},{7,6},{8,9},{9,8},{10,11... | collective-permute-start | bytes 4325384 | tf_op jit(solution)/shard_map/ppermute | solution.py:724
  21.8 24.1 %collective-permute-start.5 = (bf16[128,2816]{1,0:T(8,128)(2,1)}, bf16[128,2816]{1,0:T(8,128)(2,1)S(1)}, u32[]{:S(2)}, u32[]{:S(2)}) collective-permute-start(bf16[128,2816]{1,0:T(8,128)(2,1)} %get-tuple-element.153), channel_id=1, source_target_pairs={{0,2},{1,3},{2,0},{3,1},{4,6},{5,7},{6,4},{7,5},{8,10},{9,11},{10,... | collective-permute-start | bytes 2162696 | tf_op jit(solution)/shard_map/ppermute | solution.py:724
  30.7 15.2 %collective-permute-start.7 = (bf16[320,384]{1,0:T(8,128)(2,1)}, bf16[320,384]{1,0:T(8,128)(2,1)S(1)}, u32[]{:S(2)}, u32[]{:S(2)}) collective-permute-start(bf16[320,384]{1,0:T(8,128)(2,1)} %get-tuple-element.156.refs_0_), channel_id=1, source_target_pairs={{0,2},{1,3},{2,0},{3,1},{4,6},{5,7},{6,4},{7,5},{8,10},{9,11},{10,... | collective-permute-start | bytes 737288 | tf_op jit(solution)/shard_map/ppermute | solution.py:724
  47.5 24.5 %collective-permute-start.14 = (bf16[704,1024]{1,0:T(8,128)(2,1)S(1)}, bf16[704,1024]{1,0:T(8,128)(2,1)S(1)}, u32[]{:S(2)}, u32[]{:S(2)}) collective-permute-start(bf16[704,1024]{1,0:T(8,128)(2,1)S(1)} %copy-done.2), channel_id=1, source_target_pairs={{0,1},{1,0},{2,3},{3,2},{4,5},{5,4},{6,7},{7,6},{8,9},{9,8},{10,11... | collective-permute-start | bytes 4325384 | tf_op jit(solution)/shard_map/ppermute | solution.py:724
  47.6 24.4 %collective-permute-start.10 = (bf16[128,2816]{1,0:T(8,128)(2,1)}, bf16[128,2816]{1,0:T(8,128)(2,1)}, u32[]{:S(2)}, u32[]{:S(2)}) collective-permute-start(bf16[128,2816]{1,0:T(8,128)(2,1)} %get-tuple-element.157), channel_id=1, source_target_pairs={{0,2},{1,3},{2,0},{3,1},{4,6},{5,7},{6,4},{7,5},{8,10},{9,11},{10,... | collective-permute-start | bytes 2162696 | tf_op jit(solution)/shard_map/ppermute | solution.py:724
  49.4 22.6 %collective-permute-start.13 = (bf16[128,2816]{1,0:T(8,128)(2,1)}, bf16[128,2816]{1,0:T(8,128)(2,1)}, u32[]{:S(2)}, u32[]{:S(2)}) collective-permute-start(bf16[128,2816]{1,0:T(8,128)(2,1)} %copy-done.11), channel_id=1, source_target_pairs={{0,1},{1,0},{2,3},{3,2},{4,5},{5,4},{6,7},{7,6},{8,9},{9,8},{10,11... | collective-permute-start | bytes 2162696 | tf_op jit(solution)/shard_map/ppermute | solution.py:724
  49.5 22.5 %collective-permute-start.12 = (bf16[128,2816]{1,0:T(8,128)(2,1)}, bf16[128,2816]{1,0:T(8,128)(2,1)}, u32[]{:S(2)}, u32[]{:S(2)}) collective-permute-start(bf16[128,2816]{1,0:T(8,128)(2,1)} %copy-done.11), channel_id=1, source_target_pairs={{0,4},{4,0},{8,12},{12,8},{16,20},{20,16},{24,28},{28,24},{1,5},{5... | collective-permute-start | bytes 2162696 | tf_op jit(solution)/shard_map/ppermute | solution.py:724
  51.0 21.0 %collective-permute-start.11 = (bf16[128,1024]{1,0:T(8,128)(2,1)}, bf16[128,1024]{1,0:T(8,128)(2,1)}, u32[]{:S(2)}, u32[]{:S(2)}) collective-permute-start(bf16[128,1024]{1,0:T(8,128)(2,1)} %constant_dynamic-slice_fusion.1), channel_id=1, source_target_pairs={{0,2},{1,3},{2,0},{3,1},{4,6},{5,7},{6,4},{7,5},{8,10},{9,11},{10,... | collective-permute-start | bytes 786440 | tf_op jit(solution)/shard_map/ppermute | solution.py:724
  72.1 18.8 %collective-permute-start.15 = (bf16[128,2816]{1,0:T(8,128)(2,1)}, bf16[128,2816]{1,0:T(8,128)(2,1)S(1)}, u32[]{:S(2)}, u32[]{:S(2)}) collective-permute-start(bf16[128,2816]{1,0:T(8,128)(2,1)} %collective-permute-done.10.refs_16_.refs_14_), channel_id=1, source_target_pairs={{0,8},{4,12},{8,0},{12,4},{16,24},{20,28},{24,16},{28,20},{1,9},{5... | collective-permute-start | bytes 2162696 | tf_op jit(solution)/shard_map/ppermute | solution.py:724
  74.0 18.5 %collective-permute-start.16 = (bf16[352,1024]{1,0:T(8,128)(2,1)}, bf16[352,1024]{1,0:T(8,128)(2,1)}, u32[]{:S(2)}, u32[]{:S(2)}) collective-permute-start(bf16[352,1024]{1,0:T(8,128)(2,1)} %constant_dynamic-slice_fusion), channel_id=1, source_target_pairs={{0,2},{1,3},{2,0},{3,1},{4,6},{5,7},{6,4},{7,5},{8,10},{9,11},{10,... | collective-permute-start | bytes 2162696 | tf_op jit(solution)/shard_map/ppermute | solution.py:724
  75.5 17.0 %collective-permute-start.19 = (bf16[128,2816]{1,0:T(8,128)(2,1)}, bf16[128,2816]{1,0:T(8,128)(2,1)}, u32[]{:S(2)}, u32[]{:S(2)}) collective-permute-start(bf16[128,2816]{1,0:T(8,128)(2,1)} %collective-permute-done.12.refs_11_.refs_9_), channel_id=1, source_target_pairs={{0,1},{1,0},{2,3},{3,2},{4,5},{5,4},{6,7},{7,6},{8,9},{9,8},{10,11... | collective-permute-start | bytes 2162696 | tf_op jit(solution)/shard_map/ppermute | solution.py:724
  96.4 19.5 %collective-permute-start.24 = (bf16[352,1024]{1,0:T(8,128)(2,1)}, bf16[352,1024]{1,0:T(8,128)(2,1)}, u32[]{:S(2)}, u32[]{:S(2)}) collective-permute-start(bf16[352,1024]{1,0:T(8,128)(2,1)} %collective-permute-done.16.refs_2_), channel_id=1, source_target_pairs={{0,1},{1,0},{2,3},{3,2},{4,5},{5,4},{6,7},{7,6},{8,9},{9,8},{10,11... | collective-permute-start | bytes 2162696 | tf_op jit(solution)/shard_map/ppermute | solution.py:724
  96.7 19.2 %collective-permute-start.23 = (bf16[352,1024]{1,0:T(8,128)(2,1)}, bf16[352,1024]{1,0:T(8,128)(2,1)}, u32[]{:S(2)}, u32[]{:S(2)}) collective-permute-start(bf16[352,1024]{1,0:T(8,128)(2,1)} %collective-permute-done.16.refs_2_), channel_id=1, source_target_pairs={{0,4},{4,0},{8,12},{12,8},{16,20},{20,16},{24,28},{28,24},{1,5},{5... | collective-permute-start | bytes 2162696 | tf_op jit(solution)/shard_map/ppermute | solution.py:724
  123.1 17.6 %collective-permute-start.26 = (bf16[2,704,1024]{2,1,0:T(8,128)(2,1)}, bf16[2,704,1024]{2,1,0:T(8,128)(2,1)S(1)}, u32[]{:S(2)}, u32[]{:S(2)}) collective-permute-start(bf16[2,704,1024]{2,1,0:T(8,128)(2,1)} %get-tuple-element.183), channel_id=1, source_target_pairs={{0,1},{1,0},{2,3},{3,2},{4,5},{5,4},{6,7},{7,6},{8,9},{9,8},{10,11... | collective-permute-start | bytes 8650760 | tf_op jit(solution)/shard_map/ppermute | solution.py:724
  140.7 40.0 %collective-permute-start.28 = (bf16[2,256,2816]{2,1,0:T(8,128)(2,1)}, bf16[2,256,2816]{2,1,0:T(8,128)(2,1)}, u32[]{:S(2)}, u32[]{:S(2)}) collective-permute-start(bf16[2,256,2816]{2,1,0:T(8,128)(2,1)} %get-tuple-element.198), channel_id=1, source_target_pairs={{0,1},{1,0},{2,3},{3,2},{4,5},{5,4},{6,7},{7,6},{8,9},{9,8},{10,11... | collective-permute-start | bytes 8650760 | tf_op jit(solution)/shard_map/ppermute | solution.py:724
  147.0 33.7 %collective-permute-start.27 = (bf16[704,1024]{1,0:T(8,128)(2,1)}, bf16[704,1024]{1,0:T(8,128)(2,1)S(1)}, u32[]{:S(2)}, u32[]{:S(2)}) collective-permute-start(bf16[704,1024]{1,0:T(8,128)(2,1)} %get-tuple-element.196), channel_id=1, source_target_pairs={{0,2},{1,3},{2,0},{3,1},{4,6},{5,7},{6,4},{7,5},{8,10},{9,11},{10,... | collective-permute-start | bytes 4325384 | tf_op jit(solution)/shard_map/ppermute | solution.py:724
  180.7 51.5 %collective-permute-start.32 = (bf16[2,256,2816]{2,1,0:T(8,128)(2,1)}, bf16[2,256,2816]{2,1,0:T(8,128)(2,1)}, u32[]{:S(2)}, u32[]{:S(2)}) collective-permute-start(bf16[2,256,2816]{2,1,0:T(8,128)(2,1)} %get-tuple-element.208), channel_id=1, source_target_pairs={{0,1},{1,0},{2,3},{3,2},{4,5},{5,4},{6,7},{7,6},{8,9},{9,8},{10,11... | collective-permute-start | bytes 8650760 | tf_op jit(solution)/shard_map/ppermute | solution.py:724
  186.8 45.4 %collective-permute-start.30 = (bf16[256,3840]{1,0:T(8,128)(2,1)}, bf16[256,3840]{1,0:T(8,128)(2,1)S(1)}, u32[]{:S(2)}, u32[]{:S(2)}) collective-permute-start(bf16[256,3840]{1,0:T(8,128)(2,1)} %get-tuple-element.203), channel_id=1, source_target_pairs={{0,2},{1,3},{2,0},{3,1},{4,6},{5,7},{6,4},{7,5},{8,10},{9,11},{10,... | collective-permute-start | bytes 5898248 | tf_op jit(solution)/shard_map/ppermute | solution.py:724
  193.5 16.2 %collective-permute-start.31 = (bf16[4,88,1024]{2,1,0:T(8,128)(2,1)}, bf16[4,88,1024]{2,1,0:T(8,128)(2,1)S(1)}, u32[]{:S(2)}, u32[]{:S(2)}) collective-permute-start(bf16[4,88,1024]{2,1,0:T(8,128)(2,1)} %get-tuple-element.206), channel_id=1, source_target_pairs={{0,4},{1,9},{2,6},{3,11},{4,0},{5,13},{6,2},{7,15},{8,12},{9,1},{1... | collective-permute-start | bytes 2162696 | tf_op jit(solution)/shard_map/ppermute | solution.py:946
  242.6 18.2 %collective-permute-start.33 = (bf16[4,32,3840]{2,1,0:T(8,128)(2,1)}, bf16[4,32,3840]{2,1,0:T(8,128)(2,1)S(1)}, u32[]{:S(2)}, u32[]{:S(2)}) collective-permute-start(bf16[4,32,3840]{2,1,0:T(8,128)(2,1)} %get-tuple-element.223), channel_id=1, source_target_pairs={{0,4},{1,9},{2,6},{3,11},{4,0},{5,13},{6,2},{7,15},{8,12},{9,1},{1... | collective-permute-start | bytes 2949128 | tf_op jit(solution)/shard_map/ppermute | solution.py:946
  243.4 32.7 %collective-permute-start.38 = (bf16[256,2816]{1,0:T(8,128)(2,1)}, bf16[256,2816]{1,0:T(8,128)(2,1)S(1)}, u32[]{:S(2)}, u32[]{:S(2)}) collective-permute-start(bf16[256,2816]{1,0:T(8,128)(2,1)} %get-tuple-element.221), channel_id=1, source_target_pairs={{0,2},{1,3},{2,0},{3,1},{4,6},{5,7},{6,4},{7,5},{8,10},{9,11},{10,... | collective-permute-start | bytes 4325384 | tf_op jit(solution)/shard_map/ppermute | solution.py:724
  260.8 15.3 %collective-permute-start.35 = (bf16[2,320,384]{2,1,0:T(8,128)(2,1)}, bf16[2,320,384]{2,1,0:T(8,128)(2,1)S(1)}, u32[]{:S(2)}, u32[]{:S(2)}) collective-permute-start(bf16[2,320,384]{2,1,0:T(8,128)(2,1)} %get-tuple-element.227), channel_id=1, source_target_pairs={{0,1},{1,0},{2,3},{3,2},{4,5},{5,4},{6,7},{7,6},{8,9},{9,8},{10,11... | collective-permute-start | bytes 1474568 | tf_op jit(solution)/shard_map/ppermute | solution.py:724
  282.1 18.8 %collective-permute-start.41 = (bf16[4,32,2816]{2,1,0:T(8,128)(2,1)}, bf16[4,32,2816]{2,1,0:T(8,128)(2,1)S(1)}, u32[]{:S(2)}, u32[]{:S(2)}) collective-permute-start(bf16[4,32,2816]{2,1,0:T(8,128)(2,1)} %get-tuple-element.242), channel_id=1, source_target_pairs={{0,4},{1,9},{2,6},{3,11},{4,0},{5,13},{6,2},{7,15},{8,12},{9,1},{1... | collective-permute-start | bytes 2162696 | tf_op jit(solution)/shard_map/ppermute | solution.py:946
  314.9 22.8 %collective-permute-start.44 = (bf16[2,256,896]{2,1,0:T(8,128)(2,1)}, bf16[2,256,896]{2,1,0:T(8,128)(2,1)S(1)}, u32[]{:S(2)}, u32[]{:S(2)}) collective-permute-start(bf16[2,256,896]{2,1,0:T(8,128)(2,1)} %get-tuple-element.257), channel_id=1, source_target_pairs={{0,1},{1,0},{2,3},{3,2},{4,5},{5,4},{6,7},{7,6},{8,9},{9,8},{10,11... | collective-permute-start | bytes 2752520 | tf_op jit(solution)/shard_map/ppermute | solution.py:724
  318.0 19.7 %collective-permute-start.45 = (bf16[2,32,3840]{2,1,0:T(8,128)(2,1)}, bf16[2,32,3840]{2,1,0:T(8,128)(2,1)S(1)}, u32[]{:S(2)}, u32[]{:S(2)}) collective-permute-start(bf16[2,32,3840]{2,1,0:T(8,128)(2,1)} %get-tuple-element.267.refs_2_), channel_id=1, source_target_pairs={{0,8},{1,5},{2,10},{3,7},{4,12},{5,1},{6,14},{7,3},{8,0},{9,13},{1... | collective-permute-start | bytes 1474568 | tf_op jit(solution)/shard_map/ppermute | solution.py:946
  322.0 15.7 %collective-permute-start.47 = (bf16[1,88,1024]{2,1,0:T(8,128)(2,1)}, bf16[1,88,1024]{2,1,0:T(8,128)(2,1)S(1)}, u32[]{:S(2)}, u32[]{:S(2)}) collective-permute-start(bf16[1,88,1024]{2,1,0:T(8,128)(2,1)} %get-tuple-element.270.refs_6_), channel_id=1, source_target_pairs={{0,16},{1,17},{2,18},{3,19},{4,20},{5,21},{6,22},{7,23},{8,24},{9,... | collective-permute-start | bytes 540680 | tf_op jit(solution)/shard_map/ppermute | solution.py:946
  342.3 17.8 %collective-permute-start.49 = (bf16[4,32,3840]{2,1,0:T(8,128)(2,1)}, bf16[4,32,3840]{2,1,0:T(8,128)(2,1)S(1)}, u32[]{:S(2)}, u32[]{:S(2)}) collective-permute-start(bf16[4,32,3840]{2,1,0:T(8,128)(2,1)} %get-tuple-element.283.near), channel_id=1, source_target_pairs={{0,4},{1,9},{2,6},{3,11},{4,0},{5,13},{6,2},{7,15},{8,12},{9,1},{1... | collective-permute-start | bytes 2949128 | tf_op jit(solution)/shard_map/ppermute | solution.py:946
  343.3 16.5 %collective-permute-start.48 = (bf16[256,896]{1,0:T(8,128)(2,1)}, bf16[256,896]{1,0:T(8,128)(2,1)S(1)}, u32[]{:S(2)}, u32[]{:S(2)}) collective-permute-start(bf16[256,896]{1,0:T(8,128)(2,1)} %get-tuple-element.272), channel_id=1, source_target_pairs={{0,2},{1,3},{2,0},{3,1},{4,6},{5,7},{6,4},{7,5},{8,10},{9,11},{10,... | collective-permute-start | bytes 1376264 | tf_op jit(solution)/shard_map/ppermute | solution.py:724
  344.4 15.4 %collective-permute-start.51 = (bf16[2,88,1024]{2,1,0:T(8,128)(2,1)}, bf16[2,88,1024]{2,1,0:T(8,128)(2,1)S(1)}, u32[]{:S(2)}, u32[]{:S(2)}) collective-permute-start(bf16[2,88,1024]{2,1,0:T(8,128)(2,1)} %get-tuple-element.280.refs_2_), channel_id=1, source_target_pairs={{0,8},{1,5},{2,10},{3,7},{4,12},{5,1},{6,14},{7,3},{8,0},{9,13},{1... | collective-permute-start | bytes 1081352 | tf_op jit(solution)/shard_map/ppermute | solution.py:946
  363.2 17.8 %collective-permute-start.54 = (bf16[4,88,1024]{2,1,0:T(8,128)(2,1)}, bf16[4,88,1024]{2,1,0:T(8,128)(2,1)S(1)}, u32[]{:S(2)}, u32[]{:S(2)}) collective-permute-start(bf16[4,88,1024]{2,1,0:T(8,128)(2,1)} %get-tuple-element.289.near), channel_id=1, source_target_pairs={{0,4},{1,9},{2,6},{3,11},{4,0},{5,13},{6,2},{7,15},{8,12},{9,1},{1... | collective-permute-start | bytes 2162696 | tf_op jit(solution)/shard_map/ppermute | solution.py:946
  364.1 16.9 %collective-permute-start.53 = (bf16[2,32,2816]{2,1,0:T(8,128)(2,1)}, bf16[2,32,2816]{2,1,0:T(8,128)(2,1)S(1)}, u32[]{:S(2)}, u32[]{:S(2)}) collective-permute-start(bf16[2,32,2816]{2,1,0:T(8,128)(2,1)} %get-tuple-element.286.refs_2_), channel_id=1, source_target_pairs={{0,8},{1,5},{2,10},{3,7},{4,12},{5,1},{6,14},{7,3},{8,0},{9,13},{1... | collective-permute-start | bytes 1081352 | tf_op jit(solution)/shard_map/ppermute | solution.py:946
  (75 other events, 593.3 us)

commit v4 on v3

--- a/solution.py
+++ b/solution.py
@@ -62,22 +62,24 @@
     return first * cosine - second * sine, second * cosine + first * sine
 
 
-def front_kernel(count, cols, offs, x_ref, cos_ref, sin_ref, *refs):
-    pieces = refs[:count]
-    fac_ref, kv_ref, hid_ref, gains_ref, w, sems = refs[count:]
-    w_in = Mover(sems).pieces(offs, pieces, w)
+def front_kernel(count, offs, x_ref, cos_ref, sin_ref, *refs):
+    pieces, gain_refs = refs[:count], refs[count : 2 * count]
+    fac_ref, kv_ref, hid_ref, gains_ref, w, sems = refs[2 * count :]
+    w_in = Mover(sems).columns(offs, pieces, w)
+    for i, ref in enumerate(gain_refs):
+        size = ref.shape[1]
+        at = offs[2 * i] if size % 128 == 0 else 0
+        gains_ref[0:2, pl.ds(pl.multiple_of(at, 128), size)] = ref[...].astype(f32)
     xf = x_ref[...].astype(f32)
     normed = xf * lax.rsqrt(jnp.mean(xf * xf, axis=-1, keepdims=True) + EPS)
+    hidden = (normed * gains_ref[0:1, :]).astype(bf16)
+    turned = jnp.transpose(hidden)
+    hid_ref[...] = turned
     wait(w_in)
-    last = w.shape[1] - 128
-    gains = jnp.transpose(w[:, last:])[cols - last : cols - last + 16].astype(f32)
-    gains_ref[...] = gains[0:8]
-    hidden = (normed * gains[0:1]).astype(bf16)
-    hid_ref[...] = jnp.transpose(hidden)
-    raw = jnp.transpose(mm(hidden, w[...]))
+    raw = mm(w[...], turned)
     cosine, sine = cos_ref[...], sin_ref[...]
     fac_ref[...] = raw[:QCOLS].astype(bf16)
-    kv_ref[...] = raw[QCOLS:cols].astype(bf16)
+    kv_ref[...] = raw[QCOLS:].astype(bf16)
     for ref, first, at in [(fac_ref, 0, BQ + r * HDIM) for r in range(QRANK)] + [
         (kv_ref, QCOLS, BK + r * HDIM) for r in range(KRANK)
     ]:
@@ -86,25 +88,25 @@
         ref[at + HALF : at + HDIM, :] = two.astype(bf16)
 
 
-def front(offs, x, cosine, sine, w_fac, cols):
+def front(offs, x, cosine, sine, w_fac, gains):
     rows, width = x.shape
-    wide = w_fac[0].shape[1]
+    cols = w_fac[0].shape[0]
     count = len(w_fac)
     return pl.pallas_call(
-        functools.partial(front_kernel, count, cols),
+        functools.partial(front_kernel, count),
         out_shape=[
             like(QCOLS, rows),
             like(cols - QCOLS, rows),
             like(width, rows),
             like(8, width, dtype=f32),
         ],
-        in_specs=[smem()] + [vmem()] * 3 + [anywhere()] * count,
+        in_specs=[smem()] + [vmem()] * 3 + [anywhere()] * count + [vmem()] * count,
         out_specs=[vmem()] * 4,
-        scratch_shapes=[scratch(width, wide), pltpu.SemaphoreType.DMA((count,))],
+        scratch_shapes=[scratch(cols, width), pltpu.SemaphoreType.DMA((count,))],
         compiler_params=params(),
         cost_estimate=cost(2 * rows * width * cols, 4 * width * (cols + rows)),
         name="front",
-    )(offs, x, cosine, sine, *w_fac)
+    )(offs, x, cosine, sine, *w_fac, *gains)
 
 
 def load_factors(fac_ref, kv_refs, facf, kvf, qT, me):
@@ -351,6 +353,18 @@
             else:
                 where = dst.at[at, pl.ds(pl.multiple_of(offsets[first + 2 * i + 1], 128), cols)]
             copies.append(self.start(piece, where))
+        return copies
+
+
+    def columns(self, offsets, refs, dst):
+        copies = []
+        for i, piece in enumerate(refs):
+            cols = piece.shape[1]
+            if cols == dst.shape[1]:
+                copies.append(self.start(piece, dst))
+            else:
+                at = pl.ds(pl.multiple_of(offsets[2 * i], 128), cols)
+                copies.append(self.start(piece, dst.at[:, at]))
         return copies
 
 
@@ -616,52 +630,40 @@
     )(offs, who, upstream, gain, *w_out, *w_gate, *w_up, *mix, dg, du, mid)
 
 
-def settle_kernel(count, offs, who, hid_ref, dg_ref, act_i, mid_i, *refs):
-    pieces, (res, *outs, wd, act, mid, keep, send, sems) = refs[:count], refs[count:]
-    mover = Mover(sems)
-    later = [mover.start(act_i, act), mover.start(mid_i, mid)] + mover.pieces(offs, pieces, wd)
-    done = shard_products(who[0], hid_ref, dg_ref, (keep, send), mover, outs)
-    wait(later)
+def output_kernel(count, offs, act_ref, mid_ref, *refs):
+    pieces, (res, wd, sems) = refs[:count], refs[count:]
+    wait(Mover(sems).pieces(offs, pieces, wd))
 
     def forth(j, _):
         at = pl.ds(pl.multiple_of(j * TILE, TILE), TILE)
-        res[:, at] = (mid[:, at] + mm(act[...], wd[:, at])).astype(bf16)
+        res[:, at] = (mid_ref[:, at] + mm(act_ref[...], wd[:, at])).astype(bf16)
         return 0
 
     lax.fori_loop(0, wd.shape[1] // TILE, forth, 0, unroll=True)
-    wait(done)
-
-
-def settle(offs, who, hidT, dg, act, mid, w_down, parts):
+
+
+def output(offs, act, mid, w_down):
     rows, width = mid.shape
     count = len(w_down)
     inner = act.shape[1]
-    pair = (parts // 2, width // parts, inner)
     return pl.pallas_call(
-        functools.partial(settle_kernel, count),
-        out_shape=[like(rows, width), like(*pair), like(*pair)],
-        in_specs=[smem()] * 2 + [vmem()] * 2 + [anywhere()] * (2 + count),
-        out_specs=[vmem()] + [anywhere()] * 2,
-        scratch_shapes=[
-            scratch(inner, width),
-            scratch(rows, inner),
-            scratch(rows, width, dtype=f32),
-            scratch(*pair),
-            scratch(*pair),
-            pltpu.SemaphoreType.DMA((2 + count + parts,)),
-        ],
+        functools.partial(output_kernel, count),
+        out_shape=like(rows, width),
+        in_specs=[smem()] + [vmem()] * 2 + [anywhere()] * count,
+        out_specs=vmem(),
+        scratch_shapes=[scratch(inner, width), pltpu.SemaphoreType.DMA((count,))],
         compiler_params=params(),
-        cost_estimate=cost(2 * rows * width * (2 * inner + width), 2 * inner * (3 * width + rows)),
-        name="settle",
-    )(offs, who, hidT, dg, act, mid, *w_down)
+        cost_estimate=cost(2 * rows * width * inner, 2 * inner * (width + rows)),
+        name="output",
+    )(offs, act, mid, *w_down)
 
 
 def tail_kernel(count, cols, offs, who, dq_ref, own_ref, cos_ref, sin_ref, hid_ref, x_ref, gain_ref, dmid_ref, fgain_ref, *refs):
     pieces = refs[:count]
     grad_ref, *outs = refs[count:]
-    *outs, w, raw, sems = outs
+    *outs, w, raw, gain_cols, sems = outs
     mover = Mover(sems)
-    w_in = mover.pieces(offs, pieces, w)
+    w_in = mover.columns(offs, pieces, w)
     cosine, sine = cos_ref[...], -sin_ref[...]
     raw[0:QCOLS, :] = dq_ref[...].astype(bf16)
     raw[QCOLS:cols, :] = own_ref[...]
@@ -680,37 +682,34 @@
     wait(w_in)
     xf = x_ref[...].astype(f32)
     scale = lax.rsqrt(jnp.mean(xf * xf, axis=-1, keepdims=True) + EPS)
-    dhid = mm(draw, w[...], NT)
+    dhid = mm(draw[:, 0:cols], w[...])
     gain_grad, part = norm_back(dhid, xf * scale, scale, gain_ref[...])
     grad_ref[...] = dmid_ref[...] + part
-    width = raw.shape[0]
-    line = lax.broadcasted_iota(jnp.int32, (128, gain_grad.shape[1]), 0) + (width - 128)
-    both = jnp.where(line == cols, gain_grad, jnp.where(line == cols + 1, fgain_ref[0:1, :], 0.0))
-    both = jnp.transpose(both)
-    raw_gain = both.astype(bf16)
-    w[:, 0:128] = raw_gain
-    count_out, rows, _ = outs[0].shape
+    line = lax.broadcasted_iota(jnp.int32, (128, gain_grad.shape[1]), 0)
+    both = jnp.where(line == 0, gain_grad, jnp.where(line == 1, fgain_ref[0:1, :], 0.0))
+    gain_cols[...] = jnp.transpose(both)
+    count_out, wide, rows = outs[0].shape
     for flip in range(2 * count_out):
         at = pl.ds(pl.multiple_of((who[0] ^ flip) * rows, 16), rows)
-        got = mm(hid_ref[at, :], draw)
         out = outs[flip % 2]
-        out[flip // 2, :, 0 : width - 128] = got[:, 0 : width - 128].astype(bf16)
-        out[flip // 2, :, width - 128 :] = (got[:, width - 128 :] + w[at, 0:128].astype(f32)).astype(bf16)
+        out[flip // 2, 0:cols, :] = mm(raw[0:cols, :], hid_ref[at, :], NT).astype(bf16)
+        out[flip // 2, cols:wide, :] = jnp.transpose(gain_cols[at, :])[0 : wide - cols].astype(bf16)
 
 
 def tail(offs, who, dq, own, cosine, sine, hidT, x, gain, dmid, fgain, w_fac, cols, parts):
     rows, width = x.shape
-    wide = w_fac[0].shape[1]
+    wide = (cols // 128 + 1) * 128
     count = len(w_fac)
-    shard = (parts // 2, width // parts, wide)
+    shard = (parts // 2, wide, width // parts)
     return pl.pallas_call(
         functools.partial(tail_kernel, count, cols),
         out_shape=[like(rows, width, dtype=f32)] + [like(*shard)] * 2,
         in_specs=[smem()] * 2 + [vmem()] * 9 + [anywhere()] * count,
         out_specs=[vmem()] * 3,
         scratch_shapes=[
-            scratch(width, wide),
+            scratch(cols, width),
             scratch(wide, rows),
+            scratch(width, 128, dtype=f32),
             pltpu.SemaphoreType.DMA((count,)),
         ],
         compiler_params=params(),
@@ -859,7 +858,6 @@
 
 def finish_kernel(widths, place, near, far, *outs):
     _, rows, wide = near.shape
-    last = wide - 128
     for side, value in ((0, near), (1, far)):
         for k in range(4):
             at = place[0] ^ (side * place[1]) ^ ((k >> 1) * place[2]) ^ ((k & 1) * place[3])
@@ -868,22 +866,15 @@
             for out, cols in zip(outs, widths):
                 out[row, :] = value[k, :, col : col + cols].astype(f32)
                 col += cols
-            if col < wide:
-                outs[-1][row, :] = value[k, :, last:].astype(f32)
-    if sum(widths) < wide:
-        outs[-2][...] = jnp.transpose(outs[-1][...])[sum(widths) - last : sum(widths) - last + 8]
 
 
 def finish(place, near, far, widths):
-    _, rows, wide = near.shape
-    shapes = [like(8 * rows, cols, dtype=f32) for cols in widths]
-    more = sum(widths) < wide
+    rows = near.shape[1]
     return pl.pallas_call(
         functools.partial(finish_kernel, widths),
-        out_shape=shapes + ([like(8, 8 * rows, dtype=f32)] if more else []),
+        out_shape=[like(8 * rows, cols, dtype=f32) for cols in widths],
         in_specs=[smem()] + [vmem()] * 2,
-        out_specs=[vmem()] * (len(shapes) + more),
-        scratch_shapes=[scratch(8 * rows, 128, dtype=f32)] if more else [],
+        out_specs=[vmem()] * len(widths),
         compiler_params=params(),
         cost_estimate=cost(1, 1),
         name="finish",
@@ -960,12 +951,16 @@
         self.order.ran(self.other)
 
     def cross(self):
-        self.got = partner(self.other, "grp", 2)
-
-    def fold(self, step):
+        self.got = partner(self.order.free(self.other), "grp", 2)
+
+    def go(self, step):
+        self.got = along(self.order.free(self.other), step)
+
+    def fold(self, step, start=True):
         def then(mine, other):
             self.mine, self.other = mine, other
-            self.got = along(other, step)
+            if start:
+                self.got = along(other, step)
 
         if step == 0:
             then(*halve(self.place, self.order.now(self.mine), self.got))
@@ -980,12 +975,12 @@
 
         self.order.add("pair", 0, self.pairs[0][0], self.got[0], then)
 
-    def swap(self, step):
+    def swap(self, step, flip=0):
         def then(mine):
             self.mine = mine
-            self.got = along(mine, step % 3)
-
-        self.order.add("sum", (0, 0, 2, 1)[step] if self.mine.shape[0] > 1 else 0, self.mine, self.got, then)
+            self.got = along(mine, step)
+
+        self.order.add("sum", flip, self.mine, self.got, then)
 
     def open(self, step):
         def then(mine):
@@ -1029,23 +1024,17 @@
     x = layer_input[0]
     upstream = cotangent[0]
     shard_rows, cols = factor_weight.shape
-    wide = (cols // 128 + 1) * 128
-    factor_wide = jnp.concatenate(
-        [
-            factor_weight,
-            attention_gain[:, None],
-            feed_gain[:, None],
-            jnp.zeros((shard_rows, wide - cols - 2), bf16),
-        ],
-        axis=1,
-    )
+    own_gains = jnp.stack([attention_gain, feed_gain])
+    factor_turned = factor_weight.T
     gather = lambda value: lax.all_gather(value, "grp", axis=0, tiled=True)
 
     if parts != 4 or lax.axis_size("rep") != 8:
         whole = jnp.zeros((4,), jnp.int32)
-        w_fac, w_out, w_down = ([gather(v)] for v in (factor_wide, output_weight, down_weight))
+        w_out, w_down = [gather(output_weight)], [gather(down_weight)]
+        w_fac = [lax.all_gather(factor_turned, "grp", axis=1, tiled=True)]
         w_gate, w_up = [gather(gate_weight)], [gather(up_weight)]
-        fac, kv_own, hid_one, gains = front(whole, x, cosine, sine, w_fac, cols)
+        all_gains = lax.all_gather(own_gains, "grp", axis=1, tiled=True)
+        fac, kv_own, hid_one, gains = front(whole, x, cosine, sine, w_fac, [all_gains])
         kv = [lax.all_gather(kv_own, "grp", axis=0, tiled=False)]
         mixed, lse = ([got] for got in attend(info, fac, kv, 0, HEADS))
         mid, hid_two, act, slope, lin, act_rows = feed(
@@ -1057,7 +1046,8 @@
         dmid, fgain, dmix, *out_pair = middle_grads(
             whole, info, upstream, gains[1:2], mixed, w_out, w_gate, w_up, dgate, dup, mid, parts
         )
-        result, *gate_pair = settle(whole, info, hid_two, dgate, act, mid, w_down, parts)
+        gate_pair = products(info, hid_two, dgate, parts)
+        result = output(whole, act, mid, w_down)
         dq, *dkv = attend_back(info, fac, kv, dmix, lse, 0, HEADS, ())
         input_grad, *fac_pair = tail(
             whole, info, dq, scatter_all(*dkv), cosine, sine, hid_one, x, gains[0:1], dmid, fgain,
@@ -1067,7 +1057,6 @@
         shards = [scatter_all(*pair) for pair in pairs]
         sums = [lax.psum(shard, "rep").astype(f32) for shard in shards]
         fac_grad, out_grad, gate_grad, up_grad, down_grad = sums
-        fac_grad, gain_grads = fac_grad[:, :cols], fac_grad[:, cols : cols + 2].T
     else:
         order = Order()
         low = lax.axis_index("rep") % 2
@@ -1081,24 +1070,32 @@
         by_down = halves(low, down_weight.shape[0])
         grp = lambda value, flip: partner(order.free(value), "grp", flip)
         rep = lambda value, flip: partner(order.free(value), "rep", flip)
-        fac_x = partner(factor_wide, "grp", 2)
-        fac_c = partner(factor_wide, "grp", 1)
+        fac_x = partner(factor_turned, "grp", 2)
+        fac_c = partner(factor_turned, "grp", 1)
+        gains_x = partner(own_gains, "grp", 2)
+        gains_c = partner(own_gains, "grp", 1)
         gate_c = partner(gate_weight, "grp", 1)
-        up_c = partner(up_weight, "grp", 1)
-        out_c = partner(output_weight, "grp", 1)
         gate_half, up_half = take(gate_weight, low), take(up_weight, even)
         out_half, down_half = take(output_weight, low), take(down_weight, low)
-        order.phase(fac_x, fac_c, gate_c, up_c, out_c, gate_half, up_half, out_half, down_half)
+        order.phase(
+            fac_x, fac_c, gains_x, gains_c, gate_c, gate_half, up_half, out_half, down_half
+        )
         fac_xc = grp(fac_x, 1)
+        gains_xc = grp(gains_x, 1)
         gate_x = grp(gate_half, 2)
-        w_fac = [factor_wide, fac_c, fac_x, fac_xc]
-        fac, kv_own, hid_one, gains = front(quarter, order.now(x), cosine, sine, w_fac, cols)
+        up_c = grp(up_weight, 1)
+        out_c = grp(output_weight, 1)
+        w_fac = [factor_turned, fac_c, fac_x, fac_xc]
+        all_gains = [own_gains, gains_c, gains_x, gains_xc]
+        fac, kv_own, hid_one, gains = front(
+            quarter, order.now(x), cosine, sine, w_fac, all_gains
+        )
         kv_x = partner(kv_own, "grp", 2)
         kv_c = partner(kv_own, "grp", 1)
         kv_xc = partner(kv_x, "grp", 1)
         kv = [kv_own, kv_c, kv_x, kv_xc]
 
-        order.phase(gate_x, kv_x, kv_c, kv_xc)
+        order.phase(gate_x, kv_x, kv_c, kv_xc, up_c, out_c)
         up_x = grp(up_half, 2)
         out_x = grp(out_half, 2)
         gate_y = rep(gate_x, 1)
@@ -1156,99 +1153,99 @@
         )
         out = chunk(out_pair)
         out.core()
-        result, *terms = settle(
-            by_down, info, after(hid_two, dmix), dgate, act, mid, w_down, parts
-        )
-        gate = chunk(terms)
-
-        order.phase(down.got, *up.got, *out.got, result)
+        gate = chunk(products(info, after(hid_two, dmix), dgate, parts))
+        part = 4
+        state = attend_back(info, fac, kv, after(dmix, gate.pairs[0][0]), lse, 0, part, ())
+
+        order.phase(down.got, *up.got, *out.got, state[0])
         both = chunk(*up.pairs, *out.pairs)
         both.got = up.got + out.got
         both.add_core()
         both.cross()
         down.fold(0)
         gate.core()
-        part = 3 * HEADS // 4
-        state = attend_back(info, fac, kv, order.free(dmix), lse, 0, part, ())
-
-        order.phase(both.got, down.got, *gate.got, state[0])
-        gate.add_core()
-        gate.cross()
-        both.fold(0)
+        dq, *terms = attend_back(info, fac, kv, order.free(dmix), lse, part, HEADS - part, state)
+
+        order.phase(both.got, down.got, *gate.got, dq)
+        dkv = chunk(terms)
+        dkv.core()
         down.fold(1)
         order.flush()
-        dq, *terms = attend_back(info, fac, kv, order.free(dmix), lse, part, HEADS - part, state)
-
-        order.phase(both.got, down.got, dq)
-        dkv = chunk(terms)
-        dkv.core()
-        both.fold(1)
+        both.fold(0, start=False)
+
+        order.phase(*dkv.got, down.got, both.other)
+        both.go(0)
+        dkv.pair()
         down.fold(2)
         order.flush()
-
-        order.phase(*dkv.got, both.got, down.got, gate.got)
-        dkv.pair()
-        both.fold(2)
-        order.flush()
-        gate.fold(0)
-
-        order.phase(dkv.got, both.got, gate.got)
+        gate.add_core()
+
+        order.phase(dkv.got, down.got, gate.other)
+        gate.cross()
         sums = []
         order.add("sum", 0, dkv.mine, dkv.got, sums.append)
-        both.swap(2)
-        gate.fold(1)
+        down.swap(2)
         order.flush()
         input_grad, *terms = tail(
             quarter, info, dq, sums[0], cosine, sine, hid_one, x, gains[0:1], dmid, fgain,
             w_fac, cols, parts,
         )
 
-        order.phase(both.got, gate.got, input_grad)
+        order.phase(both.got, down.got, input_grad)
         factor = chunk(terms)
         factor.core()
-        both.open(1)
-        gate.fold(2)
-        down.swap(2)
-        order.flush()
-
-        order.phase(*factor.got, both.got, gate.got, down.got)
-        factor.pair()
-        both.open(0)
-        gate.swap(2)
+        both.fold(1)
         down.open(1)
         order.flush()
 
-        order.phase(factor.got, both.got, gate.got, down.got)
-        factor.fold(0)
-        gate.open(1)
+        order.phase(*factor.got, both.got, down.got)
+        factor.pair()
+        both.fold(2)
         down.open(0)
         order.flush()
+        gate.got = after(gate.got, factor.mine)
+        gate.fold(0)
+
+        order.phase(factor.got, both.got, down.got, gate.got)
+        factor.fold(0)
+        gate.fold(1)
+        both.swap(2)
+        order.flush()
+        (down_grad,) = down.finish(down_weight.shape[1])
+
+        order.phase(factor.got, both.got, gate.got, down_grad)
+        factor.swap(1)
+        gate.fold(2)
+        both.open(1)
+        order.flush()
+
+        order.phase(factor.got, both.got, gate.got)
+        gate.swap(2)
+        both.open(0)
+        order.flush()
+        result = output(by_down, order.free(act), mid, w_down)
+
+        order.phase(both.got, gate.got, result)
+        factor.swap(2, 2)
+        gate.open(1)
+        order.flush()
         up_grad, out_grad = both.finish(up_weight.shape[1], output_weight.shape[1])
 
-        order.phase(factor.got, gate.got, down.got, up_grad)
-        factor.swap(1)
+        order.phase(factor.got, gate.got, up_grad)
+        factor.swap(0, 1)
         gate.open(0)
         order.flush()
-        (down_grad,) = down.finish(down_weight.shape[1])
-
-        order.phase(factor.got, gate.got, down_grad)
-        factor.swap(2)
-        order.flush()
+
+        order.phase(factor.got, gate.got)
+        (fac_grad,) = factor.finish(shard_rows)
         (gate_grad,) = gate.finish(gate_weight.shape[1])
-
-        order.phase(factor.got, gate_grad)
-        factor.swap(3)
-        order.flush()
-
-        order.phase(factor.got)
-        fac_grad, gain_grads = factor.finish(cols)
     return (
         result[None],
         input_grad[None],
-        gain_grads[0],
-        fac_grad,
+        fac_grad[cols],
+        fac_grad[:cols].T,
         out_grad,
-        gain_grads[1],
+        fac_grad[cols + 1],
         gate_grad,
         up_grad,
         down_grad,

time: 435 us -> 414 us (0.952)
  waiting for transfers between devices: 155 us -> 137 us
    ppermute x22, waiting for transfers between devices: 78.3 us -> 65 us  [along(): return lax.ppermute(values, ('rep', 'grp'), pairs)]
    pallas_call x2 -> x3, Pallas kernels: 12.7 us -> 19.1 us  [products(): pl.pallas_call(products_kernel, out_shape=[like(*pair)] * 2, in_specs=[sm...]
    ppermute x37 -> x40, waiting for transfers between devices: 76.6 us -> 71.9 us  [partner(): return lax.ppermute(values, axis, [(i, i ^ flip) for i in range(size)])]
    unnamed x98 -> x112, local copies, waits for them, and re-layouts: 15.9 us -> 12.1 us
    ppermute x37 -> x40, starting transfers between devices: 26.4 us -> 25.1 us  [partner(): return lax.ppermute(values, axis, [(i, i ^ flip) for i in range(size)])]
  transfers between devices with their start and end apart: 59 -> 62, of which waited for: 28 -> 22; matrix products, arithmetic and copies ran while one was open for 4% -> 3% of each run, Pallas kernels for 36% -> 42%
where the time goes in v4:
time: 414 us; the launch traced here: 408 us
  Pallas kernels  188 us (45%)
  waiting for transfers between devices  137 us (33%)
  starting transfers between devices  53 us (13%)
  local copies, waits for them, and re-layouts  25.8 us (6%)
    ppermute x40, waiting for transfers between devices, partner(): return lax.ppermute(values, axis, [(i, i ^ flip) for i in range(size)])  71.9 us
    ppermute x22, waiting for transfers between devices, along(): return lax.ppermute(values, ('rep', 'grp'), pairs)  65 us
    ppermute x22, starting transfers between devices, along(): return lax.ppermute(values, ('rep', 'grp'), pairs)  27.9 us
    pallas_call x10, Pallas kernels, batch(): pl.pallas_call(functools.partial(batch_kernel, [task[:2] for task in task...  25.7 us
    ppermute x40, starting transfers between devices, partner(): return lax.ppermute(values, axis, [(i, i ^ flip) for i in range(size)])  25.1 us
    pallas_call x2, Pallas kernels, attend_back(): pl.pallas_call(functools.partial(attend_back_kernel, first, heads, final,...  23.2 us
    pallas_call x3, Pallas kernels, products(): pl.pallas_call(products_kernel, out_shape=[like(*pair)] * 2, in_specs=[sm...  19.1 us
    pallas_call x4, Pallas kernels, halve(): pl.pallas_call(halve_kernel, grid_spec=pltpu.PrefetchScalarGridSpec(num_s...  18 us
  transfers between devices with their start and end apart: 62, of which 22 were waited for; matrix products, arithmetic and copies ran while one was open for 3% of the time, Pallas kernels for 42%

profile of v4, /device:TPU:0, one launch (start us, length us, event | category | flops | bytes accessed | tf_op | source)
XLA Modules:
  0.0 407.9 jit_solution(8156431775858722532)
XLA Ops:
  10.9 6.8 %collective-permute-done.refs_2_ = bf16[800,256]{1,0:T(8,128)(2,1)S(1)} collective-permute-done((bf16[800,256]{1,0:T(8,128)(2,1)}, bf16[800,256]{1,0:T(8,128)(2,1)S(1)}, u32[]{:S(2)}, u32[]{:S(2)}) %collective-permute-start) | collective-permute-done | bytes 409632 | tf_op jit(solution)/shard_map/ppermute | solution.py:723
  22.3 4.7 %front.1 = (bf16[480,384]{1,0:T(8,128)(2,1)}, bf16[320,384]{1,0:T(8,128)(2,1)}, bf16[1024,384]{1,0:T(8,128)(2,1)}, f32[8,1024]{1,0:T(8,128)}) custom-call(s32[8]{0:T(128)} %stack.119.offs, bf16[384,1024]{1,0:T(8,128)(2,1)} %bitcast.46, f32[32,384]{1,0:T(8,128)} %get-tuple-element.318.cos_ref, f32[32,384]{1,0:T(8,128)} %get-tuple-element.317.sin_ref, ...), custom_call_target="tpu_custom_call" | custom-call | flops 6291 | bytes 48 | tf_op jit(solution)/shard_map/front/pallas_call | solution.py:95
  28.9 14.2 %collective-permute-done.8.refs_2_ = bf16[320,384]{1,0:T(8,128)(2,1)S(1)} collective-permute-done((bf16[320,384]{1,0:T(8,128)(2,1)}, bf16[320,384]{1,0:T(8,128)(2,1)S(1)}, u32[]{:S(2)}, u32[]{:S(2)}) %collective-permute-start.8) | collective-permute-done | bytes 245792 | tf_op jit(solution)/shard_map/ppermute | solution.py:723
  49.5 7.5 %attend.2 = (bf16[512,384]{1,0:T(8,128)(2,1)}, f32[8,384]{1,0:T(8,128)}) custom-call(s32[3]{0:T(128)} %pad_add_fusion.info_ref.who, bf16[480,384]{1,0:T(8,128)(2,1)} %get-tuple-element.179.fac_ref, bf16[320,384]{1,0:T(8,128)(2,1)} %get-tuple-element.165.refs_0_, bf16[320,384]{1,0:T(8,128)(2,1)} %copy-done.9, bf16[320,384]{1,0:T(8,128)(2,1)} %copy-done.8, ...), custom_call_target="tpu_custom_call" | custom-call | flops 289910 | bytes 19 | tf_op jit(solution)/shard_map/attend/pallas_call | solution.py:211
  56.9 12.5 %collective-permute-done.14.refs_4_.refs_2_ = bf16[128,1024]{1,0:T(8,128)(2,1)} collective-permute-done((bf16[128,1024]{1,0:T(8,128)(2,1)}, bf16[128,1024]{1,0:T(8,128)(2,1)}, u32[]{:S(2)}, u32[]{:S(2)}) %collective-permute-start.14) | collective-permute-done | bytes 262176 | tf_op jit(solution)/shard_map/ppermute | solution.py:723
  73.3 7.7 %attend.3 = (bf16[512,384]{1,0:T(8,128)(2,1)}, f32[8,384]{1,0:T(8,128)}) custom-call(s32[3]{0:T(128)} %pad_add_fusion.info_ref.who, bf16[480,384]{1,0:T(8,128)(2,1)} %get-tuple-element.179.fac_ref, bf16[320,384]{1,0:T(8,128)(2,1)} %get-tuple-element.165.refs_0_, bf16[320,384]{1,0:T(8,128)(2,1)} %copy-done.9, bf16[320,384]{1,0:T(8,128)(2,1)} %copy-done.8, ...), custom_call_target="tpu_custom_call" | custom-call | flops 289910 | bytes 19 | tf_op jit(solution)/shard_map/attend/pallas_call | solution.py:211
  80.9 7.4 %collective-permute-done.18.refs_17_.refs_15_ = bf16[128,2816]{1,0:T(8,128)(2,1)S(1)} collective-permute-done((bf16[128,2816]{1,0:T(8,128)(2,1)}, bf16[128,2816]{1,0:T(8,128)(2,1)S(1)}, u32[]{:S(2)}, u32[]{:S(2)}) %collective-permute-start.18) | collective-permute-done | bytes 720928 | tf_op jit(solution)/shard_map/ppermute | solution.py:723
  97.5 15.5 %feed.1 = (f32[384,1024]{1,0:T(8,128)}, bf16[1024,384]{1,0:T(8,128)(2,1)}, bf16[384,2816]{1,0:T(8,128)(2,1)}, bf16[384,2816]{1,0:T(8,128)(2,1)}, bf16[384,2816]{1,0:T(8,128)(2,1)}, /*index=5*/bf16[2816,384]{1,0:T(8,128)(2,1)}) custom-call(s32[24]{0:T(128)} %concatenate.3.offs, bf16[384,1024]{1,0:T(8,128)(2,1)} %bitcast.47, ...), custom_call_target="tpu_custom_call" | custom-call | flops 74490 | bytes 237 | tf_op jit(solution)/shard_map/feed/pallas_call | solution.py:461
  113.1 6.2 %products.3 = (bf16[2,704,1024]{2,1,0:T(8,128)(2,1)}, bf16[2,704,1024]{2,1,0:T(8,128)(2,1)}) custom-call(s32[3]{0:T(128)} %pad_add_fusion.info_ref.who, bf16[2816,384]{1,0:T(8,128)(2,1)} %get-tuple-element.190.left, bf16[384,1024]{1,0:T(8,128)(2,1)} %bitcast.49), custom_call_target="tpu_custom_call" | custom-call | flops 22145 | bytes 65 | tf_op jit(solution)/shard_map/products/pallas_call | solution.py:538
  121.3 9.8 %slopes.1 = (bf16[384,2816]{1,0:T(8,128)(2,1)}, bf16[384,2816]{1,0:T(8,128)(2,1)}) custom-call(s32[12]{0:T(128)} %stack.103.offs, bf16[384,2816]{1,0:T(8,128)(2,1)} %get-tuple-element.196.slope_ref, bf16[384,2816]{1,0:T(8,128)(2,1)} %get-tuple-element.197.lin_ref, bf16[384,1024]{1,0:T(8,128)(2,1)} %bitcast.50, bf16[704,1024]{1,0:T(8,128)(2,1)} %refs_0_.5, ...), custom_call_target="tpu_custom_call" | custom-call | flops 22145 | bytes 144 | tf_op jit(solution)/shard_map/slopes/pallas_call | solution.py:512
  131.1 6.6 %products.4 = (bf16[2,256,2816]{2,1,0:T(8,128)(2,1)}, bf16[2,256,2816]{2,1,0:T(8,128)(2,1)}) custom-call(s32[3]{0:T(128)} %pad_add_fusion.info_ref.who, bf16[1024,384]{1,0:T(8,128)(2,1)} %get-tuple-element.211.left, bf16[384,2816]{1,0:T(8,128)(2,1)} %get-tuple-element.199.right.refs_21_), custom_call_target="tpu_custom_call" | custom-call | flops 22145 | bytes 79 | tf_op jit(solution)/shard_map/products/pallas_call | solution.py:538
  139.3 4.7 %add_pairs.3 = (bf16[704,1024]{1,0:T(8,128)(2,1)}, bf16[704,1024]{1,0:T(8,128)(2,1)}) custom-call(bf16[2,704,1024]{2,1,0:T(8,128)(2,1)} %get-tuple-element.204.refs_0_, bf16[2,704,1024]{2,1,0:T(8,128)(2,1)} %copy-done.16), custom_call_target="tpu_custom_call" | custom-call | tf_op jit(solution)/shard_map/add_pairs/pallas_call | solution.py:764
  145.5 13.6 %middle_grads.1 = (f32[384,1024]{1,0:T(8,128)}, f32[8,1024]{1,0:T(8,128)}, bf16[1024,384]{1,0:T(8,128)(2,1)}, bf16[2,256,1024]{2,1,0:T(8,128)(2,1)}, bf16[2,256,1024]{2,1,0:T(8,128)(2,1)}) custom-call(s32[24]{0:T(128)} %concatenate.3.offs, s32[3]{0:T(128)} %pad_add_fusion.info_ref.who, bf16[384,1024]{1,0:T(8,128)(2,1)} %bitcast.51, ...), custom_call_target="tpu_custom_call" | custom-call | flops 52344 | bytes 158 | tf_op jit(solution)/shard_map/middle_grads/pallas_call | solution.py:598
  159.2 6.4 %products.5 = (bf16[2,256,2816]{2,1,0:T(8,128)(2,1)}, bf16[2,256,2816]{2,1,0:T(8,128)(2,1)}) custom-call(s32[3]{0:T(128)} %pad_add_fusion.info_ref.who, bf16[1024,384]{1,0:T(8,128)(2,1)} %get-tuple-element.211.left, bf16[384,2816]{1,0:T(8,128)(2,1)} %get-tuple-element.202.refs_20_.right), custom_call_target="tpu_custom_call" | custom-call | flops 22145 | bytes 79 | tf_op jit(solution)/shard_map/products/pallas_call | solution.py:538
  165.6 7.3 %attend_back.2 = (f32[480,384]{1,0:T(8,128)}, f32[4,320,384]{2,1,0:T(8,128)}) custom-call(s32[3]{0:T(128)} %pad_add_fusion.info_ref.who, bf16[480,384]{1,0:T(8,128)(2,1)} %get-tuple-element.179.fac_ref, bf16[1024,384]{1,0:T(8,128)(2,1)} %get-tuple-element.217.grad_ref, bf16[320,384]{1,0:T(8,128)(2,1)} %get-tuple-element.165.refs_0_, ...), custom_call_target="tpu_custom_call" | custom-call | flops 5 | bytes 39 | tf_op jit(solution)/shard_map/attend_back/pallas_call | solution.py:312
  172.9 4.9 %collective-permute-done.30 = bf16[704,1024]{1,0:T(8,128)(2,1)S(1)} collective-permute-done((bf16[704,1024]{1,0:T(8,128)(2,1)}, bf16[704,1024]{1,0:T(8,128)(2,1)S(1)}, u32[]{:S(2)}, u32[]{:S(2)}) %collective-permute-start.30) | collective-permute-done | bytes 1441824 | tf_op jit(solution)/shard_map/ppermute | solution.py:723
  177.8 6.1 %add_pairs.4 = (bf16[256,3840]{1,0:T(8,128)(2,1)}, bf16[256,3840]{1,0:T(8,128)(2,1)}) custom-call(bf16[2,256,2816]{2,1,0:T(8,128)(2,1)} %get-tuple-element.222.refs_0_, bf16[2,256,2816]{2,1,0:T(8,128)(2,1)} %collective-permute-done.31.refs_1_, bf16[2,256,1024]{2,1,0:T(8,128)(2,1)} %get-tuple-element.223.refs_2_, bf16[2,256,1024]{2,1,0:T(8,128)(2,1)} %copy-done.24), custom_call_target="tpu_custom_call" | custom-call | tf_op jit(solution)/shard_map/add_pairs/pallas_call | solution.py:764
  187.2 4.6 %halve.4 = (bf16[4,88,1024]{2,1,0:T(8,128)(2,1)}, bf16[4,88,1024]{2,1,0:T(8,128)(2,1)}) custom-call(s32[4]{0:T(128)} %pad_add_fusion.1.place, bf16[8,88,1024]{2,1,0:T(8,128)(2,1)} %bitcast.52, bf16[8,88,1024]{2,1,0:T(8,128)(2,1)} %bitcast.56, bf16[8,88,1024]{2,1,0:T(8,128)(2,1)} %bitcast.53, bf16[8,88,1024]{2,1,0:T(8,128)(2,1)} %bitcast.57), custom_call_target="tpu_custom_call" | custom-call | tf_op jit(solution)/shard_map/halve/pallas_call | solution.py:793
  192.7 15.9 %attend_back.3 = (f32[480,384]{1,0:T(8,128)}, bf16[2,320,384]{2,1,0:T(8,128)(2,1)}, bf16[2,320,384]{2,1,0:T(8,128)(2,1)}) custom-call(s32[3]{0:T(128)} %pad_add_fusion.info_ref.who, bf16[480,384]{1,0:T(8,128)(2,1)} %get-tuple-element.179.fac_ref, bf16[1024,384]{1,0:T(8,128)(2,1)} %get-tuple-element.217.grad_ref, ...), custom_call_target="tpu_custom_call" | custom-call | flops 17 | bytes 39 | tf_op jit(solution)/shard_map/attend_back/pallas_call | solution.py:312
  208.6 20.8 %collective-permute-done.33 = bf16[256,3840]{1,0:T(8,128)(2,1)S(1)} collective-permute-done((bf16[256,3840]{1,0:T(8,128)(2,1)}, bf16[256,3840]{1,0:T(8,128)(2,1)S(1)}, u32[]{:S(2)}, u32[]{:S(2)}) %collective-permute-start.33) | collective-permute-done | bytes 1966112 | tf_op jit(solution)/shard_map/ppermute | solution.py:723
  233.3 4.9 %halve.5 = (bf16[4,32,3840]{2,1,0:T(8,128)(2,1)}, bf16[4,32,3840]{2,1,0:T(8,128)(2,1)}) custom-call(s32[4]{0:T(128)} %pad_add_fusion.1.place, bf16[8,32,3840]{2,1,0:T(8,128)(2,1)} %bitcast.42, bf16[8,32,3840]{2,1,0:T(8,128)(2,1)} %bitcast.44, bf16[8,32,3840]{2,1,0:T(8,128)(2,1)} %bitcast.43, bf16[8,32,3840]{2,1,0:T(8,128)(2,1)} %bitcast.45), custom_call_target="tpu_custom_call" | custom-call | tf_op jit(solution)/shard_map/halve/pallas_call | solution.py:793
  248.6 4.7 %add_pairs.5 = (bf16[256,2816]{1,0:T(8,128)(2,1)}, bf16[256,2816]{1,0:T(8,128)(2,1)}) custom-call(bf16[2,256,2816]{2,1,0:T(8,128)(2,1)} %get-tuple-element.244.refs_0_, bf16[2,256,2816]{2,1,0:T(8,128)(2,1)} %collective-permute-done.35.refs_1_), custom_call_target="tpu_custom_call" | custom-call | tf_op jit(solution)/shard_map/add_pairs/pallas_call | solution.py:764
  260.0 7.1 %tail.1 = (f32[384,1024]{1,0:T(8,128)}, bf16[2,896,256]{2,1,0:T(8,128)(2,1)}, bf16[2,896,256]{2,1,0:T(8,128)(2,1)}) custom-call(s32[8]{0:T(128)} %stack.119.offs, s32[3]{0:T(128)} %pad_add_fusion.info_ref.who, f32[480,384]{1,0:T(8,128)} %get-tuple-element.219.dq_ref, bf16[320,384]{1,0:T(8,128)(2,1)} %get-tuple-element.249.own_ref, ...), custom_call_target="tpu_custom_call" | custom-call | flops 12582 | bytes 79 | tf_op jit(solution)/shard_map/tail/pallas_call | solution.py:704
  275.4 10.9 %collective-permute-done.44.refs_5_ = bf16[2,88,1024]{2,1,0:T(8,128)(2,1)S(1)} collective-permute-done((bf16[2,88,1024]{2,1,0:T(8,128)(2,1)}, bf16[2,88,1024]{2,1,0:T(8,128)(2,1)S(1)}, u32[]{:S(2)}, u32[]{:S(2)}) %collective-permute-start.44) | collective-permute-done | bytes 360480 | tf_op jit(solution)/shard_map/ppermute | solution.py:937
  292.6 4.7 %halve.6 = (bf16[4,32,2816]{2,1,0:T(8,128)(2,1)}, bf16[4,32,2816]{2,1,0:T(8,128)(2,1)}) custom-call(s32[4]{0:T(128)} %pad_add_fusion.1.place, bf16[8,32,2816]{2,1,0:T(8,128)(2,1)} %bitcast.54, bf16[8,32,2816]{2,1,0:T(8,128)(2,1)} %bitcast.58, bf16[8,32,2816]{2,1,0:T(8,128)(2,1)} %bitcast.55, bf16[8,32,2816]{2,1,0:T(8,128)(2,1)} %bitcast.59), custom_call_target="tpu_custom_call" | custom-call | tf_op jit(solution)/shard_map/halve/pallas_call | solution.py:793
  300.1 9.9 %collective-permute-done.46.refs_3_ = bf16[1,32,3840]{2,1,0:T(8,128)(2,1)S(1)} collective-permute-done((bf16[1,32,3840]{2,1,0:T(8,128)(2,1)S(1)}, bf16[1,32,3840]{2,1,0:T(8,128)(2,1)S(1)}, u32[]{:S(2)}, u32[]{:S(2)}) %collective-permute-start.46) | collective-permute-done | bytes 245792 | tf_op jit(solution)/shard_map/ppermute | solution.py:937
  316.4 3.8 halve.7
  332.9 10.8 %collective-permute-done.55.refs_1_ = bf16[1,32,2816]{2,1,0:T(8,128)(2,1)S(1)} collective-permute-done((bf16[1,32,2816]{2,1,0:T(8,128)(2,1)}, bf16[1,32,2816]{2,1,0:T(8,128)(2,1)S(1)}, u32[]{:S(2)}, u32[]{:S(2)}) %collective-permute-start.55) | collective-permute-done | bytes 180256 | tf_op jit(solution)/shard_map/ppermute | solution.py:937
  351.2 8.0 %output.1 = bf16[384,1024]{1,0:T(8,128)(2,1)} custom-call(s32[12]{0:T(128)} %stack.103.offs, bf16[384,2816]{1,0:T(8,128)(2,1)} %get-tuple-element.294.act_ref, f32[384,1024]{1,0:T(8,128)} %get-tuple-element.189.refs_22_.mid_ref, bf16[704,1024]{1,0:T(8,128)(2,1)} %refs_0_.5, bf16[704,1024]{1,0:T(8,128)(2,1)} %copy-done.5, ...), custom_call_target="tpu_custom_call" | custom-call | flops 22145 | bytes 79 | tf_op jit(solution)/shard_map/output/pallas_call | solution.py:649
  368.2 3.7 finish.5
  371.9 8.9 %collective-permute-done.58.refs_1_ = bf16[4,112,256]{2,1,0:T(8,128)(2,1)S(1)} collective-permute-done((bf16[4,112,256]{2,1,0:T(8,128)(2,1)}, bf16[4,112,256]{2,1,0:T(8,128)(2,1)S(1)}, u32[]{:S(2)}, u32[]{:S(2)}) %collective-permute-start.58) | collective-permute-done | bytes 229408 | tf_op jit(solution)/shard_map/ppermute | solution.py:937
  386.0 11.9 %collective-permute-done.60.far = bf16[4,112,256]{2,1,0:T(8,128)(2,1)S(1)} collective-permute-done((bf16[4,112,256]{2,1,0:T(8,128)(2,1)}, bf16[4,112,256]{2,1,0:T(8,128)(2,1)S(1)}, u32[]{:S(2)}, u32[]{:S(2)}) %collective-permute-start.60) | collective-permute-done | bytes 229408 | tf_op jit(solution)/shard_map/ppermute | solution.py:937
  (256 shorter events, 133.0 us)
Async XLA Ops:
  0.7 17.0 %collective-permute-start.4 = (bf16[256,2816]{1,0:T(8,128)(2,1)}, bf16[256,2816]{1,0:T(8,128)(2,1)}, u32[]{:S(2)}, u32[]{:S(2)}) collective-permute-start(bf16[256,2816]{1,0:T(8,128)(2,1)} %refs_6_.1), channel_id=1, source_target_pairs={{0,1},{1,0},{2,3},{3,2},{4,5},{5,4},{6,7},{7,6},{8,9},{9,8},{10,11... | collective-permute-start | bytes 4325384 | tf_op jit(solution)/shard_map/ppermute | solution.py:723
  17.7 26.9 %collective-permute-start.11 = (bf16[256,2816]{1,0:T(8,128)(2,1)}, bf16[256,2816]{1,0:T(8,128)(2,1)}, u32[]{:S(2)}, u32[]{:S(2)}) collective-permute-start(bf16[256,2816]{1,0:T(8,128)(2,1)} %refs_12_.1), channel_id=1, source_target_pairs={{0,1},{1,0},{2,3},{3,2},{4,5},{5,4},{6,7},{7,6},{8,9},{9,8},{10,11... | collective-permute-start | bytes 4325384 | tf_op jit(solution)/shard_map/ppermute | solution.py:723
  19.5 23.6 %collective-permute-start.5 = (bf16[128,2816]{1,0:T(8,128)(2,1)}, bf16[128,2816]{1,0:T(8,128)(2,1)S(1)}, u32[]{:S(2)}, u32[]{:S(2)}) collective-permute-start(bf16[128,2816]{1,0:T(8,128)(2,1)} %get-tuple-element.161), channel_id=1, source_target_pairs={{0,2},{1,3},{2,0},{3,1},{4,6},{5,7},{6,4},{7,5},{8,10},{9,11},{10,... | collective-permute-start | bytes 2162696 | tf_op jit(solution)/shard_map/ppermute | solution.py:723
  19.8 23.3 %collective-permute-start.12 = (bf16[256,1024]{1,0:T(8,128)(2,1)S(1)}, bf16[256,1024]{1,0:T(8,128)(2,1)}, u32[]{:S(2)}, u32[]{:S(2)}) collective-permute-start(bf16[256,1024]{1,0:T(8,128)(2,1)S(1)} %copy-done.11), channel_id=1, source_target_pairs={{0,1},{1,0},{2,3},{3,2},{4,5},{5,4},{6,7},{7,6},{8,9},{9,8},{10,11... | collective-permute-start | bytes 1572872 | tf_op jit(solution)/shard_map/ppermute | solution.py:723
  27.1 16.0 %collective-permute-start.8 = (bf16[320,384]{1,0:T(8,128)(2,1)}, bf16[320,384]{1,0:T(8,128)(2,1)S(1)}, u32[]{:S(2)}, u32[]{:S(2)}) collective-permute-start(bf16[320,384]{1,0:T(8,128)(2,1)} %get-tuple-element.165.refs_0_), channel_id=1, source_target_pairs={{0,2},{1,3},{2,0},{3,1},{4,6},{5,7},{6,4},{7,5},{8,10},{9,11},{10,... | collective-permute-start | bytes 737288 | tf_op jit(solution)/shard_map/ppermute | solution.py:723
  28.9 14.2 %collective-permute-start.9 = (bf16[320,384]{1,0:T(8,128)(2,1)}, bf16[320,384]{1,0:T(8,128)(2,1)S(1)}, u32[]{:S(2)}, u32[]{:S(2)}) collective-permute-start(bf16[320,384]{1,0:T(8,128)(2,1)} %get-tuple-element.165.refs_0_), channel_id=1, source_target_pairs={{0,1},{1,0},{2,3},{3,2},{4,5},{5,4},{6,7},{7,6},{8,9},{9,8},{10,11... | collective-permute-start | bytes 737288 | tf_op jit(solution)/shard_map/ppermute | solution.py:723
  44.6 24.8 %collective-permute-start.17 = (bf16[704,1024]{1,0:T(8,128)(2,1)S(1)}, bf16[704,1024]{1,0:T(8,128)(2,1)S(1)}, u32[]{:S(2)}, u32[]{:S(2)}) collective-permute-start(bf16[704,1024]{1,0:T(8,128)(2,1)S(1)} %copy-done.2), channel_id=1, source_target_pairs={{0,1},{1,0},{2,3},{3,2},{4,5},{5,4},{6,7},{7,6},{8,9},{9,8},{10,11... | collective-permute-start | bytes 4325384 | tf_op jit(solution)/shard_map/ppermute | solution.py:723
  45.3 24.1 %collective-permute-start.13 = (bf16[128,2816]{1,0:T(8,128)(2,1)}, bf16[128,2816]{1,0:T(8,128)(2,1)}, u32[]{:S(2)}, u32[]{:S(2)}) collective-permute-start(bf16[128,2816]{1,0:T(8,128)(2,1)} %get-tuple-element.168), channel_id=1, source_target_pairs={{0,2},{1,3},{2,0},{3,1},{4,6},{5,7},{6,4},{7,5},{8,10},{9,11},{10,... | collective-permute-start | bytes 2162696 | tf_op jit(solution)/shard_map/ppermute | solution.py:723
  45.6 23.8 %collective-permute-start.16 = (bf16[128,2816]{1,0:T(8,128)(2,1)}, bf16[128,2816]{1,0:T(8,128)(2,1)}, u32[]{:S(2)}, u32[]{:S(2)}) collective-permute-start(bf16[128,2816]{1,0:T(8,128)(2,1)} %copy-done.12), channel_id=1, source_target_pairs={{0,1},{1,0},{2,3},{3,2},{4,5},{5,4},{6,7},{7,6},{8,9},{9,8},{10,11... | collective-permute-start | bytes 2162696 | tf_op jit(solution)/shard_map/ppermute | solution.py:723
  45.6 23.8 %collective-permute-start.15 = (bf16[128,2816]{1,0:T(8,128)(2,1)}, bf16[128,2816]{1,0:T(8,128)(2,1)}, u32[]{:S(2)}, u32[]{:S(2)}) collective-permute-start(bf16[128,2816]{1,0:T(8,128)(2,1)} %copy-done.12), channel_id=1, source_target_pairs={{0,4},{4,0},{8,12},{12,8},{16,20},{20,16},{24,28},{28,24},{1,5},{5... | collective-permute-start | bytes 2162696 | tf_op jit(solution)/shard_map/ppermute | solution.py:723
  47.4 22.1 %collective-permute-start.14 = (bf16[128,1024]{1,0:T(8,128)(2,1)}, bf16[128,1024]{1,0:T(8,128)(2,1)}, u32[]{:S(2)}, u32[]{:S(2)}) collective-permute-start(bf16[128,1024]{1,0:T(8,128)(2,1)} %constant_dynamic-slice_fusion.2), channel_id=1, source_target_pairs={{0,2},{1,3},{2,0},{3,1},{4,6},{5,7},{6,4},{7,5},{8,10},{9,11},{10,... | collective-permute-start | bytes 786440 | tf_op jit(solution)/shard_map/ppermute | solution.py:723
  69.6 18.8 %collective-permute-start.18 = (bf16[128,2816]{1,0:T(8,128)(2,1)}, bf16[128,2816]{1,0:T(8,128)(2,1)S(1)}, u32[]{:S(2)}, u32[]{:S(2)}) collective-permute-start(bf16[128,2816]{1,0:T(8,128)(2,1)} %collective-permute-done.13.refs_16_.refs_14_), channel_id=1, source_target_pairs={{0,8},{4,12},{8,0},{12,4},{16,24},{20,28},{24,16},{28,20},{1,9},{5... | collective-permute-start | bytes 2162696 | tf_op jit(solution)/shard_map/ppermute | solution.py:723
  71.2 18.5 %collective-permute-start.19 = (bf16[352,1024]{1,0:T(8,128)(2,1)}, bf16[352,1024]{1,0:T(8,128)(2,1)}, u32[]{:S(2)}, u32[]{:S(2)}) collective-permute-start(bf16[352,1024]{1,0:T(8,128)(2,1)} %constant_dynamic-slice_fusion.1), channel_id=1, source_target_pairs={{0,2},{1,3},{2,0},{3,1},{4,6},{5,7},{6,4},{7,5},{8,10},{9,11},{10,... | collective-permute-start | bytes 2162696 | tf_op jit(solution)/shard_map/ppermute | solution.py:723
  71.7 18.0 %collective-permute-start.22 = (bf16[128,2816]{1,0:T(8,128)(2,1)}, bf16[128,2816]{1,0:T(8,128)(2,1)}, u32[]{:S(2)}, u32[]{:S(2)}) collective-permute-start(bf16[128,2816]{1,0:T(8,128)(2,1)} %collective-permute-done.15.refs_11_.refs_9_), channel_id=1, source_target_pairs={{0,1},{1,0},{2,3},{3,2},{4,5},{5,4},{6,7},{7,6},{8,9},{9,8},{10,11... | collective-permute-start | bytes 2162696 | tf_op jit(solution)/shard_map/ppermute | solution.py:723
  93.6 19.4 %collective-permute-start.27 = (bf16[352,1024]{1,0:T(8,128)(2,1)}, bf16[352,1024]{1,0:T(8,128)(2,1)}, u32[]{:S(2)}, u32[]{:S(2)}) collective-permute-start(bf16[352,1024]{1,0:T(8,128)(2,1)} %collective-permute-done.19.refs_2_), channel_id=1, source_target_pairs={{0,1},{1,0},{2,3},{3,2},{4,5},{5,4},{6,7},{7,6},{8,9},{9,8},{10,11... | collective-permute-start | bytes 2162696 | tf_op jit(solution)/shard_map/ppermute | solution.py:723
  93.9 19.2 %collective-permute-start.26 = (bf16[352,1024]{1,0:T(8,128)(2,1)}, bf16[352,1024]{1,0:T(8,128)(2,1)}, u32[]{:S(2)}, u32[]{:S(2)}) collective-permute-start(bf16[352,1024]{1,0:T(8,128)(2,1)} %collective-permute-done.19.refs_2_), channel_id=1, source_target_pairs={{0,4},{4,0},{8,12},{12,8},{16,20},{20,16},{24,28},{28,24},{1,5},{5... | collective-permute-start | bytes 2162696 | tf_op jit(solution)/shard_map/ppermute | solution.py:723
  120.2 17.6 %collective-permute-start.29 = (bf16[2,704,1024]{2,1,0:T(8,128)(2,1)}, bf16[2,704,1024]{2,1,0:T(8,128)(2,1)S(1)}, u32[]{:S(2)}, u32[]{:S(2)}) collective-permute-start(bf16[2,704,1024]{2,1,0:T(8,128)(2,1)} %get-tuple-element.194), channel_id=1, source_target_pairs={{0,1},{1,0},{2,3},{3,2},{4,5},{5,4},{6,7},{7,6},{8,9},{9,8},{10,11... | collective-permute-start | bytes 8650760 | tf_op jit(solution)/shard_map/ppermute | solution.py:723
  137.7 40.0 %collective-permute-start.31 = (bf16[2,256,2816]{2,1,0:T(8,128)(2,1)}, bf16[2,256,2816]{2,1,0:T(8,128)(2,1)}, u32[]{:S(2)}, u32[]{:S(2)}) collective-permute-start(bf16[2,256,2816]{2,1,0:T(8,128)(2,1)} %get-tuple-element.208), channel_id=1, source_target_pairs={{0,1},{1,0},{2,3},{3,2},{4,5},{5,4},{6,7},{7,6},{8,9},{9,8},{10,11... | collective-permute-start | bytes 8650760 | tf_op jit(solution)/shard_map/ppermute | solution.py:723
  144.0 33.7 %collective-permute-start.30 = (bf16[704,1024]{1,0:T(8,128)(2,1)}, bf16[704,1024]{1,0:T(8,128)(2,1)S(1)}, u32[]{:S(2)}, u32[]{:S(2)}) collective-permute-start(bf16[704,1024]{1,0:T(8,128)(2,1)} %get-tuple-element.206), channel_id=1, source_target_pairs={{0,2},{1,3},{2,0},{3,1},{4,6},{5,7},{6,4},{7,5},{8,10},{9,11},{10,... | collective-permute-start | bytes 4325384 | tf_op jit(solution)/shard_map/ppermute | solution.py:723
  177.8 51.6 %collective-permute-start.35 = (bf16[2,256,2816]{2,1,0:T(8,128)(2,1)}, bf16[2,256,2816]{2,1,0:T(8,128)(2,1)}, u32[]{:S(2)}, u32[]{:S(2)}) collective-permute-start(bf16[2,256,2816]{2,1,0:T(8,128)(2,1)} %get-tuple-element.230), channel_id=1, source_target_pairs={{0,1},{1,0},{2,3},{3,2},{4,5},{5,4},{6,7},{7,6},{8,9},{9,8},{10,11... | collective-permute-start | bytes 8650760 | tf_op jit(solution)/shard_map/ppermute | solution.py:723
  183.9 45.5 %collective-permute-start.33 = (bf16[256,3840]{1,0:T(8,128)(2,1)}, bf16[256,3840]{1,0:T(8,128)(2,1)S(1)}, u32[]{:S(2)}, u32[]{:S(2)}) collective-permute-start(bf16[256,3840]{1,0:T(8,128)(2,1)} %get-tuple-element.225), channel_id=1, source_target_pairs={{0,2},{1,3},{2,0},{3,1},{4,6},{5,7},{6,4},{7,5},{8,10},{9,11},{10,... | collective-permute-start | bytes 5898248 | tf_op jit(solution)/shard_map/ppermute | solution.py:723
  191.7 16.8 %collective-permute-start.34 = (bf16[4,88,1024]{2,1,0:T(8,128)(2,1)}, bf16[4,88,1024]{2,1,0:T(8,128)(2,1)S(1)}, u32[]{:S(2)}, u32[]{:S(2)}) collective-permute-start(bf16[4,88,1024]{2,1,0:T(8,128)(2,1)} %get-tuple-element.228), channel_id=1, source_target_pairs={{0,4},{1,9},{2,6},{3,11},{4,0},{5,13},{6,2},{7,15},{8,12},{9,1},{1... | collective-permute-start | bytes 2162696 | tf_op jit(solution)/shard_map/ppermute | solution.py:937
  240.1 29.6 %collective-permute-start.40 = (bf16[4,32,3840]{2,1,0:T(8,128)(2,1)}, bf16[4,32,3840]{2,1,0:T(8,128)(2,1)S(1)}, u32[]{:S(2)}, u32[]{:S(2)}) collective-permute-start(bf16[4,32,3840]{2,1,0:T(8,128)(2,1)} %get-tuple-element.255), channel_id=1, source_target_pairs={{0,4},{1,9},{2,6},{3,11},{4,0},{5,13},{6,2},{7,15},{8,12},{9,1},{1... | collective-permute-start | bytes 2949128 | tf_op jit(solution)/shard_map/ppermute | solution.py:937
  254.5 37.0 %collective-permute-start.48 = (bf16[256,2816]{1,0:T(8,128)(2,1)}, bf16[256,2816]{1,0:T(8,128)(2,1)S(1)}, u32[]{:S(2)}, u32[]{:S(2)}) collective-permute-start(bf16[256,2816]{1,0:T(8,128)(2,1)} %get-tuple-element.274), channel_id=1, source_target_pairs={{0,2},{1,3},{2,0},{3,1},{4,6},{5,7},{6,4},{7,5},{8,10},{9,11},{10,... | collective-permute-start | bytes 4325384 | tf_op jit(solution)/shard_map/ppermute | solution.py:723
  269.6 16.7 %collective-permute-start.42 = (bf16[2,896,256]{2,1,0:T(8,128)(2,1)}, bf16[2,896,256]{2,1,0:T(8,128)(2,1)S(1)}, u32[]{:S(2)}, u32[]{:S(2)}) collective-permute-start(bf16[2,896,256]{2,1,0:T(8,128)(2,1)} %get-tuple-element.258), channel_id=1, source_target_pairs={{0,1},{1,0},{2,3},{3,2},{4,5},{5,4},{6,7},{7,6},{8,9},{9,8},{10,11... | collective-permute-start | bytes 2752520 | tf_op jit(solution)/shard_map/ppermute | solution.py:723
  290.9 19.1 %collective-permute-start.47 = (bf16[4,88,1024]{2,1,0:T(8,128)(2,1)}, bf16[4,88,1024]{2,1,0:T(8,128)(2,1)S(1)}, u32[]{:S(2)}, u32[]{:S(2)}) collective-permute-start(bf16[4,88,1024]{2,1,0:T(8,128)(2,1)} %get-tuple-element.286.near), channel_id=1, source_target_pairs={{0,4},{1,9},{2,6},{3,11},{4,0},{5,13},{6,2},{7,15},{8,12},{9,1},{1... | collective-permute-start | bytes 2162696 | tf_op jit(solution)/shard_map/ppermute | solution.py:937
  329.8 15.4 %collective-permute-start.54 = (bf16[2,32,3840]{2,1,0:T(8,128)(2,1)}, bf16[2,32,3840]{2,1,0:T(8,128)(2,1)S(1)}, u32[]{:S(2)}, u32[]{:S(2)}) collective-permute-start(bf16[2,32,3840]{2,1,0:T(8,128)(2,1)} %get-tuple-element.297.refs_2_), channel_id=1, source_target_pairs={{0,8},{1,5},{2,10},{3,7},{4,12},{5,1},{6,14},{7,3},{8,0},{9,13},{1... | collective-permute-start | bytes 1474568 | tf_op jit(solution)/shard_map/ppermute | solution.py:937
  330.8 14.4 %collective-permute-start.53 = (bf16[4,112,256]{2,1,0:T(8,128)(2,1)}, bf16[4,112,256]{2,1,0:T(8,128)(2,1)S(1)}, u32[]{:S(2)}, u32[]{:S(2)}) collective-permute-start(bf16[4,112,256]{2,1,0:T(8,128)(2,1)} %get-tuple-element.300.refs_0_), channel_id=1, source_target_pairs={{0,8},{1,5},{2,10},{3,7},{4,12},{5,1},{6,14},{7,3},{8,0},{9,13},{1... | collective-permute-start | bytes 688136 | tf_op jit(solution)/shard_map/ppermute | solution.py:937
  348.4 14.3 %collective-permute-start.56 = (bf16[4,32,3840]{2,1,0:T(8,128)(2,1)}, bf16[4,32,3840]{2,1,0:T(8,128)(2,1)S(1)}, u32[]{:S(2)}, u32[]{:S(2)}) collective-permute-start(bf16[4,32,3840]{2,1,0:T(8,128)(2,1)} %get-tuple-element.304.near), channel_id=1, source_target_pairs={{0,4},{1,9},{2,6},{3,11},{4,0},{5,13},{6,2},{7,15},{8,12},{9,1},{1... | collective-permute-start | bytes 2949128 | tf_op jit(solution)/shard_map/ppermute | solution.py:937
  365.1 15.7 %collective-permute-start.59 = (bf16[2,32,2816]{2,1,0:T(8,128)(2,1)}, bf16[2,32,2816]{2,1,0:T(8,128)(2,1)S(1)}, u32[]{:S(2)}, u32[]{:S(2)}) collective-permute-start(bf16[2,32,2816]{2,1,0:T(8,128)(2,1)} %get-tuple-element.307.refs_2_), channel_id=1, source_target_pairs={{0,8},{1,5},{2,10},{3,7},{4,12},{5,1},{6,14},{7,3},{8,0},{9,13},{1... | collective-permute-start | bytes 1081352 | tf_op jit(solution)/shard_map/ppermute | solution.py:937
  366.3 14.5 %collective-permute-start.58 = (bf16[4,112,256]{2,1,0:T(8,128)(2,1)}, bf16[4,112,256]{2,1,0:T(8,128)(2,1)S(1)}, u32[]{:S(2)}, u32[]{:S(2)}) collective-permute-start(bf16[4,112,256]{2,1,0:T(8,128)(2,1)} %get-tuple-element.306.refs_0_), channel_id=1, source_target_pairs={{0,16},{1,17},{2,18},{3,19},{4,20},{5,21},{6,22},{7,23},{8,24},{9,... | collective-permute-start | bytes 688136 | tf_op jit(solution)/shard_map/ppermute | solution.py:937
  384.0 14.0 %collective-permute-start.61 = (bf16[4,32,2816]{2,1,0:T(8,128)(2,1)}, bf16[4,32,2816]{2,1,0:T(8,128)(2,1)S(1)}, u32[]{:S(2)}, u32[]{:S(2)}) collective-permute-start(bf16[4,32,2816]{2,1,0:T(8,128)(2,1)} %get-tuple-element.312.near), channel_id=1, source_target_pairs={{0,4},{1,9},{2,6},{3,11},{4,0},{5,13},{6,2},{7,15},{8,12},{9,1},{1... | collective-permute-start | bytes 2162696 | tf_op jit(solution)/shard_map/ppermute | solution.py:937
  (86 other events, 607.1 us)

commit v5 on v4

--- a/solution.py
+++ b/solution.py
@@ -1154,7 +1154,7 @@
         out = chunk(out_pair)
         out.core()
         gate = chunk(products(info, after(hid_two, dmix), dgate, parts))
-        part = 4
+        part = 3
         state = attend_back(info, fac, kv, after(dmix, gate.pairs[0][0]), lse, 0, part, ())
 
         order.phase(down.got, *up.got, *out.got, state[0])
@@ -1220,24 +1220,24 @@
         order.flush()
 
         order.phase(factor.got, both.got, gate.got)
+        factor.swap(2, 2)
         gate.swap(2)
         both.open(0)
         order.flush()
         result = output(by_down, order.free(act), mid, w_down)
 
-        order.phase(both.got, gate.got, result)
-        factor.swap(2, 2)
+        order.phase(factor.got, both.got, gate.got, result)
+        factor.swap(0, 1)
         gate.open(1)
         order.flush()
         up_grad, out_grad = both.finish(up_weight.shape[1], output_weight.shape[1])
 
         order.phase(factor.got, gate.got, up_grad)
-        factor.swap(0, 1)
         gate.open(0)
         order.flush()
-
-        order.phase(factor.got, gate.got)
         (fac_grad,) = factor.finish(shard_rows)
+
+        order.phase(gate.got, fac_grad)
         (gate_grad,) = gate.finish(gate_weight.shape[1])
     return (
         result[None],

time: 414 us -> 404 us (0.976)
  waiting for transfers between devices: 137 us -> 126 us
    ppermute x22, waiting for transfers between devices: 65 us -> 54.2 us  [along(): return lax.ppermute(values, ('rep', 'grp'), pairs)]
  transfers between devices with their start and end apart: 62 -> 62, of which waited for: 22 -> 22; matrix products, arithmetic and copies ran while one was open for 3% -> 4% of each run, Pallas kernels for 42% -> 43%
where the time goes in v5:
time: 404 us; the launch traced here: 398 us
  Pallas kernels  188 us (47%)
  waiting for transfers between devices  126 us (31%)
  starting transfers between devices  53.1 us (13%)
  local copies, waits for them, and re-layouts  26.7 us (7%)
    ppermute x40, waiting for transfers between devices, partner(): return lax.ppermute(values, axis, [(i, i ^ flip) for i in range(size)])  72.2 us
    ppermute x22, waiting for transfers between devices, along(): return lax.ppermute(values, ('rep', 'grp'), pairs)  54.2 us
    ppermute x22, starting transfers between devices, along(): return lax.ppermute(values, ('rep', 'grp'), pairs)  28.8 us
    pallas_call x10, Pallas kernels, batch(): pl.pallas_call(functools.partial(batch_kernel, [task[:2] for task in task...  25.6 us
    ppermute x40, starting transfers between devices, partner(): return lax.ppermute(values, axis, [(i, i ^ flip) for i in range(size)])  24.3 us
    pallas_call x2, Pallas kernels, attend_back(): pl.pallas_call(functools.partial(attend_back_kernel, first, heads, final,...  23.2 us
    pallas_call x3, Pallas kernels, products(): pl.pallas_call(products_kernel, out_shape=[like(*pair)] * 2, in_specs=[sm...  19.1 us
    pallas_call x4, Pallas kernels, halve(): pl.pallas_call(halve_kernel, grid_spec=pltpu.PrefetchScalarGridSpec(num_s...  18 us
  transfers between devices with their start and end apart: 62, of which 22 were waited for; matrix products, arithmetic and copies ran while one was open for 4% of the time, Pallas kernels for 43%

profile of v5, /device:TPU:0, one launch (start us, length us, event | category | flops | bytes accessed | tf_op | source)
XLA Modules:
  0.0 398.3 jit_solution(8283559579715838101)
XLA Ops:
  10.9 6.8 %collective-permute-done.refs_2_ = bf16[800,256]{1,0:T(8,128)(2,1)S(1)} collective-permute-done((bf16[800,256]{1,0:T(8,128)(2,1)}, bf16[800,256]{1,0:T(8,128)(2,1)S(1)}, u32[]{:S(2)}, u32[]{:S(2)}) %collective-permute-start) | collective-permute-done | bytes 409632 | tf_op jit(solution)/shard_map/ppermute | solution.py:723
  22.3 4.7 %front.1 = (bf16[480,384]{1,0:T(8,128)(2,1)}, bf16[320,384]{1,0:T(8,128)(2,1)}, bf16[1024,384]{1,0:T(8,128)(2,1)}, f32[8,1024]{1,0:T(8,128)}) custom-call(s32[8]{0:T(128)} %stack.119.offs, bf16[384,1024]{1,0:T(8,128)(2,1)} %bitcast.46, f32[32,384]{1,0:T(8,128)} %get-tuple-element.316.cos_ref, f32[32,384]{1,0:T(8,128)} %get-tuple-element.315.sin_ref, ...), custom_call_target="tpu_custom_call" | custom-call | flops 6291 | bytes 48 | tf_op jit(solution)/shard_map/front/pallas_call | solution.py:95
  28.9 14.2 %collective-permute-done.8.refs_2_ = bf16[320,384]{1,0:T(8,128)(2,1)S(1)} collective-permute-done((bf16[320,384]{1,0:T(8,128)(2,1)}, bf16[320,384]{1,0:T(8,128)(2,1)S(1)}, u32[]{:S(2)}, u32[]{:S(2)}) %collective-permute-start.8) | collective-permute-done | bytes 245792 | tf_op jit(solution)/shard_map/ppermute | solution.py:723
  49.5 7.5 %attend.2 = (bf16[512,384]{1,0:T(8,128)(2,1)}, f32[8,384]{1,0:T(8,128)}) custom-call(s32[3]{0:T(128)} %pad_add_fusion.info_ref.who, bf16[480,384]{1,0:T(8,128)(2,1)} %get-tuple-element.178.fac_ref, bf16[320,384]{1,0:T(8,128)(2,1)} %get-tuple-element.164.refs_0_, bf16[320,384]{1,0:T(8,128)(2,1)} %copy-done.9, bf16[320,384]{1,0:T(8,128)(2,1)} %copy-done.8, ...), custom_call_target="tpu_custom_call" | custom-call | flops 289910 | bytes 19 | tf_op jit(solution)/shard_map/attend/pallas_call | solution.py:211
  57.0 12.4 %collective-permute-done.14.refs_4_.refs_2_ = bf16[128,1024]{1,0:T(8,128)(2,1)} collective-permute-done((bf16[128,1024]{1,0:T(8,128)(2,1)}, bf16[128,1024]{1,0:T(8,128)(2,1)}, u32[]{:S(2)}, u32[]{:S(2)}) %collective-permute-start.14) | collective-permute-done | bytes 262176 | tf_op jit(solution)/shard_map/ppermute | solution.py:723
  73.3 7.7 %attend.3 = (bf16[512,384]{1,0:T(8,128)(2,1)}, f32[8,384]{1,0:T(8,128)}) custom-call(s32[3]{0:T(128)} %pad_add_fusion.info_ref.who, bf16[480,384]{1,0:T(8,128)(2,1)} %get-tuple-element.178.fac_ref, bf16[320,384]{1,0:T(8,128)(2,1)} %get-tuple-element.164.refs_0_, bf16[320,384]{1,0:T(8,128)(2,1)} %copy-done.9, bf16[320,384]{1,0:T(8,128)(2,1)} %copy-done.8, ...), custom_call_target="tpu_custom_call" | custom-call | flops 289910 | bytes 19 | tf_op jit(solution)/shard_map/attend/pallas_call | solution.py:211
  81.0 7.4 %collective-permute-done.18.refs_17_.refs_15_ = bf16[128,2816]{1,0:T(8,128)(2,1)S(1)} collective-permute-done((bf16[128,2816]{1,0:T(8,128)(2,1)}, bf16[128,2816]{1,0:T(8,128)(2,1)S(1)}, u32[]{:S(2)}, u32[]{:S(2)}) %collective-permute-start.18) | collective-permute-done | bytes 720928 | tf_op jit(solution)/shard_map/ppermute | solution.py:723
  97.4 15.6 %feed.1 = (f32[384,1024]{1,0:T(8,128)}, bf16[1024,384]{1,0:T(8,128)(2,1)}, bf16[384,2816]{1,0:T(8,128)(2,1)}, bf16[384,2816]{1,0:T(8,128)(2,1)}, bf16[384,2816]{1,0:T(8,128)(2,1)}, /*index=5*/bf16[2816,384]{1,0:T(8,128)(2,1)}) custom-call(s32[24]{0:T(128)} %concatenate.3.offs, bf16[384,1024]{1,0:T(8,128)(2,1)} %bitcast.47, ...), custom_call_target="tpu_custom_call" | custom-call | flops 74490 | bytes 237 | tf_op jit(solution)/shard_map/feed/pallas_call | solution.py:461
  113.1 6.2 %products.3 = (bf16[2,704,1024]{2,1,0:T(8,128)(2,1)}, bf16[2,704,1024]{2,1,0:T(8,128)(2,1)}) custom-call(s32[3]{0:T(128)} %pad_add_fusion.info_ref.who, bf16[2816,384]{1,0:T(8,128)(2,1)} %get-tuple-element.189.left, bf16[384,1024]{1,0:T(8,128)(2,1)} %bitcast.49), custom_call_target="tpu_custom_call" | custom-call | flops 22145 | bytes 65 | tf_op jit(solution)/shard_map/products/pallas_call | solution.py:538
  121.3 9.8 %slopes.1 = (bf16[384,2816]{1,0:T(8,128)(2,1)}, bf16[384,2816]{1,0:T(8,128)(2,1)}) custom-call(s32[12]{0:T(128)} %stack.103.offs, bf16[384,2816]{1,0:T(8,128)(2,1)} %get-tuple-element.195.slope_ref, bf16[384,2816]{1,0:T(8,128)(2,1)} %get-tuple-element.196.lin_ref, bf16[384,1024]{1,0:T(8,128)(2,1)} %bitcast.50, bf16[704,1024]{1,0:T(8,128)(2,1)} %refs_0_.5, ...), custom_call_target="tpu_custom_call" | custom-call | flops 22145 | bytes 144 | tf_op jit(solution)/shard_map/slopes/pallas_call | solution.py:512
  131.1 6.6 %products.4 = (bf16[2,256,2816]{2,1,0:T(8,128)(2,1)}, bf16[2,256,2816]{2,1,0:T(8,128)(2,1)}) custom-call(s32[3]{0:T(128)} %pad_add_fusion.info_ref.who, bf16[1024,384]{1,0:T(8,128)(2,1)} %get-tuple-element.210.left, bf16[384,2816]{1,0:T(8,128)(2,1)} %get-tuple-element.198.right.refs_21_), custom_call_target="tpu_custom_call" | custom-call | flops 22145 | bytes 79 | tf_op jit(solution)/shard_map/products/pallas_call | solution.py:538
  139.3 4.7 %add_pairs.3 = (bf16[704,1024]{1,0:T(8,128)(2,1)}, bf16[704,1024]{1,0:T(8,128)(2,1)}) custom-call(bf16[2,704,1024]{2,1,0:T(8,128)(2,1)} %get-tuple-element.203.refs_0_, bf16[2,704,1024]{2,1,0:T(8,128)(2,1)} %copy-done.16), custom_call_target="tpu_custom_call" | custom-call | tf_op jit(solution)/shard_map/add_pairs/pallas_call | solution.py:764
  145.7 13.6 %middle_grads.1 = (f32[384,1024]{1,0:T(8,128)}, f32[8,1024]{1,0:T(8,128)}, bf16[1024,384]{1,0:T(8,128)(2,1)}, bf16[2,256,1024]{2,1,0:T(8,128)(2,1)}, bf16[2,256,1024]{2,1,0:T(8,128)(2,1)}) custom-call(s32[24]{0:T(128)} %concatenate.3.offs, s32[3]{0:T(128)} %pad_add_fusion.info_ref.who, bf16[384,1024]{1,0:T(8,128)(2,1)} %bitcast.51, ...), custom_call_target="tpu_custom_call" | custom-call | flops 52344 | bytes 158 | tf_op jit(solution)/shard_map/middle_grads/pallas_call | solution.py:598
  159.4 6.4 %products.5 = (bf16[2,256,2816]{2,1,0:T(8,128)(2,1)}, bf16[2,256,2816]{2,1,0:T(8,128)(2,1)}) custom-call(s32[3]{0:T(128)} %pad_add_fusion.info_ref.who, bf16[1024,384]{1,0:T(8,128)(2,1)} %get-tuple-element.210.left, bf16[384,2816]{1,0:T(8,128)(2,1)} %get-tuple-element.201.refs_20_.right), custom_call_target="tpu_custom_call" | custom-call | flops 22145 | bytes 79 | tf_op jit(solution)/shard_map/products/pallas_call | solution.py:538
  165.8 6.3 %attend_back.2 = (f32[480,384]{1,0:T(8,128)}, f32[4,320,384]{2,1,0:T(8,128)}) custom-call(s32[3]{0:T(128)} %pad_add_fusion.info_ref.who, bf16[480,384]{1,0:T(8,128)(2,1)} %get-tuple-element.178.fac_ref, bf16[1024,384]{1,0:T(8,128)(2,1)} %get-tuple-element.216.grad_ref, bf16[320,384]{1,0:T(8,128)(2,1)} %get-tuple-element.164.refs_0_, ...), custom_call_target="tpu_custom_call" | custom-call | flops 4 | bytes 39 | tf_op jit(solution)/shard_map/attend_back/pallas_call | solution.py:312
  172.1 5.6 %collective-permute-done.30 = bf16[704,1024]{1,0:T(8,128)(2,1)S(1)} collective-permute-done((bf16[704,1024]{1,0:T(8,128)(2,1)}, bf16[704,1024]{1,0:T(8,128)(2,1)S(1)}, u32[]{:S(2)}, u32[]{:S(2)}) %collective-permute-start.30) | collective-permute-done | bytes 1441824 | tf_op jit(solution)/shard_map/ppermute | solution.py:723
  177.8 6.1 %add_pairs.4 = (bf16[256,3840]{1,0:T(8,128)(2,1)}, bf16[256,3840]{1,0:T(8,128)(2,1)}) custom-call(bf16[2,256,2816]{2,1,0:T(8,128)(2,1)} %get-tuple-element.221.refs_0_, bf16[2,256,2816]{2,1,0:T(8,128)(2,1)} %collective-permute-done.31.refs_1_, bf16[2,256,1024]{2,1,0:T(8,128)(2,1)} %get-tuple-element.222.refs_2_, bf16[2,256,1024]{2,1,0:T(8,128)(2,1)} %copy-done.24), custom_call_target="tpu_custom_call" | custom-call | tf_op jit(solution)/shard_map/add_pairs/pallas_call | solution.py:764
  186.2 4.6 %halve.4 = (bf16[4,88,1024]{2,1,0:T(8,128)(2,1)}, bf16[4,88,1024]{2,1,0:T(8,128)(2,1)}) custom-call(s32[4]{0:T(128)} %pad_add_fusion.1.place, bf16[8,88,1024]{2,1,0:T(8,128)(2,1)} %bitcast.52, bf16[8,88,1024]{2,1,0:T(8,128)(2,1)} %bitcast.56, bf16[8,88,1024]{2,1,0:T(8,128)(2,1)} %bitcast.53, bf16[8,88,1024]{2,1,0:T(8,128)(2,1)} %bitcast.57), custom_call_target="tpu_custom_call" | custom-call | tf_op jit(solution)/shard_map/halve/pallas_call | solution.py:793
  191.9 16.9 %attend_back.3 = (f32[480,384]{1,0:T(8,128)}, bf16[2,320,384]{2,1,0:T(8,128)(2,1)}, bf16[2,320,384]{2,1,0:T(8,128)(2,1)}) custom-call(s32[3]{0:T(128)} %pad_add_fusion.info_ref.who, bf16[480,384]{1,0:T(8,128)(2,1)} %get-tuple-element.178.fac_ref, bf16[1024,384]{1,0:T(8,128)(2,1)} %get-tuple-element.216.grad_ref, ...), custom_call_target="tpu_custom_call" | custom-call | flops 19 | bytes 39 | tf_op jit(solution)/shard_map/attend_back/pallas_call | solution.py:312
  208.8 20.4 %collective-permute-done.33 = bf16[256,3840]{1,0:T(8,128)(2,1)S(1)} collective-permute-done((bf16[256,3840]{1,0:T(8,128)(2,1)}, bf16[256,3840]{1,0:T(8,128)(2,1)S(1)}, u32[]{:S(2)}, u32[]{:S(2)}) %collective-permute-start.33) | collective-permute-done | bytes 1966112 | tf_op jit(solution)/shard_map/ppermute | solution.py:723
  232.6 4.9 %halve.5 = (bf16[4,32,3840]{2,1,0:T(8,128)(2,1)}, bf16[4,32,3840]{2,1,0:T(8,128)(2,1)}) custom-call(s32[4]{0:T(128)} %pad_add_fusion.1.place, bf16[8,32,3840]{2,1,0:T(8,128)(2,1)} %bitcast.42, bf16[8,32,3840]{2,1,0:T(8,128)(2,1)} %bitcast.44, bf16[8,32,3840]{2,1,0:T(8,128)(2,1)} %bitcast.43, bf16[8,32,3840]{2,1,0:T(8,128)(2,1)} %bitcast.45), custom_call_target="tpu_custom_call" | custom-call | tf_op jit(solution)/shard_map/halve/pallas_call | solution.py:793
  247.6 4.7 %add_pairs.5 = (bf16[256,2816]{1,0:T(8,128)(2,1)}, bf16[256,2816]{1,0:T(8,128)(2,1)}) custom-call(bf16[2,256,2816]{2,1,0:T(8,128)(2,1)} %get-tuple-element.243.refs_0_, bf16[2,256,2816]{2,1,0:T(8,128)(2,1)} %collective-permute-done.35.refs_1_), custom_call_target="tpu_custom_call" | custom-call | tf_op jit(solution)/shard_map/add_pairs/pallas_call | solution.py:764
  259.0 7.1 %tail.1 = (f32[384,1024]{1,0:T(8,128)}, bf16[2,896,256]{2,1,0:T(8,128)(2,1)}, bf16[2,896,256]{2,1,0:T(8,128)(2,1)}) custom-call(s32[8]{0:T(128)} %stack.119.offs, s32[3]{0:T(128)} %pad_add_fusion.info_ref.who, f32[480,384]{1,0:T(8,128)} %get-tuple-element.218.dq_ref, bf16[320,384]{1,0:T(8,128)(2,1)} %get-tuple-element.248.own_ref, ...), custom_call_target="tpu_custom_call" | custom-call | flops 12582 | bytes 79 | tf_op jit(solution)/shard_map/tail/pallas_call | solution.py:704
  274.2 10.9 %collective-permute-done.44.refs_5_ = bf16[2,88,1024]{2,1,0:T(8,128)(2,1)S(1)} collective-permute-done((bf16[2,88,1024]{2,1,0:T(8,128)(2,1)}, bf16[2,88,1024]{2,1,0:T(8,128)(2,1)S(1)}, u32[]{:S(2)}, u32[]{:S(2)}) %collective-permute-start.44) | collective-permute-done | bytes 360480 | tf_op jit(solution)/shard_map/ppermute | solution.py:937
  291.7 4.7 %halve.6 = (bf16[4,32,2816]{2,1,0:T(8,128)(2,1)}, bf16[4,32,2816]{2,1,0:T(8,128)(2,1)}) custom-call(s32[4]{0:T(128)} %pad_add_fusion.1.place, bf16[8,32,2816]{2,1,0:T(8,128)(2,1)} %bitcast.54, bf16[8,32,2816]{2,1,0:T(8,128)(2,1)} %bitcast.58, bf16[8,32,2816]{2,1,0:T(8,128)(2,1)} %bitcast.55, bf16[8,32,2816]{2,1,0:T(8,128)(2,1)} %bitcast.59), custom_call_target="tpu_custom_call" | custom-call | tf_op jit(solution)/shard_map/halve/pallas_call | solution.py:793
  298.9 9.9 %collective-permute-done.46.refs_3_ = bf16[1,32,3840]{2,1,0:T(8,128)(2,1)S(1)} collective-permute-done((bf16[1,32,3840]{2,1,0:T(8,128)(2,1)S(1)}, bf16[1,32,3840]{2,1,0:T(8,128)(2,1)S(1)}, u32[]{:S(2)}, u32[]{:S(2)}) %collective-permute-start.46) | collective-permute-done | bytes 245792 | tf_op jit(solution)/shard_map/ppermute | solution.py:937
  315.1 3.8 halve.7
  331.7 10.8 %collective-permute-done.55.refs_3_ = bf16[1,32,2816]{2,1,0:T(8,128)(2,1)S(1)} collective-permute-done((bf16[1,32,2816]{2,1,0:T(8,128)(2,1)}, bf16[1,32,2816]{2,1,0:T(8,128)(2,1)S(1)}, u32[]{:S(2)}, u32[]{:S(2)}) %collective-permute-start.55) | collective-permute-done | bytes 180256 | tf_op jit(solution)/shard_map/ppermute | solution.py:937
  351.5 8.0 %output.1 = bf16[384,1024]{1,0:T(8,128)(2,1)} custom-call(s32[12]{0:T(128)} %stack.103.offs, bf16[384,2816]{1,0:T(8,128)(2,1)} %get-tuple-element.293.act_ref, f32[384,1024]{1,0:T(8,128)} %get-tuple-element.188.refs_22_.mid_ref, bf16[704,1024]{1,0:T(8,128)(2,1)} %refs_0_.5, bf16[704,1024]{1,0:T(8,128)(2,1)} %copy-done.5, ...), custom_call_target="tpu_custom_call" | custom-call | flops 22145 | bytes 79 | tf_op jit(solution)/shard_map/output/pallas_call | solution.py:649
  359.5 4.4 %collective-permute-done.58.refs_3_ = bf16[1,32,2816]{2,1,0:T(8,128)(2,1)S(1)} collective-permute-done((bf16[1,32,2816]{2,1,0:T(8,128)(2,1)}, bf16[1,32,2816]{2,1,0:T(8,128)(2,1)S(1)}, u32[]{:S(2)}, u32[]{:S(2)}) %collective-permute-start.58) | collective-permute-done | bytes 180256 | tf_op jit(solution)/shard_map/ppermute | solution.py:937
  367.1 4.0 %collective-permute-start.60 = (bf16[2,32,2816]{2,1,0:T(8,128)(2,1)}, bf16[2,32,2816]{2,1,0:T(8,128)(2,1)S(1)}, u32[]{:S(2)}, u32[]{:S(2)}) collective-permute-start(bf16[2,32,2816]{2,1,0:T(8,128)(2,1)} %get-tuple-element.309.refs_0_), channel_id=1, source_target_pairs={{0,8},{1,5},{2,10},{3,7},{4,12},{5,1},{6,14},{7,3},{8,0},{9,13},{1... | collective-permute-start | bytes 1081352 | tf_op jit(solution)/shard_map/ppermute | solution.py:937
  388.7 5.1 %collective-permute-done.61.far = bf16[4,32,2816]{2,1,0:T(8,128)(2,1)S(1)} collective-permute-done((bf16[4,32,2816]{2,1,0:T(8,128)(2,1)}, bf16[4,32,2816]{2,1,0:T(8,128)(2,1)S(1)}, u32[]{:S(2)}, u32[]{:S(2)}) %collective-permute-start.61) | collective-permute-done | bytes 720928 | tf_op jit(solution)/shard_map/ppermute | solution.py:937
  (256 shorter events, 134.1 us)
Async XLA Ops:
  0.7 17.0 %collective-permute-start.4 = (bf16[256,2816]{1,0:T(8,128)(2,1)}, bf16[256,2816]{1,0:T(8,128)(2,1)}, u32[]{:S(2)}, u32[]{:S(2)}) collective-permute-start(bf16[256,2816]{1,0:T(8,128)(2,1)} %refs_6_.1), channel_id=1, source_target_pairs={{0,1},{1,0},{2,3},{3,2},{4,5},{5,4},{6,7},{7,6},{8,9},{9,8},{10,11... | collective-permute-start | bytes 4325384 | tf_op jit(solution)/shard_map/ppermute | solution.py:723
  17.7 26.9 %collective-permute-start.11 = (bf16[256,2816]{1,0:T(8,128)(2,1)}, bf16[256,2816]{1,0:T(8,128)(2,1)}, u32[]{:S(2)}, u32[]{:S(2)}) collective-permute-start(bf16[256,2816]{1,0:T(8,128)(2,1)} %refs_12_.1), channel_id=1, source_target_pairs={{0,1},{1,0},{2,3},{3,2},{4,5},{5,4},{6,7},{7,6},{8,9},{9,8},{10,11... | collective-permute-start | bytes 4325384 | tf_op jit(solution)/shard_map/ppermute | solution.py:723
  19.5 23.6 %collective-permute-start.5 = (bf16[128,2816]{1,0:T(8,128)(2,1)}, bf16[128,2816]{1,0:T(8,128)(2,1)S(1)}, u32[]{:S(2)}, u32[]{:S(2)}) collective-permute-start(bf16[128,2816]{1,0:T(8,128)(2,1)} %get-tuple-element.160), channel_id=1, source_target_pairs={{0,2},{1,3},{2,0},{3,1},{4,6},{5,7},{6,4},{7,5},{8,10},{9,11},{10,... | collective-permute-start | bytes 2162696 | tf_op jit(solution)/shard_map/ppermute | solution.py:723
  19.8 23.3 %collective-permute-start.12 = (bf16[256,1024]{1,0:T(8,128)(2,1)S(1)}, bf16[256,1024]{1,0:T(8,128)(2,1)}, u32[]{:S(2)}, u32[]{:S(2)}) collective-permute-start(bf16[256,1024]{1,0:T(8,128)(2,1)S(1)} %copy-done.11), channel_id=1, source_target_pairs={{0,1},{1,0},{2,3},{3,2},{4,5},{5,4},{6,7},{7,6},{8,9},{9,8},{10,11... | collective-permute-start | bytes 1572872 | tf_op jit(solution)/shard_map/ppermute | solution.py:723
  27.1 16.1 %collective-permute-start.8 = (bf16[320,384]{1,0:T(8,128)(2,1)}, bf16[320,384]{1,0:T(8,128)(2,1)S(1)}, u32[]{:S(2)}, u32[]{:S(2)}) collective-permute-start(bf16[320,384]{1,0:T(8,128)(2,1)} %get-tuple-element.164.refs_0_), channel_id=1, source_target_pairs={{0,2},{1,3},{2,0},{3,1},{4,6},{5,7},{6,4},{7,5},{8,10},{9,11},{10,... | collective-permute-start | bytes 737288 | tf_op jit(solution)/shard_map/ppermute | solution.py:723
  28.9 14.3 %collective-permute-start.9 = (bf16[320,384]{1,0:T(8,128)(2,1)}, bf16[320,384]{1,0:T(8,128)(2,1)S(1)}, u32[]{:S(2)}, u32[]{:S(2)}) collective-permute-start(bf16[320,384]{1,0:T(8,128)(2,1)} %get-tuple-element.164.refs_0_), channel_id=1, source_target_pairs={{0,1},{1,0},{2,3},{3,2},{4,5},{5,4},{6,7},{7,6},{8,9},{9,8},{10,11... | collective-permute-start | bytes 737288 | tf_op jit(solution)/shard_map/ppermute | solution.py:723
  44.6 24.8 %collective-permute-start.17 = (bf16[704,1024]{1,0:T(8,128)(2,1)S(1)}, bf16[704,1024]{1,0:T(8,128)(2,1)S(1)}, u32[]{:S(2)}, u32[]{:S(2)}) collective-permute-start(bf16[704,1024]{1,0:T(8,128)(2,1)S(1)} %copy-done.2), channel_id=1, source_target_pairs={{0,1},{1,0},{2,3},{3,2},{4,5},{5,4},{6,7},{7,6},{8,9},{9,8},{10,11... | collective-permute-start | bytes 4325384 | tf_op jit(solution)/shard_map/ppermute | solution.py:723
  45.3 24.1 %collective-permute-start.13 = (bf16[128,2816]{1,0:T(8,128)(2,1)}, bf16[128,2816]{1,0:T(8,128)(2,1)}, u32[]{:S(2)}, u32[]{:S(2)}) collective-permute-start(bf16[128,2816]{1,0:T(8,128)(2,1)} %get-tuple-element.167), channel_id=1, source_target_pairs={{0,2},{1,3},{2,0},{3,1},{4,6},{5,7},{6,4},{7,5},{8,10},{9,11},{10,... | collective-permute-start | bytes 2162696 | tf_op jit(solution)/shard_map/ppermute | solution.py:723
  45.6 23.8 %collective-permute-start.16 = (bf16[128,2816]{1,0:T(8,128)(2,1)}, bf16[128,2816]{1,0:T(8,128)(2,1)}, u32[]{:S(2)}, u32[]{:S(2)}) collective-permute-start(bf16[128,2816]{1,0:T(8,128)(2,1)} %copy-done.12), channel_id=1, source_target_pairs={{0,1},{1,0},{2,3},{3,2},{4,5},{5,4},{6,7},{7,6},{8,9},{9,8},{10,11... | collective-permute-start | bytes 2162696 | tf_op jit(solution)/shard_map/ppermute | solution.py:723
  45.6 23.8 %collective-permute-start.15 = (bf16[128,2816]{1,0:T(8,128)(2,1)}, bf16[128,2816]{1,0:T(8,128)(2,1)}, u32[]{:S(2)}, u32[]{:S(2)}) collective-permute-start(bf16[128,2816]{1,0:T(8,128)(2,1)} %copy-done.12), channel_id=1, source_target_pairs={{0,4},{4,0},{8,12},{12,8},{16,20},{20,16},{24,28},{28,24},{1,5},{5... | collective-permute-start | bytes 2162696 | tf_op jit(solution)/shard_map/ppermute | solution.py:723
  47.4 22.1 %collective-permute-start.14 = (bf16[128,1024]{1,0:T(8,128)(2,1)}, bf16[128,1024]{1,0:T(8,128)(2,1)}, u32[]{:S(2)}, u32[]{:S(2)}) collective-permute-start(bf16[128,1024]{1,0:T(8,128)(2,1)} %constant_dynamic-slice_fusion.2), channel_id=1, source_target_pairs={{0,2},{1,3},{2,0},{3,1},{4,6},{5,7},{6,4},{7,5},{8,10},{9,11},{10,... | collective-permute-start | bytes 786440 | tf_op jit(solution)/shard_map/ppermute | solution.py:723
  69.6 18.8 %collective-permute-start.18 = (bf16[128,2816]{1,0:T(8,128)(2,1)}, bf16[128,2816]{1,0:T(8,128)(2,1)S(1)}, u32[]{:S(2)}, u32[]{:S(2)}) collective-permute-start(bf16[128,2816]{1,0:T(8,128)(2,1)} %collective-permute-done.13.refs_16_.refs_14_), channel_id=1, source_target_pairs={{0,8},{4,12},{8,0},{12,4},{16,24},{20,28},{24,16},{28,20},{1,9},{5... | collective-permute-start | bytes 2162696 | tf_op jit(solution)/shard_map/ppermute | solution.py:723
  71.2 18.5 %collective-permute-start.19 = (bf16[352,1024]{1,0:T(8,128)(2,1)}, bf16[352,1024]{1,0:T(8,128)(2,1)}, u32[]{:S(2)}, u32[]{:S(2)}) collective-permute-start(bf16[352,1024]{1,0:T(8,128)(2,1)} %constant_dynamic-slice_fusion.1), channel_id=1, source_target_pairs={{0,2},{1,3},{2,0},{3,1},{4,6},{5,7},{6,4},{7,5},{8,10},{9,11},{10,... | collective-permute-start | bytes 2162696 | tf_op jit(solution)/shard_map/ppermute | solution.py:723
  71.7 18.0 %collective-permute-start.22 = (bf16[128,2816]{1,0:T(8,128)(2,1)}, bf16[128,2816]{1,0:T(8,128)(2,1)}, u32[]{:S(2)}, u32[]{:S(2)}) collective-permute-start(bf16[128,2816]{1,0:T(8,128)(2,1)} %collective-permute-done.15.refs_11_.refs_9_), channel_id=1, source_target_pairs={{0,1},{1,0},{2,3},{3,2},{4,5},{5,4},{6,7},{7,6},{8,9},{9,8},{10,11... | collective-permute-start | bytes 2162696 | tf_op jit(solution)/shard_map/ppermute | solution.py:723
  93.6 19.4 %collective-permute-start.27 = (bf16[352,1024]{1,0:T(8,128)(2,1)}, bf16[352,1024]{1,0:T(8,128)(2,1)}, u32[]{:S(2)}, u32[]{:S(2)}) collective-permute-start(bf16[352,1024]{1,0:T(8,128)(2,1)} %collective-permute-done.19.refs_2_), channel_id=1, source_target_pairs={{0,1},{1,0},{2,3},{3,2},{4,5},{5,4},{6,7},{7,6},{8,9},{9,8},{10,11... | collective-permute-start | bytes 2162696 | tf_op jit(solution)/shard_map/ppermute | solution.py:723
  93.9 19.1 %collective-permute-start.26 = (bf16[352,1024]{1,0:T(8,128)(2,1)}, bf16[352,1024]{1,0:T(8,128)(2,1)}, u32[]{:S(2)}, u32[]{:S(2)}) collective-permute-start(bf16[352,1024]{1,0:T(8,128)(2,1)} %collective-permute-done.19.refs_2_), channel_id=1, source_target_pairs={{0,4},{4,0},{8,12},{12,8},{16,20},{20,16},{24,28},{28,24},{1,5},{5... | collective-permute-start | bytes 2162696 | tf_op jit(solution)/shard_map/ppermute | solution.py:723
  120.2 17.5 %collective-permute-start.29 = (bf16[2,704,1024]{2,1,0:T(8,128)(2,1)}, bf16[2,704,1024]{2,1,0:T(8,128)(2,1)S(1)}, u32[]{:S(2)}, u32[]{:S(2)}) collective-permute-start(bf16[2,704,1024]{2,1,0:T(8,128)(2,1)} %get-tuple-element.193), channel_id=1, source_target_pairs={{0,1},{1,0},{2,3},{3,2},{4,5},{5,4},{6,7},{7,6},{8,9},{9,8},{10,11... | collective-permute-start | bytes 8650760 | tf_op jit(solution)/shard_map/ppermute | solution.py:723
  137.7 40.0 %collective-permute-start.31 = (bf16[2,256,2816]{2,1,0:T(8,128)(2,1)}, bf16[2,256,2816]{2,1,0:T(8,128)(2,1)}, u32[]{:S(2)}, u32[]{:S(2)}) collective-permute-start(bf16[2,256,2816]{2,1,0:T(8,128)(2,1)} %get-tuple-element.207), channel_id=1, source_target_pairs={{0,1},{1,0},{2,3},{3,2},{4,5},{5,4},{6,7},{7,6},{8,9},{9,8},{10,11... | collective-permute-start | bytes 8650760 | tf_op jit(solution)/shard_map/ppermute | solution.py:723
  144.0 33.7 %collective-permute-start.30 = (bf16[704,1024]{1,0:T(8,128)(2,1)}, bf16[704,1024]{1,0:T(8,128)(2,1)S(1)}, u32[]{:S(2)}, u32[]{:S(2)}) collective-permute-start(bf16[704,1024]{1,0:T(8,128)(2,1)} %get-tuple-element.205), channel_id=1, source_target_pairs={{0,2},{1,3},{2,0},{3,1},{4,6},{5,7},{6,4},{7,5},{8,10},{9,11},{10,... | collective-permute-start | bytes 4325384 | tf_op jit(solution)/shard_map/ppermute | solution.py:723
  177.8 51.4 %collective-permute-start.35 = (bf16[2,256,2816]{2,1,0:T(8,128)(2,1)}, bf16[2,256,2816]{2,1,0:T(8,128)(2,1)}, u32[]{:S(2)}, u32[]{:S(2)}) collective-permute-start(bf16[2,256,2816]{2,1,0:T(8,128)(2,1)} %get-tuple-element.229), channel_id=1, source_target_pairs={{0,1},{1,0},{2,3},{3,2},{4,5},{5,4},{6,7},{7,6},{8,9},{9,8},{10,11... | collective-permute-start | bytes 8650760 | tf_op jit(solution)/shard_map/ppermute | solution.py:723
  183.9 45.2 %collective-permute-start.33 = (bf16[256,3840]{1,0:T(8,128)(2,1)}, bf16[256,3840]{1,0:T(8,128)(2,1)S(1)}, u32[]{:S(2)}, u32[]{:S(2)}) collective-permute-start(bf16[256,3840]{1,0:T(8,128)(2,1)} %get-tuple-element.224), channel_id=1, source_target_pairs={{0,2},{1,3},{2,0},{3,1},{4,6},{5,7},{6,4},{7,5},{8,10},{9,11},{10,... | collective-permute-start | bytes 5898248 | tf_op jit(solution)/shard_map/ppermute | solution.py:723
  190.8 18.0 %collective-permute-start.34 = (bf16[4,88,1024]{2,1,0:T(8,128)(2,1)}, bf16[4,88,1024]{2,1,0:T(8,128)(2,1)S(1)}, u32[]{:S(2)}, u32[]{:S(2)}) collective-permute-start(bf16[4,88,1024]{2,1,0:T(8,128)(2,1)} %get-tuple-element.227), channel_id=1, source_target_pairs={{0,4},{1,9},{2,6},{3,11},{4,0},{5,13},{6,2},{7,15},{8,12},{9,1},{1... | collective-permute-start | bytes 2162696 | tf_op jit(solution)/shard_map/ppermute | solution.py:937
  239.8 28.7 %collective-permute-start.40 = (bf16[4,32,3840]{2,1,0:T(8,128)(2,1)}, bf16[4,32,3840]{2,1,0:T(8,128)(2,1)S(1)}, u32[]{:S(2)}, u32[]{:S(2)}) collective-permute-start(bf16[4,32,3840]{2,1,0:T(8,128)(2,1)} %get-tuple-element.254), channel_id=1, source_target_pairs={{0,4},{1,9},{2,6},{3,11},{4,0},{5,13},{6,2},{7,15},{8,12},{9,1},{1... | collective-permute-start | bytes 2949128 | tf_op jit(solution)/shard_map/ppermute | solution.py:937
  253.5 37.1 %collective-permute-start.48 = (bf16[256,2816]{1,0:T(8,128)(2,1)}, bf16[256,2816]{1,0:T(8,128)(2,1)S(1)}, u32[]{:S(2)}, u32[]{:S(2)}) collective-permute-start(bf16[256,2816]{1,0:T(8,128)(2,1)} %get-tuple-element.273), channel_id=1, source_target_pairs={{0,2},{1,3},{2,0},{3,1},{4,6},{5,7},{6,4},{7,5},{8,10},{9,11},{10,... | collective-permute-start | bytes 4325384 | tf_op jit(solution)/shard_map/ppermute | solution.py:723
  268.5 16.7 %collective-permute-start.42 = (bf16[2,896,256]{2,1,0:T(8,128)(2,1)}, bf16[2,896,256]{2,1,0:T(8,128)(2,1)S(1)}, u32[]{:S(2)}, u32[]{:S(2)}) collective-permute-start(bf16[2,896,256]{2,1,0:T(8,128)(2,1)} %get-tuple-element.257), channel_id=1, source_target_pairs={{0,1},{1,0},{2,3},{3,2},{4,5},{5,4},{6,7},{7,6},{8,9},{9,8},{10,11... | collective-permute-start | bytes 2752520 | tf_op jit(solution)/shard_map/ppermute | solution.py:723
  272.2 12.9 %collective-permute-start.43 = (bf16[2,32,3840]{2,1,0:T(8,128)(2,1)}, bf16[2,32,3840]{2,1,0:T(8,128)(2,1)S(1)}, u32[]{:S(2)}, u32[]{:S(2)}) collective-permute-start(bf16[2,32,3840]{2,1,0:T(8,128)(2,1)} %get-tuple-element.261), channel_id=1, source_target_pairs={{0,8},{1,5},{2,10},{3,7},{4,12},{5,1},{6,14},{7,3},{8,0},{9,13},{1... | collective-permute-start | bytes 1474568 | tf_op jit(solution)/shard_map/ppermute | solution.py:937
  289.7 19.2 %collective-permute-start.47 = (bf16[4,88,1024]{2,1,0:T(8,128)(2,1)}, bf16[4,88,1024]{2,1,0:T(8,128)(2,1)S(1)}, u32[]{:S(2)}, u32[]{:S(2)}) collective-permute-start(bf16[4,88,1024]{2,1,0:T(8,128)(2,1)} %get-tuple-element.285.near), channel_id=1, source_target_pairs={{0,4},{1,9},{2,6},{3,11},{4,0},{5,13},{6,2},{7,15},{8,12},{9,1},{1... | collective-permute-start | bytes 2162696 | tf_op jit(solution)/shard_map/ppermute | solution.py:937
  328.6 15.4 %collective-permute-start.54 = (bf16[2,32,3840]{2,1,0:T(8,128)(2,1)}, bf16[2,32,3840]{2,1,0:T(8,128)(2,1)S(1)}, u32[]{:S(2)}, u32[]{:S(2)}) collective-permute-start(bf16[2,32,3840]{2,1,0:T(8,128)(2,1)} %get-tuple-element.297.refs_4_), channel_id=1, source_target_pairs={{0,8},{1,5},{2,10},{3,7},{4,12},{5,1},{6,14},{7,3},{8,0},{9,13},{1... | collective-permute-start | bytes 1474568 | tf_op jit(solution)/shard_map/ppermute | solution.py:937
  329.5 14.4 %collective-permute-start.53 = (bf16[4,112,256]{2,1,0:T(8,128)(2,1)}, bf16[4,112,256]{2,1,0:T(8,128)(2,1)S(1)}, u32[]{:S(2)}, u32[]{:S(2)}) collective-permute-start(bf16[4,112,256]{2,1,0:T(8,128)(2,1)} %get-tuple-element.294.refs_0_), channel_id=1, source_target_pairs={{0,8},{1,5},{2,10},{3,7},{4,12},{5,1},{6,14},{7,3},{8,0},{9,13},{1... | collective-permute-start | bytes 688136 | tf_op jit(solution)/shard_map/ppermute | solution.py:937
  347.4 16.5 %collective-permute-start.57 = (bf16[4,32,3840]{2,1,0:T(8,128)(2,1)}, bf16[4,32,3840]{2,1,0:T(8,128)(2,1)S(1)}, u32[]{:S(2)}, u32[]{:S(2)}) collective-permute-start(bf16[4,32,3840]{2,1,0:T(8,128)(2,1)} %get-tuple-element.305.near), channel_id=1, source_target_pairs={{0,4},{1,9},{2,6},{3,11},{4,0},{5,13},{6,2},{7,15},{8,12},{9,1},{1... | collective-permute-start | bytes 2949128 | tf_op jit(solution)/shard_map/ppermute | solution.py:937
  348.5 15.4 %collective-permute-start.56 = (bf16[4,112,256]{2,1,0:T(8,128)(2,1)}, bf16[4,112,256]{2,1,0:T(8,128)(2,1)S(1)}, u32[]{:S(2)}, u32[]{:S(2)}) collective-permute-start(bf16[4,112,256]{2,1,0:T(8,128)(2,1)} %get-tuple-element.301.refs_0_), channel_id=1, source_target_pairs={{0,16},{1,17},{2,18},{3,19},{4,20},{5,21},{6,22},{7,23},{8,24},{9,... | collective-permute-start | bytes 688136 | tf_op jit(solution)/shard_map/ppermute | solution.py:937
  350.5 13.4 %collective-permute-start.58 = (bf16[1,32,2816]{2,1,0:T(8,128)(2,1)}, bf16[1,32,2816]{2,1,0:T(8,128)(2,1)S(1)}, u32[]{:S(2)}, u32[]{:S(2)}) collective-permute-start(bf16[1,32,2816]{2,1,0:T(8,128)(2,1)} %get-tuple-element.302.refs_2_), channel_id=1, source_target_pairs={{0,16},{1,17},{2,18},{3,19},{4,20},{5,21},{6,22},{7,23},{8,24},{9,... | collective-permute-start | bytes 540680 | tf_op jit(solution)/shard_map/ppermute | solution.py:937
  (86 other events, 586.0 us)

commit v6 on v5

--- a/solution.py
+++ b/solution.py
@@ -395,7 +395,7 @@
     return gain_grad, scale * (grad_normed - normed * mean)
 
 
-def shard_products(me, left, right, pair, mover, pair_out):
+def shard_products(me, left, right, pair, mover, pair_out, base=0):
     copies = []
     count, rows, cols = pair[0].shape
     step = rows if rows <= 352 else rows // 2
@@ -407,7 +407,7 @@
                 lhs = left[pl.ds(pl.multiple_of(row + low, 16), step), :]
                 for at in range(0, cols, width):
                     pair[odd][j, low : low + step, at : at + width] = mm(
-                        lhs, right[:, at : at + width]
+                        lhs, right[:, base + at : base + at + width]
                     ).astype(bf16)
             copies.append(mover.start(pair[odd].at[j], pair_out[odd].at[j]))
     return copies
@@ -526,23 +526,30 @@
     )(offs, slope, lin, upstream, *w_down)
 
 
-def products_kernel(who, left, right, *refs):
-    outs, pair, sems = refs[0:2], refs[2:4], refs[4]
-    wait(shard_products(who[0], left, right, pair, Mover(sems), outs))
-
-
-def products(who, left, right, parts):
+def products_kernel(cuts, who, left, right, *refs):
+    outs, pairs, sems = refs[: 2 * len(cuts)], refs[2 * len(cuts) : -1], refs[-1]
+    mover = Mover(sems)
+    done, base = [], 0
+    for i, cut in enumerate(cuts):
+        mine = slice(2 * i, 2 * i + 2)
+        done += shard_products(who[0], left, right, pairs[mine], mover, outs[mine], base)
+        base += cut
+    wait(done)
+
+
+def products(who, left, right, parts, cuts=None):
     width, rows = left.shape
-    inner = right.shape[1]
-    pair = (parts // 2, width // parts, inner)
+    cuts = cuts or (right.shape[1],)
+    shapes = [(parts // 2, width // parts, cut) for cut in cuts for _ in range(2)]
     return pl.pallas_call(
-        products_kernel,
-        out_shape=[like(*pair)] * 2,
+        functools.partial(products_kernel, cuts),
+        out_shape=[like(*shape) for shape in shapes],
         in_specs=[smem()] + [vmem()] * 2,
-        out_specs=[anywhere()] * 2,
-        scratch_shapes=[scratch(*pair)] * 2 + [pltpu.SemaphoreType.DMA((parts,))],
+        out_specs=[anywhere()] * len(shapes),
+        scratch_shapes=[scratch(*shape) for shape in shapes]
+        + [pltpu.SemaphoreType.DMA((parts * len(cuts),))],
         compiler_params=params(),
-        cost_estimate=cost(2 * rows * width * inner, 2 * inner * (width + rows)),
+        cost_estimate=cost(1, 1),
         name="products",
     )(who, left, right)
 
@@ -773,44 +780,38 @@
     )(*terms)
 
 
-def halve_kernel(place, keep_one, keep_two, send_one, send_two, keep, send):
-    keep[...] = total(keep_one[...], keep_two[...])
-    send[...] = total(send_one[...], send_two[...])
+def eighths(value):
+    return value.reshape(8, value.shape[0] // 8, value.shape[1])
+
+
+def halve_body(place, one, two, keep, send):
+    for i in range(4):
+        at = place[0] ^ ((i >> 1) * place[2]) ^ ((i & 1) * place[3])
+        keep[i] = total(one[at], two[at])
+        send[i] = total(one[at ^ place[1]], two[at ^ place[1]])
 
 
 def halve(place, one, two):
-    rows, cols = one.shape[0] // 8, one.shape[1]
-    one, two = (v.reshape(8, rows, cols) for v in (one, two))
-
-    def piece(flip):
-        def index(i, place):
-            at = place[0] ^ ((i >> 1) * place[2]) ^ ((i & 1) * place[3])
-            return (at ^ place[1] if flip else at, 0, 0)
-
-        return pl.BlockSpec((1, rows, cols), index)
-
-    out = pl.BlockSpec((1, rows, cols), lambda i, place: (i, 0, 0))
+    one, two = eighths(one), eighths(two)
     return pl.pallas_call(
-        halve_kernel,
-        grid_spec=pltpu.PrefetchScalarGridSpec(
-            num_scalar_prefetch=1,
-            grid=(4,),
-            in_specs=[piece(False)] * 2 + [piece(True)] * 2,
-            out_specs=[out] * 2,
-        ),
-        out_shape=[like(4, rows, cols)] * 2,
+        halve_body,
+        out_shape=[like(4, *one.shape[1:])] * 2,
+        in_specs=[smem()] + [vmem()] * 2,
+        out_specs=[vmem()] * 2,
         compiler_params=params(),
         cost_estimate=cost(1, 1),
         name="halve",
-    )(place, one, two, one, two)
-
-
-def batch_kernel(tasks, *refs):
+    )(place, one, two)
+
+
+def batch_kernel(tasks, place, *refs):
     ins, outs = refs[: 2 * len(tasks)], list(refs[2 * len(tasks) :])
     for i, (kind, flip) in enumerate(tasks):
         one, two = ins[2 * i : 2 * i + 2]
         out = outs.pop(0)
-        if kind == "split":
+        if kind == "halve":
+            halve_body(place, one, two, out, outs.pop(0))
+        elif kind == "split":
             half = out.shape[0]
             out[...] = total(one[:half], two[:half])
             outs.pop(0)[...] = total(one[half:], two[half:])
@@ -828,11 +829,12 @@
             out[...] = total(one[...], two[...])
 
 
-def batch(tasks):
+def batch(place, tasks):
     shapes, counts = [], []
     for kind, _, one, _ in tasks:
         first, rest = one.shape[0], one.shape[1:]
         got = {
+            "halve": [(first // 2,) + rest] * 2,
             "split": [(first // 2,) + rest] * 2,
             "pair": [rest] * 2,
             "join": [(2 * first,) + rest],
@@ -843,12 +845,12 @@
     outs = pl.pallas_call(
         functools.partial(batch_kernel, [task[:2] for task in tasks]),
         out_shape=[like(*shape) for shape in shapes],
-        in_specs=[vmem()] * (2 * len(tasks)),
+        in_specs=[smem()] + [vmem()] * (2 * len(tasks)),
         out_specs=[vmem()] * len(shapes),
         compiler_params=params(),
         cost_estimate=cost(1, 1),
         name="batch",
-    )(*[value for task in tasks for value in task[2:]])
+    )(place, *[value for task in tasks for value in task[2:]])
     groups = []
     for count in counts:
         groups.append(outs[:count])
@@ -899,7 +901,7 @@
         self.tasks.append(((kind, flip, self.free(one), two), then))
 
     def flush(self):
-        groups = batch([task for task, _ in self.tasks])
+        groups = batch(self.place, [task for task, _ in self.tasks])
         for (_, then), group in zip(self.tasks, groups):
             then(*group)
         self.tasks = []
@@ -942,7 +944,7 @@
         self.order, self.place, self.pairs = order, place, pairs
 
     def core(self):
-        send = [after(pair[1], *self.order.before) for pair in self.pairs]
+        send = [pair[1] if len(self.pairs) > 1 else after(pair[1], *self.order.before) for pair in self.pairs]
         self.got = [partner(value, "grp", 1) for value in send]
 
     def add_core(self):
@@ -956,13 +958,15 @@
     def go(self, step):
         self.got = along(self.order.free(self.other), step)
 
-    def fold(self, step, start=True):
+    def fold(self, step, start=True, alone=True):
         def then(mine, other):
             self.mine, self.other = mine, other
             if start:
                 self.got = along(other, step)
 
-        if step == 0:
+        if step == 0 and not alone:
+            self.order.add("halve", 0, eighths(self.mine), eighths(self.got), then)
+        elif step == 0:
             then(*halve(self.place, self.order.now(self.mine), self.got))
             self.order.ran(self.other)
         else:
@@ -1126,6 +1130,7 @@
         odd = me % 2
         place = jnp.stack([lax.axis_index("rep"), 1 + odd, 2 - odd, jnp.full_like(odd, 4)])
         place = place.astype(jnp.int32)
+        order.place = place
         chunk = functools.partial(Chunk, order, place)
         down_y = rep(down_x, 1)
         down_xc = grp(down_x, 1)
@@ -1141,11 +1146,14 @@
         order.phase(down_yc, down.pairs[0][0])
         down.core()
         dgate, dup = slopes(by_down, order.now(upstream), w_down, slope, lin)
-        up = chunk(products(info, hid_two, dup, parts))
-
-        order.phase(*down.got, up.pairs[0][0])
+
+        order.phase(*down.got, dgate)
         down.add_core()
         down.cross()
+        third = 1024
+        cuts = (third, third, up_weight.shape[1] - 2 * third)
+        terms = products(info, order.free(hid_two), dup, parts, cuts)
+        up = chunk(*[terms[i : i + 2] for i in range(0, 6, 2)])
         up.core()
         dmid, fgain, dmix, *out_pair = middle_grads(
             offs_feed, info, order.free(upstream), gains[1:2], mixed, w_out, w_gate, w_up,
@@ -1154,7 +1162,7 @@
         out = chunk(out_pair)
         out.core()
         gate = chunk(products(info, after(hid_two, dmix), dgate, parts))
-        part = 3
+        part = 1
         state = attend_back(info, fac, kv, after(dmix, gate.pairs[0][0]), lse, 0, part, ())
 
         order.phase(down.got, *up.got, *out.got, state[0])
@@ -1207,7 +1215,7 @@
         gate.fold(0)
 
         order.phase(factor.got, both.got, down.got, gate.got)
-        factor.fold(0)
+        factor.fold(0, alone=False)
         gate.fold(1)
         both.swap(2)
         order.flush()

time: 404 us -> 399 us (0.988)
  Pallas kernels: 188 us -> 180 us
  starting transfers between devices: 53.1 us -> 59 us
  waiting for transfers between devices: 126 us -> 121 us
    pallas_call x7 -> x6, Pallas kernels: 37.1 us -> 28.7 us  [the longest x3 18.5 us: products(): pl.pallas_call(functools.partial(products_kernel, cuts), out_shape=[like(...]
    ppermute x40 -> x42, waiting for transfers between devices: 72.2 us -> 67.3 us  [partner(): return lax.ppermute(values, axis, [(i, i ^ flip) for i in range(size)])]
    ppermute x40 -> x42, starting transfers between devices: 24.3 us -> 28.6 us  [partner(): return lax.ppermute(values, axis, [(i, i ^ flip) for i in range(size)])]
    unnamed x112 -> x110, local copies, waits for them, and re-layouts: 13 us -> 13.9 us
  transfers between devices with their start and end apart: 62 -> 64, of which waited for: 22 -> 22; matrix products, arithmetic and copies ran while one was open for 4% -> 4% of each run, Pallas kernels for 43% -> 41%
where the time goes in v6:
time: 399 us; the launch traced here: 391 us
  Pallas kernels  180 us (45%)
  waiting for transfers between devices  121 us (30%)
  starting transfers between devices  59 us (15%)
  local copies, waits for them, and re-layouts  27.7 us (7%)
    ppermute x42, waiting for transfers between devices, partner(): return lax.ppermute(values, axis, [(i, i ^ flip) for i in range(size)])  67.3 us
    ppermute x22, waiting for transfers between devices, along(): return lax.ppermute(values, ('rep', 'grp'), pairs)  53.5 us
    ppermute x22, starting transfers between devices, along(): return lax.ppermute(values, ('rep', 'grp'), pairs)  30.4 us
    ppermute x42, starting transfers between devices, partner(): return lax.ppermute(values, axis, [(i, i ^ flip) for i in range(size)])  28.6 us
    pallas_call x10, Pallas kernels, batch(): pl.pallas_call(functools.partial(batch_kernel, [task[:2] for task in task...  26.5 us
    pallas_call x2, Pallas kernels, attend_back(): pl.pallas_call(functools.partial(attend_back_kernel, first, heads, final,...  23.3 us
    pallas_call x3, Pallas kernels, products(): pl.pallas_call(functools.partial(products_kernel, cuts), out_shape=[like(...  18.5 us
    pallas_call x3, Pallas kernels, add_pairs(): pl.pallas_call(add_pairs_kernel, grid=(steps,), out_shape=[like(rows, wid...  15.6 us
  transfers between devices with their start and end apart: 64, of which 22 were waited for; matrix products, arithmetic and copies ran while one was open for 4% of the time, Pallas kernels for 41%

profile of v6, /device:TPU:0, one launch (start us, length us, event | category | flops | bytes accessed | tf_op | source)
XLA Modules:
  0.0 391.4 jit_solution(11617861280949714906)
XLA Ops:
  10.9 6.9 %collective-permute-done.refs_2_ = bf16[800,256]{1,0:T(8,128)(2,1)} collective-permute-done((bf16[800,256]{1,0:T(8,128)(2,1)}, bf16[800,256]{1,0:T(8,128)(2,1)}, u32[]{:S(2)}, u32[]{:S(2)}) %collective-permute-start) | collective-permute-done | bytes 409632 | tf_op jit(solution)/shard_map/ppermute | solution.py:730
  22.5 4.7 %front.1 = (bf16[480,384]{1,0:T(8,128)(2,1)}, bf16[320,384]{1,0:T(8,128)(2,1)}, bf16[1024,384]{1,0:T(8,128)(2,1)}, f32[8,1024]{1,0:T(8,128)}) custom-call(s32[8]{0:T(128)} %stack.119.offs, bf16[384,1024]{1,0:T(8,128)(2,1)} %bitcast.42, f32[32,384]{1,0:T(8,128)} %get-tuple-element.324.cos_ref, f32[32,384]{1,0:T(8,128)} %get-tuple-element.323.sin_ref, ...), custom_call_target="tpu_custom_call" | custom-call | flops 6291 | bytes 48 | tf_op jit(solution)/shard_map/front/pallas_call | solution.py:95
  29.0 14.2 %collective-permute-done.8.refs_2_ = bf16[320,384]{1,0:T(8,128)(2,1)S(1)} collective-permute-done((bf16[320,384]{1,0:T(8,128)(2,1)}, bf16[320,384]{1,0:T(8,128)(2,1)S(1)}, u32[]{:S(2)}, u32[]{:S(2)}) %collective-permute-start.8) | collective-permute-done | bytes 245792 | tf_op jit(solution)/shard_map/ppermute | solution.py:730
  49.8 7.5 %attend.2 = (bf16[512,384]{1,0:T(8,128)(2,1)}, f32[8,384]{1,0:T(8,128)}) custom-call(s32[3]{0:T(128)} %pad_add_fusion.info_ref.who, bf16[480,384]{1,0:T(8,128)(2,1)} %get-tuple-element.182.fac_ref, bf16[320,384]{1,0:T(8,128)(2,1)} %get-tuple-element.168.refs_0_, bf16[320,384]{1,0:T(8,128)(2,1)} %copy-done.6, bf16[320,384]{1,0:T(8,128)(2,1)} %copy-done.5, ...), custom_call_target="tpu_custom_call" | custom-call | flops 289910 | bytes 19 | tf_op jit(solution)/shard_map/attend/pallas_call | solution.py:211
  57.3 12.6 %collective-permute-done.14.refs_4_.refs_2_ = bf16[128,1024]{1,0:T(8,128)(2,1)} collective-permute-done((bf16[128,1024]{1,0:T(8,128)(2,1)}, bf16[128,1024]{1,0:T(8,128)(2,1)}, u32[]{:S(2)}, u32[]{:S(2)}) %collective-permute-start.14) | collective-permute-done | bytes 262176 | tf_op jit(solution)/shard_map/ppermute | solution.py:730
  73.7 7.7 %attend.3 = (bf16[512,384]{1,0:T(8,128)(2,1)}, f32[8,384]{1,0:T(8,128)}) custom-call(s32[3]{0:T(128)} %pad_add_fusion.info_ref.who, bf16[480,384]{1,0:T(8,128)(2,1)} %get-tuple-element.182.fac_ref, bf16[320,384]{1,0:T(8,128)(2,1)} %get-tuple-element.168.refs_0_, bf16[320,384]{1,0:T(8,128)(2,1)} %copy-done.6, bf16[320,384]{1,0:T(8,128)(2,1)} %copy-done.5, ...), custom_call_target="tpu_custom_call" | custom-call | flops 289910 | bytes 19 | tf_op jit(solution)/shard_map/attend/pallas_call | solution.py:211
  81.4 7.4 %collective-permute-done.18.refs_17_.refs_15_ = bf16[128,2816]{1,0:T(8,128)(2,1)S(1)} collective-permute-done((bf16[128,2816]{1,0:T(8,128)(2,1)}, bf16[128,2816]{1,0:T(8,128)(2,1)S(1)}, u32[]{:S(2)}, u32[]{:S(2)}) %collective-permute-start.18) | collective-permute-done | bytes 720928 | tf_op jit(solution)/shard_map/ppermute | solution.py:730
  98.0 15.5 %feed.1 = (f32[384,1024]{1,0:T(8,128)}, bf16[1024,384]{1,0:T(8,128)(2,1)}, bf16[384,2816]{1,0:T(8,128)(2,1)}, bf16[384,2816]{1,0:T(8,128)(2,1)}, bf16[384,2816]{1,0:T(8,128)(2,1)}, /*index=5*/bf16[2816,384]{1,0:T(8,128)(2,1)}) custom-call(s32[24]{0:T(128)} %concatenate.3.offs, bf16[384,1024]{1,0:T(8,128)(2,1)} %bitcast.43, ...), custom_call_target="tpu_custom_call" | custom-call | flops 74490 | bytes 237 | tf_op jit(solution)/shard_map/feed/pallas_call | solution.py:461
  113.6 6.2 %products.3 = (bf16[2,704,1024]{2,1,0:T(8,128)(2,1)}, bf16[2,704,1024]{2,1,0:T(8,128)(2,1)}) custom-call(s32[3]{0:T(128)} %pad_add_fusion.info_ref.who, bf16[2816,384]{1,0:T(8,128)(2,1)} %get-tuple-element.193.left, bf16[384,1024]{1,0:T(8,128)(2,1)} %bitcast.45), custom_call_target="tpu_custom_call" | custom-call | tf_op jit(solution)/shard_map/products/pallas_call | solution.py:544
  121.8 9.9 %slopes.1 = (bf16[384,2816]{1,0:T(8,128)(2,1)}, bf16[384,2816]{1,0:T(8,128)(2,1)}) custom-call(s32[12]{0:T(128)} %stack.103.offs, bf16[384,2816]{1,0:T(8,128)(2,1)} %get-tuple-element.198.slope_ref, bf16[384,2816]{1,0:T(8,128)(2,1)} %get-tuple-element.199.lin_ref, bf16[384,1024]{1,0:T(8,128)(2,1)} %bitcast.46, bf16[704,1024]{1,0:T(8,128)(2,1)} %refs_0_.5, ...), custom_call_target="tpu_custom_call" | custom-call | flops 22145 | bytes 144 | tf_op jit(solution)/shard_map/slopes/pallas_call | solution.py:512
  133.3 5.1 %add_pairs.3 = (bf16[704,1024]{1,0:T(8,128)(2,1)}, bf16[704,1024]{1,0:T(8,128)(2,1)}) custom-call(bf16[2,704,1024]{2,1,0:T(8,128)(2,1)} %get-tuple-element.205.refs_0_, bf16[2,704,1024]{2,1,0:T(8,128)(2,1)} %copy-done.13), custom_call_target="tpu_custom_call" | custom-call | tf_op jit(solution)/shard_map/add_pairs/pallas_call | solution.py:771
  139.9 13.7 %middle_grads.1 = (f32[384,1024]{1,0:T(8,128)}, f32[8,1024]{1,0:T(8,128)}, bf16[1024,384]{1,0:T(8,128)(2,1)}, bf16[2,256,1024]{2,1,0:T(8,128)(2,1)}, bf16[2,256,1024]{2,1,0:T(8,128)(2,1)}) custom-call(s32[24]{0:T(128)} %concatenate.3.offs, s32[3]{0:T(128)} %pad_add_fusion.info_ref.who, bf16[384,1024]{1,0:T(8,128)(2,1)} %bitcast.47, ...), custom_call_target="tpu_custom_call" | custom-call | flops 52344 | bytes 158 | tf_op jit(solution)/shard_map/middle_grads/pallas_call | solution.py:605
  153.7 5.9 %products.4 = (bf16[2,256,1024]{2,1,0:T(8,128)(2,1)}, bf16[2,256,1024]{2,1,0:T(8,128)(2,1)}, bf16[2,256,1024]{2,1,0:T(8,128)(2,1)}, bf16[2,256,1024]{2,1,0:T(8,1...) custom-call(s32[3]{0:T(128)} %pad_add_fusion.info_ref.who, ...), custom_call_target="tpu_custom_call" | custom-call | tf_op jit(solution)/shard_map/products/pallas_call | solution.py:544
  160.7 6.4 %products.5 = (bf16[2,256,2816]{2,1,0:T(8,128)(2,1)}, bf16[2,256,2816]{2,1,0:T(8,128)(2,1)}) custom-call(s32[3]{0:T(128)} %pad_add_fusion.info_ref.who, bf16[1024,384]{1,0:T(8,128)(2,1)} %get-tuple-element.215.left, bf16[384,2816]{1,0:T(8,128)(2,1)} %get-tuple-element.201.refs_20_.right), custom_call_target="tpu_custom_call" | custom-call | tf_op jit(solution)/shard_map/products/pallas_call | solution.py:544
  167.1 4.4 %attend_back.2 = (f32[480,384]{1,0:T(8,128)}, f32[4,320,384]{2,1,0:T(8,128)}) custom-call(s32[3]{0:T(128)} %pad_add_fusion.info_ref.who, bf16[480,384]{1,0:T(8,128)(2,1)} %get-tuple-element.182.fac_ref, bf16[1024,384]{1,0:T(8,128)(2,1)} %get-tuple-element.221.grad_ref, bf16[320,384]{1,0:T(8,128)(2,1)} %get-tuple-element.168.refs_0_, ...), custom_call_target="tpu_custom_call" | custom-call | flops 1 | bytes 39 | tf_op jit(solution)/shard_map/attend_back/pallas_call | solution.py:312
  174.1 5.7 %add_pairs.4 = (bf16[256,3840]{1,0:T(8,128)(2,1)}, bf16[256,3840]{1,0:T(8,128)(2,1)}) custom-call(bf16[2,256,1024]{2,1,0:T(8,128)(2,1)} %get-tuple-element.227.refs_0_, bf16[2,256,1024]{2,1,0:T(8,128)(2,1)} %copy-done.23, bf16[2,256,1024]{2,1,0:T(8,128)(2,1)} %get-tuple-element.228.refs_2_, bf16[2,256,1024]{2,1,0:T(8,128)(2,1)} %collective-permute-done.32.refs_3_, ...), custom_call_target="tpu_custom_call" | custom-call | tf_op jit(solution)/shard_map/add_pairs/pallas_call | solution.py:771
  185.8 18.9 %attend_back.3 = (f32[480,384]{1,0:T(8,128)}, bf16[2,320,384]{2,1,0:T(8,128)(2,1)}, bf16[2,320,384]{2,1,0:T(8,128)(2,1)}) custom-call(s32[3]{0:T(128)} %pad_add_fusion.info_ref.who, bf16[480,384]{1,0:T(8,128)(2,1)} %get-tuple-element.182.fac_ref, bf16[1024,384]{1,0:T(8,128)(2,1)} %get-tuple-element.221.grad_ref, ...), custom_call_target="tpu_custom_call" | custom-call | flops 22 | bytes 39 | tf_op jit(solution)/shard_map/attend_back/pallas_call | solution.py:312
  204.7 20.2 %collective-permute-done.35 = bf16[256,3840]{1,0:T(8,128)(2,1)} collective-permute-done((bf16[256,3840]{1,0:T(8,128)(2,1)}, bf16[256,3840]{1,0:T(8,128)(2,1)}, u32[]{:S(2)}, u32[]{:S(2)}) %collective-permute-start.35) | collective-permute-done | bytes 1966112 | tf_op jit(solution)/shard_map/ppermute | solution.py:730
  224.9 3.3 batch.10
  228.6 3.8 halve.4
  232.4 3.4 collective-permute-done.39.refs_3_
  239.3 3.7 collective-permute-start.40
  245.7 4.7 %add_pairs.5 = (bf16[256,2816]{1,0:T(8,128)(2,1)}, bf16[256,2816]{1,0:T(8,128)(2,1)}) custom-call(bf16[2,256,2816]{2,1,0:T(8,128)(2,1)} %get-tuple-element.251.refs_0_, bf16[2,256,2816]{2,1,0:T(8,128)(2,1)} %copy-done.12), custom_call_target="tpu_custom_call" | custom-call | tf_op jit(solution)/shard_map/add_pairs/pallas_call | solution.py:771
  256.5 7.1 %tail.1 = (f32[384,1024]{1,0:T(8,128)}, bf16[2,896,256]{2,1,0:T(8,128)(2,1)}, bf16[2,896,256]{2,1,0:T(8,128)(2,1)}) custom-call(s32[8]{0:T(128)} %stack.119.offs, s32[3]{0:T(128)} %pad_add_fusion.info_ref.who, f32[480,384]{1,0:T(8,128)} %get-tuple-element.223.dq_ref, bf16[320,384]{1,0:T(8,128)(2,1)} %get-tuple-element.256.own_ref, ...), custom_call_target="tpu_custom_call" | custom-call | flops 12582 | bytes 79 | tf_op jit(solution)/shard_map/tail/pallas_call | solution.py:711
  271.6 10.9 %collective-permute-done.46.refs_5_ = bf16[2,88,1024]{2,1,0:T(8,128)(2,1)S(1)} collective-permute-done((bf16[2,88,1024]{2,1,0:T(8,128)(2,1)}, bf16[2,88,1024]{2,1,0:T(8,128)(2,1)S(1)}, u32[]{:S(2)}, u32[]{:S(2)}) %collective-permute-start.46) | collective-permute-done | bytes 360480 | tf_op jit(solution)/shard_map/ppermute | solution.py:939
  283.7 3.4 batch.14
  296.7 8.7 %collective-permute-done.48.refs_5_ = bf16[1,32,3840]{2,1,0:T(8,128)(2,1)S(1)} collective-permute-done((bf16[1,32,3840]{2,1,0:T(8,128)(2,1)S(1)}, bf16[1,32,3840]{2,1,0:T(8,128)(2,1)S(1)}, u32[]{:S(2)}, u32[]{:S(2)}) %collective-permute-start.48) | collective-permute-done | bytes 245792 | tf_op jit(solution)/shard_map/ppermute | solution.py:939
  319.0 4.4 %collective-permute-done.52.refs_1_ = bf16[4,112,256]{2,1,0:T(8,128)(2,1)S(1)} collective-permute-done((bf16[4,112,256]{2,1,0:T(8,128)(2,1)}, bf16[4,112,256]{2,1,0:T(8,128)(2,1)S(1)}, u32[]{:S(2)}, u32[]{:S(2)}) %collective-permute-start.52) | collective-permute-done | bytes 229408 | tf_op jit(solution)/shard_map/ppermute | solution.py:939
  331.2 9.8 %collective-permute-done.57.refs_3_ = bf16[1,32,2816]{2,1,0:T(8,128)(2,1)S(1)} collective-permute-done((bf16[1,32,2816]{2,1,0:T(8,128)(2,1)}, bf16[1,32,2816]{2,1,0:T(8,128)(2,1)S(1)}, u32[]{:S(2)}, u32[]{:S(2)}) %collective-permute-start.57) | collective-permute-done | bytes 180256 | tf_op jit(solution)/shard_map/ppermute | solution.py:939
  349.5 8.0 %output.1 = bf16[384,1024]{1,0:T(8,128)(2,1)} custom-call(s32[12]{0:T(128)} %stack.103.offs, bf16[384,2816]{1,0:T(8,128)(2,1)} %get-tuple-element.301.act_ref, f32[384,1024]{1,0:T(8,128)} %get-tuple-element.192.refs_22_.mid_ref, bf16[704,1024]{1,0:T(8,128)(2,1)} %refs_0_.5, bf16[704,1024]{1,0:T(8,128)(2,1)} %copy-done.4, ...), custom_call_target="tpu_custom_call" | custom-call | flops 22145 | bytes 79 | tf_op jit(solution)/shard_map/output/pallas_call | solution.py:656
  366.8 3.7 finish.5
  381.7 5.6 %collective-permute-done.63.far = bf16[4,32,2816]{2,1,0:T(8,128)(2,1)S(1)} collective-permute-done((bf16[4,32,2816]{2,1,0:T(8,128)(2,1)}, bf16[4,32,2816]{2,1,0:T(8,128)(2,1)S(1)}, u32[]{:S(2)}, u32[]{:S(2)}) %collective-permute-start.63) | collective-permute-done | bytes 720928 | tf_op jit(solution)/shard_map/ppermute | solution.py:939
  (257 shorter events, 136.1 us)
Async XLA Ops:
  0.7 17.1 %collective-permute-start.4 = (bf16[256,2816]{1,0:T(8,128)(2,1)}, bf16[256,2816]{1,0:T(8,128)(2,1)}, u32[]{:S(2)}, u32[]{:S(2)}) collective-permute-start(bf16[256,2816]{1,0:T(8,128)(2,1)} %refs_6_.1), channel_id=1, source_target_pairs={{0,1},{1,0},{2,3},{3,2},{4,5},{5,4},{6,7},{7,6},{8,9},{9,8},{10,11... | collective-permute-start | bytes 4325384 | tf_op jit(solution)/shard_map/ppermute | solution.py:730
  17.8 27.6 %collective-permute-start.11 = (bf16[256,2816]{1,0:T(8,128)(2,1)}, bf16[256,2816]{1,0:T(8,128)(2,1)}, u32[]{:S(2)}, u32[]{:S(2)}) collective-permute-start(bf16[256,2816]{1,0:T(8,128)(2,1)} %refs_12_.1), channel_id=1, source_target_pairs={{0,1},{1,0},{2,3},{3,2},{4,5},{5,4},{6,7},{7,6},{8,9},{9,8},{10,11... | collective-permute-start | bytes 4325384 | tf_op jit(solution)/shard_map/ppermute | solution.py:730
  19.6 23.6 %collective-permute-start.5 = (bf16[128,2816]{1,0:T(8,128)(2,1)}, bf16[128,2816]{1,0:T(8,128)(2,1)}, u32[]{:S(2)}, u32[]{:S(2)}) collective-permute-start(bf16[128,2816]{1,0:T(8,128)(2,1)} %get-tuple-element.164), channel_id=1, source_target_pairs={{0,2},{1,3},{2,0},{3,1},{4,6},{5,7},{6,4},{7,5},{8,10},{9,11},{10,... | collective-permute-start | bytes 2162696 | tf_op jit(solution)/shard_map/ppermute | solution.py:730
  19.9 23.3 %collective-permute-start.12 = (bf16[256,1024]{1,0:T(8,128)(2,1)S(1)}, bf16[256,1024]{1,0:T(8,128)(2,1)S(1)}, u32[]{:S(2)}, u32[]{:S(2)}) collective-permute-start(bf16[256,1024]{1,0:T(8,128)(2,1)S(1)} %copy-done.8), channel_id=1, source_target_pairs={{0,1},{1,0},{2,3},{3,2},{4,5},{5,4},{6,7},{7,6},{8,9},{9,8},{10,11... | collective-permute-start | bytes 1572872 | tf_op jit(solution)/shard_map/ppermute | solution.py:730
  27.2 16.0 %collective-permute-start.8 = (bf16[320,384]{1,0:T(8,128)(2,1)}, bf16[320,384]{1,0:T(8,128)(2,1)S(1)}, u32[]{:S(2)}, u32[]{:S(2)}) collective-permute-start(bf16[320,384]{1,0:T(8,128)(2,1)} %get-tuple-element.168.refs_0_), channel_id=1, source_target_pairs={{0,2},{1,3},{2,0},{3,1},{4,6},{5,7},{6,4},{7,5},{8,10},{9,11},{10,... | collective-permute-start | bytes 737288 | tf_op jit(solution)/shard_map/ppermute | solution.py:730
  29.0 14.2 %collective-permute-start.9 = (bf16[320,384]{1,0:T(8,128)(2,1)}, bf16[320,384]{1,0:T(8,128)(2,1)S(1)}, u32[]{:S(2)}, u32[]{:S(2)}) collective-permute-start(bf16[320,384]{1,0:T(8,128)(2,1)} %get-tuple-element.168.refs_0_), channel_id=1, source_target_pairs={{0,1},{1,0},{2,3},{3,2},{4,5},{5,4},{6,7},{7,6},{8,9},{9,8},{10,11... | collective-permute-start | bytes 737288 | tf_op jit(solution)/shard_map/ppermute | solution.py:730
  45.4 24.5 %collective-permute-start.17 = (bf16[704,1024]{1,0:T(8,128)(2,1)S(1)}, bf16[704,1024]{1,0:T(8,128)(2,1)S(1)}, u32[]{:S(2)}, u32[]{:S(2)}) collective-permute-start(bf16[704,1024]{1,0:T(8,128)(2,1)S(1)} %copy-done.2), channel_id=1, source_target_pairs={{0,1},{1,0},{2,3},{3,2},{4,5},{5,4},{6,7},{7,6},{8,9},{9,8},{10,11... | collective-permute-start | bytes 4325384 | tf_op jit(solution)/shard_map/ppermute | solution.py:730
  45.6 24.4 %collective-permute-start.13 = (bf16[128,2816]{1,0:T(8,128)(2,1)}, bf16[128,2816]{1,0:T(8,128)(2,1)}, u32[]{:S(2)}, u32[]{:S(2)}) collective-permute-start(bf16[128,2816]{1,0:T(8,128)(2,1)} %get-tuple-element.171), channel_id=1, source_target_pairs={{0,2},{1,3},{2,0},{3,1},{4,6},{5,7},{6,4},{7,5},{8,10},{9,11},{10,... | collective-permute-start | bytes 2162696 | tf_op jit(solution)/shard_map/ppermute | solution.py:730
  45.9 24.1 %collective-permute-start.16 = (bf16[128,2816]{1,0:T(8,128)(2,1)}, bf16[128,2816]{1,0:T(8,128)(2,1)}, u32[]{:S(2)}, u32[]{:S(2)}) collective-permute-start(bf16[128,2816]{1,0:T(8,128)(2,1)} %collective-permute-done.5.refs_10_.refs_8_), channel_id=1, source_target_pairs={{0,1},{1,0},{2,3},{3,2},{4,5},{5,4},{6,7},{7,6},{8,9},{9,8},{10,11... | collective-permute-start | bytes 2162696 | tf_op jit(solution)/shard_map/ppermute | solution.py:730
  46.0 24.0 %collective-permute-start.15 = (bf16[128,2816]{1,0:T(8,128)(2,1)}, bf16[128,2816]{1,0:T(8,128)(2,1)}, u32[]{:S(2)}, u32[]{:S(2)}) collective-permute-start(bf16[128,2816]{1,0:T(8,128)(2,1)} %collective-permute-done.5.refs_10_.refs_8_), channel_id=1, source_target_pairs={{0,4},{4,0},{8,12},{12,8},{16,20},{20,16},{24,28},{28,24},{1,5},{5... | collective-permute-start | bytes 2162696 | tf_op jit(solution)/shard_map/ppermute | solution.py:730
  47.7 22.2 %collective-permute-start.14 = (bf16[128,1024]{1,0:T(8,128)(2,1)}, bf16[128,1024]{1,0:T(8,128)(2,1)}, u32[]{:S(2)}, u32[]{:S(2)}) collective-permute-start(bf16[128,1024]{1,0:T(8,128)(2,1)} %constant_dynamic-slice_fusion.2), channel_id=1, source_target_pairs={{0,2},{1,3},{2,0},{3,1},{4,6},{5,7},{6,4},{7,5},{8,10},{9,11},{10,... | collective-permute-start | bytes 786440 | tf_op jit(solution)/shard_map/ppermute | solution.py:730
  70.0 18.8 %collective-permute-start.18 = (bf16[128,2816]{1,0:T(8,128)(2,1)}, bf16[128,2816]{1,0:T(8,128)(2,1)S(1)}, u32[]{:S(2)}, u32[]{:S(2)}) collective-permute-start(bf16[128,2816]{1,0:T(8,128)(2,1)} %collective-permute-done.13.refs_16_.refs_14_), channel_id=1, source_target_pairs={{0,8},{4,12},{8,0},{12,4},{16,24},{20,28},{24,16},{28,20},{1,9},{5... | collective-permute-start | bytes 2162696 | tf_op jit(solution)/shard_map/ppermute | solution.py:730
  71.7 18.5 %collective-permute-start.19 = (bf16[352,1024]{1,0:T(8,128)(2,1)}, bf16[352,1024]{1,0:T(8,128)(2,1)}, u32[]{:S(2)}, u32[]{:S(2)}) collective-permute-start(bf16[352,1024]{1,0:T(8,128)(2,1)} %constant_dynamic-slice_fusion.1), channel_id=1, source_target_pairs={{0,2},{1,3},{2,0},{3,1},{4,6},{5,7},{6,4},{7,5},{8,10},{9,11},{10,... | collective-permute-start | bytes 2162696 | tf_op jit(solution)/shard_map/ppermute | solution.py:730
  72.2 18.0 %collective-permute-start.22 = (bf16[128,2816]{1,0:T(8,128)(2,1)}, bf16[128,2816]{1,0:T(8,128)(2,1)}, u32[]{:S(2)}, u32[]{:S(2)}) collective-permute-start(bf16[128,2816]{1,0:T(8,128)(2,1)} %collective-permute-done.15.refs_11_.refs_9_), channel_id=1, source_target_pairs={{0,1},{1,0},{2,3},{3,2},{4,5},{5,4},{6,7},{7,6},{8,9},{9,8},{10,11... | collective-permute-start | bytes 2162696 | tf_op jit(solution)/shard_map/ppermute | solution.py:730
  94.1 19.4 %collective-permute-start.27 = (bf16[352,1024]{1,0:T(8,128)(2,1)}, bf16[352,1024]{1,0:T(8,128)(2,1)}, u32[]{:S(2)}, u32[]{:S(2)}) collective-permute-start(bf16[352,1024]{1,0:T(8,128)(2,1)} %collective-permute-done.19.refs_2_), channel_id=1, source_target_pairs={{0,1},{1,0},{2,3},{3,2},{4,5},{5,4},{6,7},{7,6},{8,9},{9,8},{10,11... | collective-permute-start | bytes 2162696 | tf_op jit(solution)/shard_map/ppermute | solution.py:730
  94.4 19.1 %collective-permute-start.26 = (bf16[352,1024]{1,0:T(8,128)(2,1)}, bf16[352,1024]{1,0:T(8,128)(2,1)}, u32[]{:S(2)}, u32[]{:S(2)}) collective-permute-start(bf16[352,1024]{1,0:T(8,128)(2,1)} %collective-permute-done.19.refs_2_), channel_id=1, source_target_pairs={{0,4},{4,0},{8,12},{12,8},{16,20},{20,16},{24,28},{28,24},{1,5},{5... | collective-permute-start | bytes 2162696 | tf_op jit(solution)/shard_map/ppermute | solution.py:730
  138.4 33.8 %collective-permute-start.30 = (bf16[704,1024]{1,0:T(8,128)(2,1)}, bf16[704,1024]{1,0:T(8,128)(2,1)S(1)}, u32[]{:S(2)}, u32[]{:S(2)}) collective-permute-start(bf16[704,1024]{1,0:T(8,128)(2,1)} %get-tuple-element.207), channel_id=1, source_target_pairs={{0,2},{1,3},{2,0},{3,1},{4,6},{5,7},{6,4},{7,5},{8,10},{9,11},{10,... | collective-permute-start | bytes 4325384 | tf_op jit(solution)/shard_map/ppermute | solution.py:730
  153.6 17.9 %collective-permute-start.34 = (bf16[2,256,1024]{2,1,0:T(8,128)(2,1)}, bf16[2,256,1024]{2,1,0:T(8,128)(2,1)S(1)}, u32[]{:S(2)}, u32[]{:S(2)}) collective-permute-start(bf16[2,256,1024]{2,1,0:T(8,128)(2,1)} %get-tuple-element.214), channel_id=1, source_target_pairs={{0,1},{1,0},{2,3},{3,2},{4,5},{5,4},{6,7},{7,6},{8,9},{9,8},{10,11... | collective-permute-start | bytes 3145736 | tf_op jit(solution)/shard_map/ppermute | solution.py:730
  173.3 51.6 %collective-permute-start.37 = (bf16[2,256,2816]{2,1,0:T(8,128)(2,1)}, bf16[2,256,2816]{2,1,0:T(8,128)(2,1)S(1)}, u32[]{:S(2)}, u32[]{:S(2)}) collective-permute-start(bf16[2,256,2816]{2,1,0:T(8,128)(2,1)} %get-tuple-element.237), channel_id=1, source_target_pairs={{0,1},{1,0},{2,3},{3,2},{4,5},{5,4},{6,7},{7,6},{8,9},{9,8},{10,11... | collective-permute-start | bytes 8650760 | tf_op jit(solution)/shard_map/ppermute | solution.py:730
  179.8 45.1 %collective-permute-start.35 = (bf16[256,3840]{1,0:T(8,128)(2,1)}, bf16[256,3840]{1,0:T(8,128)(2,1)}, u32[]{:S(2)}, u32[]{:S(2)}) collective-permute-start(bf16[256,3840]{1,0:T(8,128)(2,1)} %get-tuple-element.232), channel_id=1, source_target_pairs={{0,2},{1,3},{2,0},{3,1},{4,6},{5,7},{6,4},{7,5},{8,10},{9,11},{10,... | collective-permute-start | bytes 5898248 | tf_op jit(solution)/shard_map/ppermute | solution.py:730
  184.9 19.9 %collective-permute-start.36 = (bf16[4,88,1024]{2,1,0:T(8,128)(2,1)}, bf16[4,88,1024]{2,1,0:T(8,128)(2,1)}, u32[]{:S(2)}, u32[]{:S(2)}) collective-permute-start(bf16[4,88,1024]{2,1,0:T(8,128)(2,1)} %get-tuple-element.235), channel_id=1, source_target_pairs={{0,4},{1,9},{2,6},{3,11},{4,0},{5,13},{6,2},{7,15},{8,12},{9,1},{1... | collective-permute-start | bytes 2162696 | tf_op jit(solution)/shard_map/ppermute | solution.py:939
  235.9 30.0 %collective-permute-start.42 = (bf16[4,32,3840]{2,1,0:T(8,128)(2,1)}, bf16[4,32,3840]{2,1,0:T(8,128)(2,1)S(1)}, u32[]{:S(2)}, u32[]{:S(2)}) collective-permute-start(bf16[4,32,3840]{2,1,0:T(8,128)(2,1)} %get-tuple-element.262), channel_id=1, source_target_pairs={{0,4},{1,9},{2,6},{3,11},{4,0},{5,13},{6,2},{7,15},{8,12},{9,1},{1... | collective-permute-start | bytes 2949128 | tf_op jit(solution)/shard_map/ppermute | solution.py:939
  251.7 36.4 %collective-permute-start.50 = (bf16[256,2816]{1,0:T(8,128)(2,1)}, bf16[256,2816]{1,0:T(8,128)(2,1)S(1)}, u32[]{:S(2)}, u32[]{:S(2)}) collective-permute-start(bf16[256,2816]{1,0:T(8,128)(2,1)} %get-tuple-element.281), channel_id=1, source_target_pairs={{0,2},{1,3},{2,0},{3,1},{4,6},{5,7},{6,4},{7,5},{8,10},{9,11},{10,... | collective-permute-start | bytes 4325384 | tf_op jit(solution)/shard_map/ppermute | solution.py:730
  265.9 16.7 %collective-permute-start.44 = (bf16[2,896,256]{2,1,0:T(8,128)(2,1)}, bf16[2,896,256]{2,1,0:T(8,128)(2,1)S(1)}, u32[]{:S(2)}, u32[]{:S(2)}) collective-permute-start(bf16[2,896,256]{2,1,0:T(8,128)(2,1)} %get-tuple-element.265), channel_id=1, source_target_pairs={{0,1},{1,0},{2,3},{3,2},{4,5},{5,4},{6,7},{7,6},{8,9},{9,8},{10,11... | collective-permute-start | bytes 2752520 | tf_op jit(solution)/shard_map/ppermute | solution.py:730
  269.6 12.9 %collective-permute-start.45 = (bf16[2,32,3840]{2,1,0:T(8,128)(2,1)}, bf16[2,32,3840]{2,1,0:T(8,128)(2,1)S(1)}, u32[]{:S(2)}, u32[]{:S(2)}) collective-permute-start(bf16[2,32,3840]{2,1,0:T(8,128)(2,1)} %get-tuple-element.269), channel_id=1, source_target_pairs={{0,8},{1,5},{2,10},{3,7},{4,12},{5,1},{6,14},{7,3},{8,0},{9,13},{1... | collective-permute-start | bytes 1474568 | tf_op jit(solution)/shard_map/ppermute | solution.py:939
  287.1 18.4 %collective-permute-start.49 = (bf16[4,88,1024]{2,1,0:T(8,128)(2,1)}, bf16[4,88,1024]{2,1,0:T(8,128)(2,1)S(1)}, u32[]{:S(2)}, u32[]{:S(2)}) collective-permute-start(bf16[4,88,1024]{2,1,0:T(8,128)(2,1)} %get-tuple-element.293.near), channel_id=1, source_target_pairs={{0,4},{1,9},{2,6},{3,11},{4,0},{5,13},{6,2},{7,15},{8,12},{9,1},{1... | collective-permute-start | bytes 2162696 | tf_op jit(solution)/shard_map/ppermute | solution.py:939
  292.4 14.0 %collective-permute-start.51 = (bf16[4,32,2816]{2,1,0:T(8,128)(2,1)}, bf16[4,32,2816]{2,1,0:T(8,128)(2,1)S(1)}, u32[]{:S(2)}, u32[]{:S(2)}) collective-permute-start(bf16[4,32,2816]{2,1,0:T(8,128)(2,1)} %get-tuple-element.283), channel_id=1, source_target_pairs={{0,4},{1,9},{2,6},{3,11},{4,0},{5,13},{6,2},{7,15},{8,12},{9,1},{1... | collective-permute-start | bytes 2162696 | tf_op jit(solution)/shard_map/ppermute | solution.py:939
  310.2 13.2 %collective-permute-start.54 = (bf16[2,32,2816]{2,1,0:T(8,128)(2,1)}, bf16[2,32,2816]{2,1,0:T(8,128)(2,1)S(1)}, u32[]{:S(2)}, u32[]{:S(2)}) collective-permute-start(bf16[2,32,2816]{2,1,0:T(8,128)(2,1)} %get-tuple-element.292), channel_id=1, source_target_pairs={{0,8},{1,5},{2,10},{3,7},{4,12},{5,1},{6,14},{7,3},{8,0},{9,13},{1... | collective-permute-start | bytes 1081352 | tf_op jit(solution)/shard_map/ppermute | solution.py:939
  326.8 15.4 %collective-permute-start.56 = (bf16[2,32,3840]{2,1,0:T(8,128)(2,1)}, bf16[2,32,3840]{2,1,0:T(8,128)(2,1)S(1)}, u32[]{:S(2)}, u32[]{:S(2)}) collective-permute-start(bf16[2,32,3840]{2,1,0:T(8,128)(2,1)} %get-tuple-element.305.refs_4_), channel_id=1, source_target_pairs={{0,8},{1,5},{2,10},{3,7},{4,12},{5,1},{6,14},{7,3},{8,0},{9,13},{1... | collective-permute-start | bytes 1474568 | tf_op jit(solution)/shard_map/ppermute | solution.py:939
  328.0 14.1 %collective-permute-start.55 = (bf16[4,112,256]{2,1,0:T(8,128)(2,1)}, bf16[4,112,256]{2,1,0:T(8,128)(2,1)S(1)}, u32[]{:S(2)}, u32[]{:S(2)}) collective-permute-start(bf16[4,112,256]{2,1,0:T(8,128)(2,1)} %get-tuple-element.302.refs_0_), channel_id=1, source_target_pairs={{0,8},{1,5},{2,10},{3,7},{4,12},{5,1},{6,14},{7,3},{8,0},{9,13},{1... | collective-permute-start | bytes 688136 | tf_op jit(solution)/shard_map/ppermute | solution.py:939
  345.7 14.7 %collective-permute-start.59 = (bf16[4,32,3840]{2,1,0:T(8,128)(2,1)}, bf16[4,32,3840]{2,1,0:T(8,128)(2,1)S(1)}, u32[]{:S(2)}, u32[]{:S(2)}) collective-permute-start(bf16[4,32,3840]{2,1,0:T(8,128)(2,1)} %get-tuple-element.313.near), channel_id=1, source_target_pairs={{0,4},{1,9},{2,6},{3,11},{4,0},{5,13},{6,2},{7,15},{8,12},{9,1},{1... | collective-permute-start | bytes 2949128 | tf_op jit(solution)/shard_map/ppermute | solution.py:939
  346.6 13.8 %collective-permute-start.58 = (bf16[4,112,256]{2,1,0:T(8,128)(2,1)}, bf16[4,112,256]{2,1,0:T(8,128)(2,1)S(1)}, u32[]{:S(2)}, u32[]{:S(2)}) collective-permute-start(bf16[4,112,256]{2,1,0:T(8,128)(2,1)} %get-tuple-element.309.refs_0_), channel_id=1, source_target_pairs={{0,16},{1,17},{2,18},{3,19},{4,20},{5,21},{6,22},{7,23},{8,24},{9,... | collective-permute-start | bytes 688136 | tf_op jit(solution)/shard_map/ppermute | solution.py:939
  (87 other events, 570.2 us)

commit v7 on v6

--- a/solution.py
+++ b/solution.py
@@ -1078,17 +1078,16 @@
         fac_c = partner(factor_turned, "grp", 1)
         gains_x = partner(own_gains, "grp", 2)
         gains_c = partner(own_gains, "grp", 1)
-        gate_c = partner(gate_weight, "grp", 1)
         gate_half, up_half = take(gate_weight, low), take(up_weight, even)
         out_half, down_half = take(output_weight, low), take(down_weight, low)
         order.phase(
-            fac_x, fac_c, gains_x, gains_c, gate_c, gate_half, up_half, out_half, down_half
+            fac_x, fac_c, gains_x, gains_c, gate_half, up_half, out_half, down_half
         )
         fac_xc = grp(fac_x, 1)
         gains_xc = grp(gains_x, 1)
         gate_x = grp(gate_half, 2)
         up_c = grp(up_weight, 1)
-        out_c = grp(output_weight, 1)
+        gate_c = grp(gate_weight, 1)
         w_fac = [factor_turned, fac_c, fac_x, fac_xc]
         all_gains = [own_gains, gains_c, gains_x, gains_xc]
         fac, kv_own, hid_one, gains = front(
@@ -1099,7 +1098,7 @@
         kv_xc = partner(kv_x, "grp", 1)
         kv = [kv_own, kv_c, kv_x, kv_xc]
 
-        order.phase(gate_x, kv_x, kv_c, kv_xc, up_c, out_c)
+        order.phase(gate_x, kv_x, kv_c, kv_xc, up_c, gate_c)
         up_x = grp(up_half, 2)
         out_x = grp(out_half, 2)
         gate_y = rep(gate_x, 1)
@@ -1119,6 +1118,7 @@
 
         order.phase(down_x, up_z, up_xc, out_y, gate_yc, heads[1][0])
         up_zc = grp(up_z, 1)
+        out_c = grp(output_weight, 1)
         out_xc = grp(out_x, 1)
         out_yc = grp(out_y, 1)
         w_out = [output_weight, out_c, out_x, out_y, out_xc, out_yc]
@@ -1126,7 +1126,7 @@
         w_up = [up_weight, up_c, up_x, up_z, up_xc, up_zc]
         offs_feed = jnp.concatenate([by_side, by_line])
 
-        order.phase(up_zc, out_xc, out_yc)
+        order.phase(up_zc, out_c, out_xc, out_yc)
         odd = me % 2
         place = jnp.stack([lax.axis_index("rep"), 1 + odd, 2 - odd, jnp.full_like(odd, 4)])
         place = place.astype(jnp.int32)

time: 399 us -> 399 us (level)
    unnamed x110 -> x112, local copies, waits for them, and re-layouts: 13.9 us -> 13.5 us
  transfers between devices with their start and end apart: 64 -> 64, of which waited for: 22 -> 24; matrix products, arithmetic and copies ran while one was open for 4% -> 4% of each run, Pallas kernels for 41% -> 41%
where the time goes in v7:
time: 399 us; the launch traced here: 392 us
  Pallas kernels  180 us (45%)
  waiting for transfers between devices  123 us (31%)
  starting transfers between devices  57.7 us (14%)
  local copies, waits for them, and re-layouts  27.4 us (7%)
    ppermute x42, waiting for transfers between devices, partner(): return lax.ppermute(values, axis, [(i, i ^ flip) for i in range(size)])  70 us
    ppermute x22, waiting for transfers between devices, along(): return lax.ppermute(values, ('rep', 'grp'), pairs)  53.1 us
    ppermute x22, starting transfers between devices, along(): return lax.ppermute(values, ('rep', 'grp'), pairs)  30.5 us
    ppermute x42, starting transfers between devices, partner(): return lax.ppermute(values, axis, [(i, i ^ flip) for i in range(size)])  27.1 us
    pallas_call x10, Pallas kernels, batch(): pl.pallas_call(functools.partial(batch_kernel, [task[:2] for task in task...  26.5 us
    pallas_call x2, Pallas kernels, attend_back(): pl.pallas_call(functools.partial(attend_back_kernel, first, heads, final,...  23.3 us
    pallas_call x3, Pallas kernels, products(): pl.pallas_call(functools.partial(products_kernel, cuts), out_shape=[like(...  18.5 us
    pallas_call x3, Pallas kernels, add_pairs(): pl.pallas_call(add_pairs_kernel, grid=(steps,), out_shape=[like(rows, wid...  15.6 us
  transfers between devices with their start and end apart: 64, of which 24 were waited for; matrix products, arithmetic and copies ran while one was open for 4% of the time, Pallas kernels for 41%

profile of v7, /device:TPU:0, one launch (start us, length us, event | category | flops | bytes accessed | tf_op | source)
XLA Modules:
  0.0 392.2 jit_solution(10826075361605552030)
XLA Ops:
  10.8 6.6 %collective-permute-done.refs_2_ = bf16[800,256]{1,0:T(8,128)(2,1)} collective-permute-done((bf16[800,256]{1,0:T(8,128)(2,1)}, bf16[800,256]{1,0:T(8,128)(2,1)}, u32[]{:S(2)}, u32[]{:S(2)}) %collective-permute-start) | collective-permute-done | bytes 409632 | tf_op jit(solution)/shard_map/ppermute | solution.py:730
  23.6 4.7 %front.1 = (bf16[480,384]{1,0:T(8,128)(2,1)}, bf16[320,384]{1,0:T(8,128)(2,1)}, bf16[1024,384]{1,0:T(8,128)(2,1)}, f32[8,1024]{1,0:T(8,128)}) custom-call(s32[8]{0:T(128)} %stack.119.offs, bf16[384,1024]{1,0:T(8,128)(2,1)} %bitcast.42, f32[32,384]{1,0:T(8,128)} %get-tuple-element.326.cos_ref, f32[32,384]{1,0:T(8,128)} %get-tuple-element.325.sin_ref, ...), custom_call_target="tpu_custom_call" | custom-call | flops 6291 | bytes 48 | tf_op jit(solution)/shard_map/front/pallas_call | solution.py:95
  28.7 14.6 %collective-permute-done.7.refs_2_ = bf16[320,384]{1,0:T(8,128)(2,1)S(1)} collective-permute-done((bf16[320,384]{1,0:T(8,128)(2,1)}, bf16[320,384]{1,0:T(8,128)(2,1)S(1)}, u32[]{:S(2)}, u32[]{:S(2)}) %collective-permute-start.7) | collective-permute-done | bytes 245792 | tf_op jit(solution)/shard_map/ppermute | solution.py:730
  49.6 7.5 %attend.2 = (bf16[512,384]{1,0:T(8,128)(2,1)}, f32[8,384]{1,0:T(8,128)}) custom-call(s32[3]{0:T(128)} %pad_add_fusion.info_ref.who, bf16[480,384]{1,0:T(8,128)(2,1)} %get-tuple-element.183.fac_ref, bf16[320,384]{1,0:T(8,128)(2,1)} %get-tuple-element.169.refs_0_, bf16[320,384]{1,0:T(8,128)(2,1)} %copy-done.6, bf16[320,384]{1,0:T(8,128)(2,1)} %copy-done.5, ...), custom_call_target="tpu_custom_call" | custom-call | flops 289910 | bytes 19 | tf_op jit(solution)/shard_map/attend/pallas_call | solution.py:211
  57.1 12.5 %collective-permute-done.13.refs_4_.refs_2_ = bf16[128,1024]{1,0:T(8,128)(2,1)} collective-permute-done((bf16[128,1024]{1,0:T(8,128)(2,1)}, bf16[128,1024]{1,0:T(8,128)(2,1)}, u32[]{:S(2)}, u32[]{:S(2)}) %collective-permute-start.13) | collective-permute-done | bytes 262176 | tf_op jit(solution)/shard_map/ppermute | solution.py:730
  73.4 7.7 %attend.3 = (bf16[512,384]{1,0:T(8,128)(2,1)}, f32[8,384]{1,0:T(8,128)}) custom-call(s32[3]{0:T(128)} %pad_add_fusion.info_ref.who, bf16[480,384]{1,0:T(8,128)(2,1)} %get-tuple-element.183.fac_ref, bf16[320,384]{1,0:T(8,128)(2,1)} %get-tuple-element.169.refs_0_, bf16[320,384]{1,0:T(8,128)(2,1)} %copy-done.6, bf16[320,384]{1,0:T(8,128)(2,1)} %copy-done.5, ...), custom_call_target="tpu_custom_call" | custom-call | flops 289910 | bytes 19 | tf_op jit(solution)/shard_map/attend/pallas_call | solution.py:211
  81.1 7.4 %collective-permute-done.17.refs_17_.refs_15_ = bf16[128,2816]{1,0:T(8,128)(2,1)S(1)} collective-permute-done((bf16[128,2816]{1,0:T(8,128)(2,1)}, bf16[128,2816]{1,0:T(8,128)(2,1)S(1)}, u32[]{:S(2)}, u32[]{:S(2)}) %collective-permute-start.17) | collective-permute-done | bytes 720928 | tf_op jit(solution)/shard_map/ppermute | solution.py:730
  98.5 15.5 %feed.1 = (f32[384,1024]{1,0:T(8,128)}, bf16[1024,384]{1,0:T(8,128)(2,1)}, bf16[384,2816]{1,0:T(8,128)(2,1)}, bf16[384,2816]{1,0:T(8,128)(2,1)}, bf16[384,2816]{1,0:T(8,128)(2,1)}, /*index=5*/bf16[2816,384]{1,0:T(8,128)(2,1)}) custom-call(s32[24]{0:T(128)} %concatenate.3.offs, bf16[384,1024]{1,0:T(8,128)(2,1)} %bitcast.43, ...), custom_call_target="tpu_custom_call" | custom-call | flops 74490 | bytes 237 | tf_op jit(solution)/shard_map/feed/pallas_call | solution.py:461
  114.2 6.2 %products.3 = (bf16[2,704,1024]{2,1,0:T(8,128)(2,1)}, bf16[2,704,1024]{2,1,0:T(8,128)(2,1)}) custom-call(s32[3]{0:T(128)} %pad_add_fusion.info_ref.who, bf16[2816,384]{1,0:T(8,128)(2,1)} %get-tuple-element.195.left, bf16[384,1024]{1,0:T(8,128)(2,1)} %bitcast.45), custom_call_target="tpu_custom_call" | custom-call | tf_op jit(solution)/shard_map/products/pallas_call | solution.py:544
  122.3 9.9 %slopes.1 = (bf16[384,2816]{1,0:T(8,128)(2,1)}, bf16[384,2816]{1,0:T(8,128)(2,1)}) custom-call(s32[12]{0:T(128)} %stack.103.offs, bf16[384,2816]{1,0:T(8,128)(2,1)} %get-tuple-element.200.slope_ref, bf16[384,2816]{1,0:T(8,128)(2,1)} %get-tuple-element.201.lin_ref, bf16[384,1024]{1,0:T(8,128)(2,1)} %bitcast.46, bf16[704,1024]{1,0:T(8,128)(2,1)} %refs_0_.5, ...), custom_call_target="tpu_custom_call" | custom-call | flops 22145 | bytes 144 | tf_op jit(solution)/shard_map/slopes/pallas_call | solution.py:512
  133.8 5.1 %add_pairs.3 = (bf16[704,1024]{1,0:T(8,128)(2,1)}, bf16[704,1024]{1,0:T(8,128)(2,1)}) custom-call(bf16[2,704,1024]{2,1,0:T(8,128)(2,1)} %get-tuple-element.207.refs_0_, bf16[2,704,1024]{2,1,0:T(8,128)(2,1)} %copy-done.14), custom_call_target="tpu_custom_call" | custom-call | tf_op jit(solution)/shard_map/add_pairs/pallas_call | solution.py:771
  141.0 13.7 %middle_grads.1 = (f32[384,1024]{1,0:T(8,128)}, f32[8,1024]{1,0:T(8,128)}, bf16[1024,384]{1,0:T(8,128)(2,1)}, bf16[2,256,1024]{2,1,0:T(8,128)(2,1)}, bf16[2,256,1024]{2,1,0:T(8,128)(2,1)}) custom-call(s32[24]{0:T(128)} %concatenate.3.offs, s32[3]{0:T(128)} %pad_add_fusion.info_ref.who, bf16[384,1024]{1,0:T(8,128)(2,1)} %bitcast.47, ...), custom_call_target="tpu_custom_call" | custom-call | flops 52344 | bytes 158 | tf_op jit(solution)/shard_map/middle_grads/pallas_call | solution.py:605
  154.8 5.9 %products.4 = (bf16[2,256,1024]{2,1,0:T(8,128)(2,1)}, bf16[2,256,1024]{2,1,0:T(8,128)(2,1)}, bf16[2,256,1024]{2,1,0:T(8,128)(2,1)}, bf16[2,256,1024]{2,1,0:T(8,1...) custom-call(s32[3]{0:T(128)} %pad_add_fusion.info_ref.who, ...), custom_call_target="tpu_custom_call" | custom-call | tf_op jit(solution)/shard_map/products/pallas_call | solution.py:544
  161.8 6.4 %products.5 = (bf16[2,256,2816]{2,1,0:T(8,128)(2,1)}, bf16[2,256,2816]{2,1,0:T(8,128)(2,1)}) custom-call(s32[3]{0:T(128)} %pad_add_fusion.info_ref.who, bf16[1024,384]{1,0:T(8,128)(2,1)} %get-tuple-element.217.left, bf16[384,2816]{1,0:T(8,128)(2,1)} %get-tuple-element.203.refs_20_.right), custom_call_target="tpu_custom_call" | custom-call | tf_op jit(solution)/shard_map/products/pallas_call | solution.py:544
  168.2 4.4 %attend_back.2 = (f32[480,384]{1,0:T(8,128)}, f32[4,320,384]{2,1,0:T(8,128)}) custom-call(s32[3]{0:T(128)} %pad_add_fusion.info_ref.who, bf16[480,384]{1,0:T(8,128)(2,1)} %get-tuple-element.183.fac_ref, bf16[1024,384]{1,0:T(8,128)(2,1)} %get-tuple-element.223.grad_ref, bf16[320,384]{1,0:T(8,128)(2,1)} %get-tuple-element.169.refs_0_, ...), custom_call_target="tpu_custom_call" | custom-call | flops 1 | bytes 39 | tf_op jit(solution)/shard_map/attend_back/pallas_call | solution.py:312
  175.2 5.7 %add_pairs.4 = (bf16[256,3840]{1,0:T(8,128)(2,1)}, bf16[256,3840]{1,0:T(8,128)(2,1)}) custom-call(bf16[2,256,1024]{2,1,0:T(8,128)(2,1)} %get-tuple-element.229.refs_0_, bf16[2,256,1024]{2,1,0:T(8,128)(2,1)} %copy-done.24, bf16[2,256,1024]{2,1,0:T(8,128)(2,1)} %get-tuple-element.230.refs_2_, bf16[2,256,1024]{2,1,0:T(8,128)(2,1)} %collective-permute-done.32.refs_3_, ...), custom_call_target="tpu_custom_call" | custom-call | tf_op jit(solution)/shard_map/add_pairs/pallas_call | solution.py:771
  186.6 18.9 %attend_back.3 = (f32[480,384]{1,0:T(8,128)}, bf16[2,320,384]{2,1,0:T(8,128)(2,1)}, bf16[2,320,384]{2,1,0:T(8,128)(2,1)}) custom-call(s32[3]{0:T(128)} %pad_add_fusion.info_ref.who, bf16[480,384]{1,0:T(8,128)(2,1)} %get-tuple-element.183.fac_ref, bf16[1024,384]{1,0:T(8,128)(2,1)} %get-tuple-element.223.grad_ref, ...), custom_call_target="tpu_custom_call" | custom-call | flops 22 | bytes 39 | tf_op jit(solution)/shard_map/attend_back/pallas_call | solution.py:312
  205.5 20.5 %collective-permute-done.35 = bf16[256,3840]{1,0:T(8,128)(2,1)} collective-permute-done((bf16[256,3840]{1,0:T(8,128)(2,1)}, bf16[256,3840]{1,0:T(8,128)(2,1)}, u32[]{:S(2)}, u32[]{:S(2)}) %collective-permute-start.35) | collective-permute-done | bytes 1966112 | tf_op jit(solution)/shard_map/ppermute | solution.py:730
  226.0 3.3 batch.10
  229.8 3.8 halve.4
  233.6 3.3 collective-permute-done.39.refs_3_
  240.5 3.8 collective-permute-start.40
  246.8 4.8 %add_pairs.5 = (bf16[256,2816]{1,0:T(8,128)(2,1)}, bf16[256,2816]{1,0:T(8,128)(2,1)}) custom-call(bf16[2,256,2816]{2,1,0:T(8,128)(2,1)} %get-tuple-element.253.refs_0_, bf16[2,256,2816]{2,1,0:T(8,128)(2,1)} %copy-done.13), custom_call_target="tpu_custom_call" | custom-call | tf_op jit(solution)/shard_map/add_pairs/pallas_call | solution.py:771
  257.6 7.2 %tail.1 = (f32[384,1024]{1,0:T(8,128)}, bf16[2,896,256]{2,1,0:T(8,128)(2,1)}, bf16[2,896,256]{2,1,0:T(8,128)(2,1)}) custom-call(s32[8]{0:T(128)} %stack.119.offs, s32[3]{0:T(128)} %pad_add_fusion.info_ref.who, f32[480,384]{1,0:T(8,128)} %get-tuple-element.225.dq_ref, bf16[320,384]{1,0:T(8,128)(2,1)} %get-tuple-element.258.own_ref, ...), custom_call_target="tpu_custom_call" | custom-call | flops 12582 | bytes 79 | tf_op jit(solution)/shard_map/tail/pallas_call | solution.py:711
  272.9 10.9 %collective-permute-done.46.refs_5_ = bf16[2,88,1024]{2,1,0:T(8,128)(2,1)S(1)} collective-permute-done((bf16[2,88,1024]{2,1,0:T(8,128)(2,1)}, bf16[2,88,1024]{2,1,0:T(8,128)(2,1)S(1)}, u32[]{:S(2)}, u32[]{:S(2)}) %collective-permute-start.46) | collective-permute-done | bytes 360480 | tf_op jit(solution)/shard_map/ppermute | solution.py:939
  285.0 3.4 batch.14
  297.9 8.7 %collective-permute-done.48.refs_5_ = bf16[1,32,3840]{2,1,0:T(8,128)(2,1)S(1)} collective-permute-done((bf16[1,32,3840]{2,1,0:T(8,128)(2,1)S(1)}, bf16[1,32,3840]{2,1,0:T(8,128)(2,1)S(1)}, u32[]{:S(2)}, u32[]{:S(2)}) %collective-permute-start.48) | collective-permute-done | bytes 245792 | tf_op jit(solution)/shard_map/ppermute | solution.py:939
  320.0 4.6 %collective-permute-done.52.refs_1_ = bf16[4,112,256]{2,1,0:T(8,128)(2,1)S(1)} collective-permute-done((bf16[4,112,256]{2,1,0:T(8,128)(2,1)}, bf16[4,112,256]{2,1,0:T(8,128)(2,1)S(1)}, u32[]{:S(2)}, u32[]{:S(2)}) %collective-permute-start.52) | collective-permute-done | bytes 229408 | tf_op jit(solution)/shard_map/ppermute | solution.py:939
  332.3 9.9 %collective-permute-done.57.refs_3_ = bf16[1,32,2816]{2,1,0:T(8,128)(2,1)S(1)} collective-permute-done((bf16[1,32,2816]{2,1,0:T(8,128)(2,1)}, bf16[1,32,2816]{2,1,0:T(8,128)(2,1)S(1)}, u32[]{:S(2)}, u32[]{:S(2)}) %collective-permute-start.57) | collective-permute-done | bytes 180256 | tf_op jit(solution)/shard_map/ppermute | solution.py:939
  350.8 8.0 %output.1 = bf16[384,1024]{1,0:T(8,128)(2,1)} custom-call(s32[12]{0:T(128)} %stack.103.offs, bf16[384,2816]{1,0:T(8,128)(2,1)} %get-tuple-element.303.act_ref, f32[384,1024]{1,0:T(8,128)} %get-tuple-element.194.refs_22_.mid_ref, bf16[704,1024]{1,0:T(8,128)(2,1)} %refs_0_.5, bf16[704,1024]{1,0:T(8,128)(2,1)} %copy-done.4, ...), custom_call_target="tpu_custom_call" | custom-call | flops 22145 | bytes 79 | tf_op jit(solution)/shard_map/output/pallas_call | solution.py:656
  368.0 3.7 finish.5
  382.9 5.1 %collective-permute-done.63.far = bf16[4,32,2816]{2,1,0:T(8,128)(2,1)S(1)} collective-permute-done((bf16[4,32,2816]{2,1,0:T(8,128)(2,1)}, bf16[4,32,2816]{2,1,0:T(8,128)(2,1)S(1)}, u32[]{:S(2)}, u32[]{:S(2)}) %collective-permute-start.63) | collective-permute-done | bytes 720928 | tf_op jit(solution)/shard_map/ppermute | solution.py:939
  (259 shorter events, 136.9 us)
Async XLA Ops:
  17.4 27.4 %collective-permute-start.10 = (bf16[256,2816]{1,0:T(8,128)(2,1)}, bf16[256,2816]{1,0:T(8,128)(2,1)}, u32[]{:S(2)}, u32[]{:S(2)}) collective-permute-start(bf16[256,2816]{1,0:T(8,128)(2,1)} %refs_12_.1), channel_id=1, source_target_pairs={{0,1},{1,0},{2,3},{3,2},{4,5},{5,4},{6,7},{7,6},{8,9},{9,8},{10,11... | collective-permute-start | bytes 4325384 | tf_op jit(solution)/shard_map/ppermute | solution.py:730
  17.4 27.4 %collective-permute-start.11 = (bf16[256,2816]{1,0:T(8,128)(2,1)S(1)}, bf16[256,2816]{1,0:T(8,128)(2,1)}, u32[]{:S(2)}, u32[]{:S(2)}) collective-permute-start(bf16[256,2816]{1,0:T(8,128)(2,1)S(1)} %copy-done.3), channel_id=1, source_target_pairs={{0,1},{1,0},{2,3},{3,2},{4,5},{5,4},{6,7},{7,6},{8,9},{9,8},{10,11... | collective-permute-start | bytes 4325384 | tf_op jit(solution)/shard_map/ppermute | solution.py:730
  19.2 24.0 %collective-permute-start.4 = (bf16[128,2816]{1,0:T(8,128)(2,1)}, bf16[128,2816]{1,0:T(8,128)(2,1)}, u32[]{:S(2)}, u32[]{:S(2)}) collective-permute-start(bf16[128,2816]{1,0:T(8,128)(2,1)} %get-tuple-element.165), channel_id=1, source_target_pairs={{0,2},{1,3},{2,0},{3,1},{4,6},{5,7},{6,4},{7,5},{8,10},{9,11},{10,... | collective-permute-start | bytes 2162696 | tf_op jit(solution)/shard_map/ppermute | solution.py:730
  28.4 14.9 %collective-permute-start.7 = (bf16[320,384]{1,0:T(8,128)(2,1)}, bf16[320,384]{1,0:T(8,128)(2,1)S(1)}, u32[]{:S(2)}, u32[]{:S(2)}) collective-permute-start(bf16[320,384]{1,0:T(8,128)(2,1)} %get-tuple-element.169.refs_0_), channel_id=1, source_target_pairs={{0,2},{1,3},{2,0},{3,1},{4,6},{5,7},{6,4},{7,5},{8,10},{9,11},{10,... | collective-permute-start | bytes 737288 | tf_op jit(solution)/shard_map/ppermute | solution.py:730
  28.7 14.6 %collective-permute-start.8 = (bf16[320,384]{1,0:T(8,128)(2,1)}, bf16[320,384]{1,0:T(8,128)(2,1)S(1)}, u32[]{:S(2)}, u32[]{:S(2)}) collective-permute-start(bf16[320,384]{1,0:T(8,128)(2,1)} %get-tuple-element.169.refs_0_), channel_id=1, source_target_pairs={{0,1},{1,0},{2,3},{3,2},{4,5},{5,4},{6,7},{7,6},{8,9},{9,8},{10,11... | collective-permute-start | bytes 737288 | tf_op jit(solution)/shard_map/ppermute | solution.py:730
  44.8 24.8 %collective-permute-start.16 = (bf16[704,1024]{1,0:T(8,128)(2,1)S(1)}, bf16[704,1024]{1,0:T(8,128)(2,1)S(1)}, u32[]{:S(2)}, u32[]{:S(2)}) collective-permute-start(bf16[704,1024]{1,0:T(8,128)(2,1)S(1)} %copy-done.2), channel_id=1, source_target_pairs={{0,1},{1,0},{2,3},{3,2},{4,5},{5,4},{6,7},{7,6},{8,9},{9,8},{10,11... | collective-permute-start | bytes 4325384 | tf_op jit(solution)/shard_map/ppermute | solution.py:730
  45.5 24.1 %collective-permute-start.12 = (bf16[128,2816]{1,0:T(8,128)(2,1)}, bf16[128,2816]{1,0:T(8,128)(2,1)}, u32[]{:S(2)}, u32[]{:S(2)}) collective-permute-start(bf16[128,2816]{1,0:T(8,128)(2,1)} %get-tuple-element.172), channel_id=1, source_target_pairs={{0,2},{1,3},{2,0},{3,1},{4,6},{5,7},{6,4},{7,5},{8,10},{9,11},{10,... | collective-permute-start | bytes 2162696 | tf_op jit(solution)/shard_map/ppermute | solution.py:730
  45.8 23.8 %collective-permute-start.15 = (bf16[128,2816]{1,0:T(8,128)(2,1)}, bf16[128,2816]{1,0:T(8,128)(2,1)}, u32[]{:S(2)}, u32[]{:S(2)}) collective-permute-start(bf16[128,2816]{1,0:T(8,128)(2,1)} %collective-permute-done.4.refs_10_.refs_8_), channel_id=1, source_target_pairs={{0,1},{1,0},{2,3},{3,2},{4,5},{5,4},{6,7},{7,6},{8,9},{9,8},{10,11... | collective-permute-start | bytes 2162696 | tf_op jit(solution)/shard_map/ppermute | solution.py:730
  45.8 23.8 %collective-permute-start.14 = (bf16[128,2816]{1,0:T(8,128)(2,1)}, bf16[128,2816]{1,0:T(8,128)(2,1)}, u32[]{:S(2)}, u32[]{:S(2)}) collective-permute-start(bf16[128,2816]{1,0:T(8,128)(2,1)} %collective-permute-done.4.refs_10_.refs_8_), channel_id=1, source_target_pairs={{0,4},{4,0},{8,12},{12,8},{16,20},{20,16},{24,28},{28,24},{1,5},{5... | collective-permute-start | bytes 2162696 | tf_op jit(solution)/shard_map/ppermute | solution.py:730
  47.5 22.1 %collective-permute-start.13 = (bf16[128,1024]{1,0:T(8,128)(2,1)}, bf16[128,1024]{1,0:T(8,128)(2,1)}, u32[]{:S(2)}, u32[]{:S(2)}) collective-permute-start(bf16[128,1024]{1,0:T(8,128)(2,1)} %constant_dynamic-slice_fusion.2), channel_id=1, source_target_pairs={{0,2},{1,3},{2,0},{3,1},{4,6},{5,7},{6,4},{7,5},{8,10},{9,11},{10,... | collective-permute-start | bytes 786440 | tf_op jit(solution)/shard_map/ppermute | solution.py:730
  69.7 18.8 %collective-permute-start.17 = (bf16[128,2816]{1,0:T(8,128)(2,1)}, bf16[128,2816]{1,0:T(8,128)(2,1)S(1)}, u32[]{:S(2)}, u32[]{:S(2)}) collective-permute-start(bf16[128,2816]{1,0:T(8,128)(2,1)} %collective-permute-done.12.refs_16_.refs_14_), channel_id=1, source_target_pairs={{0,8},{4,12},{8,0},{12,4},{16,24},{20,28},{24,16},{28,20},{1,9},{5... | collective-permute-start | bytes 2162696 | tf_op jit(solution)/shard_map/ppermute | solution.py:730
  71.3 18.5 %collective-permute-start.18 = (bf16[352,1024]{1,0:T(8,128)(2,1)}, bf16[352,1024]{1,0:T(8,128)(2,1)}, u32[]{:S(2)}, u32[]{:S(2)}) collective-permute-start(bf16[352,1024]{1,0:T(8,128)(2,1)} %constant_dynamic-slice_fusion.1), channel_id=1, source_target_pairs={{0,2},{1,3},{2,0},{3,1},{4,6},{5,7},{6,4},{7,5},{8,10},{9,11},{10,... | collective-permute-start | bytes 2162696 | tf_op jit(solution)/shard_map/ppermute | solution.py:730
  71.9 18.0 %collective-permute-start.21 = (bf16[128,2816]{1,0:T(8,128)(2,1)}, bf16[128,2816]{1,0:T(8,128)(2,1)}, u32[]{:S(2)}, u32[]{:S(2)}) collective-permute-start(bf16[128,2816]{1,0:T(8,128)(2,1)} %collective-permute-done.14.refs_11_.refs_9_), channel_id=1, source_target_pairs={{0,1},{1,0},{2,3},{3,2},{4,5},{5,4},{6,7},{7,6},{8,9},{9,8},{10,11... | collective-permute-start | bytes 2162696 | tf_op jit(solution)/shard_map/ppermute | solution.py:730
  94.7 19.3 %collective-permute-start.27 = (bf16[352,1024]{1,0:T(8,128)(2,1)}, bf16[352,1024]{1,0:T(8,128)(2,1)}, u32[]{:S(2)}, u32[]{:S(2)}) collective-permute-start(bf16[352,1024]{1,0:T(8,128)(2,1)} %collective-permute-done.18.refs_2_), channel_id=1, source_target_pairs={{0,1},{1,0},{2,3},{3,2},{4,5},{5,4},{6,7},{7,6},{8,9},{9,8},{10,11... | collective-permute-start | bytes 2162696 | tf_op jit(solution)/shard_map/ppermute | solution.py:730
  94.9 19.2 %collective-permute-start.26 = (bf16[352,1024]{1,0:T(8,128)(2,1)}, bf16[352,1024]{1,0:T(8,128)(2,1)}, u32[]{:S(2)}, u32[]{:S(2)}) collective-permute-start(bf16[352,1024]{1,0:T(8,128)(2,1)} %collective-permute-done.18.refs_2_), channel_id=1, source_target_pairs={{0,4},{4,0},{8,12},{12,8},{16,20},{20,16},{24,28},{28,24},{1,5},{5... | collective-permute-start | bytes 2162696 | tf_op jit(solution)/shard_map/ppermute | solution.py:730
  138.9 34.1 %collective-permute-start.30 = (bf16[704,1024]{1,0:T(8,128)(2,1)}, bf16[704,1024]{1,0:T(8,128)(2,1)S(1)}, u32[]{:S(2)}, u32[]{:S(2)}) collective-permute-start(bf16[704,1024]{1,0:T(8,128)(2,1)} %get-tuple-element.209), channel_id=1, source_target_pairs={{0,2},{1,3},{2,0},{3,1},{4,6},{5,7},{6,4},{7,5},{8,10},{9,11},{10,... | collective-permute-start | bytes 4325384 | tf_op jit(solution)/shard_map/ppermute | solution.py:730
  154.7 17.9 %collective-permute-start.34 = (bf16[2,256,1024]{2,1,0:T(8,128)(2,1)}, bf16[2,256,1024]{2,1,0:T(8,128)(2,1)S(1)}, u32[]{:S(2)}, u32[]{:S(2)}) collective-permute-start(bf16[2,256,1024]{2,1,0:T(8,128)(2,1)} %get-tuple-element.216), channel_id=1, source_target_pairs={{0,1},{1,0},{2,3},{3,2},{4,5},{5,4},{6,7},{7,6},{8,9},{9,8},{10,11... | collective-permute-start | bytes 3145736 | tf_op jit(solution)/shard_map/ppermute | solution.py:730
  174.4 51.6 %collective-permute-start.37 = (bf16[2,256,2816]{2,1,0:T(8,128)(2,1)}, bf16[2,256,2816]{2,1,0:T(8,128)(2,1)S(1)}, u32[]{:S(2)}, u32[]{:S(2)}) collective-permute-start(bf16[2,256,2816]{2,1,0:T(8,128)(2,1)} %get-tuple-element.239), channel_id=1, source_target_pairs={{0,1},{1,0},{2,3},{3,2},{4,5},{5,4},{6,7},{7,6},{8,9},{9,8},{10,11... | collective-permute-start | bytes 8650760 | tf_op jit(solution)/shard_map/ppermute | solution.py:730
  180.9 45.1 %collective-permute-start.35 = (bf16[256,3840]{1,0:T(8,128)(2,1)}, bf16[256,3840]{1,0:T(8,128)(2,1)}, u32[]{:S(2)}, u32[]{:S(2)}) collective-permute-start(bf16[256,3840]{1,0:T(8,128)(2,1)} %get-tuple-element.234), channel_id=1, source_target_pairs={{0,2},{1,3},{2,0},{3,1},{4,6},{5,7},{6,4},{7,5},{8,10},{9,11},{10,... | collective-permute-start | bytes 5898248 | tf_op jit(solution)/shard_map/ppermute | solution.py:730
  185.6 20.0 %collective-permute-start.36 = (bf16[4,88,1024]{2,1,0:T(8,128)(2,1)}, bf16[4,88,1024]{2,1,0:T(8,128)(2,1)}, u32[]{:S(2)}, u32[]{:S(2)}) collective-permute-start(bf16[4,88,1024]{2,1,0:T(8,128)(2,1)} %get-tuple-element.237), channel_id=1, source_target_pairs={{0,4},{1,9},{2,6},{3,11},{4,0},{5,13},{6,2},{7,15},{8,12},{9,1},{1... | collective-permute-start | bytes 2162696 | tf_op jit(solution)/shard_map/ppermute | solution.py:939
  237.0 30.2 %collective-permute-start.42 = (bf16[4,32,3840]{2,1,0:T(8,128)(2,1)}, bf16[4,32,3840]{2,1,0:T(8,128)(2,1)S(1)}, u32[]{:S(2)}, u32[]{:S(2)}) collective-permute-start(bf16[4,32,3840]{2,1,0:T(8,128)(2,1)} %get-tuple-element.264), channel_id=1, source_target_pairs={{0,4},{1,9},{2,6},{3,11},{4,0},{5,13},{6,2},{7,15},{8,12},{9,1},{1... | collective-permute-start | bytes 2949128 | tf_op jit(solution)/shard_map/ppermute | solution.py:939
  240.5 12.3 %collective-permute-start.40 = (bf16[320,384]{1,0:T(8,128)(2,1)}, bf16[320,384]{1,0:T(8,128)(2,1)S(1)}, u32[]{:S(2)}, u32[]{:S(2)}) collective-permute-start(bf16[320,384]{1,0:T(8,128)(2,1)} %get-tuple-element.251), channel_id=1, source_target_pairs={{0,2},{1,3},{2,0},{3,1},{4,6},{5,7},{6,4},{7,5},{8,10},{9,11},{10,... | collective-permute-start | bytes 737288 | tf_op jit(solution)/shard_map/ppermute | solution.py:730
  252.8 36.7 %collective-permute-start.50 = (bf16[256,2816]{1,0:T(8,128)(2,1)}, bf16[256,2816]{1,0:T(8,128)(2,1)S(1)}, u32[]{:S(2)}, u32[]{:S(2)}) collective-permute-start(bf16[256,2816]{1,0:T(8,128)(2,1)} %get-tuple-element.283), channel_id=1, source_target_pairs={{0,2},{1,3},{2,0},{3,1},{4,6},{5,7},{6,4},{7,5},{8,10},{9,11},{10,... | collective-permute-start | bytes 4325384 | tf_op jit(solution)/shard_map/ppermute | solution.py:730
  267.1 16.7 %collective-permute-start.44 = (bf16[2,896,256]{2,1,0:T(8,128)(2,1)}, bf16[2,896,256]{2,1,0:T(8,128)(2,1)S(1)}, u32[]{:S(2)}, u32[]{:S(2)}) collective-permute-start(bf16[2,896,256]{2,1,0:T(8,128)(2,1)} %get-tuple-element.267), channel_id=1, source_target_pairs={{0,1},{1,0},{2,3},{3,2},{4,5},{5,4},{6,7},{7,6},{8,9},{9,8},{10,11... | collective-permute-start | bytes 2752520 | tf_op jit(solution)/shard_map/ppermute | solution.py:730
  270.9 12.9 %collective-permute-start.45 = (bf16[2,32,3840]{2,1,0:T(8,128)(2,1)}, bf16[2,32,3840]{2,1,0:T(8,128)(2,1)S(1)}, u32[]{:S(2)}, u32[]{:S(2)}) collective-permute-start(bf16[2,32,3840]{2,1,0:T(8,128)(2,1)} %get-tuple-element.271), channel_id=1, source_target_pairs={{0,8},{1,5},{2,10},{3,7},{4,12},{5,1},{6,14},{7,3},{8,0},{9,13},{1... | collective-permute-start | bytes 1474568 | tf_op jit(solution)/shard_map/ppermute | solution.py:939
  288.4 18.3 %collective-permute-start.49 = (bf16[4,88,1024]{2,1,0:T(8,128)(2,1)}, bf16[4,88,1024]{2,1,0:T(8,128)(2,1)S(1)}, u32[]{:S(2)}, u32[]{:S(2)}) collective-permute-start(bf16[4,88,1024]{2,1,0:T(8,128)(2,1)} %get-tuple-element.295.near), channel_id=1, source_target_pairs={{0,4},{1,9},{2,6},{3,11},{4,0},{5,13},{6,2},{7,15},{8,12},{9,1},{1... | collective-permute-start | bytes 2162696 | tf_op jit(solution)/shard_map/ppermute | solution.py:939
  293.8 13.9 %collective-permute-start.51 = (bf16[4,32,2816]{2,1,0:T(8,128)(2,1)}, bf16[4,32,2816]{2,1,0:T(8,128)(2,1)S(1)}, u32[]{:S(2)}, u32[]{:S(2)}) collective-permute-start(bf16[4,32,2816]{2,1,0:T(8,128)(2,1)} %get-tuple-element.285), channel_id=1, source_target_pairs={{0,4},{1,9},{2,6},{3,11},{4,0},{5,13},{6,2},{7,15},{8,12},{9,1},{1... | collective-permute-start | bytes 2162696 | tf_op jit(solution)/shard_map/ppermute | solution.py:939
  311.5 13.1 %collective-permute-start.54 = (bf16[2,32,2816]{2,1,0:T(8,128)(2,1)}, bf16[2,32,2816]{2,1,0:T(8,128)(2,1)S(1)}, u32[]{:S(2)}, u32[]{:S(2)}) collective-permute-start(bf16[2,32,2816]{2,1,0:T(8,128)(2,1)} %get-tuple-element.294), channel_id=1, source_target_pairs={{0,8},{1,5},{2,10},{3,7},{4,12},{5,1},{6,14},{7,3},{8,0},{9,13},{1... | collective-permute-start | bytes 1081352 | tf_op jit(solution)/shard_map/ppermute | solution.py:939
  327.9 15.4 %collective-permute-start.56 = (bf16[2,32,3840]{2,1,0:T(8,128)(2,1)}, bf16[2,32,3840]{2,1,0:T(8,128)(2,1)S(1)}, u32[]{:S(2)}, u32[]{:S(2)}) collective-permute-start(bf16[2,32,3840]{2,1,0:T(8,128)(2,1)} %get-tuple-element.307.refs_4_), channel_id=1, source_target_pairs={{0,8},{1,5},{2,10},{3,7},{4,12},{5,1},{6,14},{7,3},{8,0},{9,13},{1... | collective-permute-start | bytes 1474568 | tf_op jit(solution)/shard_map/ppermute | solution.py:939
  329.2 14.0 %collective-permute-start.55 = (bf16[4,112,256]{2,1,0:T(8,128)(2,1)}, bf16[4,112,256]{2,1,0:T(8,128)(2,1)S(1)}, u32[]{:S(2)}, u32[]{:S(2)}) collective-permute-start(bf16[4,112,256]{2,1,0:T(8,128)(2,1)} %get-tuple-element.304.refs_0_), channel_id=1, source_target_pairs={{0,8},{1,5},{2,10},{3,7},{4,12},{5,1},{6,14},{7,3},{8,0},{9,13},{1... | collective-permute-start | bytes 688136 | tf_op jit(solution)/shard_map/ppermute | solution.py:939
  346.8 14.8 %collective-permute-start.59 = (bf16[4,32,3840]{2,1,0:T(8,128)(2,1)}, bf16[4,32,3840]{2,1,0:T(8,128)(2,1)S(1)}, u32[]{:S(2)}, u32[]{:S(2)}) collective-permute-start(bf16[4,32,3840]{2,1,0:T(8,128)(2,1)} %get-tuple-element.315.near), channel_id=1, source_target_pairs={{0,4},{1,9},{2,6},{3,11},{4,0},{5,13},{6,2},{7,15},{8,12},{9,1},{1... | collective-permute-start | bytes 2949128 | tf_op jit(solution)/shard_map/ppermute | solution.py:939
  347.8 13.8 %collective-permute-start.58 = (bf16[4,112,256]{2,1,0:T(8,128)(2,1)}, bf16[4,112,256]{2,1,0:T(8,128)(2,1)S(1)}, u32[]{:S(2)}, u32[]{:S(2)}) collective-permute-start(bf16[4,112,256]{2,1,0:T(8,128)(2,1)} %get-tuple-element.311.refs_0_), channel_id=1, source_target_pairs={{0,16},{1,17},{2,18},{3,19},{4,20},{5,21},{6,22},{7,23},{8,24},{9,... | collective-permute-start | bytes 688136 | tf_op jit(solution)/shard_map/ppermute | solution.py:939
  (88 other events, 607.4 us)
